TPU v7x, 32 devices: a whole 2x2x4 slice. The times are simulated.
32 devices in a mesh: fsdp: 4 (over x, core), ctx: 4 (over z), tp: 2 (over y).
Axes of the slice: x: 2, y: 2, z: 4, core: 2. Of those that a mesh axis runs over, the one named last changes fastest.
Arguments:
- tokens: bfloat16 [6144, 1536], P(('fsdp', 'ctx')), may hold values from -6 to 6
- out_grad: bfloat16 [6144, 1536], P(('fsdp', 'ctx')), may hold values from -6 to 6
- lengths: int32 [4, 4], P('fsdp'), may hold values from 1 to 1344, 1536 in all within a row
- routes: int32 [6144, 8], P(('fsdp', 'ctx')), may hold values from 0 to 15, all different within a row; in each aligned block of 384 rows (0 to 383, 384 to 767, ...) at most 240 rows name the same one
- gate_weights: float32 [6144, 8], P(('fsdp', 'ctx')), may hold values from 0.2 to 0.6
- qkv_weight: float32 [1536, 2560], P(('fsdp', 'ctx'), 'tp'), may hold values from -0.15625 to 0.15625
- out_weight: float32 [1536, 1536], P('tp', ('fsdp', 'ctx')), may hold values from -6 to 6
- norm_gains: float32 [2, 1536], P(None, ('fsdp', 'ctx')), may hold values from 0.5 to 1.5
- expert_in: float32 [16, 2, 1536, 512], P(('fsdp', 'ctx'), None, None, 'tp'), may hold values from -0.15625 to 0.15625
- expert_down: float32 [16, 512, 1536], P(('fsdp', 'ctx'), 'tp'), may hold values from -0.25 to 0.25
- qkv_moment: float32 [1536, 2560], P(('fsdp', 'ctx'), 'tp'), may hold values from -448 to 448
- qkv_average: float32 [1536, 2560], P(('fsdp', 'ctx'), 'tp'), may hold values from -0.15625 to 0.15625
- out_moment: float32 [1536, 1536], P('tp', ('fsdp', 'ctx')), may hold values from -16 to 16
- out_average: float32 [1536, 1536], P('tp', ('fsdp', 'ctx')), may hold values from -6 to 6
- gain_moment: float32 [2, 1536], P(None, ('fsdp', 'ctx')), may hold values from -448 to 448
- gain_average: float32 [2, 1536], P(None, ('fsdp', 'ctx')), may hold values from 0.5 to 1.5
- in_moment: float32 [16, 2, 1536, 512], P(('fsdp', 'ctx'), None, None, 'tp'), may hold values from -96 to 96
- in_average: float32 [16, 2, 1536, 512], P(('fsdp', 'ctx'), None, None, 'tp'), may hold values from -0.15625 to 0.15625
- down_moment: float32 [16, 512, 1536], P(('fsdp', 'ctx'), 'tp'), may hold values from -64 to 64
- down_average: float32 [16, 512, 1536], P(('fsdp', 'ctx'), 'tp'), may hold values from -0.25 to 0.25
Outputs:
- block_out: bfloat16 [6144, 1536], P(('fsdp', 'ctx'))
- in_grad: bfloat16 [6144, 1536], P(('fsdp', 'ctx'))
- qkv_moment_new: float32 [1536, 2560], P(('fsdp', 'ctx'), 'tp')
- qkv_average_new: float32 [1536, 2560], P(('fsdp', 'ctx'), 'tp')
- qkv_weight_new: float32 [1536, 2560], P(('fsdp', 'ctx'), 'tp')
- out_moment_new: float32 [1536, 1536], P('tp', ('fsdp', 'ctx'))
- out_average_new: float32 [1536, 1536], P('tp', ('fsdp', 'ctx'))
- out_weight_new: float32 [1536, 1536], P('tp', ('fsdp', 'ctx'))
- gain_moment_new: float32 [2, 1536], P(None, ('fsdp', 'ctx'))
- gain_average_new: float32 [2, 1536], P(None, ('fsdp', 'ctx'))
- gain_weight_new: float32 [2, 1536], P(None, ('fsdp', 'ctx'))
- in_moment_new: float32 [16, 2, 1536, 512], P(('fsdp', 'ctx'), None, None, 'tp')
- in_average_new: float32 [16, 2, 1536, 512], P(('fsdp', 'ctx'), None, None, 'tp')
- in_weight_new: float32 [16, 2, 1536, 512], P(('fsdp', 'ctx'), None, None, 'tp')
- down_moment_new: float32 [16, 512, 1536], P(('fsdp', 'ctx'), 'tp')
- down_average_new: float32 [16, 512, 1536], P(('fsdp', 'ctx'), 'tp')
- down_weight_new: float32 [16, 512, 1536], P(('fsdp', 'ctx'), 'tp')
Inputs may be any that keep to these rules, and one draw needn't show every extreme that they name: `lengths`: row f lists the documents of the packed stream of fsdp index f in order; they sum to 1536. `routes`: among the 384 rows of one device no expert is named more than 240 times; in some device's rows some expert is named exactly 240 times.
All inputs are finite; a program needn't handle non-finite values.
Results may differ from a plain program's by a relative error of at most 0.02.
Values may be sent and summed in bfloat16 or wider, within the bound.
No kernel may reach another device: no remote copies, remote signals or barrier semaphores. Data moves between devices by JAX's collectives and lax.ppermute only.
A program may use at most 256 MiB of HBM per device.

v0:
```python
import math

import jax
import jax.numpy as jnp
from jax import lax
from jax.sharding import PartitionSpec as P

HD = 64
GROUP = 3


EPSILON = 1e-05
ROPE_BASE = 10000.0
MOMENTUM = 0.9
AVERAGE = 0.7
RATE_QKV = 7e-05
RATE_OUT = 0.15
RATE_GAIN = 0.0005
RATE_IN = 0.0004
RATE_DOWN = 0.001


def rotate(values, position, direction):
    half_width = values.shape[-1] // 2
    frequency = jnp.exp(
        jnp.arange(half_width, dtype=jnp.float32) * (-2.0 * math.log(ROPE_BASE) / values.shape[-1])
    )
    angles = position.astype(jnp.float32)[:, None] * frequency[None, :]
    cosine = jnp.cos(angles)[:, None, :]
    sine_part = direction * jnp.sin(angles)[:, None, :]
    first_half = values[..., :half_width]
    second = values[..., half_width:]
    return jnp.concatenate(
        [first_half * cosine - second * sine_part, second * cosine + first_half * sine_part],
        axis=-1,
    )


def doc_positions(lengths_row, places):
    doc_ends = jnp.cumsum(lengths_row)
    passed = places[:, None] >= doc_ends[None, :]
    segment = jnp.sum(passed.astype(jnp.int32), axis=1)
    doc_start = jnp.sum(jnp.where(passed, lengths_row[None, :], 0), axis=1)
    return (segment, places - doc_start)


def contract_rows(left_mat, right_mat):
    return lax.dot_general(
        left_mat, right_mat, (((0,), (0,)), ((), ())), preferred_element_type=jnp.float32
    )


def contract_cols(left_mat, right_mat):
    return lax.dot_general(
        left_mat, right_mat, (((1,), (1,)), ((), ())), preferred_element_type=jnp.float32
    )


def norm_back(grad_out, normed, inverse, gain_row):
    scaled = grad_out * gain_row
    return inverse * (scaled - normed * jnp.mean(scaled * normed, axis=-1, keepdims=True))


def combine(returned, slot_flat, gate_weights):
    flat_rows = returned.reshape(-1, returned.shape[-1])
    picked = jnp.take(flat_rows, slot_flat, axis=0).astype(jnp.float32)
    picked = picked.reshape(gate_weights.shape[0], gate_weights.shape[1], -1)
    return jnp.sum(picked * gate_weights[:, :, None], axis=1)


def advance(weight, gradient, moment, average, step_rate):
    moment_new = MOMENTUM * moment + gradient
    weight_new = weight - step_rate * (gradient + MOMENTUM * moment_new)
    average_new = AVERAGE * average + (1.0 - AVERAGE) * weight_new
    return (moment_new, average_new, weight_new)


def per_device(
    tokens,
    out_grad,
    lengths,
    routes,
    gate_weights,
    qkv_weight,
    out_weight,
    norm_gains,
    expert_in,
    expert_down,
    qkv_moment,
    qkv_average,
    out_moment,
    out_average,
    gain_moment,
    gain_average,
    in_moment,
    in_average,
    down_moment,
    down_average,
):
    tok_rows, model_width = tokens.shape
    top_count = routes.shape[1]
    n_ctx = lax.axis_size("ctx")
    experts = lax.axis_size(("fsdp", "ctx"))
    capacity = min(tok_rows, tok_rows * top_count * 5 // (4 * experts))
    seq_len = tok_rows * n_ctx
    score_scale = HD ** (-0.5)
    qkv_local, out_local, gain_local = (
        lax.all_gather(qkv_weight.astype(jnp.bfloat16), ("fsdp", "ctx"), axis=0, tiled=True),
        lax.all_gather(out_weight.astype(jnp.bfloat16), ("fsdp", "ctx"), axis=1, tiled=True),
        lax.all_gather(norm_gains.astype(jnp.bfloat16), ("fsdp", "ctx"), axis=1, tiled=True),
    )
    gain_one = gain_local[0].astype(jnp.float32)
    gain_two = gain_local[1].astype(jnp.float32)
    places = jnp.arange(seq_len, dtype=jnp.int32)
    seg_all, pos_all = doc_positions(lengths[0], places)
    first_row = lax.axis_index("ctx") * tok_rows
    seg_query = lax.dynamic_slice_in_dim(seg_all, first_row, tok_rows)
    pos_query = lax.dynamic_slice_in_dim(pos_all, first_row, tok_rows)
    place_query = first_row + jnp.arange(tok_rows, dtype=jnp.int32)
    allowed = (seg_query[:, None] == seg_all[None, :]) & (places[None, :] <= place_query[:, None])
    inputs = tokens.astype(jnp.float32)
    inverse_one = lax.rsqrt(jnp.mean(inputs * inputs, axis=-1, keepdims=True) + EPSILON)
    normed_one = inputs * inverse_one
    normed_low = (normed_one * gain_one).astype(jnp.bfloat16)
    projected = jnp.dot(normed_low, qkv_local, preferred_element_type=jnp.float32)
    kv_local = projected.shape[1] // ((GROUP + 2) * HD)
    heads_local = kv_local * GROUP
    pieces = projected.reshape(tok_rows, kv_local, GROUP + 2, HD)
    queries = rotate(
        pieces[:, :, :GROUP, :].reshape(tok_rows, heads_local, HD), pos_query, 1.0
    ).astype(jnp.bfloat16)
    keys_own = rotate(pieces[:, :, GROUP, :], pos_query, 1.0).astype(jnp.bfloat16)
    values_own = pieces[:, :, GROUP + 1, :].astype(jnp.bfloat16)
    keys_all, values_all = (
        lax.all_gather(keys_own.reshape(tok_rows, kv_local * HD), "ctx", axis=0, tiled=True),
        lax.all_gather(values_own.reshape(tok_rows, kv_local * HD), "ctx", axis=0, tiled=True),
    )
    key_heads = jnp.transpose(keys_all.reshape(seq_len, kv_local, HD), (1, 0, 2))
    value_heads = jnp.transpose(values_all.reshape(seq_len, kv_local, HD), (1, 0, 2))
    query_heads = jnp.transpose(queries, (1, 0, 2))
    kv_of_head = jnp.arange(heads_local, dtype=jnp.int32) // GROUP

    def scores_of(query_head, kv_index):
        raw_scores = contract_cols(query_head, key_heads[kv_index]) * score_scale
        return jnp.where(allowed, raw_scores, -1e30)

    def attend(operands):
        query_head, kv_index = operands
        masked = scores_of(query_head, kv_index)
        top_score = jnp.max(masked, axis=-1, keepdims=True)
        exponent = jnp.exp(masked - top_score)
        row_total = jnp.sum(exponent, axis=-1, keepdims=True)
        soft_low = (exponent / row_total).astype(jnp.bfloat16)
        attended = jnp.dot(soft_low, value_heads[kv_index], preferred_element_type=jnp.float32)
        return (attended, (top_score + jnp.log(row_total))[:, 0])

    attended_all, log_totals = lax.map(attend, (query_heads, kv_of_head))
    head_out = (
        jnp.transpose(attended_all, (1, 0, 2))
        .reshape(tok_rows, heads_local * HD)
        .astype(jnp.bfloat16)
    )
    attn_part = jnp.dot(head_out, out_local, preferred_element_type=jnp.float32)
    attn_sum = lax.psum(attn_part, "tp")
    hidden_one = inputs + attn_sum
    inverse_two = lax.rsqrt(jnp.mean(hidden_one * hidden_one, axis=-1, keepdims=True) + EPSILON)
    normed_two = hidden_one * inverse_two
    normed_two_low = (normed_two * gain_two).astype(jnp.bfloat16)
    flat_routes = routes.reshape(-1)
    expert_ids = jnp.arange(experts, dtype=jnp.int32)
    chosen = (flat_routes[:, None] == expert_ids[None, :]).astype(jnp.int32)
    slot_rank = jnp.sum((jnp.cumsum(chosen, axis=0) - chosen) * chosen, axis=1)
    slot_flat = flat_routes * capacity + slot_rank
    slot_ids = jnp.arange(experts * capacity, dtype=jnp.int32)
    matches = slot_ids[:, None, None] == slot_flat.reshape(tok_rows, top_count)[None, :, :]
    dispatch = jnp.any(matches, axis=2).astype(jnp.bfloat16)
    slot_gate = jnp.sum(jnp.where(matches, gate_weights[None, :, :], 0.0), axis=(1, 2))
    gate_w = expert_in[0, 0].astype(jnp.bfloat16)
    up_w = expert_in[0, 1].astype(jnp.bfloat16)
    down_w = expert_down[0].astype(jnp.bfloat16)
    sent_rows = jnp.dot(dispatch, normed_two_low, preferred_element_type=jnp.float32).astype(
        jnp.bfloat16
    )
    received = lax.all_to_all(
        sent_rows.reshape(experts, capacity, model_width),
        ("fsdp", "ctx"),
        split_axis=0,
        concat_axis=0,
        tiled=True,
    )
    expert_rows_in = received.reshape(experts * capacity, model_width)
    gate_pre = jnp.dot(expert_rows_in, gate_w, preferred_element_type=jnp.float32)
    up_pre = jnp.dot(expert_rows_in, up_w, preferred_element_type=jnp.float32)
    gate_sig = jax.nn.sigmoid(gate_pre)
    gate_act = gate_pre * gate_sig
    activated = (gate_act * up_pre).astype(jnp.bfloat16)
    out_part = jnp.dot(activated, down_w, preferred_element_type=jnp.float32)
    out_share = lax.psum_scatter(
        out_part.astype(jnp.bfloat16), "tp", scatter_dimension=1, tiled=True
    )
    out_rows = lax.all_gather(out_share, "tp", axis=1, tiled=True)
    returned = lax.all_to_all(
        out_rows.reshape(experts, capacity, model_width),
        ("fsdp", "ctx"),
        split_axis=0,
        concat_axis=0,
        tiled=True,
    )
    mixture = combine(returned, slot_flat, gate_weights)
    block_out = (hidden_one + mixture).astype(jnp.bfloat16)
    grad_slots = jnp.dot(dispatch, out_grad, preferred_element_type=jnp.float32)
    grad_slots = (grad_slots * slot_gate[:, None]).astype(jnp.bfloat16)
    grad_received = lax.all_to_all(
        grad_slots.reshape(experts, capacity, model_width),
        ("fsdp", "ctx"),
        split_axis=0,
        concat_axis=0,
        tiled=True,
    )
    grad_received = grad_received.reshape(experts * capacity, model_width)
    grad_act = contract_cols(grad_received, down_w)
    down_grad = contract_rows(activated, grad_received)
    grad_gate = (grad_act * up_pre * gate_sig * (1.0 + gate_pre * (1.0 - gate_sig))).astype(
        jnp.bfloat16
    )
    grad_up = (grad_act * gate_act).astype(jnp.bfloat16)
    gate_grad = contract_rows(expert_rows_in, grad_gate)
    up_grad = contract_rows(expert_rows_in, grad_up)
    grad_rows_part = contract_cols(grad_gate, gate_w) + contract_cols(grad_up, up_w)
    grad_rows_share = lax.psum_scatter(
        grad_rows_part.astype(jnp.bfloat16), "tp", scatter_dimension=1, tiled=True
    )
    grad_back = lax.all_to_all(
        grad_rows_share.reshape(experts, capacity, -1),
        ("fsdp", "ctx"),
        split_axis=0,
        concat_axis=0,
        tiled=True,
    )
    grad_share = contract_rows(dispatch, grad_back.reshape(experts * capacity, -1))
    grad_normed_two = lax.all_gather(
        grad_share.astype(jnp.bfloat16), "tp", axis=1, tiled=True
    ).astype(grad_share.dtype)
    gain_grad_two = jnp.sum(grad_normed_two * normed_two, axis=0)
    grad_hidden = out_grad.astype(jnp.float32) + norm_back(
        grad_normed_two, normed_two, inverse_two, gain_two
    )
    grad_attn = grad_hidden.astype(jnp.bfloat16)
    out_weight_grad = contract_rows(head_out, grad_attn)
    head_grad = contract_cols(grad_attn, out_local).astype(jnp.bfloat16)
    grad_heads = jnp.transpose(head_grad.reshape(tok_rows, heads_local, HD), (1, 0, 2))

    def attend_back(operands):
        query_head, kv_index, grad_head, log_total = operands
        masked = scores_of(query_head, kv_index)
        soft_probs = jnp.exp(masked - log_total[:, None])
        grad_probs = contract_cols(grad_head, value_heads[kv_index])
        inner_sum = jnp.sum(soft_probs * grad_probs, axis=-1, keepdims=True)
        grad_scores = (soft_probs * (grad_probs - inner_sum)).astype(jnp.bfloat16)
        grad_query = (
            jnp.dot(grad_scores, key_heads[kv_index], preferred_element_type=jnp.float32)
            * score_scale
        )
        grad_key = contract_rows(grad_scores, query_head) * score_scale
        grad_value = contract_rows(soft_probs.astype(jnp.bfloat16), grad_head)
        return (grad_query, grad_key, grad_value)

    grad_query_all, grad_key_all, grad_value_all = lax.map(
        attend_back, (query_heads, kv_of_head, grad_heads, log_totals)
    )
    grad_key_all = jnp.sum(grad_key_all.reshape(kv_local, GROUP, seq_len, HD), axis=1)
    grad_value_all = jnp.sum(grad_value_all.reshape(kv_local, GROUP, seq_len, HD), axis=1)
    grad_key_own, grad_value_own = (
        lax.psum_scatter(
            jnp.transpose(grad_key_all, (1, 0, 2))
            .reshape(seq_len, kv_local * HD)
            .astype(jnp.bfloat16),
            "ctx",
            scatter_dimension=0,
            tiled=True,
        ).astype(jnp.float32),
        lax.psum_scatter(
            jnp.transpose(grad_value_all, (1, 0, 2))
            .reshape(seq_len, kv_local * HD)
            .astype(jnp.bfloat16),
            "ctx",
            scatter_dimension=0,
            tiled=True,
        ).astype(jnp.float32),
    )
    grad_query_pre = rotate(jnp.transpose(grad_query_all, (1, 0, 2)), pos_query, -1.0)
    grad_key_pre = rotate(grad_key_own.reshape(tok_rows, kv_local, HD), pos_query, -1.0)
    grad_projected = (
        jnp.concatenate(
            [
                grad_query_pre.reshape(tok_rows, kv_local, GROUP, HD),
                grad_key_pre[:, :, None, :],
                grad_value_own.reshape(tok_rows, kv_local, 1, HD),
            ],
            axis=2,
        )
        .reshape(tok_rows, -1)
        .astype(jnp.bfloat16)
    )
    qkv_grad_part = contract_rows(normed_low, grad_projected)
    grad_normed_part = contract_cols(grad_projected, qkv_local)
    grad_normed_one = lax.psum(grad_normed_part.astype(jnp.bfloat16), "tp").astype(jnp.float32)
    gain_grad_one = jnp.sum(grad_normed_one * normed_one, axis=0)
    in_grad = (grad_hidden + norm_back(grad_normed_one, normed_one, inverse_one, gain_one)).astype(
        jnp.bfloat16
    )
    qkv_grad, out_grad_sum, gains_grad = (
        lax.psum_scatter(
            qkv_grad_part.astype(jnp.bfloat16), ("fsdp", "ctx"), scatter_dimension=0, tiled=True
        ).astype(jnp.float32),
        lax.psum_scatter(
            out_weight_grad.astype(jnp.bfloat16), ("fsdp", "ctx"), scatter_dimension=1, tiled=True
        ).astype(jnp.float32),
        lax.psum_scatter(
            jnp.stack([gain_grad_one, gain_grad_two]).astype(jnp.bfloat16),
            ("fsdp", "ctx"),
            scatter_dimension=1,
            tiled=True,
        ).astype(jnp.float32),
    )
    in_grad_local = jnp.stack([gate_grad, up_grad])[None]
    down_grad_local = down_grad[None]
    qkv_new = advance(qkv_weight, qkv_grad, qkv_moment, qkv_average, RATE_QKV)
    out_new = advance(out_weight, out_grad_sum, out_moment, out_average, RATE_OUT)
    gain_new = advance(norm_gains, gains_grad, gain_moment, gain_average, RATE_GAIN)
    in_new = advance(expert_in, in_grad_local, in_moment, in_average, RATE_IN)
    down_new = advance(expert_down, down_grad_local, down_moment, down_average, RATE_DOWN)
    return (
        block_out,
        in_grad,
        qkv_new[0],
        qkv_new[1],
        qkv_new[2],
        out_new[0],
        out_new[1],
        out_new[2],
        gain_new[0],
        gain_new[1],
        gain_new[2],
        in_new[0],
        in_new[1],
        in_new[2],
        down_new[0],
        down_new[1],
        down_new[2],
    )


def solution(mesh):
    return jax.shard_map(
        per_device,
        mesh=mesh,
        in_specs=(
            P(("fsdp", "ctx"), None),
            P(("fsdp", "ctx"), None),
            P("fsdp", None),
            P(("fsdp", "ctx"), None),
            P(("fsdp", "ctx"), None),
            P(("fsdp", "ctx"), "tp"),
            P("tp", ("fsdp", "ctx")),
            P(None, ("fsdp", "ctx")),
            P(("fsdp", "ctx"), None, None, "tp"),
            P(("fsdp", "ctx"), "tp", None),
            P(("fsdp", "ctx"), "tp"),
            P(("fsdp", "ctx"), "tp"),
            P("tp", ("fsdp", "ctx")),
            P("tp", ("fsdp", "ctx")),
            P(None, ("fsdp", "ctx")),
            P(None, ("fsdp", "ctx")),
            P(("fsdp", "ctx"), None, None, "tp"),
            P(("fsdp", "ctx"), None, None, "tp"),
            P(("fsdp", "ctx"), "tp", None),
            P(("fsdp", "ctx"), "tp", None),
        ),
        out_specs=(
            P(("fsdp", "ctx"), None),
            P(("fsdp", "ctx"), None),
            P(("fsdp", "ctx"), "tp"),
            P(("fsdp", "ctx"), "tp"),
            P(("fsdp", "ctx"), "tp"),
            P("tp", ("fsdp", "ctx")),
            P("tp", ("fsdp", "ctx")),
            P("tp", ("fsdp", "ctx")),
            P(None, ("fsdp", "ctx")),
            P(None, ("fsdp", "ctx")),
            P(None, ("fsdp", "ctx")),
            P(("fsdp", "ctx"), None, None, "tp"),
            P(("fsdp", "ctx"), None, None, "tp"),
            P(("fsdp", "ctx"), None, None, "tp"),
            P(("fsdp", "ctx"), "tp", None),
            P(("fsdp", "ctx"), "tp", None),
            P(("fsdp", "ctx"), "tp", None),
        ),
        check_vma=False,
    )
```

profile of v0, /device:TPU:0, one launch (start us, length us, event | category | flops | bytes accessed | tf_op | source)
XLA Modules:
  0.0 2049.2 jit_solution(3989495933169013668)
XLA Ops:
  13.9 33.8 %all-gather = bf16[16,96,2]{1,2,0:T(2,128)(2,1)S(1)} all-gather(bf16[1,96,2]{1,2,0:T(2,128)(2,1)S(1)} %convert_bitcast_fusion), channel_id=1, replica_groups=mesh['fsdp'=4,'ctx'=4,'tp'=2] {'fsdp','ctx'}, dimensions={0}, use_global_device_ids=true | all-gather | bytes 6528 | tf_op jit(solution)/shard_map/all_gather | solution.py:110
  51.8 10.7 all-gather.6.cloned.1.call-done
  62.4 4.4 fusion.83
  68.8 23.4 %all_gather.23 = bf16[1536,256]{0,1:T(8,128)(2,1)S(1)} all-gather(bf16[384,256]{0,1:T(8,128)(2,1)S(1)} %bitcast.276), channel_id=1, replica_groups=mesh['fsdp'=4,'ctx'=4,'tp'=2] {'ctx'}, dimensions={0}, use_global_device_ids=true | all-gather | bytes 983040 | tf_op jit(solution)/shard_map/all_gather | solution.py:135
  93.8 24.8 %all_gather.24 = bf16[1536,256]{0,1:T(8,128)(2,1)S(1)} all-gather(bf16[384,256]{0,1:T(8,128)(2,1)S(1)} %bitcast.275), channel_id=1, replica_groups=mesh['fsdp'=4,'ctx'=4,'tp'=2] {'ctx'}, dimensions={0}, use_global_device_ids=true | all-gather | bytes 983040 | tf_op jit(solution)/shard_map/all_gather | solution.py:136
  120.1 109.2 %while.30 = (s32[]{:T(128)}, bf16[12,384,64]{1,2,0:T(8,128)(2,1)}, f32[12,384]{1,0:T(8,128)}, bf16[12,384,64]{2,1,0:T(8,128)(2,1)}, s32[12]{0:T(128)}, /*index=5...) while((s32[]{:T(128)}, bf16[12,384,64]{1,2,0:T(8,128)(2,1)}, ...), condition=%wide.region_7.8_spmd.clone.clone, body=%wide.region_4.7_spmd.clone.sunk.clone | while | flops 157482624 | bytes 8092319 | solution.py:157
  126.9 2.3 fusion.174
  136.0 2.3 fusion.174
  145.1 2.3 fusion.174
  154.2 2.3 fusion.174
  163.3 2.3 fusion.174
  172.5 2.3 fusion.174
  181.6 2.3 fusion.174
  190.7 2.3 fusion.174
  199.8 2.3 fusion.174
  208.9 2.3 fusion.174
  218.0 2.3 fusion.174
  227.1 2.3 fusion.174
  229.3 4.4 fusion.109
  234.9 4.6 reduce-window.19
  241.1 24.2 %fusion.49 = pred[3840,384]{1,0:T(8,128)(4,1)} fusion(s32[384,8]{0,1:T(8,128)S(1)} %get-tuple-element.365), kind=kLoop, calls=%fused_computation.63 | loop fusion | flops 22118400 | bytes 1486848 | tf_op jit(solution)/shard_map/reduce_or | solution.py:176
  265.3 36.7 %all-reduce.3.cloned.1.call-done = f32[384,1536]{1,0:T(8,128)} async-done(((f32[384,1536]{1,0:T(8,128)}), f32[384,1536]{1,0:T(8,128)}) %all-reduce.3.cloned.1.call-update) | async-done | bytes 2359312 | tf_op jit(solution)/shard_map/psum | solution.py:164
  304.2 9.2 convolution_convert_fusion.1
  313.5 6.2 all-to-all-start
  319.7 30.0 %select_reduce_fusion = f32[3840]{0:T(1024)S(1)} fusion(f32[384,8]{0,1:T(8,128)} %param.28, s32[384,8]{0,1:T(8,128)} %copy-done.30), kind=kLoop, calls=%fused_computation.61 | loop fusion | flops 35385600 | bytes 39936 | tf_op jit(solution)/shard_map/reduce_sum | solution.py:177
  349.7 10.4 multiply_convert_fusion.1
  360.1 217.0 %all-to-all-done = bf16[16,240,1536]{2,1,0:T(8,128)(2,1)} async-done(((bf16[16,240,1536]{2,1,0:T(8,128)(2,1)}), bf16[16,240,1536]{2,1,0:T(8,128)(2,1)}, u32[]{:S(2)}, u32[]{:S(2)}) %all-to-all-start) | async-done | bytes 11796512 | tf_op jit(solution)/shard_map/all_to_all | solution.py:184
  577.0 4.9 all-to-all-start.2
  582.0 10.0 fusion.86
  592.0 9.5 fusion.90
  601.6 237.7 %all-to-all-done.2 = bf16[16,240,1536]{2,1,0:T(8,128)(2,1)} async-done(((bf16[16,240,1536]{2,1,0:T(8,128)(2,1)}), bf16[16,240,1536]{2,1,0:T(8,128)(2,1)}, u32[]{:S(2)}, u32[]{:S(2)}) %all-to-all-start.2) | async-done | bytes 11796512 | tf_op jit(solution)/shard_map/all_to_all | solution.py:213
  839.2 13.7 multiply_convert_fusion.2
  854.2 6.3 convolution_convert_fusion
  860.6 13.1 fusion.88
  873.7 15.6 add_convert_fusion
  889.3 105.1 %reduce-scatter.14.cloned.1.call-done = bf16[3840,768]{1,0:T(8,128)(2,1)} async-done(((bf16[3840,1536]{1,0:T(8,128)(2,1)}), bf16[3840,768]{1,0:T(8,128)(2,1)}) %reduce-scatter.14.cloned.1.call-update) | async-done | bytes 5898256 | tf_op jit(solution)/shard_map/reduce_scatter | solution.py:198
  994.4 138.3 %reduce-scatter.16.cloned.1.call-done = bf16[3840,768]{1,0:T(8,128)(2,1)} async-done(((bf16[3840,1536]{1,0:T(8,128)(2,1)}), bf16[3840,768]{1,0:T(8,128)(2,1)}) %reduce-scatter.16.cloned.1.call-update) | async-done | bytes 5898256 | tf_op jit(solution)/shard_map/reduce_scatter | solution.py:230
  1132.7 136.8 %all_to_all.20 = bf16[16,240,768]{2,1,0:T(8,128)(2,1)} all-to-all(bf16[16,240,768]{2,1,0:T(8,128)(2,1)} %bitcast.254), channel_id=1, replica_groups=mesh['fsdp'=4,'ctx'=4,'tp'=2] {'fsdp','ctx'}, dimensions={0} | all-to-all | bytes 11796480 | tf_op jit(solution)/shard_map/all_to_all | solution.py:233
  1269.5 8.7 all-gather.10.cloned.1.call-done
  1278.1 5.7 all-to-all-start.1
  1283.9 6.5 convolution_convert_fusion.6
  1291.2 22.5 %all-gather.12.cloned.1.call-done = bf16[384,1536]{1,0:T(8,128)(2,1)} async-done(((bf16[384,768]{1,0:T(8,128)(2,1)}), bf16[384,1536]{1,0:T(8,128)(2,1)}) %all-gather.12.cloned.1.call-update) | async-done | bytes 1179664 | tf_op jit(solution)/shard_map/all_gather | solution.py:241
  1313.7 2.6 fusion.64
  1316.4 224.8 %all-to-all-done.1 = bf16[16,240,1536]{2,1,0:T(8,128)(2,1)} async-done(((bf16[16,240,1536]{2,1,0:T(8,128)(2,1)}), bf16[16,240,1536]{2,1,0:T(8,128)(2,1)}, u32[]{:S(2)}, u32[]{:S(2)}) %all-to-all-start.1) | async-done | bytes 11796512 | tf_op jit(solution)/shard_map/all_to_all | solution.py:202
  1541.1 25.6 %gather_fusion = bf16[3072,1536]{1,0:T(8,128)(2,1)} fusion(bf16[3840,1536]{1,0:T(8,128)(2,1)} %bitcast.25, s32[3072]{0:T(1024)S(1)} %broadcast_clamp_fusion), kind=kCustom, calls=%fused_computation | custom fusion | bytes 18886656 | tf_op jit(solution)/shard_map/jit(_take)/gather | solution.py:66
  1566.7 23.3 %multiply_reduce_fusion.1 = f32[384,1536]{1,0:T(8,128)S(1)} fusion(bf16[3072,1536]{1,0:T(8,128)(2,1)} %gather_fusion, f32[384,8]{1,0:T(8,128)S(1)} %copy.109, pred[384,8]{1,0:T(8,128)(4,1)S(1)} %copy.107), kind=kLoop, calls=%fused_computation.66 | loop fusion | flops 18284544 | bytes 11811840 | tf_op jit(solution)/shard_map/reduce_sum | solution.py:68
  1593.3 146.2 %while.31 = (s32[]{:T(128)}, f32[12,384,64]{1,2,0:T(8,128)}, f32[12,1536,64]{1,2,0:T(8,128)}, f32[12,1536,64]{1,2,0:T(8,128)}, bf16[12,384,64]{2,1,0:T(8,128)(2,...) while((s32[]{:T(128)}, f32[12,384,64]{1,2,0:T(8,128)}, ...), condition=%wide.region_21.22_spmd.clone.clone, body=%wide.region_19.21_spmd.clone.sunk.clone | while | flops 384687744 | bytes 23224024 | solution.py:268
  1739.6 2.9 reduce_sum.149
  1743.7 2.9 reduce_sum.150
  1749.6 15.2 reduce-scatter.22.cloned.1.call-done
  1766.0 24.4 %reduce-scatter.24.cloned.1.call-done = bf16[384,256]{1,0:T(8,128)(2,1)} async-done(((bf16[1536,256]{1,0:T(8,128)(2,1)}), bf16[384,256]{1,0:T(8,128)(2,1)}) %reduce-scatter.24.cloned.1.call-update) | async-done | bytes 196624
  1792.7 5.0 convolution_convert_fusion.4
  1798.4 41.5 %all-reduce.5.cloned.1.call-done = bf16[384,1536]{1,0:T(8,128)(2,1)} async-done(((bf16[384,1536]{1,0:T(8,128)(2,1)}), bf16[384,1536]{1,0:T(8,128)(2,1)}) %all-reduce.5.cloned.1.call-update) | async-done | bytes 1179664 | tf_op jit(solution)/shard_map/psum | solution.py:307
  1839.9 2.7 fusion.67
  1845.0 3.9 convolution_convert_fusion.3
  1849.5 5.4 convolution_convert_fusion.2
  1855.0 9.6 convolution_bitcast_fusion.2
  1864.6 8.9 convolution_bitcast_fusion.3
  1873.5 8.5 multiply_add_fusion
  1882.0 10.2 multiply_add_fusion.2
  1894.0 6.6 reduce-scatter.26.cloned.1.call-done
  1902.7 64.0 %reduce-scatter.20.cloned.1.call-done = bf16[768,96]{0,1:T(8,128)(2,1)} async-done(((bf16[768,1536]{0,1:T(8,128)(2,1)}), bf16[768,96]{0,1:T(8,128)(2,1)}) %reduce-scatter.20.cloned.1.call-update) | async-done | bytes 147472 | tf_op jit(solution)/shard_map/reduce_scatter | solution.py:316
  1968.9 70.9 %reduce-scatter.18.cloned.1.call-done = bf16[96,1280]{1,0:T(8,128)(2,1)} async-done(((bf16[1536,1280]{1,0:T(8,128)(2,1)}), bf16[96,1280]{1,0:T(8,128)(2,1)}) %reduce-scatter.18.cloned.1.call-update) | async-done | bytes 245776 | tf_op jit(solution)/shard_map/reduce_scatter | solution.py:313
  2039.8 2.6 multiply_add_fusion.4
  (373 shorter events, 224.3 us)
Async XLA Ops:
  7.2 41.6 %copy-start.39 = (s32[1,4]{1,0:T(1,128)S(1)}, s32[1,4]{1,0:T(1,128)}, u32[]{:S(2)}) copy-start(s32[1,4]{1,0:T(1,128)} %param.26) | copy-start | bytes 52
  7.2 41.2 %copy-start.2 = (bf16[384,1536]{1,0:T(8,128)(2,1)S(1)}, bf16[384,1536]{1,0:T(8,128)(2,1)}, u32[]{:S(2)}) copy-start(bf16[384,1536]{1,0:T(8,128)(2,1)} %param.24) | copy-start | bytes 3538948
  7.2 55.2 %all-gather.6.cloned.1.call-start = ((), (), s32[]{:S(2)}) async-start(), calls=%async_computation.11 | async-start | bytes 4177920 | tf_op jit(solution)/shard_map/all_gather | solution.py:108
  9.1 220.2 %all-gather.8.cloned.1.call-start = ((), (), s32[]{:S(2)}) async-start(), calls=%async_computation.12 | async-start | bytes 2506752 | tf_op jit(solution)/shard_map/all_gather | solution.py:109
  10.8 291.2 %all-reduce.3.cloned.1.call-start = ((), (), s32[]{:S(2)}) async-start(), calls=%async_computation.13 | async-start | bytes 4718592 | tf_op jit(solution)/shard_map/psum | solution.py:164
  48.4 18.5 copy-start.25
  48.7 18.1 copy-start.31
  51.8 17.0 copy-start.16
  229.3 4.4 copy-start.36
  240.3 25.0 %copy-start.23 = (s32[3072]{0:T(1024)}, s32[3072]{0:T(1024)S(1)}, u32[]{:S(2)}) copy-start(s32[3072]{0:T(1024)S(1)} %fusion.96) | copy-start | bytes 36868
  241.1 24.2 %copy-start.30 = (s32[384,8]{0,1:T(8,128)}, s32[384,8]{0,1:T(8,128)S(1)}, u32[]{:S(2)}) copy-start(s32[384,8]{0,1:T(8,128)S(1)} %get-tuple-element.365) | copy-start | bytes 36868
  302.0 2.2 copy-start.15
  302.0 2.2 copy-start.27
  304.2 1009.5 %copy-start = (f32[384,1536]{1,0:T(8,128)}, f32[384,1536]{1,0:T(8,128)S(1)}, u32[]{:S(2)}) copy-start(f32[384,1536]{1,0:T(8,128)S(1)} %get-tuple-element.367) | copy-start | bytes 7077892
  313.5 36.2 %copy-start.18 = (bf16[384,1536]{1,0:T(8,128)(2,1)S(1)}, bf16[384,1536]{1,0:T(8,128)(2,1)}, u32[]{:S(2)}) copy-start(bf16[384,1536]{1,0:T(8,128)(2,1)} %param.25) | copy-start | bytes 3538948
  313.5 263.6 %all-to-all-start = ((bf16[16,240,1536]{2,1,0:T(8,128)(2,1)}), bf16[16,240,1536]{2,1,0:T(8,128)(2,1)}, u32[]{:S(2)}, u32[]{:S(2)}) async-start(bf16[16,240,1536]{2,1,0:T(8,128)(2,1)} %bitcast.253), calls=%async_computation | async-start | bytes 23592960 | tf_op jit(solution)/shard_map/all_to_all | solution.py:184
  577.0 262.2 %all-to-all-start.2 = ((bf16[16,240,1536]{2,1,0:T(8,128)(2,1)}), bf16[16,240,1536]{2,1,0:T(8,128)(2,1)}, u32[]{:S(2)}, u32[]{:S(2)}) async-start(bf16[16,240,1536]{2,1,0:T(8,128)(2,1)} %bitcast.252), calls=%async_computation.3 | async-start | bytes 23592960 | tf_op jit(solution)/shard_map/all_to_all | solution.py:213
  581.9 412.5 %reduce-scatter.14.cloned.1.call-start = ((), (), s32[]{:S(2)}) async-start(), calls=%async_computation.14 | async-start | bytes 17694720 | tf_op jit(solution)/shard_map/reduce_scatter | solution.py:198
  582.0 10.1 copy-start.6
  839.2 15.0 copy-start.9
  860.6 272.1 %reduce-scatter.16.cloned.1.call-start = ((), (), s32[]{:S(2)}) async-start(), calls=%async_computation.16 | async-start | bytes 17694720 | tf_op jit(solution)/shard_map/reduce_scatter | solution.py:230
  889.3 388.8 %all-gather.10.cloned.1.call-start = ((), (), s32[]{:S(2)}) async-start(), calls=%async_computation.15 | async-start | bytes 17694720 | tf_op jit(solution)/shard_map/all_gather | solution.py:201
  1278.1 263.0 %all-to-all-start.1 = ((bf16[16,240,1536]{2,1,0:T(8,128)(2,1)}), bf16[16,240,1536]{2,1,0:T(8,128)(2,1)}, u32[]{:S(2)}, u32[]{:S(2)}) async-start(bf16[16,240,1536]{2,1,0:T(8,128)(2,1)} %bitcast.251), calls=%async_computation.2 | async-start | bytes 23592960 | tf_op jit(solution)/shard_map/all_to_all | solution.py:202
  1283.8 29.9 %all-gather.12.cloned.1.call-start = ((), (), s32[]{:S(2)}) async-start(), calls=%async_computation.17 | async-start | bytes 1769472 | tf_op jit(solution)/shard_map/all_gather | solution.py:241
  1283.8 6.7 copy-start.33
  1283.8 7.1 copy-start.34
  1283.9 7.3 copy-start.24
  1283.9 29.9 %copy-start.28 = (f32[1536]{0:T(1024)S(1)}, f32[1536]{0:T(1024)}, u32[]{:S(2)}) copy-start(f32[1536]{0:T(1024)} %get-tuple-element.299) | copy-start | bytes 18436
  1290.4 474.4 %reduce-scatter.22.cloned.1.call-start = ((), (), s32[]{:S(2)}) async-start(), calls=%async_computation.21 | async-start | bytes 983040
  1566.7 23.3 %copy-start.1 = (f32[384,1536]{1,0:T(8,128)S(1)}, f32[384,1536]{1,0:T(8,128)}, u32[]{:S(2)}) copy-start(f32[384,1536]{1,0:T(8,128)} %copy-done) | copy-start | bytes 7077892
  1566.7 23.3 %copy-start.12 = (bf16[384,1536]{1,0:T(8,128)(2,1)S(1)}, bf16[384,1536]{1,0:T(8,128)(2,1)}, u32[]{:S(2)}) copy-start(bf16[384,1536]{1,0:T(8,128)(2,1)} %all-gather.12.cloned.1.call-done) | copy-start | bytes 3538948
  1566.7 23.3 %copy-start.19 = (bf16[384,1536]{1,0:T(8,128)(2,1)S(1)}, bf16[384,1536]{1,0:T(8,128)(2,1)}, u32[]{:S(2)}) copy-start(bf16[384,1536]{1,0:T(8,128)(2,1)} %param.25) | copy-start | bytes 3538948
  1566.7 23.3 %copy-start.29 = (f32[1536]{0:T(1024)S(1)}, f32[1536]{0:T(1024)}, u32[]{:S(2)}) copy-start(f32[1536]{0:T(1024)} %get-tuple-element.299) | copy-start | bytes 18436
  1590.0 1.9 copy-start.40
  1591.9 1.4 copy-start.37
  1596.5 2.4 copy-start.8
  1608.7 2.4 copy-start.8
  1620.9 2.4 copy-start.8
  1633.1 2.4 copy-start.8
  1645.2 2.4 copy-start.8
  1657.4 2.4 copy-start.8
  1669.6 2.4 copy-start.8
  1681.9 2.4 copy-start.8
  1694.1 2.4 copy-start.8
  1706.3 2.4 copy-start.8
  1718.4 2.4 copy-start.8
  1730.6 2.4 copy-start.8
  1743.7 46.8 %reduce-scatter.24.cloned.1.call-start = ((), (), s32[]{:S(2)}) async-start(), calls=%async_computation.22 | async-start | bytes 983040
  1746.6 1.4 copy-start.17
  1746.6 1.4 copy-start.21
  1747.8 92.1 %all-reduce.5.cloned.1.call-start = ((), (), s32[]{:S(2)}) async-start(), calls=%async_computation.18 | async-start | bytes 2359296 | tf_op jit(solution)/shard_map/psum | solution.py:307
  1792.7 47.3 %copy-start.3 = (bf16[384,1536]{1,0:T(8,128)(2,1)S(1)}, bf16[384,1536]{1,0:T(8,128)(2,1)}, u32[]{:S(2)}) copy-start(bf16[384,1536]{1,0:T(8,128)(2,1)} %param.24) | copy-start | bytes 3538948
  1792.7 47.3 %copy-start.26 = (f32[1536]{0:T(1024)S(1)}, f32[1536]{0:T(1024)}, u32[]{:S(2)}) copy-start(f32[1536]{0:T(1024)} %copy-done.25) | copy-start | bytes 18436
  1797.6 103.0 %reduce-scatter.26.cloned.1.call-start = ((), (), s32[]{:S(2)}) async-start(), calls=%async_computation.23 | async-start | bytes 417792
  1844.9 121.8 %reduce-scatter.20.cloned.1.call-start = ((), (), s32[]{:S(2)}) async-start(), calls=%async_computation.20 | async-start | bytes 2506752 | tf_op jit(solution)/shard_map/reduce_scatter | solution.py:316
  1848.9 190.9 %reduce-scatter.18.cloned.1.call-start = ((), (), s32[]{:S(2)}) async-start(), calls=%async_computation.19 | async-start | bytes 4177920 | tf_op jit(solution)/shard_map/reduce_scatter | solution.py:313
  1855.0 9.6 copy-start.13
  1864.6 8.9 copy-start.7
  1873.5 8.5 copy-start.5
  1873.5 8.5 copy-start.10
  1873.5 8.5 copy-start.14
  1882.0 10.2 copy-start.35
  1882.0 10.2 copy-start.11
  1892.2 9.2 copy-start.38
  (4 other events, 3.6 us)
Sparse Core Ops, SparseCore 0:
  10.9 51.4 all-gather.5
  65.3 50.6 all-gather.7
  233.9 68.1 all-reduce.2
  860.7 133.6 reduce-scatter.13
  996.7 135.9 reduce-scatter.15
  1134.2 143.8 all-gather.9
  1290.6 23.1 all-gather.11
  1743.8 20.9 reduce-scatter.21
  1767.8 22.6 reduce-scatter.23
  1797.8 42.1 all-reduce.4
  1845.0 55.5 reduce-scatter.25
  1904.7 61.9 reduce-scatter.19
  1970.6 69.1 reduce-scatter.17
where the time goes:
time: 2060 us; the launch traced here: 2050 us
  waiting for transfers between devices  1220 us (59%)
  matrix products  292 us (14%)
  blocking collectives  219 us (11%)
  other arithmetic  135 us (7%)
  local copies, waits for them, and re-layouts  99.3 us (5%)
  loops' own time  47.1 us (2%)
    all_to_all x1, waiting for transfers between devices, per_device(): lax.all_to_all(grad_slots.reshape(experts, capacity, model_width), ('fsdp...  238 us
    all_to_all x1, waiting for transfers between devices, per_device(): lax.all_to_all(out_rows.reshape(experts, capacity, model_width), ('fsdp',...  225 us
    all_to_all x1, waiting for transfers between devices, per_device(): lax.all_to_all(sent_rows.reshape(experts, capacity, model_width), ('fsdp'...  217 us
    reduce_scatter x1, waiting for transfers between devices, per_device(): lax.psum_scatter(grad_rows_part.astype(jnp.bfloat16), 'tp', scatter_dimen...  138 us
    all_to_all x1, blocking collectives, per_device(): lax.all_to_all(grad_rows_share.reshape(experts, capacity, -1), ('fsdp', '...  137 us
    dot_general x41, matrix products, contract_cols(): lax.dot_general(left_mat, right_mat, (((1,), (1,)), ((), ())), preferred_...  115 us
    reduce_scatter x1, waiting for transfers between devices, per_device(): lax.psum_scatter(out_part.astype(jnp.bfloat16), 'tp', scatter_dimension=1...  105 us
    dot_general x30, matrix products, contract_rows(): lax.dot_general(left_mat, right_mat, (((0,), (0,)), ((), ())), preferred_...  82 us
  transfers between devices with their start and end apart: 16, of which 15 were waited for; matrix products, arithmetic and copies ran while one was open for 14% of the time, Pallas kernels for 0%

commit v1 on v0

--- a/solution.py
+++ b/solution.py
@@ -1,8 +1,11 @@
+import functools
 import math
 
 import jax
 import jax.numpy as jnp
 from jax import lax
+from jax.experimental import pallas as pl
+from jax.experimental.pallas import tpu as pltpu
 from jax.sharding import PartitionSpec as P
 
 HD = 64
@@ -61,11 +64,234 @@
     return inverse * (scaled - normed * jnp.mean(scaled * normed, axis=-1, keepdims=True))
 
 
-def combine(returned, slot_flat, gate_weights):
-    flat_rows = returned.reshape(-1, returned.shape[-1])
-    picked = jnp.take(flat_rows, slot_flat, axis=0).astype(jnp.float32)
-    picked = picked.reshape(gate_weights.shape[0], gate_weights.shape[1], -1)
-    return jnp.sum(picked * gate_weights[:, :, None], axis=1)
+F_MASKS = (0, 2, 1, 3)
+VMEM_LIMIT = 60 * 1024 * 1024
+
+
+def swap(value, axis, mask):
+    size = lax.axis_size(axis)
+    return lax.ppermute(value, axis, [(i, i ^ mask) for i in range(size)])
+
+
+def gather_pieces(own_in, own_down):
+    over_tp = range(lax.axis_size("tp"))
+    far_in = swap(own_in, "fsdp", 2)
+    downs_near = [own_down] + [swap(own_down, "tp", m) for m in over_tp[1:]]
+    ins_near = [own_in] + [swap(own_in, "tp", m) for m in over_tp[1:]]
+    downs_far = [swap(piece, "fsdp", 2) for piece in downs_near]
+    ins_far = [far_in] + [swap(far_in, "tp", m) for m in over_tp[1:]]
+    ins, downs = ins_near + ins_far, downs_near + downs_far
+    ins += [swap(piece, "fsdp", 1) for piece in ins]
+    downs += [swap(piece, "fsdp", 1) for piece in downs]
+    return ins, downs
+
+
+def nt_dot(left_mat, right_mat):
+    return lax.dot_general(
+        left_mat, right_mat, (((1,), (1,)), ((), ())), preferred_element_type=jnp.float32
+    )
+
+
+def expert_kernel(blocks, pieces, *refs):
+    x_refs, refs = refs[:blocks], refs[blocks:]
+    og_refs, refs = refs[:blocks], refs[blocks:]
+    gate_refs, refs = refs[:blocks], refs[blocks:]
+    in_refs, refs = refs[:pieces], refs[pieces:]
+    down_refs, refs = refs[:pieces], refs[pieces:]
+    gx_refs, refs = refs[:blocks], refs[blocks:]
+    act_ref, gg_ref, gu_ref, w_in, w_down, x_all, og_all, gates, total, sem_in, sem_down = refs
+    for p in range(pieces):
+        pltpu.make_async_copy(in_refs[p], w_in.at[p], sem_in.at[p]).start()
+        pltpu.make_async_copy(down_refs[p], w_down.at[p], sem_down.at[p]).start()
+    rows = x_refs[0].shape[0]
+    width = w_down.shape[1]
+    for b in range(blocks):
+        x_all[b * rows : (b + 1) * rows] = x_refs[b][...]
+        og_all[b * rows : (b + 1) * rows] = og_refs[b][...]
+        for m in range(len(F_MASKS)):
+            gates[m, b * rows : (b + 1) * rows] = gate_refs[b][m]
+    total[...] = jnp.zeros_like(total)
+
+    @pl.loop(0, pieces)
+    def _(p):
+        pltpu.make_async_copy(w_in.at[p], w_in.at[p], sem_in.at[p]).wait()
+        pltpu.make_async_copy(w_down.at[p], w_down.at[p], sem_down.at[p]).wait()
+        x = x_all[...]
+        gate = jnp.dot(x, w_in[p, 0], preferred_element_type=jnp.float32)
+        up = jnp.dot(x, w_in[p, 1], preferred_element_type=jnp.float32)
+        back = nt_dot(og_all[...], w_down[p])
+        weight = gates[p // (pieces // len(F_MASKS))]
+        sig = jax.nn.sigmoid(gate)
+        silu = gate * sig
+        back = back * weight
+        cols = pl.ds(pl.multiple_of(p * width, width), width)
+        act_ref[:, cols] = (silu * up * weight).astype(jnp.bfloat16)
+        grad_gate = (back * up * (sig * (1.0 + gate * (1.0 - sig)))).astype(jnp.bfloat16)
+        grad_up = (back * silu).astype(jnp.bfloat16)
+        gg_ref[:, cols] = grad_gate
+        gu_ref[:, cols] = grad_up
+        total[...] += nt_dot(grad_gate, w_in[p, 0]) + nt_dot(grad_up, w_in[p, 1])
+
+    for b in range(blocks):
+        gx_refs[b][...] = total[b * rows : (b + 1) * rows].astype(jnp.bfloat16)
+
+
+def expert_rows(xs, ogs, gates, ins, downs):
+    blocks, (rows, width), hidden = len(xs), xs[0].shape, downs[0].shape[0]
+    pieces = len(ins)
+    vmem = pl.BlockSpec(memory_space=pltpu.VMEM)
+    anywhere = pl.BlockSpec(memory_space=pl.ANY)
+    low = jnp.bfloat16
+    wide = jax.ShapeDtypeStruct((blocks * rows, pieces * hidden), low)
+    flops = 2 * 5 * blocks * rows * width * pieces * hidden
+    outs = pl.pallas_call(
+        functools.partial(expert_kernel, blocks, pieces),
+        out_shape=[jax.ShapeDtypeStruct((rows, width), low)] * blocks + [wide] * 3,
+        in_specs=[vmem] * (3 * blocks) + [anywhere] * (2 * pieces),
+        out_specs=[vmem] * (blocks + 3),
+        scratch_shapes=[
+            pltpu.VMEM((pieces, 2, width, hidden), low),
+            pltpu.VMEM((pieces, hidden, width), low),
+            pltpu.VMEM((blocks * rows, width), low),
+            pltpu.VMEM((blocks * rows, width), low),
+            pltpu.VMEM((len(F_MASKS), blocks * rows, 1), jnp.float32),
+            pltpu.VMEM((blocks * rows, width), jnp.float32),
+            pltpu.SemaphoreType.DMA((pieces,)),
+            pltpu.SemaphoreType.DMA((pieces,)),
+        ],
+        compiler_params=pltpu.CompilerParams(vmem_limit_bytes=VMEM_LIMIT),
+        cost_estimate=pl.CostEstimate(flops=flops, bytes_accessed=25 << 20, transcendentals=0),
+        name="expert_rows",
+    )(*xs, *ogs, *gates, *ins, *downs)
+    return outs[:blocks], outs[blocks:]
+
+
+def mix_kernel(blocks, calls, pieces, *refs):
+    act_refs, refs = refs[:calls], refs[calls:]
+    down_refs, refs = refs[:pieces], refs[pieces:]
+    mix_refs, refs = refs[:blocks], refs[blocks:]
+    w_down, sem = refs
+    hidden = down_refs[0].shape[0]
+    for p in range(pieces):
+        pltpu.make_async_copy(
+            down_refs[p], w_down.at[p * hidden : (p + 1) * hidden], sem.at[p]
+        ).start()
+    for p in range(pieces):
+        pltpu.make_async_copy(
+            down_refs[p], w_down.at[p * hidden : (p + 1) * hidden], sem.at[p]
+        ).wait()
+    rows = mix_refs[0].shape[0]
+    per_call = blocks // calls
+    for b in range(blocks):
+        at = (b % per_call) * rows
+        mix_refs[b][...] = jnp.dot(
+            act_refs[b // per_call][at : at + rows], w_down[...], preferred_element_type=jnp.float32
+        ).astype(jnp.bfloat16)
+
+
+def mix_rows(acts, downs, blocks):
+    hidden, width = downs[0].shape
+    pieces, calls = len(downs), len(acts)
+    rows = acts[0].shape[0] * calls // blocks
+    vmem = pl.BlockSpec(memory_space=pltpu.VMEM)
+    anywhere = pl.BlockSpec(memory_space=pl.ANY)
+    return pl.pallas_call(
+        functools.partial(mix_kernel, blocks, calls, pieces),
+        out_shape=[jax.ShapeDtypeStruct((rows, width), jnp.bfloat16)] * blocks,
+        in_specs=[vmem] * calls + [anywhere] * pieces,
+        out_specs=[vmem] * blocks,
+        scratch_shapes=[
+            pltpu.VMEM((pieces * hidden, width), jnp.bfloat16),
+            pltpu.SemaphoreType.DMA((pieces,)),
+        ],
+        compiler_params=pltpu.CompilerParams(vmem_limit_bytes=VMEM_LIMIT),
+        cost_estimate=pl.CostEstimate(
+            flops=2 * blocks * rows * width * pieces * hidden, bytes_accessed=12 << 20, transcendentals=0
+        ),
+        name="mix_rows",
+    )(*acts, *downs)
+
+
+def weight_kernel(blocks, calls, *refs):
+    x_refs, refs = refs[:blocks], refs[blocks:]
+    og_refs, refs = refs[:blocks], refs[blocks:]
+    act_refs, refs = refs[:calls], refs[calls:]
+    gg_refs, refs = refs[:calls], refs[calls:]
+    gu_refs, refs = refs[:calls], refs[calls:]
+    in_ref, down_ref, x_t, og_all, act_all, gg_all, gu_all = refs
+    rows = x_refs[0].shape[0]
+
+    @pl.when(pl.program_id(0) == 0)
+    def _():
+        for b in range(blocks):
+            x_t[:, b * rows : (b + 1) * rows] = x_refs[b][...].T
+            og_all[b * rows : (b + 1) * rows] = og_refs[b][...]
+
+    some = act_refs[0].shape[0]
+    for i in range(calls):
+        act_all[i * some : (i + 1) * some] = act_refs[i][...]
+        gg_all[i * some : (i + 1) * some] = gg_refs[i][...]
+        gu_all[i * some : (i + 1) * some] = gu_refs[i][...]
+    in_ref[0, 0] = jnp.dot(x_t[...], gg_all[...], preferred_element_type=jnp.float32).astype(jnp.bfloat16)
+    in_ref[0, 1] = jnp.dot(x_t[...], gu_all[...], preferred_element_type=jnp.float32).astype(jnp.bfloat16)
+    down_ref[0] = jnp.dot(
+        act_all[...].T, og_all[...], preferred_element_type=jnp.float32
+    ).astype(jnp.bfloat16)
+
+
+def weight_grads(xs, ogs, acts, ggs, gus, hidden, first, count):
+    blocks, calls, (rows, width) = len(xs), len(acts), xs[0].shape
+    some = acts[0].shape[0]
+    vmem = pl.BlockSpec(memory_space=pltpu.VMEM)
+    column = pl.BlockSpec((some, hidden), lambda i: (0, first + i))
+    low = jnp.bfloat16
+    total = blocks * rows
+    return pl.pallas_call(
+        functools.partial(weight_kernel, blocks, calls),
+        grid=(count,),
+        out_shape=[
+            jax.ShapeDtypeStruct((count, 2, width, hidden), low),
+            jax.ShapeDtypeStruct((count, hidden, width), low),
+        ],
+        in_specs=[vmem] * (2 * blocks) + [column] * (3 * calls),
+        out_specs=[
+            pl.BlockSpec((1, 2, width, hidden), lambda i: (i, 0, 0, 0)),
+            pl.BlockSpec((1, hidden, width), lambda i: (i, 0, 0)),
+        ],
+        scratch_shapes=[
+            pltpu.VMEM((width, total), low),
+            pltpu.VMEM((total, width), low),
+            pltpu.VMEM((total, hidden), low),
+            pltpu.VMEM((total, hidden), low),
+            pltpu.VMEM((total, hidden), low),
+        ],
+        compiler_params=pltpu.CompilerParams(vmem_limit_bytes=VMEM_LIMIT),
+        cost_estimate=pl.CostEstimate(
+            flops=2 * 3 * total * width * count * hidden, bytes_accessed=20 << 20, transcendentals=0
+        ),
+        name="weight_grads",
+    )(*xs, *ogs, *acts, *ggs, *gus)
+
+
+def added(left_mat, right_mat):
+    return (left_mat.astype(jnp.float32) + right_mat.astype(jnp.float32)).astype(jnp.bfloat16)
+
+
+def scatter_pieces(kept, sent):
+    back_in, back_down = swap(sent[0], "fsdp", 1), swap(sent[1], "fsdp", 1)
+    count = lax.axis_size("tp")
+    ins = [added(kept[0][i], back_in[i]) for i in range(2 * count)]
+    downs = [added(kept[1][i], back_down[i]) for i in range(2 * count)]
+    downs = [added(downs[i], swap(downs[count + i], "fsdp", 2)) for i in range(count)]
+    far_in, own_in = ins[count], ins[0]
+    for m in range(1, count):
+        far_in = added(far_in, swap(ins[count + m], "tp", m))
+        own_in = added(own_in, swap(ins[m], "tp", m))
+    f32 = jnp.float32
+    own_down = downs[0].astype(f32)
+    for m in range(1, count):
+        own_down += swap(downs[m], "tp", m).astype(f32)
+    return own_in.astype(f32) + swap(far_in, "fsdp", 2).astype(f32), own_down
 
 
 def advance(weight, gradient, moment, average, step_rate):
@@ -97,11 +323,9 @@
     down_moment,
     down_average,
 ):
-    tok_rows, model_width = tokens.shape
-    top_count = routes.shape[1]
+    tok_rows = tokens.shape[0]
     n_ctx = lax.axis_size("ctx")
     experts = lax.axis_size(("fsdp", "ctx"))
-    capacity = min(tok_rows, tok_rows * top_count * 5 // (4 * experts))
     seq_len = tok_rows * n_ctx
     score_scale = HD ** (-0.5)
     qkv_local, out_local, gain_local = (
@@ -161,91 +385,92 @@
         .astype(jnp.bfloat16)
     )
     attn_part = jnp.dot(head_out, out_local, preferred_element_type=jnp.float32)
-    attn_sum = lax.psum(attn_part, "tp")
-    hidden_one = inputs + attn_sum
+    half_rows = tok_rows // lax.axis_size("tp")
+    tp_index = lax.axis_index("tp")
+    fsdp_index, ctx_index = lax.axis_index("fsdp"), lax.axis_index("ctx")
+
+    over_tp = range(lax.axis_size("tp"))
+
+    def part_of(value, mask):
+        return lax.dynamic_slice_in_dim(value, (tp_index ^ mask) * half_rows, half_rows)
+
+    def own_half(value):
+        return part_of(value, 0)
+
+    def sum_own(value):
+        total = own_half(value)
+        for m in over_tp[1:]:
+            total += swap(part_of(value, m).astype(jnp.bfloat16), "tp", m).astype(jnp.float32)
+        return total
+
+    def both_halves(own):
+        parts = [own] + [swap(own, "tp", m) for m in over_tp[1:]]
+        ordered = []
+        for at in over_tp:
+            chosen = parts[0]
+            for m in over_tp[1:]:
+                chosen = jnp.where(tp_index ^ m == at, parts[m], chosen)
+            ordered.append(chosen)
+        return jnp.concatenate(ordered, axis=0)
+
+    attn_sum = sum_own(attn_part)
+    hidden_one = own_half(inputs) + attn_sum
     inverse_two = lax.rsqrt(jnp.mean(hidden_one * hidden_one, axis=-1, keepdims=True) + EPSILON)
     normed_two = hidden_one * inverse_two
     normed_two_low = (normed_two * gain_two).astype(jnp.bfloat16)
-    flat_routes = routes.reshape(-1)
+
+    ins, downs = gather_pieces(expert_in[0].astype(jnp.bfloat16), expert_down[0].astype(jnp.bfloat16))
     expert_ids = jnp.arange(experts, dtype=jnp.int32)
-    chosen = (flat_routes[:, None] == expert_ids[None, :]).astype(jnp.int32)
-    slot_rank = jnp.sum((jnp.cumsum(chosen, axis=0) - chosen) * chosen, axis=1)
-    slot_flat = flat_routes * capacity + slot_rank
-    slot_ids = jnp.arange(experts * capacity, dtype=jnp.int32)
-    matches = slot_ids[:, None, None] == slot_flat.reshape(tok_rows, top_count)[None, :, :]
-    dispatch = jnp.any(matches, axis=2).astype(jnp.bfloat16)
-    slot_gate = jnp.sum(jnp.where(matches, gate_weights[None, :, :], 0.0), axis=(1, 2))
-    gate_w = expert_in[0, 0].astype(jnp.bfloat16)
-    up_w = expert_in[0, 1].astype(jnp.bfloat16)
-    down_w = expert_down[0].astype(jnp.bfloat16)
-    sent_rows = jnp.dot(dispatch, normed_two_low, preferred_element_type=jnp.float32).astype(
-        jnp.bfloat16
-    )
-    received = lax.all_to_all(
-        sent_rows.reshape(experts, capacity, model_width),
-        ("fsdp", "ctx"),
-        split_axis=0,
-        concat_axis=0,
-        tiled=True,
-    )
-    expert_rows_in = received.reshape(experts * capacity, model_width)
-    gate_pre = jnp.dot(expert_rows_in, gate_w, preferred_element_type=jnp.float32)
-    up_pre = jnp.dot(expert_rows_in, up_w, preferred_element_type=jnp.float32)
-    gate_sig = jax.nn.sigmoid(gate_pre)
-    gate_act = gate_pre * gate_sig
-    activated = (gate_act * up_pre).astype(jnp.bfloat16)
-    out_part = jnp.dot(activated, down_w, preferred_element_type=jnp.float32)
-    out_share = lax.psum_scatter(
-        out_part.astype(jnp.bfloat16), "tp", scatter_dimension=1, tiled=True
-    )
-    out_rows = lax.all_gather(out_share, "tp", axis=1, tiled=True)
-    returned = lax.all_to_all(
-        out_rows.reshape(experts, capacity, model_width),
-        ("fsdp", "ctx"),
-        split_axis=0,
-        concat_axis=0,
-        tiled=True,
-    )
-    mixture = combine(returned, slot_flat, gate_weights)
-    block_out = (hidden_one + mixture).astype(jnp.bfloat16)
-    grad_slots = jnp.dot(dispatch, out_grad, preferred_element_type=jnp.float32)
-    grad_slots = (grad_slots * slot_gate[:, None]).astype(jnp.bfloat16)
-    grad_received = lax.all_to_all(
-        grad_slots.reshape(experts, capacity, model_width),
-        ("fsdp", "ctx"),
-        split_axis=0,
-        concat_axis=0,
-        tiled=True,
-    )
-    grad_received = grad_received.reshape(experts * capacity, model_width)
-    grad_act = contract_cols(grad_received, down_w)
-    down_grad = contract_rows(activated, grad_received)
-    grad_gate = (grad_act * up_pre * gate_sig * (1.0 + gate_pre * (1.0 - gate_sig))).astype(
-        jnp.bfloat16
-    )
-    grad_up = (grad_act * gate_act).astype(jnp.bfloat16)
-    gate_grad = contract_rows(expert_rows_in, grad_gate)
-    up_grad = contract_rows(expert_rows_in, grad_up)
-    grad_rows_part = contract_cols(grad_gate, gate_w) + contract_cols(grad_up, up_w)
-    grad_rows_share = lax.psum_scatter(
-        grad_rows_part.astype(jnp.bfloat16), "tp", scatter_dimension=1, tiled=True
-    )
-    grad_back = lax.all_to_all(
-        grad_rows_share.reshape(experts, capacity, -1),
-        ("fsdp", "ctx"),
-        split_axis=0,
-        concat_axis=0,
-        tiled=True,
-    )
-    grad_share = contract_rows(dispatch, grad_back.reshape(experts * capacity, -1))
-    grad_normed_two = lax.all_gather(
-        grad_share.astype(jnp.bfloat16), "tp", axis=1, tiled=True
-    ).astype(grad_share.dtype)
+    dense_gates = jnp.sum(
+        jnp.where(
+            own_half(routes)[:, :, None] == expert_ids[None, None, :],
+            own_half(gate_weights)[:, :, None],
+            0.0,
+        ),
+        axis=1,
+    )
+    grad_own = own_half(out_grad)
+    xs = [normed_two_low] + [swap(normed_two_low, "ctx", m) for m in range(1, n_ctx)]
+    ogs = [grad_own] + [swap(grad_own, "ctx", m) for m in range(1, n_ctx)]
+    all_gates = [dense_gates] + [swap(dense_gates, "ctx", m) for m in range(1, n_ctx)]
+
+    def of_pieces(block_gates):
+        columns = []
+        for f_mask in F_MASKS:
+            expert = (fsdp_index ^ f_mask) * n_ctx + ctx_index
+            columns.append(
+                jnp.sum(jnp.where(expert_ids[None, :] == expert, block_gates, 0.0), axis=1)
+            )
+        return jnp.stack(columns)[:, :, None]
+
+    all_gates = [of_pieces(g) for g in all_gates]
+    grads_x, acts, ggs, gus = [], [], [], []
+    for at in range(0, n_ctx, 2):
+        some_x, (act, gg, gu) = expert_rows(
+            xs[at : at + 2], ogs[at : at + 2], all_gates[at : at + 2], ins, downs
+        )
+        grads_x += some_x
+        acts.append(act)
+        ggs.append(gg)
+        gus.append(gu)
+    grad_normed_two = grads_x[0].astype(jnp.float32)
+    for m in range(1, n_ctx):
+        grad_normed_two += swap(grads_x[m], "ctx", m).astype(jnp.float32)
+    mixes = mix_rows(acts, downs, n_ctx)
+    mixture = mixes[0].astype(jnp.float32)
+    for m in range(1, n_ctx):
+        mixture += swap(mixes[m], "ctx", m).astype(jnp.float32)
+    block_out = both_halves((hidden_one + mixture).astype(jnp.bfloat16))
+    hidden, near = downs[0].shape[0], len(downs) // 2
+    sent = weight_grads(xs, ogs, acts, ggs, gus, hidden, near, near)
+    kept = weight_grads(xs, ogs, acts, ggs, gus, hidden, 0, near)
+    in_grad_sum, down_grad_sum = scatter_pieces(kept, sent)
+
     gain_grad_two = jnp.sum(grad_normed_two * normed_two, axis=0)
-    grad_hidden = out_grad.astype(jnp.float32) + norm_back(
+    grad_hidden_half = grad_own.astype(jnp.float32) + norm_back(
         grad_normed_two, normed_two, inverse_two, gain_two
     )
-    grad_attn = grad_hidden.astype(jnp.bfloat16)
+    grad_attn = both_halves(grad_hidden_half.astype(jnp.bfloat16))
     out_weight_grad = contract_rows(head_out, grad_attn)
     head_grad = contract_cols(grad_attn, out_local).astype(jnp.bfloat16)
     grad_heads = jnp.transpose(head_grad.reshape(tok_rows, heads_local, HD), (1, 0, 2))
@@ -304,10 +529,14 @@
     )
     qkv_grad_part = contract_rows(normed_low, grad_projected)
     grad_normed_part = contract_cols(grad_projected, qkv_local)
-    grad_normed_one = lax.psum(grad_normed_part.astype(jnp.bfloat16), "tp").astype(jnp.float32)
-    gain_grad_one = jnp.sum(grad_normed_one * normed_one, axis=0)
-    in_grad = (grad_hidden + norm_back(grad_normed_one, normed_one, inverse_one, gain_one)).astype(
-        jnp.bfloat16
+    grad_normed_one = sum_own(grad_normed_part)
+    normed_one_half = own_half(normed_one)
+    gain_grad_one = jnp.sum(grad_normed_one * normed_one_half, axis=0)
+    in_grad = both_halves(
+        (
+            grad_hidden_half
+            + norm_back(grad_normed_one, normed_one_half, own_half(inverse_one), gain_one)
+        ).astype(jnp.bfloat16)
     )
     qkv_grad, out_grad_sum, gains_grad = (
         lax.psum_scatter(
@@ -323,8 +552,9 @@
             tiled=True,
         ).astype(jnp.float32),
     )
-    in_grad_local = jnp.stack([gate_grad, up_grad])[None]
-    down_grad_local = down_grad[None]
+    gains_grad = lax.psum(gains_grad, "tp")
+    in_grad_local = in_grad_sum[None]
+    down_grad_local = down_grad_sum[None]
     qkv_new = advance(qkv_weight, qkv_grad, qkv_moment, qkv_average, RATE_QKV)
     out_new = advance(out_weight, out_grad_sum, out_moment, out_average, RATE_OUT)
     gain_new = advance(norm_gains, gains_grad, gain_moment, gain_average, RATE_GAIN)

time: 2060 us -> 940 us (0.46)
  waiting for transfers between devices: 1220 us -> 260 us
  matrix products: 292 us -> 160 us
  Pallas kernels: 0 us -> 95.5 us
  blocking collectives: 219 us -> 151 us
  other arithmetic: 135 us -> 78.7 us
  starting transfers between devices: 17.5 us -> 57.4 us
  local copies, waits for them, and re-layouts: 99.3 us -> 65.4 us
    all_to_all x3 -> x0, waiting for transfers between devices: 679 us -> none  [the longest x1 238 us: per_device(): lax.all_to_all(grad_slots.reshape(experts, capacity, model_width), ('fsdp...]
    reduce_scatter x2 -> x0, waiting for transfers between devices: 243 us -> none  [the longest x1 138 us: per_device(): lax.psum_scatter(grad_rows_part.astype(jnp.bfloat16), 'tp', scatter_dimen...]
    all_to_all x1 -> x0, blocking collectives: 137 us -> none  [per_device(): lax.all_to_all(grad_rows_share.reshape(experts, capacity, -1), ('fsdp', '...]
    ppermute x0 -> x42, waiting for transfers between devices: none -> 111 us  [swap(): return lax.ppermute(value, axis, [(i, i ^ mask) for i in range(size)])]
    pallas_call x0 -> x5, Pallas kernels: none -> 95.5 us  [the longest x2 58 us: expert_rows(): pl.pallas_call(functools.partial(expert_kernel, blocks, pieces), out_shap...]
    psum x2 -> x0, waiting for transfers between devices: 78.2 us -> none  [the longest x1 41.5 us: per_device(): lax.psum(grad_normed_part.astype(jnp.bfloat16), 'tp').astype(jnp.float32)]
    ppermute x0 -> x42, starting transfers between devices: none -> 56.6 us  [swap(): return lax.ppermute(value, axis, [(i, i ^ mask) for i in range(size)])]
    reduce_sum x4 -> x3, other arithmetic: 56 us -> 1.2 us  [the longest x1 1.04 us: per_device(): gain_grad_one = jnp.sum(grad_normed_one * normed_one_half, axis=0)]
  transfers between devices with their start and end apart: 16 -> 49, of which waited for: 15 -> 11; matrix products, arithmetic and copies ran while one was open for 14% -> 17% of each run, Pallas kernels for 0% -> 10%
where the time goes in v1:
time: 940 us; the launch traced here: 931 us
  waiting for transfers between devices  260 us (28%)
  matrix products  160 us (17%)
  blocking collectives  151 us (16%)
  Pallas kernels  95.5 us (10%)
  other arithmetic  78.7 us (8%)
  local copies, waits for them, and re-layouts  65.4 us (7%)
  starting transfers between devices  57.4 us (6%)
  loops' own time  47.6 us (5%)
  between operations  15.1 us (2%)
    ppermute x42, waiting for transfers between devices, swap(): return lax.ppermute(value, axis, [(i, i ^ mask) for i in range(size)])  111 us
    all_gather x1, blocking collectives, per_device(): lax.all_gather(norm_gains.astype(jnp.bfloat16), ('fsdp', 'ctx'), axis=1,...  80.9 us
    dot_general x38, matrix products, contract_cols(): lax.dot_general(left_mat, right_mat, (((1,), (1,)), ((), ())), preferred_...  71.7 us
    reduce_scatter x1, waiting for transfers between devices, per_device(): lax.psum_scatter(qkv_grad_part.astype(jnp.bfloat16), ('fsdp', 'ctx'), sca...  65.6 us
    pallas_call x2, Pallas kernels, expert_rows(): pl.pallas_call(functools.partial(expert_kernel, blocks, pieces), out_shap...  58 us
    ppermute x42, starting transfers between devices, swap(): return lax.ppermute(value, axis, [(i, i ^ mask) for i in range(size)])  56.6 us
    unnamed x10, waiting for transfers between devices  55.6 us
    dot_general x26, matrix products, contract_rows(): lax.dot_general(left_mat, right_mat, (((0,), (0,)), ((), ())), preferred_...  47.1 us
  transfers between devices with their start and end apart: 49, of which 11 were waited for; matrix products, arithmetic and copies ran while one was open for 17% of the time, Pallas kernels for 10%

profile of v1, /device:TPU:0, one launch (start us, length us, event | category | flops | bytes accessed | tf_op | source)
XLA Modules:
  0.0 931.1 jit_solution(13703866918220090658)
XLA Ops:
  11.0 4.0 collective-permute-start.20
  16.6 2.5 collective-permute-start.23
  19.2 3.2 convert_bitcast_fusion.refs_6_
  28.0 80.9 %all-gather = bf16[16,96,2]{1,2,0:T(2,128)(2,1)S(1)} all-gather(bf16[1,96,2]{1,2,0:T(2,128)(2,1)S(1)} %convert_bitcast_fusion.2), channel_id=1, replica_groups=mesh['fsdp'=4,'ctx'=4,'tp'=2] {'fsdp','ctx'}, dimensions={0}, use_global_device_ids=true | all-gather | bytes 6528 | tf_op jit(solution)/shard_map/all_gather | solution.py:334
  110.7 4.5 fusion.67
  115.3 24.6 %all_gather.17 = bf16[1536,256]{0,1:T(8,128)(2,1)S(1)} all-gather(bf16[384,256]{0,1:T(8,128)(2,1)S(1)} %bitcast.276), channel_id=1, replica_groups=mesh['fsdp'=4,'ctx'=4,'tp'=2] {'ctx'}, dimensions={0}, use_global_device_ids=true | all-gather | bytes 983040 | tf_op jit(solution)/shard_map/all_gather | solution.py:359
  140.0 18.5 %all_gather.18 = bf16[1536,256]{0,1:T(8,128)(2,1)S(1)} all-gather(bf16[384,256]{0,1:T(8,128)(2,1)S(1)} %bitcast.277), channel_id=1, replica_groups=mesh['fsdp'=4,'ctx'=4,'tp'=2] {'ctx'}, dimensions={0}, use_global_device_ids=true | all-gather | bytes 983040 | tf_op jit(solution)/shard_map/all_gather | solution.py:360
  159.6 3.7 collective-permute-done.22
  165.5 2.3 copy.84
  174.1 94.9 %while.30 = (s32[]{:T(128)}, bf16[12,384,64]{1,2,0:T(8,128)(2,1)S(1)}, f32[12,384]{1,0:T(8,128)}, bf16[12,384,64]{2,1,0:T(8,128)(2,1)}, s32[12]{0:T(128)S(1)}, /...) while((s32[]{:T(128)}, ...), condition=%wide.region_7.8_spmd.clone.clone, body=%wide.region_4.7_spmd.clone.sunk.clone | while | flops 157482624 | bytes 8089775 | solution.py:381
  269.1 3.0 fusion.81
  277.2 14.9 %collective-permute-done.13.refs_17_.refs_5_ = bf16[256,1536]{1,0:T(8,128)(2,1)} collective-permute-done((bf16[256,1536]{1,0:T(8,128)(2,1)}, bf16[256,1536]{1,0:T(8,128)(2,1)}, u32[]{:S(2)}, u32[]{:S(2)}) %collective-permute-start.13) | collective-permute-done | bytes 786464 | tf_op jit(solution)/shard_map/ppermute | solution.py:73
  296.0 2.5 collective-permute-start.18
  306.0 32.2 %collective-permute-done.18.refs_0_.refs_2_ = bf16[192,1536]{1,0:T(8,128)(2,1)} collective-permute-done((bf16[192,1536]{1,0:T(8,128)(2,1)}, bf16[192,1536]{1,0:T(8,128)(2,1)}, u32[]{:S(2)}, u32[]{:S(2)}) %collective-permute-start.18) | collective-permute-done | bytes 589856 | tf_op jit(solution)/shard_map/ppermute | solution.py:73
  338.1 28.9 %expert_rows.3 = (bf16[192,1536]{1,0:T(8,128)(2,1)}, bf16[192,1536]{1,0:T(8,128)(2,1)}, bf16[384,2048]{1,0:T(8,128)(2,1)}, bf16[384,2048]{1,0:T(8,128)(2,1)}, bf16[384,2048]{1,0:T(8,128)(2,1)}) custom-call(bf16[192,1536]{1,0:T(8,128)(2,1)} %collective-permute-done.18.refs_0_.refs_2_, bf16[192,1536]{1,0:T(8,128)(2,1)} %collective-permute-done.19.refs_1_.refs_3_, ...), custom_call_target="tpu_custom_call" | custom-call | flops 12079595520 | bytes 26214400 | tf_op jit(solution)/shard_map/expert_rows/pallas_call | solution.py:147
  367.0 2.6 collective-permute-start.30
  369.6 11.8 %collective-permute-start.29 = (bf16[192,1536]{1,0:T(8,128)(2,1)}, bf16[192,1536]{1,0:T(8,128)(2,1)S(1)}, u32[]{:S(2)}, u32[]{:S(2)}) collective-permute-start(bf16[192,1536]{1,0:T(8,128)(2,1)} %get-tuple-element.146), channel_id=1, source_target_pairs={{0,4},{2,6},{4,0},{6,2},{1,5},{3,7},{5,1},{7,3},{8,12},{10,14},{12... | collective-permute-start | bytes 1769480 | tf_op jit(solution)/shard_map/ppermute | solution.py:73
  381.4 29.1 %expert_rows.2 = (bf16[192,1536]{1,0:T(8,128)(2,1)}, bf16[192,1536]{1,0:T(8,128)(2,1)}, bf16[384,2048]{1,0:T(8,128)(2,1)}, bf16[384,2048]{1,0:T(8,128)(2,1)}, bf16[384,2048]{1,0:T(8,128)(2,1)}) custom-call(bf16[192,1536]{1,0:T(8,128)(2,1)} %multiply_convert_fusion.2.refs_0_, bf16[192,1536]{1,0:T(8,128)(2,1)} %collective-permute-done.1.refs_1_, ...), custom_call_target="tpu_custom_call" | custom-call | flops 12079595520 | bytes 26214400 | tf_op jit(solution)/shard_map/expert_rows/pallas_call | solution.py:147
  410.6 10.6 %mix_rows.1 = (bf16[192,1536]{1,0:T(8,128)(2,1)}, bf16[192,1536]{1,0:T(8,128)(2,1)}, bf16[192,1536]{1,0:T(8,128)(2,1)}, bf16[192,1536]{1,0:T(8,128)(2,1)}) custom-call(bf16[384,2048]{1,0:T(8,128)(2,1)} %get-tuple-element.138.refs_0_.refs_8_, bf16[384,2048]{1,0:T(8,128)(2,1)} %get-tuple-element.139.refs_1_.refs_9_, ...), custom_call_target="tpu_custom_call" | custom-call | flops 4831838208 | bytes 12582912 | tf_op jit(solution)/shard_map/mix_rows/pallas_call | solution.py:198
  421.3 2.0 collective-permute-start.26
  425.7 21.5 %collective-permute-done.28 = bf16[192,1536]{1,0:T(8,128)(2,1)} collective-permute-done((bf16[192,1536]{1,0:T(8,128)(2,1)}, bf16[192,1536]{1,0:T(8,128)(2,1)}, u32[]{:S(2)}, u32[]{:S(2)}) %collective-permute-start.28) | collective-permute-done | bytes 589856 | tf_op jit(solution)/shard_map/ppermute | solution.py:73
  447.3 2.6 multiply_reduce_fusion.2
  449.9 25.3 %collective-permute-done.25 = bf16[192,1536]{1,0:T(8,128)(2,1)S(1)} collective-permute-done((bf16[192,1536]{1,0:T(8,128)(2,1)}, bf16[192,1536]{1,0:T(8,128)(2,1)S(1)}, u32[]{:S(2)}, u32[]{:S(2)}) %collective-permute-start.25) | collective-permute-done | bytes 589856 | tf_op jit(solution)/shard_map/ppermute | solution.py:73
  475.1 3.4 fusion.79
  480.3 13.0 %collective-permute-done.31 = bf16[192,1536]{1,0:T(8,128)(2,1)S(1)} collective-permute-done((bf16[192,1536]{1,0:T(8,128)(2,1)}, bf16[192,1536]{1,0:T(8,128)(2,1)S(1)}, u32[]{:S(2)}, u32[]{:S(2)}) %collective-permute-start.31) | collective-permute-done | bytes 589856 | tf_op jit(solution)/shard_map/ppermute | solution.py:73
  496.9 138.8 %while.31 = (s32[]{:T(128)}, f32[12,384,64]{1,2,0:T(8,128)}, f32[12,1536,64]{1,2,0:T(8,128)}, f32[12,1536,64]{1,2,0:T(8,128)}, bf16[12,384,64]{2,1,0:T(8,128)(2,...) while((s32[]{:T(128)}, f32[12,384,64]{1,2,0:T(8,128)}, ...), condition=%wide.region_29.30_spmd.clone.clone, body=%wide.region_27.29_spmd.clone.sunk.clone | while | flops 384687744 | bytes 23259684 | solution.py:493
  501.8 2.1 multiply_reduce_fusion.9
  513.4 2.1 multiply_reduce_fusion.9
  516.9 2.0 fusion.142
  525.0 2.1 multiply_reduce_fusion.9
  528.5 2.0 fusion.142
  536.5 2.1 multiply_reduce_fusion.9
  548.1 2.0 multiply_reduce_fusion.9
  559.6 2.0 multiply_reduce_fusion.9
  571.2 2.0 multiply_reduce_fusion.9
  574.7 2.0 fusion.142
  582.7 2.0 multiply_reduce_fusion.9
  594.3 2.0 multiply_reduce_fusion.9
  605.9 2.0 multiply_reduce_fusion.9
  617.5 2.1 multiply_reduce_fusion.9
  621.0 2.0 fusion.142
  629.1 2.0 multiply_reduce_fusion.9
  632.6 2.0 fusion.142
  635.7 2.9 reduce_sum.283
  639.8 2.9 reduce_sum.284
  645.9 15.3 %reduce-scatter.16.cloned.1.call-done = bf16[384,256]{1,0:T(8,128)(2,1)} async-done(((bf16[1536,256]{1,0:T(8,128)(2,1)}), bf16[384,256]{1,0:T(8,128)(2,1)}) %reduce-scatter.16.cloned.1.call-update) | async-done | bytes 196624
  664.0 22.5 %reduce-scatter.18.cloned.1.call-done = bf16[384,256]{1,0:T(8,128)(2,1)} async-done(((bf16[1536,256]{1,0:T(8,128)(2,1)}), bf16[384,256]{1,0:T(8,128)(2,1)}) %reduce-scatter.18.cloned.1.call-update) | async-done | bytes 196624
  687.8 4.2 fusion.82
  695.9 13.5 %weight_grads.3 = (bf16[4,2,1536,256]{3,2,1,0:T(8,128)(2,1)}, bf16[4,256,1536]{2,1,0:T(8,128)(2,1)}) custom-call(bf16[192,1536]{1,0:T(8,128)(2,1)} %multiply_convert_fusion.2.refs_0_, bf16[192,1536]{1,0:T(8,128)(2,1)} %collective-permute-done.1.refs_1_, bf16[192,1536]{1,0:T(8,128)(2,1)} %collective-permute-done.18.refs_0_.refs_2_, ...), custom_call_target="tpu_custom_call" | custom-call | flops 7247757312 | bytes 20971520 | tf_op jit(solution)/shard_map/weight_grads/pallas_call | solution.py:249
  715.2 4.1 convolution_convert_fusion.1
  720.9 13.5 %weight_grads.2 = (bf16[4,2,1536,256]{3,2,1,0:T(8,128)(2,1)}, bf16[4,256,1536]{2,1,0:T(8,128)(2,1)}) custom-call(bf16[192,1536]{1,0:T(8,128)(2,1)} %multiply_convert_fusion.2.refs_0_, bf16[192,1536]{1,0:T(8,128)(2,1)} %collective-permute-done.1.refs_1_, bf16[192,1536]{1,0:T(8,128)(2,1)} %collective-permute-done.18.refs_0_.refs_2_, ...), custom_call_target="tpu_custom_call" | custom-call | flops 7247757312 | bytes 20971520 | tf_op jit(solution)/shard_map/weight_grads/pallas_call | solution.py:249
  734.4 5.5 convolution_convert_fusion
  742.4 3.5 fusion.62
  747.9 4.5 fusion.54
  755.0 17.6 %reduce-scatter.20.cloned.1.call-done = bf16[96,2]{1,0:T(8,128)(2,1)} async-done(((bf16[1536,2]{1,0:T(8,128)(2,1)}), bf16[96,2]{1,0:T(8,128)(2,1)}) %reduce-scatter.20.cloned.1.call-update) | async-done | bytes 400
  773.4 27.2 %psum.7 = f32[2,96]{1,0:T(2,128)S(1)} all-reduce(bf16[2,96]{1,0:T(2,128)(2,1)S(1)} %copy.104), channel_id=1, replica_groups=mesh['fsdp'=4,'ctx'=4,'tp'=2] {'tp'}, use_global_device_ids=true, to_apply=%region_40.41 | all-reduce | flops 192 | bytes 1152 | tf_op jit(solution)/shard_map/psum | solution.py:555
  801.2 2.8 fusion.57
  807.2 4.2 fusion.49
  812.9 27.8 %reduce-scatter.14.cloned.1.call-done = bf16[768,96]{0,1:T(8,128)(2,1)} async-done(((bf16[768,1536]{0,1:T(8,128)(2,1)}), bf16[768,96]{0,1:T(8,128)(2,1)}) %reduce-scatter.14.cloned.1.call-update) | async-done | bytes 147472 | tf_op jit(solution)/shard_map/reduce_scatter | solution.py:545
  840.7 2.1 multiply_add_fusion.4
  842.9 5.3 multiply_add_fusion.1
  848.2 65.6 %reduce-scatter.12.cloned.1.call-done = bf16[96,1280]{1,0:T(8,128)(2,1)} async-done(((bf16[1536,1280]{1,0:T(8,128)(2,1)}), bf16[96,1280]{1,0:T(8,128)(2,1)}) %reduce-scatter.12.cloned.1.call-update) | async-done | bytes 245776 | tf_op jit(solution)/shard_map/reduce_scatter | solution.py:542
  913.8 2.6 multiply_add_fusion.3
  916.4 7.6 multiply_add_fusion
  (560 shorter events, 230.7 us)
Async XLA Ops:
  7.2 103.5 %all-gather.4.cloned.1.call-start = ((), (), s32[]{:S(2)}) async-start(), calls=%async_computation.5 | async-start | bytes 4177920 | tf_op jit(solution)/shard_map/all_gather | solution.py:332
  9.0 260.0 %all-gather.6.cloned.1.call-start = ((), (), s32[]{:S(2)}) async-start(), calls=%async_computation.6 | async-start | bytes 2506752 | tf_op jit(solution)/shard_map/all_gather | solution.py:333
  11.0 161.6 %collective-permute-start.20 = (bf16[192,1536]{1,0:T(8,128)(2,1)}, bf16[192,1536]{1,0:T(8,128)(2,1)}, u32[]{:S(2)}, u32[]{:S(2)}) collective-permute-start(bf16[192,1536]{1,0:T(8,128)(2,1)} %constant_dynamic-slice_fusion.3.refs_2_.refs_4_), channel_id=1, source_target_pairs={{0,4},{2,6},{4,0},{6,2},{1,5},{3,7},{5,1},{7,3},{8,12},{10,14},{12... | collective-permute-start | bytes 1769480 | tf_op jit(solution)/shard_map/ppermute | solution.py:73
  15.1 157.6 %collective-permute-start.21 = (bf16[192,1536]{1,0:T(8,128)(2,1)}, bf16[192,1536]{1,0:T(8,128)(2,1)}, u32[]{:S(2)}, u32[]{:S(2)}) collective-permute-start(bf16[192,1536]{1,0:T(8,128)(2,1)} %constant_dynamic-slice_fusion.3.refs_2_.refs_4_), channel_id=1, source_target_pairs={{0,6},{2,4},{4,2},{6,0},{1,7},{3,5},{5,3},{7,1},{8,14},{10,12},{12... | collective-permute-start | bytes 1769480 | tf_op jit(solution)/shard_map/ppermute | solution.py:73
  16.6 142.0 %collective-permute-start.23 = (f32[192,16]{0,1:T(8,128)S(1)}, f32[192,16]{0,1:T(8,128)S(1)}, u32[]{:S(2)}, u32[]{:S(2)}) collective-permute-start(f32[192,16]{0,1:T(8,128)S(1)} %select_reduce_fusion), channel_id=1, source_target_pairs={{0,6},{2,4},{4,2},{6,0},{1,7},{3,5},{5,3},{7,1},{8,14},{10,12},{12... | collective-permute-start | bytes 36872 | tf_op jit(solution)/shard_map/ppermute | solution.py:73
  22.4 86.7 %copy-start.3 = (bf16[384,1536]{1,0:T(8,128)(2,1)S(1)}, bf16[384,1536]{1,0:T(8,128)(2,1)}, u32[]{:S(2)}) copy-start(bf16[384,1536]{1,0:T(8,128)(2,1)} %param.24) | copy-start | bytes 3538948
  22.4 151.3 %collective-permute-start.5 = (bf16[2,1536,256]{2,1,0:T(8,128)(2,1)}, bf16[2,1536,256]{2,1,0:T(8,128)(2,1)}, u32[]{:S(2)}, u32[]{:S(2)}) collective-permute-start(bf16[2,1536,256]{2,1,0:T(8,128)(2,1)} %convert_bitcast_fusion.refs_6_), channel_id=1, source_target_pairs={{0,16},{8,24},{16,0},{24,8},{1,17},{9,25},{17,1},{25,9},{2,18},{10... | collective-permute-start | bytes 4718600 | tf_op jit(solution)/shard_map/ppermute | solution.py:73
  24.8 84.6 %copy-start.51 = (s32[1,4]{1,0:T(1,128)S(1)}, s32[1,4]{1,0:T(1,128)}, u32[]{:S(2)}) copy-start(s32[1,4]{1,0:T(1,128)} %param.26) | copy-start | bytes 52
  24.8 148.7 %collective-permute-start.11 = (bf16[256,1536]{1,0:T(8,128)(2,1)}, bf16[256,1536]{1,0:T(8,128)(2,1)}, u32[]{:S(2)}, u32[]{:S(2)}) collective-permute-start(bf16[256,1536]{1,0:T(8,128)(2,1)} %convert_bitcast_fusion.1.refs_14_.refs_2_), channel_id=1, source_target_pairs={{0,1},{1,0},{2,3},{3,2},{4,5},{5,4},{6,7},{7,6},{8,9},{9,8},{10,11... | collective-permute-start | bytes 2359304 | tf_op jit(solution)/shard_map/ppermute | solution.py:73
  27.0 634.2 %reduce-scatter.16.cloned.1.call-start = ((), (), s32[]{:S(2)}) async-start(), calls=%async_computation.9 | async-start | bytes 983040
  110.7 48.7 %copy-start.20 = (f32[384,32]{0,1:T(8,128)}, f32[384,32]{0,1:T(8,128)S(1)}, u32[]{:S(2)}) copy-start(f32[384,32]{0,1:T(8,128)S(1)} %get-tuple-element.434) | copy-start | bytes 147460
  158.6 4.7 collective-permute-start.22
  163.3 7.5 collective-permute-start.3
  170.8 103.0 %collective-permute-start.4 = (bf16[2,1536,256]{2,1,0:T(8,128)(2,1)}, bf16[2,1536,256]{2,1,0:T(8,128)(2,1)}, u32[]{:S(2)}, u32[]{:S(2)}) collective-permute-start(bf16[2,1536,256]{2,1,0:T(8,128)(2,1)} %convert_bitcast_fusion.refs_6_), channel_id=1, source_target_pairs={{0,1},{1,0},{2,3},{3,2},{4,5},{5,4},{6,7},{7,6},{8,9},{9,8},{10,11... | collective-permute-start | bytes 4718600 | tf_op jit(solution)/shard_map/ppermute | solution.py:73
  172.6 104.5 %collective-permute-start.7 = (bf16[2,1536,256]{2,1,0:T(8,128)(2,1)}, bf16[2,1536,256]{2,1,0:T(8,128)(2,1)}, u32[]{:S(2)}, u32[]{:S(2)}) collective-permute-start(bf16[2,1536,256]{2,1,0:T(8,128)(2,1)} %convert_bitcast_fusion.refs_6_), channel_id=1, source_target_pairs={{0,8},{8,0},{16,24},{24,16},{1,9},{9,1},{17,25},{25,17},{2,10},{10... | collective-permute-start | bytes 4718600 | tf_op jit(solution)/shard_map/ppermute | solution.py:73
  172.6 99.5 %collective-permute-start.12 = (bf16[256,1536]{1,0:T(8,128)(2,1)}, bf16[256,1536]{1,0:T(8,128)(2,1)S(1)}, u32[]{:S(2)}, u32[]{:S(2)}) collective-permute-start(bf16[256,1536]{1,0:T(8,128)(2,1)} %convert_bitcast_fusion.1.refs_14_.refs_2_), channel_id=1, source_target_pairs={{0,16},{8,24},{16,0},{24,8},{1,17},{9,25},{17,1},{25,9},{2,18},{10... | collective-permute-start | bytes 2359304 | tf_op jit(solution)/shard_map/ppermute | solution.py:73
  173.6 99.6 %collective-permute-start.14 = (bf16[256,1536]{1,0:T(8,128)(2,1)}, bf16[256,1536]{1,0:T(8,128)(2,1)}, u32[]{:S(2)}, u32[]{:S(2)}) collective-permute-start(bf16[256,1536]{1,0:T(8,128)(2,1)} %convert_bitcast_fusion.1.refs_14_.refs_2_), channel_id=1, source_target_pairs={{0,8},{8,0},{16,24},{24,16},{1,9},{9,1},{17,25},{25,17},{2,10},{10... | collective-permute-start | bytes 2359304 | tf_op jit(solution)/shard_map/ppermute | solution.py:73
  173.7 118.9 %collective-permute-start.6 = (bf16[2,1536,256]{2,1,0:T(8,128)(2,1)}, bf16[2,1536,256]{2,1,0:T(8,128)(2,1)}, u32[]{:S(2)}, u32[]{:S(2)}) collective-permute-start(bf16[2,1536,256]{2,1,0:T(8,128)(2,1)} %collective-permute-done.5.refs_8_), channel_id=1, source_target_pairs={{0,1},{1,0},{2,3},{3,2},{4,5},{5,4},{6,7},{7,6},{8,9},{9,8},{10,11... | collective-permute-start | bytes 4718600 | tf_op jit(solution)/shard_map/ppermute | solution.py:73
  272.2 19.9 %collective-permute-start.13 = (bf16[256,1536]{1,0:T(8,128)(2,1)}, bf16[256,1536]{1,0:T(8,128)(2,1)}, u32[]{:S(2)}, u32[]{:S(2)}) collective-permute-start(bf16[256,1536]{1,0:T(8,128)(2,1)} %collective-permute-done.11.refs_15_.refs_3_), channel_id=1, source_target_pairs={{0,16},{8,24},{16,0},{24,8},{1,17},{9,25},{17,1},{25,9},{2,18},{10... | collective-permute-start | bytes 2359304 | tf_op jit(solution)/shard_map/ppermute | solution.py:73
  273.2 18.9 %collective-permute-start.15 = (bf16[256,1536]{1,0:T(8,128)(2,1)}, bf16[256,1536]{1,0:T(8,128)(2,1)}, u32[]{:S(2)}, u32[]{:S(2)}) collective-permute-start(bf16[256,1536]{1,0:T(8,128)(2,1)} %collective-permute-done.11.refs_15_.refs_3_), channel_id=1, source_target_pairs={{0,8},{8,0},{16,24},{24,16},{1,9},{9,1},{17,25},{25,17},{2,10},{10... | collective-permute-start | bytes 2359304 | tf_op jit(solution)/shard_map/ppermute | solution.py:73
  273.8 18.9 %collective-permute-start = (bf16[192,1536]{1,0:T(8,128)(2,1)S(1)}, bf16[192,1536]{1,0:T(8,128)(2,1)S(1)}, u32[]{:S(2)}, u32[]{:S(2)}) collective-permute-start(bf16[192,1536]{1,0:T(8,128)(2,1)S(1)} %dynamic-slice_convert_fusion.1), channel_id=1, source_target_pairs={{0,1},{1,0},{2,3},{3,2},{4,5},{5,4},{6,7},{7,6},{8,9},{9,8},{10,11... | collective-permute-start | bytes 1769480 | tf_op jit(solution)/shard_map/ppermute | solution.py:73
  277.1 18.9 %collective-permute-start.16 = (bf16[256,1536]{1,0:T(8,128)(2,1)}, bf16[256,1536]{1,0:T(8,128)(2,1)S(1)}, u32[]{:S(2)}, u32[]{:S(2)}) collective-permute-start(bf16[256,1536]{1,0:T(8,128)(2,1)} %copy-done.53), channel_id=1, source_target_pairs={{0,8},{8,0},{16,24},{24,16},{1,9},{9,1},{17,25},{25,17},{2,10},{10... | collective-permute-start | bytes 2359304 | tf_op jit(solution)/shard_map/ppermute | solution.py:73
  292.1 13.0 %collective-permute-start.9 = (bf16[2,1536,256]{2,1,0:T(8,128)(2,1)}, bf16[2,1536,256]{2,1,0:T(8,128)(2,1)}, u32[]{:S(2)}, u32[]{:S(2)}) collective-permute-start(bf16[2,1536,256]{2,1,0:T(8,128)(2,1)} %collective-permute-done.5.refs_8_), channel_id=1, source_target_pairs={{0,8},{8,0},{16,24},{24,16},{1,9},{9,1},{17,25},{25,17},{2,10},{10... | collective-permute-start | bytes 4718600 | tf_op jit(solution)/shard_map/ppermute | solution.py:73
  292.1 11.9 %collective-permute-start.8 = (bf16[2,1536,256]{2,1,0:T(8,128)(2,1)}, bf16[2,1536,256]{2,1,0:T(8,128)(2,1)}, u32[]{:S(2)}, u32[]{:S(2)}) collective-permute-start(bf16[2,1536,256]{2,1,0:T(8,128)(2,1)} %collective-permute-done.4.refs_7_), channel_id=1, source_target_pairs={{0,8},{8,0},{16,24},{24,16},{1,9},{9,1},{17,25},{25,17},{2,10},{10... | collective-permute-start | bytes 4718600 | tf_op jit(solution)/shard_map/ppermute | solution.py:73
  292.6 6.0 collective-permute-start.17
  292.6 13.3 %collective-permute-start.10 = (bf16[2,1536,256]{2,1,0:T(8,128)(2,1)}, bf16[2,1536,256]{2,1,0:T(8,128)(2,1)}, u32[]{:S(2)}, u32[]{:S(2)}) collective-permute-start(bf16[2,1536,256]{2,1,0:T(8,128)(2,1)} %collective-permute-done.6.refs_9_), channel_id=1, source_target_pairs={{0,8},{8,0},{16,24},{24,16},{1,9},{9,1},{17,25},{25,17},{2,10},{10... | collective-permute-start | bytes 4718600 | tf_op jit(solution)/shard_map/ppermute | solution.py:73
  296.0 42.1 %collective-permute-start.18 = (bf16[192,1536]{1,0:T(8,128)(2,1)}, bf16[192,1536]{1,0:T(8,128)(2,1)}, u32[]{:S(2)}, u32[]{:S(2)}) collective-permute-start(bf16[192,1536]{1,0:T(8,128)(2,1)} %multiply_convert_fusion.2.refs_0_), channel_id=1, source_target_pairs={{0,4},{2,6},{4,0},{6,2},{1,5},{3,7},{5,1},{7,3},{8,12},{10,14},{12... | collective-permute-start | bytes 1769480 | tf_op jit(solution)/shard_map/ppermute | solution.py:73
  298.5 39.6 %collective-permute-start.19 = (bf16[192,1536]{1,0:T(8,128)(2,1)}, bf16[192,1536]{1,0:T(8,128)(2,1)}, u32[]{:S(2)}, u32[]{:S(2)}) collective-permute-start(bf16[192,1536]{1,0:T(8,128)(2,1)} %multiply_convert_fusion.2.refs_0_), channel_id=1, source_target_pairs={{0,6},{2,4},{4,2},{6,0},{1,7},{3,5},{5,3},{7,1},{8,14},{10,12},{12... | collective-permute-start | bytes 1769480 | tf_op jit(solution)/shard_map/ppermute | solution.py:73
  303.9 77.5 %collective-permute-start.2 = (bf16[192,1536]{1,0:T(8,128)(2,1)}, bf16[192,1536]{1,0:T(8,128)(2,1)}, u32[]{:S(2)}, u32[]{:S(2)}) collective-permute-start(bf16[192,1536]{1,0:T(8,128)(2,1)} %constant_dynamic-slice_fusion.3.refs_2_.refs_4_), channel_id=1, source_target_pairs={{0,2},{2,0},{4,6},{6,4},{1,3},{3,1},{5,7},{7,5},{8,10},{10,8},{12,... | collective-permute-start | bytes 1769480 | tf_op jit(solution)/shard_map/ppermute | solution.py:73
  305.0 76.4 %collective-permute-start.1 = (bf16[192,1536]{1,0:T(8,128)(2,1)}, bf16[192,1536]{1,0:T(8,128)(2,1)}, u32[]{:S(2)}, u32[]{:S(2)}) collective-permute-start(bf16[192,1536]{1,0:T(8,128)(2,1)} %multiply_convert_fusion.2.refs_0_), channel_id=1, source_target_pairs={{0,2},{2,0},{4,6},{6,4},{1,3},{3,1},{5,7},{7,5},{8,10},{10,8},{12,... | collective-permute-start | bytes 1769480 | tf_op jit(solution)/shard_map/ppermute | solution.py:73
  367.0 57.8 %collective-permute-start.30 = (bf16[192,1536]{1,0:T(8,128)(2,1)}, bf16[192,1536]{1,0:T(8,128)(2,1)S(1)}, u32[]{:S(2)}, u32[]{:S(2)}) collective-permute-start(bf16[192,1536]{1,0:T(8,128)(2,1)} %get-tuple-element.147), channel_id=1, source_target_pairs={{0,6},{2,4},{4,2},{6,0},{1,7},{3,5},{5,3},{7,1},{8,14},{10,12},{12... | collective-permute-start | bytes 1769480 | tf_op jit(solution)/shard_map/ppermute | solution.py:73
  369.6 56.1 %collective-permute-start.29 = (bf16[192,1536]{1,0:T(8,128)(2,1)}, bf16[192,1536]{1,0:T(8,128)(2,1)S(1)}, u32[]{:S(2)}, u32[]{:S(2)}) collective-permute-start(bf16[192,1536]{1,0:T(8,128)(2,1)} %get-tuple-element.146), channel_id=1, source_target_pairs={{0,4},{2,6},{4,0},{6,2},{1,5},{3,7},{5,1},{7,3},{8,12},{10,14},{12... | collective-permute-start | bytes 1769480 | tf_op jit(solution)/shard_map/ppermute | solution.py:73
  410.5 36.7 %collective-permute-start.28 = (bf16[192,1536]{1,0:T(8,128)(2,1)}, bf16[192,1536]{1,0:T(8,128)(2,1)}, u32[]{:S(2)}, u32[]{:S(2)}) collective-permute-start(bf16[192,1536]{1,0:T(8,128)(2,1)} %get-tuple-element.145), channel_id=1, source_target_pairs={{0,2},{2,0},{4,6},{6,4},{1,3},{3,1},{5,7},{7,5},{8,10},{10,8},{12,... | collective-permute-start | bytes 1769480 | tf_op jit(solution)/shard_map/ppermute | solution.py:73
  410.6 36.6 %copy-start.35 = (f32[192]{0:T(256)S(1)}, f32[192]{0:T(256)}, u32[]{:S(2)}) copy-start(f32[192]{0:T(256)} %copy-done.34) | copy-start | bytes 2308
  421.3 28.6 %collective-permute-start.26 = (bf16[192,1536]{1,0:T(8,128)(2,1)}, bf16[192,1536]{1,0:T(8,128)(2,1)S(1)}, u32[]{:S(2)}, u32[]{:S(2)}) collective-permute-start(bf16[192,1536]{1,0:T(8,128)(2,1)} %get-tuple-element.143), channel_id=1, source_target_pairs={{0,6},{2,4},{4,2},{6,0},{1,7},{3,5},{5,3},{7,1},{8,14},{10,12},{12... | collective-permute-start | bytes 1769480 | tf_op jit(solution)/shard_map/ppermute | solution.py:73
  423.3 51.8 %collective-permute-start.25 = (bf16[192,1536]{1,0:T(8,128)(2,1)}, bf16[192,1536]{1,0:T(8,128)(2,1)S(1)}, u32[]{:S(2)}, u32[]{:S(2)}) collective-permute-start(bf16[192,1536]{1,0:T(8,128)(2,1)} %get-tuple-element.142), channel_id=1, source_target_pairs={{0,4},{2,6},{4,0},{6,2},{1,5},{3,7},{5,1},{7,3},{8,12},{10,14},{12... | collective-permute-start | bytes 1769480 | tf_op jit(solution)/shard_map/ppermute | solution.py:73
  424.8 25.1 %copy-start.15 = (bf16[192,1536]{1,0:T(8,128)(2,1)}, bf16[192,1536]{1,0:T(8,128)(2,1)S(1)}, u32[]{:S(2)}) copy-start(bf16[192,1536]{1,0:T(8,128)(2,1)S(1)} %collective-permute-done.30) | copy-start | bytes 1769476
  424.8 50.3 %collective-permute-start.24 = (bf16[192,1536]{1,0:T(8,128)(2,1)}, bf16[192,1536]{1,0:T(8,128)(2,1)S(1)}, u32[]{:S(2)}, u32[]{:S(2)}) collective-permute-start(bf16[192,1536]{1,0:T(8,128)(2,1)} %get-tuple-element.141), channel_id=1, source_target_pairs={{0,2},{2,0},{4,6},{6,4},{1,3},{3,1},{5,7},{7,5},{8,10},{10,8},{12,... | collective-permute-start | bytes 1769480 | tf_op jit(solution)/shard_map/ppermute | solution.py:73
  447.2 27.9 %copy-start.17 = (bf16[192,1536]{1,0:T(8,128)(2,1)S(1)}, bf16[192,1536]{1,0:T(8,128)(2,1)}, u32[]{:S(2)}) copy-start(bf16[192,1536]{1,0:T(8,128)(2,1)} %get-tuple-element.144) | copy-start | bytes 1769476
  447.2 27.9 %copy-start.22 = (bf16[384,1536]{1,0:T(8,128)(2,1)S(1)}, bf16[384,1536]{1,0:T(8,128)(2,1)}, u32[]{:S(2)}) copy-start(bf16[384,1536]{1,0:T(8,128)(2,1)} %param.25) | copy-start | bytes 3538948
  447.2 27.9 %copy-start.26 = (bf16[192,1536]{1,0:T(8,128)(2,1)S(1)}, bf16[192,1536]{1,0:T(8,128)(2,1)}, u32[]{:S(2)}) copy-start(bf16[192,1536]{1,0:T(8,128)(2,1)} %get-tuple-element.140) | copy-start | bytes 1769476
  478.5 14.8 %collective-permute-start.31 = (bf16[192,1536]{1,0:T(8,128)(2,1)}, bf16[192,1536]{1,0:T(8,128)(2,1)S(1)}, u32[]{:S(2)}, u32[]{:S(2)}) collective-permute-start(bf16[192,1536]{1,0:T(8,128)(2,1)} %get-tuple-element.405), channel_id=1, source_target_pairs={{0,1},{1,0},{2,3},{3,2},{4,5},{5,4},{6,7},{7,6},{8,9},{9,8},{10,11... | collective-permute-start | bytes 1769480 | tf_op jit(solution)/shard_map/ppermute | solution.py:73
  639.8 46.8 %reduce-scatter.18.cloned.1.call-start = ((), (), s32[]{:S(2)}) async-start(), calls=%async_computation.10 | async-start | bytes 983040
  643.9 128.7 %reduce-scatter.20.cloned.1.call-start = ((), (), s32[]{:S(2)}) async-start(), calls=%async_computation.11 | async-start | bytes 417792
  694.4 15.6 %collective-permute-start.32 = (bf16[192,1536]{1,0:T(8,128)(2,1)}, bf16[192,1536]{1,0:T(8,128)(2,1)S(1)}, u32[]{:S(2)}, u32[]{:S(2)}) collective-permute-start(bf16[192,1536]{1,0:T(8,128)(2,1)} %dynamic-slice_convert_fusion), channel_id=1, source_target_pairs={{0,1},{1,0},{2,3},{3,2},{4,5},{5,4},{6,7},{7,6},{8,9},{9,8},{10,11... | collective-permute-start | bytes 1769480 | tf_op jit(solution)/shard_map/ppermute | solution.py:73
  709.3 38.6 %collective-permute-start.34 = (bf16[4,2,1536,256]{3,2,1,0:T(8,128)(2,1)}, bf16[4,2,1536,256]{3,2,1,0:T(8,128)(2,1)}, u32[]{:S(2)}, u32[]{:S(2)}) collective-permute-start(bf16[4,2,1536,256]{3,2,1,0:T(8,128)(2,1)} %get-tuple-element.157), channel_id=1, source_target_pairs={{0,8},{8,0},{16,24},{24,16},{1,9},{9,1},{17,25},{25,17},{2,10},{10... | collective-permute-start | bytes 18874376 | tf_op jit(solution)/shard_map/ppermute | solution.py:73
  715.2 125.5 %reduce-scatter.14.cloned.1.call-start = ((), (), s32[]{:S(2)}) async-start(), calls=%async_computation.8 | async-start | bytes 2506752 | tf_op jit(solution)/shard_map/reduce_scatter | solution.py:545
  719.3 194.4 %reduce-scatter.12.cloned.1.call-start = ((), (), s32[]{:S(2)}) async-start(), calls=%async_computation.7 | async-start | bytes 4177920 | tf_op jit(solution)/shard_map/reduce_scatter | solution.py:542
  719.6 22.8 %collective-permute-start.38 = (bf16[4,256,1536]{2,1,0:T(8,128)(2,1)}, bf16[4,256,1536]{2,1,0:T(8,128)(2,1)}, u32[]{:S(2)}, u32[]{:S(2)}) collective-permute-start(bf16[4,256,1536]{2,1,0:T(8,128)(2,1)} %get-tuple-element.159), channel_id=1, source_target_pairs={{0,8},{8,0},{16,24},{24,16},{1,9},{9,1},{17,25},{25,17},{2,10},{10... | collective-permute-start | bytes 9437192 | tf_op jit(solution)/shard_map/ppermute | solution.py:73
  720.4 19.6 %collective-permute-start.27 = (bf16[192,1536]{1,0:T(8,128)(2,1)S(1)}, bf16[192,1536]{1,0:T(8,128)(2,1)}, u32[]{:S(2)}, u32[]{:S(2)}) collective-permute-start(bf16[192,1536]{1,0:T(8,128)(2,1)S(1)} %copy-done.14), channel_id=1, source_target_pairs={{0,1},{1,0},{2,3},{3,2},{4,5},{5,4},{6,7},{7,6},{8,9},{9,8},{10,11... | collective-permute-start | bytes 1769480 | tf_op jit(solution)/shard_map/ppermute | solution.py:73
  745.9 55.4 %collective-permute-start.40 = (bf16[256,1536]{1,0:T(8,128)(2,1)S(1)}, bf16[256,1536]{1,0:T(8,128)(2,1)}, u32[]{:S(2)}, u32[]{:S(2)}) collective-permute-start(bf16[256,1536]{1,0:T(8,128)(2,1)S(1)} %get-tuple-element.416), channel_id=1, source_target_pairs={{0,16},{8,24},{16,0},{24,8},{1,17},{9,25},{17,1},{25,9},{2,18},{10... | collective-permute-start | bytes 2359304 | tf_op jit(solution)/shard_map/ppermute | solution.py:73
  747.3 95.6 %collective-permute-start.39 = (bf16[256,1536]{1,0:T(8,128)(2,1)}, bf16[256,1536]{1,0:T(8,128)(2,1)}, u32[]{:S(2)}, u32[]{:S(2)}) collective-permute-start(bf16[256,1536]{1,0:T(8,128)(2,1)} %get-tuple-element.415), channel_id=1, source_target_pairs={{0,16},{8,24},{16,0},{24,8},{1,17},{9,25},{17,1},{25,9},{2,18},{10... | collective-permute-start | bytes 2359304 | tf_op jit(solution)/shard_map/ppermute | solution.py:73
  752.5 54.8 %collective-permute-start.36 = (bf16[2,1536,256]{2,1,0:T(8,128)(2,1)}, bf16[2,1536,256]{2,1,0:T(8,128)(2,1)}, u32[]{:S(2)}, u32[]{:S(2)}) collective-permute-start(bf16[2,1536,256]{2,1,0:T(8,128)(2,1)} %get-tuple-element.414), channel_id=1, source_target_pairs={{0,1},{1,0},{2,3},{3,2},{4,5},{5,4},{6,7},{7,6},{8,9},{9,8},{10,11... | collective-permute-start | bytes 4718600 | tf_op jit(solution)/shard_map/ppermute | solution.py:73
  753.9 46.8 %copy-start.48 = (f32[2,96]{1,0:T(2,128)S(1)}, f32[2,96]{1,0:T(2,128)}, u32[]{:S(2)}) copy-start(f32[2,96]{1,0:T(2,128)} %param.31) | copy-start | bytes 2308
  753.9 46.8 %copy-start.49 = (f32[2,96]{1,0:T(2,128)S(1)}, f32[2,96]{1,0:T(2,128)}, u32[]{:S(2)}) copy-start(f32[2,96]{1,0:T(2,128)} %param.39) | copy-start | bytes 2308
  753.9 46.8 %copy-start.50 = (f32[2,96]{1,0:T(2,128)S(1)}, f32[2,96]{1,0:T(2,128)}, u32[]{:S(2)}) copy-start(f32[2,96]{1,0:T(2,128)} %param.38) | copy-start | bytes 2308
  754.3 51.2 %collective-permute-start.33 = (bf16[192,1536]{1,0:T(8,128)(2,1)S(1)}, bf16[192,1536]{1,0:T(8,128)(2,1)S(1)}, u32[]{:S(2)}, u32[]{:S(2)}) collective-permute-start(bf16[192,1536]{1,0:T(8,128)(2,1)S(1)} %add_convert_fusion.8), channel_id=1, source_target_pairs={{0,1},{1,0},{2,3},{3,2},{4,5},{5,4},{6,7},{7,6},{8,9},{9,8},{10,11... | collective-permute-start | bytes 1769480 | tf_op jit(solution)/shard_map/ppermute | solution.py:73
  804.0 38.9 %collective-permute-start.41 = (bf16[256,1536]{1,0:T(8,128)(2,1)}, bf16[256,1536]{1,0:T(8,128)(2,1)}, u32[]{:S(2)}, u32[]{:S(2)}) collective-permute-start(bf16[256,1536]{1,0:T(8,128)(2,1)} %fusion.57), channel_id=1, source_target_pairs={{0,1},{1,0},{2,3},{3,2},{4,5},{5,4},{6,7},{7,6},{8,9},{9,8},{10,11... | collective-permute-start | bytes 2359304 | tf_op jit(solution)/shard_map/ppermute | solution.py:73
  806.6 34.1 %copy-start.24 = (f32[768,96]{0,1:T(8,128)S(1)}, f32[768,96]{0,1:T(8,128)}, u32[]{:S(2)}) copy-start(f32[768,96]{0,1:T(8,128)} %param.30) | copy-start | bytes 884740
  806.7 109.7 %collective-permute-start.35 = (bf16[2,1536,256]{2,1,0:T(8,128)(2,1)}, bf16[2,1536,256]{2,1,0:T(8,128)(2,1)}, u32[]{:S(2)}, u32[]{:S(2)}) collective-permute-start(bf16[2,1536,256]{2,1,0:T(8,128)(2,1)} %get-tuple-element.413), channel_id=1, source_target_pairs={{0,1},{1,0},{2,3},{3,2},{4,5},{5,4},{6,7},{7,6},{8,9},{9,8},{10,11... | collective-permute-start | bytes 4718600 | tf_op jit(solution)/shard_map/ppermute | solution.py:73
  807.2 35.6 %copy-start.18 = (f32[1,256,1536]{2,1,0:T(8,128)S(1)}, f32[1,256,1536]{2,1,0:T(8,128)}, u32[]{:S(2)}) copy-start(f32[1,256,1536]{2,1,0:T(8,128)} %param.43) | copy-start | bytes 4718596
  811.4 31.4 %copy-start.8 = (f32[1,256,1536]{2,1,0:T(8,128)S(1)}, f32[1,256,1536]{2,1,0:T(8,128)}, u32[]{:S(2)}) copy-start(f32[1,256,1536]{2,1,0:T(8,128)} %param.33) | copy-start | bytes 4718596
  811.4 105.0 %collective-permute-start.37 = (bf16[2,1536,256]{2,1,0:T(8,128)(2,1)}, bf16[2,1536,256]{2,1,0:T(8,128)(2,1)}, u32[]{:S(2)}, u32[]{:S(2)}) collective-permute-start(bf16[2,1536,256]{2,1,0:T(8,128)(2,1)} %fusion.49), channel_id=1, source_target_pairs={{0,16},{8,24},{16,0},{24,8},{1,17},{9,25},{17,1},{25,9},{2,18},{10... | collective-permute-start | bytes 4718600 | tf_op jit(solution)/shard_map/ppermute | solution.py:73
  848.2 68.2 %copy-start.2 = (f32[1,2,1536,256]{3,2,1,0:T(8,128)S(1)}, f32[1,2,1536,256]{3,2,1,0:T(8,128)}, u32[]{:S(2)}) copy-start(f32[1,2,1536,256]{3,2,1,0:T(8,128)} %param.32) | copy-start | bytes 9437188
  (99 other events, 407.5 us)
Sparse Core Ops, SparseCore 0:
  10.9 81.4 all-gather.3
  95.3 48.3 all-gather.5
  639.9 21.2 reduce-scatter.15
  663.9 22.5 reduce-scatter.17
  715.3 57.2 reduce-scatter.19
  776.7 63.9 reduce-scatter.13
  844.6 69.0 reduce-scatter.11

commit v2 on v1

--- a/solution.py
+++ b/solution.py
@@ -23,40 +23,12 @@
 RATE_DOWN = 0.001
 
 
-def rotate(values, position, direction):
-    half_width = values.shape[-1] // 2
-    frequency = jnp.exp(
-        jnp.arange(half_width, dtype=jnp.float32) * (-2.0 * math.log(ROPE_BASE) / values.shape[-1])
-    )
-    angles = position.astype(jnp.float32)[:, None] * frequency[None, :]
-    cosine = jnp.cos(angles)[:, None, :]
-    sine_part = direction * jnp.sin(angles)[:, None, :]
-    first_half = values[..., :half_width]
-    second = values[..., half_width:]
-    return jnp.concatenate(
-        [first_half * cosine - second * sine_part, second * cosine + first_half * sine_part],
-        axis=-1,
-    )
-
-
 def doc_positions(lengths_row, places):
     doc_ends = jnp.cumsum(lengths_row)
     passed = places[:, None] >= doc_ends[None, :]
     segment = jnp.sum(passed.astype(jnp.int32), axis=1)
     doc_start = jnp.sum(jnp.where(passed, lengths_row[None, :], 0), axis=1)
     return (segment, places - doc_start)
-
-
-def contract_rows(left_mat, right_mat):
-    return lax.dot_general(
-        left_mat, right_mat, (((0,), (0,)), ((), ())), preferred_element_type=jnp.float32
-    )
-
-
-def contract_cols(left_mat, right_mat):
-    return lax.dot_general(
-        left_mat, right_mat, (((1,), (1,)), ((), ())), preferred_element_type=jnp.float32
-    )
 
 
 def norm_back(grad_out, normed, inverse, gain_row):
@@ -292,6 +264,386 @@
     for m in range(1, count):
         own_down += swap(downs[m], "tp", m).astype(f32)
     return own_in.astype(f32) + swap(far_in, "fsdp", 2).astype(f32), own_down
+
+
+def gather_shards(own):
+    near = [own] + [swap(own, "ctx", m) for m in range(1, lax.axis_size("ctx"))]
+    near = near + [swap(piece, "fsdp", 2) for piece in near]
+    return near + [swap(piece, "fsdp", 1) for piece in near]
+
+
+def load_shards(place_ref, shard_refs, whole, sems, n_ctx):
+    rows = shard_refs[0].shape[0]
+    copies = []
+    for i, shard in enumerate(shard_refs):
+        index = (place_ref[0] ^ F_MASKS[i // n_ctx]) * n_ctx + (place_ref[1] ^ (i % n_ctx))
+        at = pl.multiple_of(index * rows, rows)
+        copies.append(pltpu.make_async_copy(shard, whole.at[pl.ds(at, rows)], sems.at[i]))
+    return copies
+
+
+def turn(first, second, cosine, sine):
+    return first * cosine - second * sine, second * cosine + first * sine
+
+
+def project_kernel(n_ctx, shards, q_rows, k_rows, v_rows, *refs):
+    place, tok, cos_ref, sin_ref = refs[:4]
+    shard_refs, refs = refs[4 : 4 + shards], refs[4 + shards :]
+    q_ref, kv_ref, norm_t, whole, gain_ref, sems = refs
+    copies = load_shards(place, shard_refs, whole, sems, n_ctx)
+    for copy in copies:
+        copy.start()
+    x = tok[...].astype(jnp.float32)
+    hat = x * lax.rsqrt(jnp.mean(x * x, axis=-1, keepdims=True) + EPSILON)
+    for copy in copies:
+        copy.wait()
+    columns = q_rows + k_rows + v_rows
+    gains = whole[:, columns:].astype(jnp.float32).T
+    gain_ref[...] = gains[:8]
+    normed = (hat * gains[:1]).astype(jnp.bfloat16)
+    norm_t[...] = normed.T
+    cosine, sine = cos_ref[...], sin_ref[...]
+    half = HD // 2
+    heads = jnp.dot(normed, whole[:, :columns], preferred_element_type=jnp.float32).T
+    for at in range(0, q_rows, HD):
+        a, b = turn(heads[at : at + half], heads[at + half : at + HD], cosine, sine)
+        q_ref[at : at + half] = a.astype(jnp.bfloat16) * jnp.bfloat16(HD**-0.5)
+        q_ref[at + half : at + HD] = b.astype(jnp.bfloat16) * jnp.bfloat16(HD**-0.5)
+    for at in range(0, k_rows, HD):
+        here = q_rows + at
+        a, b = turn(heads[here : here + half], heads[here + half : here + HD], cosine, sine)
+        kv_ref[at : at + half] = a.astype(jnp.bfloat16)
+        kv_ref[at + half : at + HD] = b.astype(jnp.bfloat16)
+    kv_ref[k_rows:] = heads[q_rows + k_rows :].astype(jnp.bfloat16)
+
+
+def vmem_spec():
+    return pl.BlockSpec(memory_space=pltpu.VMEM)
+
+
+def any_spec():
+    return pl.BlockSpec(memory_space=pl.ANY)
+
+
+def smem_spec():
+    return pl.BlockSpec(memory_space=pltpu.SMEM)
+
+
+def project(place, tokens, cosine, sine, shards, q_rows, k_rows):
+    n_ctx = lax.axis_size("ctx")
+    rows, width = tokens.shape
+    low = jnp.bfloat16
+    columns = shards[0].shape[1]
+    return pl.pallas_call(
+        functools.partial(project_kernel, n_ctx, len(shards), q_rows, k_rows, k_rows),
+        out_shape=[
+            jax.ShapeDtypeStruct((q_rows, rows), low),
+            jax.ShapeDtypeStruct((2 * k_rows, rows), low),
+            jax.ShapeDtypeStruct((width, rows), low),
+            jax.ShapeDtypeStruct((width, columns), low),
+            jax.ShapeDtypeStruct((8, width), jnp.float32),
+        ],
+        in_specs=[smem_spec()] + [vmem_spec()] * 3 + [any_spec()] * len(shards),
+        out_specs=[vmem_spec()] * 5,
+        scratch_shapes=[pltpu.SemaphoreType.DMA((len(shards),))],
+        compiler_params=pltpu.CompilerParams(vmem_limit_bytes=VMEM_LIMIT),
+        cost_estimate=pl.CostEstimate(
+            flops=2 * rows * width * columns, bytes_accessed=12 << 20, transcendentals=0
+        ),
+        name="project",
+    )(place, tokens, cosine, sine, *shards)
+
+
+def attend_kernel(n_ctx, shards, *refs):
+    place, start_ref, q_ref = refs[:3]
+    piece_refs, refs = refs[3 : 3 + n_ctx], refs[3 + n_ctx :]
+    shard_refs, refs = refs[:shards], refs[shards:]
+    p_ref, head_ref, part_ref, kv_all, out_t, bias, scores, q3, sems = refs
+    rows = q_ref.shape[1]
+    half_kv = kv_all.shape[0] // 2
+    step = pl.program_id(0)
+    copies = load_shards(place, shard_refs, out_t, sems, n_ctx)
+
+    @pl.when(step == 0)
+    def _():
+        for copy in copies:
+            copy.start()
+        key_at = lax.broadcasted_iota(jnp.int32, (rows, rows), 0)
+        query_at = lax.broadcasted_iota(jnp.int32, (rows, rows), 1)
+        for j in range(n_ctx):
+            kv_all[:, j * rows : (j + 1) * rows] = piece_refs[j][...]
+            allowed = key_at + (place[1] - j) * rows >= start_ref[...]
+            if j == 0:
+                allowed = allowed & (key_at <= query_at)
+            bias[j * rows : (j + 1) * rows] = jnp.where(allowed, 0.0, -1e30)
+
+    for h in range(GROUP):
+        q3[:, h * rows : (h + 1) * rows] = q_ref[h * HD : (h + 1) * HD]
+    keys = kv_all[pl.ds(pl.multiple_of(step * HD, HD), HD)]
+    values = kv_all[pl.ds(pl.multiple_of(half_kv + step * HD, HD), HD)]
+    scores[...] = jnp.dot(keys.T, q3[...], preferred_element_type=jnp.float32)
+    for h in range(GROUP):
+        cols = slice(h * rows, (h + 1) * rows)
+        masked = scores[:, cols] + bias[...]
+        exponent = jnp.exp(masked - jnp.max(masked, axis=0, keepdims=True))
+        inverse = 1.0 / jnp.sum(exponent, axis=0, keepdims=True)
+        p_ref[0, :, cols] = (exponent * inverse).astype(jnp.bfloat16)
+    attended = jnp.dot(values, p_ref[0], preferred_element_type=jnp.float32).astype(jnp.bfloat16)
+    for h in range(GROUP):
+        at = pl.multiple_of((step * GROUP + h) * HD, HD)
+        head_ref[pl.ds(at, HD)] = attended[:, h * rows : (h + 1) * rows]
+
+    @pl.when(step == pl.num_programs(0) - 1)
+    def _():
+        for copy in copies:
+            copy.wait()
+        part_ref[...] = nt_dot(head_ref[...].T, out_t[...])
+
+
+def attend(place, starts, q_t, pieces, shards):
+    n_ctx = lax.axis_size("ctx")
+    q_rows, rows = q_t.shape
+    kv = q_rows // (GROUP * HD)
+    width = shards[0].shape[0] * len(shards)
+    seq = rows * n_ctx
+    low = jnp.bfloat16
+    return pl.pallas_call(
+        functools.partial(attend_kernel, n_ctx, len(shards)),
+        grid=(kv,),
+        out_shape=[
+            jax.ShapeDtypeStruct((kv, seq, GROUP * rows), low),
+            jax.ShapeDtypeStruct((q_rows, rows), low),
+            jax.ShapeDtypeStruct((rows, width), jnp.float32),
+            jax.ShapeDtypeStruct((2 * kv * HD, seq), low),
+            jax.ShapeDtypeStruct((width, q_rows), low),
+        ],
+        in_specs=[smem_spec(), vmem_spec(), pl.BlockSpec((GROUP * HD, rows), lambda i: (i, 0))]
+        + [vmem_spec()] * n_ctx
+        + [any_spec()] * len(shards),
+        out_specs=[pl.BlockSpec((1, seq, GROUP * rows), lambda i: (i, 0, 0))] + [vmem_spec()] * 4,
+        scratch_shapes=[
+            pltpu.VMEM((seq, rows), jnp.float32),
+            pltpu.VMEM((seq, GROUP * rows), jnp.float32),
+            pltpu.VMEM((HD, GROUP * rows), low),
+            pltpu.SemaphoreType.DMA((len(shards),)),
+        ],
+        compiler_params=pltpu.CompilerParams(vmem_limit_bytes=VMEM_LIMIT),
+        cost_estimate=pl.CostEstimate(
+            flops=2 * q_rows * rows * (2 * seq + width), bytes_accessed=20 << 20, transcendentals=0
+        ),
+        name="attend",
+    )(place, starts, q_t, *pieces, *shards)
+
+
+def attend_back_kernel(n_ctx, *refs):
+    p_ref, q_ref, kv_all, grad_ref, out_t, cos_ref, sin_ref = refs[:7]
+    dq_ref, own_ref = refs[7:9]
+    piece_refs, refs = refs[9 : 8 + n_ctx], refs[8 + n_ctx :]
+    grads, q3, g3 = refs
+    rows = q_ref.shape[1]
+    half_kv = kv_all.shape[0] // 2
+    step = pl.program_id(0)
+
+    @pl.when(step == 0)
+    def _():
+        back = jnp.dot(grad_ref[...], out_t[...], preferred_element_type=jnp.float32)
+        grads[...] = back.astype(jnp.bfloat16).T
+
+    for h in range(GROUP):
+        cols = slice(h * rows, (h + 1) * rows)
+        q3[:, cols] = q_ref[h * HD : (h + 1) * HD]
+        g3[:, cols] = grads[pl.ds(pl.multiple_of((step * GROUP + h) * HD, HD), HD)]
+    keys = kv_all[pl.ds(pl.multiple_of(step * HD, HD), HD)]
+    values = kv_all[pl.ds(pl.multiple_of(half_kv + step * HD, HD), HD)]
+    probs = p_ref[0].astype(jnp.float32)
+    grad_probs = jnp.dot(values.T, g3[...], preferred_element_type=jnp.float32)
+    inner = jnp.sum(probs * grad_probs, axis=0, keepdims=True)
+    grad_scores = (probs * (grad_probs - inner)).astype(jnp.bfloat16)
+    grad_query = jnp.dot(keys, grad_scores, preferred_element_type=jnp.float32) * HD**-0.5
+    grad_key = nt_dot(grad_scores, q3[...]).T
+    grad_value = nt_dot(p_ref[0], g3[...]).T
+    half = HD // 2
+    cosine, sine = cos_ref[...], -sin_ref[...]
+    for h in range(GROUP):
+        cols = slice(h * rows, (h + 1) * rows)
+        a, b = turn(grad_query[:half, cols], grad_query[half:, cols], cosine, sine)
+        dq_ref[h * HD : h * HD + half] = a.astype(jnp.bfloat16)
+        dq_ref[h * HD + half : (h + 1) * HD] = b.astype(jnp.bfloat16)
+    key_at = pl.ds(pl.multiple_of(step * HD, HD), HD)
+    value_at = pl.ds(pl.multiple_of(half_kv + step * HD, HD), HD)
+    own_ref[key_at] = grad_key[:, :rows]
+    own_ref[value_at] = grad_value[:, :rows]
+    for j in range(1, n_ctx):
+        cols = slice(j * rows, (j + 1) * rows)
+        piece_refs[j - 1][key_at] = grad_key[:, cols].astype(jnp.bfloat16)
+        piece_refs[j - 1][value_at] = grad_value[:, cols].astype(jnp.bfloat16)
+
+
+def attend_back(probs, q_t, kv_all, grad_attn, out_t, cosine, sine):
+    n_ctx = lax.axis_size("ctx")
+    q_rows, rows = q_t.shape
+    kv, seq = probs.shape[:2]
+    low = jnp.bfloat16
+    block = pl.BlockSpec((GROUP * HD, rows), lambda i: (i, 0))
+    return pl.pallas_call(
+        functools.partial(attend_back_kernel, n_ctx),
+        grid=(kv,),
+        out_shape=[
+            jax.ShapeDtypeStruct((q_rows, rows), low),
+            jax.ShapeDtypeStruct((2 * kv * HD, rows), jnp.float32),
+        ]
+        + [jax.ShapeDtypeStruct((2 * kv * HD, rows), low)] * (n_ctx - 1),
+        in_specs=[pl.BlockSpec((1, seq, GROUP * rows), lambda i: (i, 0, 0)), block] + [vmem_spec()] * 5,
+        out_specs=[block] + [vmem_spec()] * n_ctx,
+        scratch_shapes=[
+            pltpu.VMEM((q_rows, rows), low),
+            pltpu.VMEM((HD, GROUP * rows), low),
+            pltpu.VMEM((HD, GROUP * rows), low),
+        ],
+        compiler_params=pltpu.CompilerParams(vmem_limit_bytes=VMEM_LIMIT),
+        cost_estimate=pl.CostEstimate(
+            flops=2 * q_rows * rows * (4 * seq + out_t.shape[0]), bytes_accessed=20 << 20, transcendentals=0
+        ),
+        name="attend_back",
+    )(probs, q_t, kv_all, grad_attn, out_t, cosine, sine)
+
+
+def store_products(place, left_t, right, out_refs):
+    rows = out_refs[0].shape[0]
+    for mask, out in zip(F_MASKS, out_refs):
+        at = pl.multiple_of((place[0] ^ mask) * rows, rows)
+        out[...] = jnp.dot(
+            left_t[pl.ds(at, rows)], right, preferred_element_type=jnp.float32
+        ).astype(jnp.bfloat16)
+
+
+def out_grad_kernel(place, grad_ref, head_ref, *refs):
+    out_refs, grad_t = refs[:-1], refs[-1]
+    grad_t[...] = grad_ref[...].T
+    store_products(place, grad_t, head_ref[...].T, out_refs)
+
+
+def out_weight_grads(place, grad_attn, head_t):
+    rows, width = grad_attn.shape
+    parts = len(F_MASKS)
+    return pl.pallas_call(
+        out_grad_kernel,
+        out_shape=[jax.ShapeDtypeStruct((width // parts, head_t.shape[0]), jnp.bfloat16)] * parts,
+        in_specs=[smem_spec()] + [vmem_spec()] * 2,
+        out_specs=[vmem_spec()] * parts,
+        scratch_shapes=[pltpu.VMEM((width, rows), jnp.bfloat16)],
+        compiler_params=pltpu.CompilerParams(vmem_limit_bytes=VMEM_LIMIT),
+        cost_estimate=pl.CostEstimate(
+            flops=2 * rows * width * head_t.shape[0], bytes_accessed=5 << 20, transcendentals=0
+        ),
+        name="out_weight_grads",
+    )(place, grad_attn, head_t)
+
+
+def query_grad_kernel(place, dq_ref, norm_t, whole, *refs):
+    out_refs, part_ref = refs[:-1], refs[-1]
+    back = dq_ref[...].T
+    store_products(place, norm_t, back, out_refs)
+    part_ref[...] = nt_dot(back, whole[:, : back.shape[1]])
+
+
+def query_grads(place, dq_t, norm_t, whole):
+    q_rows, rows = dq_t.shape
+    width = norm_t.shape[0]
+    parts = len(F_MASKS)
+    outs = pl.pallas_call(
+        query_grad_kernel,
+        out_shape=[jax.ShapeDtypeStruct((width // parts, q_rows), jnp.bfloat16)] * parts
+        + [jax.ShapeDtypeStruct((rows, width), jnp.float32)],
+        in_specs=[smem_spec()] + [vmem_spec()] * 3,
+        out_specs=[vmem_spec()] * (parts + 1),
+        compiler_params=pltpu.CompilerParams(vmem_limit_bytes=VMEM_LIMIT),
+        cost_estimate=pl.CostEstimate(
+            flops=4 * rows * width * q_rows, bytes_accessed=10 << 20, transcendentals=0
+        ),
+        name="query_grads",
+    )(place, dq_t, norm_t, whole)
+    return outs[:parts], outs[parts]
+
+
+def key_grad_kernel(n_ctx, q_rows, *refs):
+    place, own_ref = refs[:2]
+    piece_refs, refs = refs[2 : 1 + n_ctx], refs[1 + n_ctx :]
+    cos_ref, sin_ref, norm_t, whole, tok, query_part, gain_two_ref = refs[:7]
+    out_refs, part_ref, back_t, right = refs[7:-3], refs[-3], refs[-2], refs[-1]
+    kv_rows, rows = own_ref.shape
+    total = own_ref[...]
+    for piece in piece_refs:
+        total += piece[...].astype(jnp.float32)
+    cosine, sine = cos_ref[...], -sin_ref[...]
+    half = HD // 2
+    for at in range(0, kv_rows // 2, HD):
+        a, b = turn(total[at : at + half], total[at + half : at + HD], cosine, sine)
+        back_t[at : at + half] = a.astype(jnp.bfloat16)
+        back_t[at + half : at + HD] = b.astype(jnp.bfloat16)
+    back_t[kv_rows // 2 :] = total[kv_rows // 2 :].astype(jnp.bfloat16)
+    back = back_t[...].T
+    part = query_part[...] + nt_dot(back, whole[:, q_rows : q_rows + kv_rows])
+    part_ref[...] = part
+    store_products(place, norm_t, back, [out.at[:, :kv_rows] for out in out_refs])
+    x = tok[...].astype(jnp.float32)
+    hat = x * lax.rsqrt(jnp.mean(x * x, axis=-1, keepdims=True) + EPSILON)
+    gain_one = jnp.sum(part * hat, axis=0, keepdims=True)
+    row = lax.broadcasted_iota(jnp.int32, (128, x.shape[1]), 0)
+    columns = jnp.where(row == 0, gain_one, jnp.where(row == 1, gain_two_ref[...], 0.0))
+    right[...] = columns.T
+    count = out_refs[0].shape[0]
+    for mask, out in zip(F_MASKS, out_refs):
+        at = pl.multiple_of((place[0] ^ mask) * count, count)
+        out[:, kv_rows:] = right[pl.ds(at, count)].astype(jnp.bfloat16)
+
+
+def key_grads(place, own, pieces, cosine, sine, norm_t, whole, tokens, query_part, gain_two, q_rows):
+    n_ctx = lax.axis_size("ctx")
+    kv_rows, rows = own.shape
+    width = norm_t.shape[0]
+    parts = len(F_MASKS)
+    outs = pl.pallas_call(
+        functools.partial(key_grad_kernel, n_ctx, q_rows),
+        out_shape=[jax.ShapeDtypeStruct((width // parts, kv_rows + 128), jnp.bfloat16)] * parts
+        + [jax.ShapeDtypeStruct((rows, width), jnp.float32)],
+        in_specs=[smem_spec()] + [vmem_spec()] * (n_ctx + 7),
+        out_specs=[vmem_spec()] * (parts + 1),
+        scratch_shapes=[
+            pltpu.VMEM((kv_rows, rows), jnp.bfloat16),
+            pltpu.VMEM((width, 128), jnp.float32),
+        ],
+        compiler_params=pltpu.CompilerParams(vmem_limit_bytes=VMEM_LIMIT),
+        cost_estimate=pl.CostEstimate(
+            flops=4 * rows * width * kv_rows, bytes_accessed=12 << 20, transcendentals=0
+        ),
+        name="key_grads",
+    )(place, own, *pieces, cosine, sine, norm_t, whole, tokens, query_part, gain_two)
+    return outs[:parts], outs[parts]
+
+
+def scatter_rows(parts):
+    n_ctx = lax.axis_size("ctx")
+    ctx_index = lax.axis_index("ctx")
+    near, far, near_core, far_core = parts
+    far = added(far, swap(far_core, "fsdp", 1))
+    near = added(near, swap(near_core, "fsdp", 1))
+    near = added(near, swap(far, "fsdp", 2))
+    rows = near.shape[0] // n_ctx
+
+    def block(mask):
+        return lax.dynamic_slice_in_dim(near, (ctx_index ^ mask) * rows, rows)
+
+    total = block(0).astype(jnp.float32)
+    for m in range(1, n_ctx):
+        total += swap(block(m), "ctx", m).astype(jnp.float32)
+    return total
+
+
+def shift(value, distance):
+    size = lax.axis_size("ctx")
+    pairs = [(i, i - distance) for i in range(size) if 0 <= i - distance < size]
+    return lax.ppermute(value, "ctx", pairs)
 
 
 def advance(weight, gradient, moment, average, step_rate):
@@ -326,65 +678,42 @@
     tok_rows = tokens.shape[0]
     n_ctx = lax.axis_size("ctx")
     experts = lax.axis_size(("fsdp", "ctx"))
-    seq_len = tok_rows * n_ctx
-    score_scale = HD ** (-0.5)
-    qkv_local, out_local, gain_local = (
-        lax.all_gather(qkv_weight.astype(jnp.bfloat16), ("fsdp", "ctx"), axis=0, tiled=True),
-        lax.all_gather(out_weight.astype(jnp.bfloat16), ("fsdp", "ctx"), axis=1, tiled=True),
-        lax.all_gather(norm_gains.astype(jnp.bfloat16), ("fsdp", "ctx"), axis=1, tiled=True),
+    fsdp_index, ctx_index = lax.axis_index("fsdp"), lax.axis_index("ctx")
+    place = jnp.stack([fsdp_index, ctx_index]).astype(jnp.int32)
+    low = jnp.bfloat16
+    shard_rows, qkv_columns = qkv_weight.shape
+    kv_local = qkv_columns // ((GROUP + 2) * HD)
+    q_rows, k_rows = kv_local * GROUP * HD, kv_local * HD
+    by_head = qkv_weight.astype(low).reshape(shard_rows, kv_local, GROUP + 2, HD)
+    gain_columns = jnp.pad(norm_gains.astype(low).T, ((0, 0), (0, 126)))
+    qkv_own = jnp.concatenate(
+        [
+            by_head[:, :, :GROUP].reshape(shard_rows, q_rows),
+            by_head[:, :, GROUP].reshape(shard_rows, k_rows),
+            by_head[:, :, GROUP + 1].reshape(shard_rows, k_rows),
+            gain_columns,
+        ],
+        axis=1,
     )
-    gain_one = gain_local[0].astype(jnp.float32)
-    gain_two = gain_local[1].astype(jnp.float32)
-    places = jnp.arange(seq_len, dtype=jnp.int32)
-    seg_all, pos_all = doc_positions(lengths[0], places)
-    first_row = lax.axis_index("ctx") * tok_rows
-    seg_query = lax.dynamic_slice_in_dim(seg_all, first_row, tok_rows)
-    pos_query = lax.dynamic_slice_in_dim(pos_all, first_row, tok_rows)
-    place_query = first_row + jnp.arange(tok_rows, dtype=jnp.int32)
-    allowed = (seg_query[:, None] == seg_all[None, :]) & (places[None, :] <= place_query[:, None])
+    qkv_shards = gather_shards(qkv_own)
+    out_shards = gather_shards(out_weight.astype(low).T)
+    places = ctx_index * tok_rows + jnp.arange(tok_rows, dtype=jnp.int32)
+    _, position = doc_positions(lengths[0], places)
+    starts = (places - position)[None, :]
+    frequency = jnp.exp(
+        jnp.arange(HD // 2, dtype=jnp.float32) * (-2.0 * math.log(ROPE_BASE) / HD)
+    )
+    angles = frequency[:, None] * position.astype(jnp.float32)[None, :]
+    cosine, sine = jnp.cos(angles), jnp.sin(angles)
     inputs = tokens.astype(jnp.float32)
     inverse_one = lax.rsqrt(jnp.mean(inputs * inputs, axis=-1, keepdims=True) + EPSILON)
     normed_one = inputs * inverse_one
-    normed_low = (normed_one * gain_one).astype(jnp.bfloat16)
-    projected = jnp.dot(normed_low, qkv_local, preferred_element_type=jnp.float32)
-    kv_local = projected.shape[1] // ((GROUP + 2) * HD)
-    heads_local = kv_local * GROUP
-    pieces = projected.reshape(tok_rows, kv_local, GROUP + 2, HD)
-    queries = rotate(
-        pieces[:, :, :GROUP, :].reshape(tok_rows, heads_local, HD), pos_query, 1.0
-    ).astype(jnp.bfloat16)
-    keys_own = rotate(pieces[:, :, GROUP, :], pos_query, 1.0).astype(jnp.bfloat16)
-    values_own = pieces[:, :, GROUP + 1, :].astype(jnp.bfloat16)
-    keys_all, values_all = (
-        lax.all_gather(keys_own.reshape(tok_rows, kv_local * HD), "ctx", axis=0, tiled=True),
-        lax.all_gather(values_own.reshape(tok_rows, kv_local * HD), "ctx", axis=0, tiled=True),
+    q_t, kv_t, norm_t, qkv_whole, gains = project(
+        place, tokens, cosine, sine, qkv_shards, q_rows, k_rows
     )
-    key_heads = jnp.transpose(keys_all.reshape(seq_len, kv_local, HD), (1, 0, 2))
-    value_heads = jnp.transpose(values_all.reshape(seq_len, kv_local, HD), (1, 0, 2))
-    query_heads = jnp.transpose(queries, (1, 0, 2))
-    kv_of_head = jnp.arange(heads_local, dtype=jnp.int32) // GROUP
-
-    def scores_of(query_head, kv_index):
-        raw_scores = contract_cols(query_head, key_heads[kv_index]) * score_scale
-        return jnp.where(allowed, raw_scores, -1e30)
-
-    def attend(operands):
-        query_head, kv_index = operands
-        masked = scores_of(query_head, kv_index)
-        top_score = jnp.max(masked, axis=-1, keepdims=True)
-        exponent = jnp.exp(masked - top_score)
-        row_total = jnp.sum(exponent, axis=-1, keepdims=True)
-        soft_low = (exponent / row_total).astype(jnp.bfloat16)
-        attended = jnp.dot(soft_low, value_heads[kv_index], preferred_element_type=jnp.float32)
-        return (attended, (top_score + jnp.log(row_total))[:, 0])
-
-    attended_all, log_totals = lax.map(attend, (query_heads, kv_of_head))
-    head_out = (
-        jnp.transpose(attended_all, (1, 0, 2))
-        .reshape(tok_rows, heads_local * HD)
-        .astype(jnp.bfloat16)
-    )
-    attn_part = jnp.dot(head_out, out_local, preferred_element_type=jnp.float32)
+    gain_one, gain_two = gains[0], gains[1]
+    kv_pieces = [kv_t] + [shift(kv_t, -j) for j in range(1, n_ctx)]
+    probs, head_t, attn_part, kv_all, out_t = attend(place, starts, q_t, kv_pieces, out_shards)
     half_rows = tok_rows // lax.axis_size("tp")
     tp_index = lax.axis_index("tp")
     fsdp_index, ctx_index = lax.axis_index("fsdp"), lax.axis_index("ctx")
@@ -471,88 +800,34 @@
         grad_normed_two, normed_two, inverse_two, gain_two
     )
     grad_attn = both_halves(grad_hidden_half.astype(jnp.bfloat16))
-    out_weight_grad = contract_rows(head_out, grad_attn)
-    head_grad = contract_cols(grad_attn, out_local).astype(jnp.bfloat16)
-    grad_heads = jnp.transpose(head_grad.reshape(tok_rows, heads_local, HD), (1, 0, 2))
-
-    def attend_back(operands):
-        query_head, kv_index, grad_head, log_total = operands
-        masked = scores_of(query_head, kv_index)
-        soft_probs = jnp.exp(masked - log_total[:, None])
-        grad_probs = contract_cols(grad_head, value_heads[kv_index])
-        inner_sum = jnp.sum(soft_probs * grad_probs, axis=-1, keepdims=True)
-        grad_scores = (soft_probs * (grad_probs - inner_sum)).astype(jnp.bfloat16)
-        grad_query = (
-            jnp.dot(grad_scores, key_heads[kv_index], preferred_element_type=jnp.float32)
-            * score_scale
-        )
-        grad_key = contract_rows(grad_scores, query_head) * score_scale
-        grad_value = contract_rows(soft_probs.astype(jnp.bfloat16), grad_head)
-        return (grad_query, grad_key, grad_value)
-
-    grad_query_all, grad_key_all, grad_value_all = lax.map(
-        attend_back, (query_heads, kv_of_head, grad_heads, log_totals)
+    out_parts = out_weight_grads(place, grad_attn, head_t)
+    out_grad_sum = scatter_rows(out_parts).T
+    dq_t, own_grads, *far_grads = attend_back(probs, q_t, kv_all, grad_attn, out_t, cosine, sine)
+    query_parts, query_part = query_grads(place, dq_t, norm_t, qkv_whole)
+    come = [shift(far_grads[j - 1], j) for j in range(1, n_ctx)]
+    key_parts, grad_normed_part = key_grads(
+        place, own_grads, come, cosine, sine, norm_t, qkv_whole, tokens, query_part,
+        gain_grad_two[None], q_rows,
     )
-    grad_key_all = jnp.sum(grad_key_all.reshape(kv_local, GROUP, seq_len, HD), axis=1)
-    grad_value_all = jnp.sum(grad_value_all.reshape(kv_local, GROUP, seq_len, HD), axis=1)
-    grad_key_own, grad_value_own = (
-        lax.psum_scatter(
-            jnp.transpose(grad_key_all, (1, 0, 2))
-            .reshape(seq_len, kv_local * HD)
-            .astype(jnp.bfloat16),
-            "ctx",
-            scatter_dimension=0,
-            tiled=True,
-        ).astype(jnp.float32),
-        lax.psum_scatter(
-            jnp.transpose(grad_value_all, (1, 0, 2))
-            .reshape(seq_len, kv_local * HD)
-            .astype(jnp.bfloat16),
-            "ctx",
-            scatter_dimension=0,
-            tiled=True,
-        ).astype(jnp.float32),
-    )
-    grad_query_pre = rotate(jnp.transpose(grad_query_all, (1, 0, 2)), pos_query, -1.0)
-    grad_key_pre = rotate(grad_key_own.reshape(tok_rows, kv_local, HD), pos_query, -1.0)
-    grad_projected = (
-        jnp.concatenate(
-            [
-                grad_query_pre.reshape(tok_rows, kv_local, GROUP, HD),
-                grad_key_pre[:, :, None, :],
-                grad_value_own.reshape(tok_rows, kv_local, 1, HD),
-            ],
-            axis=2,
-        )
-        .reshape(tok_rows, -1)
-        .astype(jnp.bfloat16)
-    )
-    qkv_grad_part = contract_rows(normed_low, grad_projected)
-    grad_normed_part = contract_cols(grad_projected, qkv_local)
     grad_normed_one = sum_own(grad_normed_part)
     normed_one_half = own_half(normed_one)
-    gain_grad_one = jnp.sum(grad_normed_one * normed_one_half, axis=0)
     in_grad = both_halves(
         (
             grad_hidden_half
             + norm_back(grad_normed_one, normed_one_half, own_half(inverse_one), gain_one)
         ).astype(jnp.bfloat16)
     )
-    qkv_grad, out_grad_sum, gains_grad = (
-        lax.psum_scatter(
-            qkv_grad_part.astype(jnp.bfloat16), ("fsdp", "ctx"), scatter_dimension=0, tiled=True
-        ).astype(jnp.float32),
-        lax.psum_scatter(
-            out_weight_grad.astype(jnp.bfloat16), ("fsdp", "ctx"), scatter_dimension=1, tiled=True
-        ).astype(jnp.float32),
-        lax.psum_scatter(
-            jnp.stack([gain_grad_one, gain_grad_two]).astype(jnp.bfloat16),
-            ("fsdp", "ctx"),
-            scatter_dimension=1,
-            tiled=True,
-        ).astype(jnp.float32),
-    )
-    gains_grad = lax.psum(gains_grad, "tp")
+    query_grad, key_grad = scatter_rows(query_parts), scatter_rows(key_parts)
+    gains_grad = key_grad[:, 2 * k_rows : 2 * k_rows + 2].T
+    gains_grad = gains_grad + sum(swap(gains_grad, "tp", m) for m in over_tp[1:])
+    qkv_grad = jnp.concatenate(
+        [
+            query_grad.reshape(shard_rows, kv_local, GROUP, HD),
+            key_grad[:, :k_rows].reshape(shard_rows, kv_local, 1, HD),
+            key_grad[:, k_rows : 2 * k_rows].reshape(shard_rows, kv_local, 1, HD),
+        ],
+        axis=2,
+    ).reshape(shard_rows, qkv_columns)
     in_grad_local = in_grad_sum[None]
     down_grad_local = down_grad_sum[None]
     qkv_new = advance(qkv_weight, qkv_grad, qkv_moment, qkv_average, RATE_QKV)

time: 940 us -> 666 us (0.71)
  matrix products: 160 us -> 0 us
  blocking collectives: 151 us -> 0 us
  Pallas kernels: 95.5 us -> 166 us
  starting transfers between devices: 57.4 us -> 123 us
  loops' own time: 47.6 us -> 0 us
  local copies, waits for them, and re-layouts: 65.4 us -> 39.6 us
  other arithmetic: 78.7 us -> 63.2 us
  between operations: 15.1 us -> 2.24 us
    dot_general x90 -> x0, matrix products: 160 us -> none  [the longest x38 71.7 us: contract_cols(): lax.dot_general(left_mat, right_mat, (((1,), (1,)), ((), ())), preferred_...]
    ppermute x42 -> x91, waiting for transfers between devices: 111 us -> 236 us  [swap(): return lax.ppermute(value, axis, [(i, i ^ mask) for i in range(size)])]
    all_gather x3 -> x0, blocking collectives: 124 us -> none  [the longest x1 80.9 us: per_device(): lax.all_gather(norm_gains.astype(jnp.bfloat16), ('fsdp', 'ctx'), axis=1,...]
    reduce_scatter x2 -> x0, waiting for transfers between devices: 93.4 us -> none  [the longest x1 65.6 us: per_device(): lax.psum_scatter(qkv_grad_part.astype(jnp.bfloat16), ('fsdp', 'ctx'), sca...]
    pallas_call x0 -> x6, Pallas kernels: none -> 70.5 us  [the longest x1 24.1 us: attend_back(): pl.pallas_call(functools.partial(attend_back_kernel, n_ctx), grid=(kv,),...]
    unnamed x10 -> x0, waiting for transfers between devices: 55.6 us -> none
    another operation x2 -> x0, loops' own time: 47.6 us -> none  [the longest x1 24 us: per_device(): lax.map(attend_back, (query_heads, kv_of_head, grad_heads, log_totals))]
    ppermute x42 -> x91, starting transfers between devices: 56.6 us -> 101 us  [swap(): return lax.ppermute(value, axis, [(i, i ^ mask) for i in range(size)])]
  transfers between devices with their start and end apart: 49 -> 97, of which waited for: 11 -> 33; matrix products, arithmetic and copies ran while one was open for 17% -> 14% of each run, Pallas kernels for 10% -> 25%
where the time goes in v2:
time: 666 us; the launch traced here: 659 us
  waiting for transfers between devices  265 us (40%)
  Pallas kernels  166 us (25%)
  starting transfers between devices  123 us (18%)
  other arithmetic  63.2 us (9%)
  local copies, waits for them, and re-layouts  39.6 us (6%)
    ppermute x91, waiting for transfers between devices, swap(): return lax.ppermute(value, axis, [(i, i ^ mask) for i in range(size)])  236 us
    ppermute x91, starting transfers between devices, swap(): return lax.ppermute(value, axis, [(i, i ^ mask) for i in range(size)])  101 us
    pallas_call x2, Pallas kernels, expert_rows(): pl.pallas_call(functools.partial(expert_kernel, blocks, pieces), out_shap...  58.1 us
    ppermute x6, waiting for transfers between devices, shift(): return lax.ppermute(value, 'ctx', pairs)  28.7 us
    pallas_call x2, Pallas kernels, weight_grads(): pl.pallas_call(functools.partial(weight_kernel, blocks, calls), grid=(cou...  27.1 us
    pallas_call x1, Pallas kernels, attend_back(): pl.pallas_call(functools.partial(attend_back_kernel, n_ctx), grid=(kv,),...  24.1 us
    ppermute x6, starting transfers between devices, shift(): return lax.ppermute(value, 'ctx', pairs)  22.6 us
    unnamed x164, local copies, waits for them, and re-layouts  22 us
  transfers between devices with their start and end apart: 97, of which 33 were waited for; matrix products, arithmetic and copies ran while one was open for 14% of the time, Pallas kernels for 25%

profile of v2, /device:TPU:0, one launch (start us, length us, event | category | flops | bytes accessed | tf_op | source)
XLA Modules:
  0.0 659.2 jit_solution(15866324220441230620)
XLA Ops:
  2.3 3.0 collective-permute-start.18
  5.4 2.6 collective-permute-start.19
  11.4 2.5 collective-permute-start.36
  13.8 2.3 copy.110
  22.1 3.8 collective-permute-start.1
  27.7 2.6 collective-permute-start.3
  30.2 7.2 %collective-permute-done.refs_5_ = bf16[96,1408]{1,0:T(8,128)(2,1)S(1)} collective-permute-done((bf16[96,1408]{1,0:T(8,128)(2,1)S(1)}, bf16[96,1408]{1,0:T(8,128)(2,1)S(1)}, u32[]{:S(2)}, u32[]{:S(2)}) %collective-permute-start) | collective-permute-done | bytes 270368 | tf_op jit(solution)/shard_map/ppermute | solution.py:45
  38.7 6.8 %collective-permute-done.1.refs_6_ = bf16[96,1408]{1,0:T(8,128)(2,1)} collective-permute-done((bf16[96,1408]{1,0:T(8,128)(2,1)S(1)}, bf16[96,1408]{1,0:T(8,128)(2,1)}, u32[]{:S(2)}, u32[]{:S(2)}) %collective-permute-start.1) | collective-permute-done | bytes 270368 | tf_op jit(solution)/shard_map/ppermute | solution.py:45
  49.0 2.1 collective-permute-done.23.refs_13_
  59.8 3.7 collective-permute-done.4.refs_9_
  63.9 5.4 collective-permute-done.5.refs_10_
  70.8 4.3 collective-permute-done.6.refs_11_
  77.3 4.7 collective-permute-start.53
  82.0 2.1 collective-permute-start.54
  87.0 6.8 %project.1 = (bf16[768,384]{1,0:T(8,128)(2,1)}, bf16[512,384]{1,0:T(8,128)(2,1)}, bf16[1536,384]{1,0:T(8,128)(2,1)}, bf16[1536,1408]{1,0:T(8,128)(2,1)}, f32[8,1536]{1,0:T(8,128)}) custom-call(s32[2]{0:T(128)} %pad_add_fusion.refs_0_.place, bf16[384,1536]{1,0:T(8,128)(2,1)} %refs_9_.1, f32[32,384]{1,0:T(8,128)} %get-tuple-element.255.refs_2_.refs_5_, ...), custom_call_target="tpu_custom_call" | custom-call | flops 1660944384 | bytes 12582912 | tf_op jit(solution)/shard_map/project/pallas_call | solution.py:337
  93.7 27.8 %collective-permute-done.53.refs_2_.refs_6_ = bf16[192,1536]{1,0:T(8,128)(2,1)S(1)} collective-permute-done((bf16[192,1536]{1,0:T(8,128)(2,1)S(1)}, bf16[192,1536]{1,0:T(8,128)(2,1)S(1)}, u32[]{:S(2)}, u32[]{:S(2)}) %collective-permute-start.53) | collective-permute-done | bytes 589856 | tf_op jit(solution)/shard_map/ppermute | solution.py:45
  122.8 14.6 %collective-permute-start.16 = (bf16[512,384]{1,0:T(8,128)(2,1)}, bf16[512,384]{1,0:T(8,128)(2,1)S(1)}, u32[]{:S(2)}, u32[]{:S(2)}) collective-permute-start(bf16[512,384]{1,0:T(8,128)(2,1)} %get-tuple-element.65.refs_3_), channel_id=1, source_target_pairs={{0,4},{2,6},{1,5},{3,7},{8,12},{10,14},{9,13},{11,15},{16,20},{18,... | collective-permute-start | bytes 1179656 | tf_op jit(solution)/shard_map/ppermute | solution.py:646
  137.4 2.6 collective-permute-start.17
  141.6 5.6 collective-permute-done.16.refs_5_
  148.5 5.9 collective-permute-done.17.refs_6_
  155.5 21.0 %attend.1 = (bf16[4,1536,1152]{2,1,0:T(8,128)(2,1)}, bf16[768,384]{1,0:T(8,128)(2,1)}, f32[384,1536]{1,0:T(8,128)}, bf16[512,1536]{1,0:T(8,128)(2,1)}, bf16[1536,768]{1,0:T(8,128)(2,1)}) custom-call(s32[2]{0:T(128)} %pad_add_fusion.refs_0_.place, s32[1,384]{1,0:T(1,128)} %broadcast_in_dim.158.refs_1_, bf16[768,384]{1,0:T(8,128)(2,1)} %get-tuple-element.64.refs_2_.refs_1_, ...), custom_call_target="tpu_custom_call" | custom-call | flops 2717908992 | bytes 20971520 | tf_op jit(solution)/shard_map/attend/pallas_call | solution.py:410
  178.2 2.4 dynamic-slice_convert_fusion.1
  185.7 10.9 %collective-permute-done.46.refs_17_.refs_5_ = bf16[256,1536]{1,0:T(8,128)(2,1)} collective-permute-done((bf16[256,1536]{1,0:T(8,128)(2,1)}, bf16[256,1536]{1,0:T(8,128)(2,1)}, u32[]{:S(2)}, u32[]{:S(2)}) %collective-permute-start.46) | collective-permute-done | bytes 786464 | tf_op jit(solution)/shard_map/ppermute | solution.py:45
  197.2 7.0 %collective-permute-done.33 = bf16[192,1536]{1,0:T(8,128)(2,1)} collective-permute-done((bf16[192,1536]{1,0:T(8,128)(2,1)}, bf16[192,1536]{1,0:T(8,128)(2,1)}, u32[]{:S(2)}, u32[]{:S(2)}) %collective-permute-start.33) | collective-permute-done | bytes 589856 | tf_op jit(solution)/shard_map/ppermute | solution.py:45
  207.5 9.1 %collective-permute-start.51 = (bf16[192,1536]{1,0:T(8,128)(2,1)}, bf16[192,1536]{1,0:T(8,128)(2,1)}, u32[]{:S(2)}, u32[]{:S(2)}) collective-permute-start(bf16[192,1536]{1,0:T(8,128)(2,1)} %multiply_convert_fusion.refs_0_), channel_id=1, source_target_pairs={{0,4},{2,6},{4,0},{6,2},{1,5},{3,7},{5,1},{7,3},{8,12},{10,14},{12... | collective-permute-start | bytes 1769480 | tf_op jit(solution)/shard_map/ppermute | solution.py:45
  216.6 7.7 %collective-permute-start.52 = (bf16[192,1536]{1,0:T(8,128)(2,1)}, bf16[192,1536]{1,0:T(8,128)(2,1)}, u32[]{:S(2)}, u32[]{:S(2)}) collective-permute-start(bf16[192,1536]{1,0:T(8,128)(2,1)} %multiply_convert_fusion.refs_0_), channel_id=1, source_target_pairs={{0,6},{2,4},{4,2},{6,0},{1,7},{3,5},{5,3},{7,1},{8,14},{10,12},{12... | collective-permute-start | bytes 1769480 | tf_op jit(solution)/shard_map/ppermute | solution.py:45
  226.9 2.1 copy.125
  229.1 2.1 copy.119
  241.5 14.8 %collective-permute-done.51.refs_0_.refs_2_ = bf16[192,1536]{1,0:T(8,128)(2,1)} collective-permute-done((bf16[192,1536]{1,0:T(8,128)(2,1)}, bf16[192,1536]{1,0:T(8,128)(2,1)}, u32[]{:S(2)}, u32[]{:S(2)}) %collective-permute-start.51) | collective-permute-done | bytes 589856 | tf_op jit(solution)/shard_map/ppermute | solution.py:45
  256.5 12.5 %collective-permute-start.34 = (bf16[192,1536]{1,0:T(8,128)(2,1)}, bf16[192,1536]{1,0:T(8,128)(2,1)}, u32[]{:S(2)}, u32[]{:S(2)}) collective-permute-start(bf16[192,1536]{1,0:T(8,128)(2,1)} %multiply_convert_fusion.refs_0_), channel_id=1, source_target_pairs={{0,2},{2,0},{4,6},{6,4},{1,3},{3,1},{5,7},{7,5},{8,10},{10,8},{12,... | collective-permute-start | bytes 1769480 | tf_op jit(solution)/shard_map/ppermute | solution.py:45
  269.1 29.1 %expert_rows.3 = (bf16[192,1536]{1,0:T(8,128)(2,1)}, bf16[192,1536]{1,0:T(8,128)(2,1)}, bf16[384,2048]{1,0:T(8,128)(2,1)}, bf16[384,2048]{1,0:T(8,128)(2,1)}, bf16[384,2048]{1,0:T(8,128)(2,1)}) custom-call(bf16[192,1536]{1,0:T(8,128)(2,1)} %collective-permute-done.51.refs_0_.refs_2_, bf16[192,1536]{1,0:T(8,128)(2,1)} %collective-permute-done.52.refs_1_.refs_3_, ...), custom_call_target="tpu_custom_call" | custom-call | flops 12079595520 | bytes 26214400 | tf_op jit(solution)/shard_map/expert_rows/pallas_call | solution.py:119
  298.1 3.4 collective-permute-start.63
  301.6 29.0 %expert_rows.2 = (bf16[192,1536]{1,0:T(8,128)(2,1)}, bf16[192,1536]{1,0:T(8,128)(2,1)}, bf16[384,2048]{1,0:T(8,128)(2,1)}, bf16[384,2048]{1,0:T(8,128)(2,1)}, bf16[384,2048]{1,0:T(8,128)(2,1)}) custom-call(bf16[192,1536]{1,0:T(8,128)(2,1)} %multiply_convert_fusion.refs_0_, bf16[192,1536]{1,0:T(8,128)(2,1)} %collective-permute-done.34.refs_1_, ...), custom_call_target="tpu_custom_call" | custom-call | flops 12079595520 | bytes 26214400 | tf_op jit(solution)/shard_map/expert_rows/pallas_call | solution.py:119
  331.7 10.6 %mix_rows.1 = (bf16[192,1536]{1,0:T(8,128)(2,1)}, bf16[192,1536]{1,0:T(8,128)(2,1)}, bf16[192,1536]{1,0:T(8,128)(2,1)}, bf16[192,1536]{1,0:T(8,128)(2,1)}) custom-call(bf16[384,2048]{1,0:T(8,128)(2,1)} %get-tuple-element.68.refs_0_.refs_8_, bf16[384,2048]{1,0:T(8,128)(2,1)} %get-tuple-element.69.refs_1_.refs_9_, bf16[256,1536]{1,0:T(8,128)(2,1)} %copy-done.24, ...), custom_call_target="tpu_custom_call" | custom-call | flops 4831838208 | bytes 12582912 | tf_op jit(solution)/shard_map/mix_rows/pallas_call | solution.py:170
  342.3 3.5 collective-permute-start.59
  346.8 13.5 %weight_grads.3 = (bf16[4,2,1536,256]{3,2,1,0:T(8,128)(2,1)}, bf16[4,256,1536]{2,1,0:T(8,128)(2,1)}) custom-call(bf16[192,1536]{1,0:T(8,128)(2,1)} %multiply_convert_fusion.refs_0_, bf16[192,1536]{1,0:T(8,128)(2,1)} %collective-permute-done.34.refs_1_, bf16[192,1536]{1,0:T(8,128)(2,1)} %collective-permute-done.51.refs_0_.refs_2_, ...), custom_call_target="tpu_custom_call" | custom-call | flops 7247757312 | bytes 20971520 | tf_op jit(solution)/shard_map/weight_grads/pallas_call | solution.py:221
  360.2 17.6 %collective-permute-done.62 = bf16[192,1536]{1,0:T(8,128)(2,1)} collective-permute-done((bf16[192,1536]{1,0:T(8,128)(2,1)}, bf16[192,1536]{1,0:T(8,128)(2,1)}, u32[]{:S(2)}, u32[]{:S(2)}) %collective-permute-start.62) | collective-permute-done | bytes 589856 | tf_op jit(solution)/shard_map/ppermute | solution.py:45
  377.9 2.4 multiply_reduce_fusion.2
  380.3 22.2 %collective-permute-done.58 = bf16[192,1536]{1,0:T(8,128)(2,1)} collective-permute-done((bf16[192,1536]{1,0:T(8,128)(2,1)}, bf16[192,1536]{1,0:T(8,128)(2,1)}, u32[]{:S(2)}, u32[]{:S(2)}) %collective-permute-start.58) | collective-permute-done | bytes 589856 | tf_op jit(solution)/shard_map/ppermute | solution.py:45
  402.6 4.1 fusion.29
  407.5 13.6 %weight_grads.2 = (bf16[4,2,1536,256]{3,2,1,0:T(8,128)(2,1)}, bf16[4,256,1536]{2,1,0:T(8,128)(2,1)}) custom-call(bf16[192,1536]{1,0:T(8,128)(2,1)} %multiply_convert_fusion.refs_0_, bf16[192,1536]{1,0:T(8,128)(2,1)} %collective-permute-done.34.refs_1_, bf16[192,1536]{1,0:T(8,128)(2,1)} %collective-permute-done.51.refs_0_.refs_2_, ...), custom_call_target="tpu_custom_call" | custom-call | flops 7247757312 | bytes 20971520 | tf_op jit(solution)/shard_map/weight_grads/pallas_call | solution.py:221
  425.4 24.1 %attend_back.1 = (bf16[768,384]{1,0:T(8,128)(2,1)}, f32[512,384]{1,0:T(8,128)}, bf16[512,384]{1,0:T(8,128)(2,1)}, bf16[512,384]{1,0:T(8,128)(2,1)}, bf16[512,384]{1,0:T(8,128)(2,1)}) custom-call(bf16[4,1536,1152]{2,1,0:T(8,128)(2,1)} %get-tuple-element.78.refs_0_, bf16[768,384]{1,0:T(8,128)(2,1)} %get-tuple-element.64.refs_2_.refs_1_, ...), custom_call_target="tpu_custom_call" | custom-call | flops 4529848320 | bytes 20971520 | tf_op jit(solution)/shard_map/attend_back/pallas_call | solution.py:488
  453.7 6.6 query_grads.1
  463.1 4.0 out_weight_grads.1
  468.7 17.2 %collective-permute-done.66.refs_3_ = bf16[512,384]{1,0:T(8,128)(2,1)} collective-permute-done((bf16[512,384]{1,0:T(8,128)(2,1)}, bf16[512,384]{1,0:T(8,128)(2,1)}, u32[]{:S(2)}, u32[]{:S(2)}) %collective-permute-start.66) | collective-permute-done | bytes 393248 | tf_op jit(solution)/shard_map/ppermute | solution.py:646
  485.9 8.0 %key_grads.1 = (bf16[384,640]{1,0:T(8,128)(2,1)}, bf16[384,640]{1,0:T(8,128)(2,1)}, bf16[384,640]{1,0:T(8,128)(2,1)}, bf16[384,640]{1,0:T(8,128)(2,1)}, f32[384,1536]{1,0:T(8,128)}) custom-call(s32[2]{0:T(128)} %pad_add_fusion.refs_0_.place, f32[512,384]{1,0:T(8,128)} %get-tuple-element.81.refs_1_, bf16[512,384]{1,0:T(8,128)(2,1)} %copy-done.34, ...), custom_call_target="tpu_custom_call" | custom-call | flops 1207959552 | bytes 12582912 | tf_op jit(solution)/shard_map/key_grads/pallas_call | solution.py:606
  499.3 11.9 %collective-permute-done.68 = bf16[192,1536]{1,0:T(8,128)(2,1)S(1)} collective-permute-done((bf16[192,1536]{1,0:T(8,128)(2,1)S(1)}, bf16[192,1536]{1,0:T(8,128)(2,1)S(1)}, u32[]{:S(2)}, u32[]{:S(2)}) %collective-permute-start.68) | collective-permute-done | bytes 589856 | tf_op jit(solution)/shard_map/ppermute | solution.py:45
  516.4 11.0 %collective-permute-done.72 = bf16[384,768]{1,0:T(8,128)(2,1)S(1)} collective-permute-done((bf16[384,768]{1,0:T(8,128)(2,1)S(1)}, bf16[384,768]{1,0:T(8,128)(2,1)S(1)}, u32[]{:S(2)}, u32[]{:S(2)}) %collective-permute-start.72) | collective-permute-done | bytes 589856 | tf_op jit(solution)/shard_map/ppermute | solution.py:45
  528.6 5.6 collective-permute-done.85
  537.0 4.1 collective-permute-done.78
  542.7 11.3 %collective-permute-done.74 = bf16[96,768]{1,0:T(8,128)(2,1)S(1)} collective-permute-done((bf16[96,768]{1,0:T(8,128)(2,1)S(1)}, bf16[96,768]{1,0:T(8,128)(2,1)S(1)}, u32[]{:S(2)}, u32[]{:S(2)}) %collective-permute-start.74) | collective-permute-done | bytes 147488 | tf_op jit(solution)/shard_map/ppermute | solution.py:45
  555.2 4.6 collective-permute-done.80
  562.2 5.4 fusion.5
  568.8 3.1 fusion.13
  574.7 2.1 copy.131
  576.8 2.1 copy.132
  578.9 2.1 copy.133
  587.6 3.4 collective-permute-done.95
  595.0 10.2 %collective-permute-done.91 = bf16[2,1536,256]{2,1,0:T(8,128)(2,1)} collective-permute-done((bf16[2,1536,256]{2,1,0:T(8,128)(2,1)}, bf16[2,1536,256]{2,1,0:T(8,128)(2,1)}, u32[]{:S(2)}, u32[]{:S(2)}) %collective-permute-start.91) | collective-permute-done | bytes 1572896 | tf_op jit(solution)/shard_map/ppermute | solution.py:45
  605.3 3.0 fusion
  612.2 9.8 %collective-permute-done.96 = bf16[256,1536]{1,0:T(8,128)(2,1)S(1)} collective-permute-done((bf16[256,1536]{1,0:T(8,128)(2,1)S(1)}, bf16[256,1536]{1,0:T(8,128)(2,1)S(1)}, u32[]{:S(2)}, u32[]{:S(2)}) %collective-permute-start.96) | collective-permute-done | bytes 786464 | tf_op jit(solution)/shard_map/ppermute | solution.py:45
  622.1 4.5 multiply_add_fusion.1
  626.5 26.3 %collective-permute-done.90 = bf16[2,1536,256]{2,1,0:T(8,128)(2,1)S(1)} collective-permute-done((bf16[2,1536,256]{2,1,0:T(8,128)(2,1)S(1)}, bf16[2,1536,256]{2,1,0:T(8,128)(2,1)S(1)}, u32[]{:S(2)}, u32[]{:S(2)}) %collective-permute-start.90) | collective-permute-done | bytes 1572896 | tf_op jit(solution)/shard_map/ppermute | solution.py:45
  652.8 5.9 multiply_add_fusion
  (393 shorter events, 115.6 us)
Async XLA Ops:
  2.3 19.3 %collective-permute-start.18 = (bf16[96,768]{1,0:T(8,128)(2,1)}, bf16[96,768]{1,0:T(8,128)(2,1)}, u32[]{:S(2)}, u32[]{:S(2)}) collective-permute-start(bf16[96,768]{1,0:T(8,128)(2,1)} %convert_bitcast_fusion.2.refs_7_), channel_id=1, source_target_pairs={{0,2},{2,0},{4,6},{6,4},{1,3},{3,1},{5,7},{7,5},{8,10},{10,8},{12,... | collective-permute-start | bytes 442376 | tf_op jit(solution)/shard_map/ppermute | solution.py:45
  5.4 16.7 %collective-permute-start.19 = (bf16[96,768]{1,0:T(8,128)(2,1)}, bf16[96,768]{1,0:T(8,128)(2,1)}, u32[]{:S(2)}, u32[]{:S(2)}) collective-permute-start(bf16[96,768]{1,0:T(8,128)(2,1)} %convert_bitcast_fusion.2.refs_7_), channel_id=1, source_target_pairs={{0,4},{2,6},{4,0},{6,2},{1,5},{3,7},{5,1},{7,3},{8,12},{10,14},{12... | collective-permute-start | bytes 442376 | tf_op jit(solution)/shard_map/ppermute | solution.py:45
  21.7 15.8 %collective-permute-start = (bf16[96,1408]{1,0:T(8,128)(2,1)S(1)}, bf16[96,1408]{1,0:T(8,128)(2,1)S(1)}, u32[]{:S(2)}, u32[]{:S(2)}) collective-permute-start(bf16[96,1408]{1,0:T(8,128)(2,1)S(1)} %fusion.21.refs_4_), channel_id=1, source_target_pairs={{0,2},{2,0},{4,6},{6,4},{1,3},{3,1},{5,7},{7,5},{8,10},{10,8},{12,... | collective-permute-start | bytes 811016 | tf_op jit(solution)/shard_map/ppermute | solution.py:45
  22.1 23.5 %collective-permute-start.1 = (bf16[96,1408]{1,0:T(8,128)(2,1)S(1)}, bf16[96,1408]{1,0:T(8,128)(2,1)}, u32[]{:S(2)}, u32[]{:S(2)}) collective-permute-start(bf16[96,1408]{1,0:T(8,128)(2,1)S(1)} %fusion.21.refs_4_), channel_id=1, source_target_pairs={{0,4},{2,6},{4,0},{6,2},{1,5},{3,7},{5,1},{7,3},{8,12},{10,14},{12... | collective-permute-start | bytes 811016 | tf_op jit(solution)/shard_map/ppermute | solution.py:45
  27.6 19.5 %collective-permute-start.2 = (bf16[96,1408]{1,0:T(8,128)(2,1)S(1)}, bf16[96,1408]{1,0:T(8,128)(2,1)}, u32[]{:S(2)}, u32[]{:S(2)}) collective-permute-start(bf16[96,1408]{1,0:T(8,128)(2,1)S(1)} %fusion.21.refs_4_), channel_id=1, source_target_pairs={{0,6},{2,4},{4,2},{6,0},{1,7},{3,5},{5,3},{7,1},{8,14},{10,12},{12... | collective-permute-start | bytes 811016 | tf_op jit(solution)/shard_map/ppermute | solution.py:45
  27.7 19.5 %collective-permute-start.3 = (bf16[96,1408]{1,0:T(8,128)(2,1)S(1)}, bf16[96,1408]{1,0:T(8,128)(2,1)S(1)}, u32[]{:S(2)}, u32[]{:S(2)}) collective-permute-start(bf16[96,1408]{1,0:T(8,128)(2,1)S(1)} %fusion.21.refs_4_), channel_id=1, source_target_pairs={{0,16},{8,24},{16,0},{24,8},{1,17},{9,25},{17,1},{25,9},{2,18},{10... | collective-permute-start | bytes 811016 | tf_op jit(solution)/shard_map/ppermute | solution.py:45
  30.2 17.4 %collective-permute-start.7 = (bf16[96,1408]{1,0:T(8,128)(2,1)S(1)}, bf16[96,1408]{1,0:T(8,128)(2,1)S(1)}, u32[]{:S(2)}, u32[]{:S(2)}) collective-permute-start(bf16[96,1408]{1,0:T(8,128)(2,1)S(1)} %fusion.21.refs_4_), channel_id=1, source_target_pairs={{0,8},{8,0},{16,24},{24,16},{1,9},{9,1},{17,25},{25,17},{2,10},{10... | collective-permute-start | bytes 811016 | tf_op jit(solution)/shard_map/ppermute | solution.py:45
  55.6 13.6 %collective-permute-start.5 = (bf16[96,1408]{1,0:T(8,128)(2,1)}, bf16[96,1408]{1,0:T(8,128)(2,1)S(1)}, u32[]{:S(2)}, u32[]{:S(2)}) collective-permute-start(bf16[96,1408]{1,0:T(8,128)(2,1)} %collective-permute-done.1.refs_6_), channel_id=1, source_target_pairs={{0,16},{8,24},{16,0},{24,8},{1,17},{9,25},{17,1},{25,9},{2,18},{10... | collective-permute-start | bytes 811016 | tf_op jit(solution)/shard_map/ppermute | solution.py:45
  57.7 17.4 %collective-permute-start.8 = (bf16[96,1408]{1,0:T(8,128)(2,1)S(1)}, bf16[96,1408]{1,0:T(8,128)(2,1)S(1)}, u32[]{:S(2)}, u32[]{:S(2)}) collective-permute-start(bf16[96,1408]{1,0:T(8,128)(2,1)S(1)} %collective-permute-done.refs_5_), channel_id=1, source_target_pairs={{0,8},{8,0},{16,24},{24,16},{1,9},{9,1},{17,25},{25,17},{2,10},{10... | collective-permute-start | bytes 811016 | tf_op jit(solution)/shard_map/ppermute | solution.py:45
  57.8 17.8 %collective-permute-start.9 = (bf16[96,1408]{1,0:T(8,128)(2,1)}, bf16[96,1408]{1,0:T(8,128)(2,1)S(1)}, u32[]{:S(2)}, u32[]{:S(2)}) collective-permute-start(bf16[96,1408]{1,0:T(8,128)(2,1)} %collective-permute-done.1.refs_6_), channel_id=1, source_target_pairs={{0,8},{8,0},{16,24},{24,16},{1,9},{9,1},{17,25},{25,17},{2,10},{10... | collective-permute-start | bytes 811016 | tf_op jit(solution)/shard_map/ppermute | solution.py:45
  58.3 16.8 %collective-permute-start.6 = (bf16[96,1408]{1,0:T(8,128)(2,1)}, bf16[96,1408]{1,0:T(8,128)(2,1)S(1)}, u32[]{:S(2)}, u32[]{:S(2)}) collective-permute-start(bf16[96,1408]{1,0:T(8,128)(2,1)} %collective-permute-done.2.refs_7_), channel_id=1, source_target_pairs={{0,16},{8,24},{16,0},{24,8},{1,17},{9,25},{17,1},{25,9},{2,18},{10... | collective-permute-start | bytes 811016 | tf_op jit(solution)/shard_map/ppermute | solution.py:45
  63.5 13.8 %collective-permute-start.10 = (bf16[96,1408]{1,0:T(8,128)(2,1)}, bf16[96,1408]{1,0:T(8,128)(2,1)}, u32[]{:S(2)}, u32[]{:S(2)}) collective-permute-start(bf16[96,1408]{1,0:T(8,128)(2,1)} %collective-permute-done.2.refs_7_), channel_id=1, source_target_pairs={{0,8},{8,0},{16,24},{24,16},{1,9},{9,1},{17,25},{25,17},{2,10},{10... | collective-permute-start | bytes 811016 | tf_op jit(solution)/shard_map/ppermute | solution.py:45
  69.3 85.1 %collective-permute-start.38 = (bf16[2,1536,256]{2,1,0:T(8,128)(2,1)}, bf16[2,1536,256]{2,1,0:T(8,128)(2,1)}, u32[]{:S(2)}, u32[]{:S(2)}) collective-permute-start(bf16[2,1536,256]{2,1,0:T(8,128)(2,1)} %convert_bitcast_fusion.refs_6_), channel_id=1, source_target_pairs={{0,16},{8,24},{16,0},{24,8},{1,17},{9,25},{17,1},{25,9},{2,18},{10... | collective-permute-start | bytes 4718600 | tf_op jit(solution)/shard_map/ppermute | solution.py:45
  75.7 61.7 %collective-permute-start.44 = (bf16[256,1536]{1,0:T(8,128)(2,1)S(1)}, bf16[256,1536]{1,0:T(8,128)(2,1)}, u32[]{:S(2)}, u32[]{:S(2)}) collective-permute-start(bf16[256,1536]{1,0:T(8,128)(2,1)S(1)} %convert_bitcast_fusion.1.refs_14_.refs_2_), channel_id=1, source_target_pairs={{0,1},{1,0},{2,3},{3,2},{4,5},{5,4},{6,7},{7,6},{8,9},{9,8},{10,11... | collective-permute-start | bytes 2359304 | tf_op jit(solution)/shard_map/ppermute | solution.py:45
  77.3 44.2 %collective-permute-start.53 = (bf16[192,1536]{1,0:T(8,128)(2,1)S(1)}, bf16[192,1536]{1,0:T(8,128)(2,1)S(1)}, u32[]{:S(2)}, u32[]{:S(2)}) collective-permute-start(bf16[192,1536]{1,0:T(8,128)(2,1)S(1)} %constant_dynamic-slice_fusion.11.refs_2_.refs_4_), channel_id=1, source_target_pairs={{0,4},{2,6},{4,0},{6,2},{1,5},{3,7},{5,1},{7,3},{8,12},{10,14},{12... | collective-permute-start | bytes 1769480 | tf_op jit(solution)/shard_map/ppermute | solution.py:45
  82.0 40.8 %collective-permute-start.54 = (bf16[192,1536]{1,0:T(8,128)(2,1)S(1)}, bf16[192,1536]{1,0:T(8,128)(2,1)}, u32[]{:S(2)}, u32[]{:S(2)}) collective-permute-start(bf16[192,1536]{1,0:T(8,128)(2,1)S(1)} %constant_dynamic-slice_fusion.11.refs_2_.refs_4_), channel_id=1, source_target_pairs={{0,6},{2,4},{4,2},{6,0},{1,7},{3,5},{5,3},{7,1},{8,14},{10,12},{12... | collective-permute-start | bytes 1769480 | tf_op jit(solution)/shard_map/ppermute | solution.py:45
  86.0 94.6 %collective-permute-start.37 = (bf16[2,1536,256]{2,1,0:T(8,128)(2,1)}, bf16[2,1536,256]{2,1,0:T(8,128)(2,1)}, u32[]{:S(2)}, u32[]{:S(2)}) collective-permute-start(bf16[2,1536,256]{2,1,0:T(8,128)(2,1)} %convert_bitcast_fusion.refs_6_), channel_id=1, source_target_pairs={{0,1},{1,0},{2,3},{3,2},{4,5},{5,4},{6,7},{7,6},{8,9},{9,8},{10,11... | collective-permute-start | bytes 4718600 | tf_op jit(solution)/shard_map/ppermute | solution.py:45
  121.5 18.5 %collective-permute-start.15 = (bf16[512,384]{1,0:T(8,128)(2,1)}, bf16[512,384]{1,0:T(8,128)(2,1)S(1)}, u32[]{:S(2)}, u32[]{:S(2)}) collective-permute-start(bf16[512,384]{1,0:T(8,128)(2,1)} %get-tuple-element.65.refs_3_), channel_id=1, source_target_pairs={{0,2},{2,4},{4,6},{1,3},{3,5},{5,7},{8,10},{10,12},{12,14},{9,11},... | collective-permute-start | bytes 1179656 | tf_op jit(solution)/shard_map/ppermute | solution.py:646
  122.8 24.4 %collective-permute-start.16 = (bf16[512,384]{1,0:T(8,128)(2,1)}, bf16[512,384]{1,0:T(8,128)(2,1)S(1)}, u32[]{:S(2)}, u32[]{:S(2)}) collective-permute-start(bf16[512,384]{1,0:T(8,128)(2,1)} %get-tuple-element.65.refs_3_), channel_id=1, source_target_pairs={{0,4},{2,6},{1,5},{3,7},{8,12},{10,14},{9,13},{11,15},{16,20},{18,... | collective-permute-start | bytes 1179656 | tf_op jit(solution)/shard_map/ppermute | solution.py:646
  137.4 17.0 %collective-permute-start.17 = (bf16[512,384]{1,0:T(8,128)(2,1)}, bf16[512,384]{1,0:T(8,128)(2,1)}, u32[]{:S(2)}, u32[]{:S(2)}) collective-permute-start(bf16[512,384]{1,0:T(8,128)(2,1)} %get-tuple-element.65.refs_3_), channel_id=1, source_target_pairs={{0,6},{1,7},{8,14},{9,15},{16,22},{17,23},{24,30},{25,31}} | collective-permute-start | bytes 1179656 | tf_op jit(solution)/shard_map/ppermute | solution.py:646
  140.0 36.6 %collective-permute-start.45 = (bf16[256,1536]{1,0:T(8,128)(2,1)S(1)}, bf16[256,1536]{1,0:T(8,128)(2,1)S(1)}, u32[]{:S(2)}, u32[]{:S(2)}) collective-permute-start(bf16[256,1536]{1,0:T(8,128)(2,1)S(1)} %convert_bitcast_fusion.1.refs_14_.refs_2_), channel_id=1, source_target_pairs={{0,16},{8,24},{16,0},{24,8},{1,17},{9,25},{17,1},{25,9},{2,18},{10... | collective-permute-start | bytes 2359304 | tf_op jit(solution)/shard_map/ppermute | solution.py:45
  148.0 30.2 %collective-permute-start.47 = (bf16[256,1536]{1,0:T(8,128)(2,1)S(1)}, bf16[256,1536]{1,0:T(8,128)(2,1)S(1)}, u32[]{:S(2)}, u32[]{:S(2)}) collective-permute-start(bf16[256,1536]{1,0:T(8,128)(2,1)S(1)} %convert_bitcast_fusion.1.refs_14_.refs_2_), channel_id=1, source_target_pairs={{0,8},{8,0},{16,24},{24,16},{1,9},{9,1},{17,25},{25,17},{2,10},{10... | collective-permute-start | bytes 2359304 | tf_op jit(solution)/shard_map/ppermute | solution.py:45
  154.4 31.3 %collective-permute-start.40 = (bf16[2,1536,256]{2,1,0:T(8,128)(2,1)}, bf16[2,1536,256]{2,1,0:T(8,128)(2,1)}, u32[]{:S(2)}, u32[]{:S(2)}) collective-permute-start(bf16[2,1536,256]{2,1,0:T(8,128)(2,1)} %convert_bitcast_fusion.refs_6_), channel_id=1, source_target_pairs={{0,8},{8,0},{16,24},{24,16},{1,9},{9,1},{17,25},{25,17},{2,10},{10... | collective-permute-start | bytes 4718600 | tf_op jit(solution)/shard_map/ppermute | solution.py:45
  154.4 49.8 %collective-permute-start.39 = (bf16[2,1536,256]{2,1,0:T(8,128)(2,1)}, bf16[2,1536,256]{2,1,0:T(8,128)(2,1)}, u32[]{:S(2)}, u32[]{:S(2)}) collective-permute-start(bf16[2,1536,256]{2,1,0:T(8,128)(2,1)} %collective-permute-done.38.refs_8_), channel_id=1, source_target_pairs={{0,1},{1,0},{2,3},{3,2},{4,5},{5,4},{6,7},{7,6},{8,9},{9,8},{10,11... | collective-permute-start | bytes 4718600 | tf_op jit(solution)/shard_map/ppermute | solution.py:45
  176.6 20.1 %collective-permute-start.46 = (bf16[256,1536]{1,0:T(8,128)(2,1)}, bf16[256,1536]{1,0:T(8,128)(2,1)}, u32[]{:S(2)}, u32[]{:S(2)}) collective-permute-start(bf16[256,1536]{1,0:T(8,128)(2,1)} %collective-permute-done.44.refs_15_.refs_3_), channel_id=1, source_target_pairs={{0,16},{8,24},{16,0},{24,8},{1,17},{9,25},{17,1},{25,9},{2,18},{10... | collective-permute-start | bytes 2359304 | tf_op jit(solution)/shard_map/ppermute | solution.py:45
  178.1 18.5 %collective-permute-start.48 = (bf16[256,1536]{1,0:T(8,128)(2,1)}, bf16[256,1536]{1,0:T(8,128)(2,1)}, u32[]{:S(2)}, u32[]{:S(2)}) collective-permute-start(bf16[256,1536]{1,0:T(8,128)(2,1)} %collective-permute-done.44.refs_15_.refs_3_), channel_id=1, source_target_pairs={{0,8},{8,0},{16,24},{24,16},{1,9},{9,1},{17,25},{25,17},{2,10},{10... | collective-permute-start | bytes 2359304 | tf_op jit(solution)/shard_map/ppermute | solution.py:45
  180.6 23.6 %collective-permute-start.33 = (bf16[192,1536]{1,0:T(8,128)(2,1)}, bf16[192,1536]{1,0:T(8,128)(2,1)}, u32[]{:S(2)}, u32[]{:S(2)}) collective-permute-start(bf16[192,1536]{1,0:T(8,128)(2,1)} %dynamic-slice_convert_fusion.1), channel_id=1, source_target_pairs={{0,1},{1,0},{2,3},{3,2},{4,5},{5,4},{6,7},{7,6},{8,9},{9,8},{10,11... | collective-permute-start | bytes 1769480 | tf_op jit(solution)/shard_map/ppermute | solution.py:45
  185.7 21.7 %collective-permute-start.49 = (bf16[256,1536]{1,0:T(8,128)(2,1)}, bf16[256,1536]{1,0:T(8,128)(2,1)}, u32[]{:S(2)}, u32[]{:S(2)}) collective-permute-start(bf16[256,1536]{1,0:T(8,128)(2,1)} %copy-done.48), channel_id=1, source_target_pairs={{0,8},{8,0},{16,24},{24,16},{1,9},{9,1},{17,25},{25,17},{2,10},{10... | collective-permute-start | bytes 2359304 | tf_op jit(solution)/shard_map/ppermute | solution.py:45
  196.7 72.4 %collective-permute-start.42 = (bf16[2,1536,256]{2,1,0:T(8,128)(2,1)}, bf16[2,1536,256]{2,1,0:T(8,128)(2,1)}, u32[]{:S(2)}, u32[]{:S(2)}) collective-permute-start(bf16[2,1536,256]{2,1,0:T(8,128)(2,1)} %collective-permute-done.38.refs_8_), channel_id=1, source_target_pairs={{0,8},{8,0},{16,24},{24,16},{1,9},{9,1},{17,25},{25,17},{2,10},{10... | collective-permute-start | bytes 4718600 | tf_op jit(solution)/shard_map/ppermute | solution.py:45
  196.7 72.4 %collective-permute-start.41 = (bf16[2,1536,256]{2,1,0:T(8,128)(2,1)}, bf16[2,1536,256]{2,1,0:T(8,128)(2,1)}, u32[]{:S(2)}, u32[]{:S(2)}) collective-permute-start(bf16[2,1536,256]{2,1,0:T(8,128)(2,1)} %collective-permute-done.37.refs_7_), channel_id=1, source_target_pairs={{0,8},{8,0},{16,24},{24,16},{1,9},{9,1},{17,25},{25,17},{2,10},{10... | collective-permute-start | bytes 4718600 | tf_op jit(solution)/shard_map/ppermute | solution.py:45
  204.2 64.9 %collective-permute-start.43 = (bf16[2,1536,256]{2,1,0:T(8,128)(2,1)}, bf16[2,1536,256]{2,1,0:T(8,128)(2,1)}, u32[]{:S(2)}, u32[]{:S(2)}) collective-permute-start(bf16[2,1536,256]{2,1,0:T(8,128)(2,1)} %collective-permute-done.39.refs_9_), channel_id=1, source_target_pairs={{0,8},{8,0},{16,24},{24,16},{1,9},{9,1},{17,25},{25,17},{2,10},{10... | collective-permute-start | bytes 4718600 | tf_op jit(solution)/shard_map/ppermute | solution.py:45
  207.5 48.9 %collective-permute-start.51 = (bf16[192,1536]{1,0:T(8,128)(2,1)}, bf16[192,1536]{1,0:T(8,128)(2,1)}, u32[]{:S(2)}, u32[]{:S(2)}) collective-permute-start(bf16[192,1536]{1,0:T(8,128)(2,1)} %multiply_convert_fusion.refs_0_), channel_id=1, source_target_pairs={{0,4},{2,6},{4,0},{6,2},{1,5},{3,7},{5,1},{7,3},{8,12},{10,14},{12... | collective-permute-start | bytes 1769480 | tf_op jit(solution)/shard_map/ppermute | solution.py:45
  216.6 39.9 %collective-permute-start.52 = (bf16[192,1536]{1,0:T(8,128)(2,1)}, bf16[192,1536]{1,0:T(8,128)(2,1)}, u32[]{:S(2)}, u32[]{:S(2)}) collective-permute-start(bf16[192,1536]{1,0:T(8,128)(2,1)} %multiply_convert_fusion.refs_0_), channel_id=1, source_target_pairs={{0,6},{2,4},{4,2},{6,0},{1,7},{3,5},{5,3},{7,1},{8,14},{10,12},{12... | collective-permute-start | bytes 1769480 | tf_op jit(solution)/shard_map/ppermute | solution.py:45
  256.3 45.2 %collective-permute-start.35 = (bf16[192,1536]{1,0:T(8,128)(2,1)}, bf16[192,1536]{1,0:T(8,128)(2,1)}, u32[]{:S(2)}, u32[]{:S(2)}) collective-permute-start(bf16[192,1536]{1,0:T(8,128)(2,1)} %copy-done.28), channel_id=1, source_target_pairs={{0,2},{2,0},{4,6},{6,4},{1,3},{3,1},{5,7},{7,5},{8,10},{10,8},{12,... | collective-permute-start | bytes 1769480 | tf_op jit(solution)/shard_map/ppermute | solution.py:45
  256.5 45.1 %collective-permute-start.34 = (bf16[192,1536]{1,0:T(8,128)(2,1)}, bf16[192,1536]{1,0:T(8,128)(2,1)}, u32[]{:S(2)}, u32[]{:S(2)}) collective-permute-start(bf16[192,1536]{1,0:T(8,128)(2,1)} %multiply_convert_fusion.refs_0_), channel_id=1, source_target_pairs={{0,2},{2,0},{4,6},{6,4},{1,3},{3,1},{5,7},{7,5},{8,10},{10,8},{12,... | collective-permute-start | bytes 1769480 | tf_op jit(solution)/shard_map/ppermute | solution.py:45
  298.1 47.6 %collective-permute-start.63 = (bf16[192,1536]{1,0:T(8,128)(2,1)}, bf16[192,1536]{1,0:T(8,128)(2,1)}, u32[]{:S(2)}, u32[]{:S(2)}) collective-permute-start(bf16[192,1536]{1,0:T(8,128)(2,1)} %get-tuple-element.77), channel_id=1, source_target_pairs={{0,6},{2,4},{4,2},{6,0},{1,7},{3,5},{5,3},{7,1},{8,14},{10,12},{12... | collective-permute-start | bytes 1769480 | tf_op jit(solution)/shard_map/ppermute | solution.py:45
  301.6 76.3 %collective-permute-start.62 = (bf16[192,1536]{1,0:T(8,128)(2,1)}, bf16[192,1536]{1,0:T(8,128)(2,1)}, u32[]{:S(2)}, u32[]{:S(2)}) collective-permute-start(bf16[192,1536]{1,0:T(8,128)(2,1)} %get-tuple-element.76), channel_id=1, source_target_pairs={{0,4},{2,6},{4,0},{6,2},{1,5},{3,7},{5,1},{7,3},{8,12},{10,14},{12... | collective-permute-start | bytes 1769480 | tf_op jit(solution)/shard_map/ppermute | solution.py:45
  330.7 47.2 %collective-permute-start.61 = (bf16[192,1536]{1,0:T(8,128)(2,1)}, bf16[192,1536]{1,0:T(8,128)(2,1)}, u32[]{:S(2)}, u32[]{:S(2)}) collective-permute-start(bf16[192,1536]{1,0:T(8,128)(2,1)} %get-tuple-element.75), channel_id=1, source_target_pairs={{0,2},{2,0},{4,6},{6,4},{1,3},{3,1},{5,7},{7,5},{8,10},{10,8},{12,... | collective-permute-start | bytes 1769480 | tf_op jit(solution)/shard_map/ppermute | solution.py:45
  342.3 38.0 %collective-permute-start.59 = (bf16[192,1536]{1,0:T(8,128)(2,1)}, bf16[192,1536]{1,0:T(8,128)(2,1)}, u32[]{:S(2)}, u32[]{:S(2)}) collective-permute-start(bf16[192,1536]{1,0:T(8,128)(2,1)} %get-tuple-element.73), channel_id=1, source_target_pairs={{0,6},{2,4},{4,2},{6,0},{1,7},{3,5},{5,3},{7,1},{8,14},{10,12},{12... | collective-permute-start | bytes 1769480 | tf_op jit(solution)/shard_map/ppermute | solution.py:45
  345.8 56.8 %collective-permute-start.58 = (bf16[192,1536]{1,0:T(8,128)(2,1)}, bf16[192,1536]{1,0:T(8,128)(2,1)}, u32[]{:S(2)}, u32[]{:S(2)}) collective-permute-start(bf16[192,1536]{1,0:T(8,128)(2,1)} %get-tuple-element.72), channel_id=1, source_target_pairs={{0,4},{2,6},{4,0},{6,2},{1,5},{3,7},{5,1},{7,3},{8,12},{10,14},{12... | collective-permute-start | bytes 1769480 | tf_op jit(solution)/shard_map/ppermute | solution.py:45
  345.8 56.8 %collective-permute-start.57 = (bf16[192,1536]{1,0:T(8,128)(2,1)}, bf16[192,1536]{1,0:T(8,128)(2,1)}, u32[]{:S(2)}, u32[]{:S(2)}) collective-permute-start(bf16[192,1536]{1,0:T(8,128)(2,1)} %get-tuple-element.71), channel_id=1, source_target_pairs={{0,2},{2,0},{4,6},{6,4},{1,3},{3,1},{5,7},{7,5},{8,10},{10,8},{12,... | collective-permute-start | bytes 1769480 | tf_op jit(solution)/shard_map/ppermute | solution.py:45
  377.9 184.3 %collective-permute-start.89 = (bf16[4,2,1536,256]{3,2,1,0:T(8,128)(2,1)}, bf16[4,2,1536,256]{3,2,1,0:T(8,128)(2,1)}, u32[]{:S(2)}, u32[]{:S(2)}) collective-permute-start(bf16[4,2,1536,256]{3,2,1,0:T(8,128)(2,1)} %get-tuple-element.108), channel_id=1, source_target_pairs={{0,8},{8,0},{16,24},{24,16},{1,9},{9,1},{17,25},{25,17},{2,10},{10... | collective-permute-start | bytes 18874376 | tf_op jit(solution)/shard_map/ppermute | solution.py:45
  406.7 16.4 %collective-permute-start.64 = (bf16[192,1536]{1,0:T(8,128)(2,1)}, bf16[192,1536]{1,0:T(8,128)(2,1)}, u32[]{:S(2)}, u32[]{:S(2)}) collective-permute-start(bf16[192,1536]{1,0:T(8,128)(2,1)} %get-tuple-element.225), channel_id=1, source_target_pairs={{0,1},{1,0},{2,3},{3,2},{4,5},{5,4},{6,7},{7,6},{8,9},{9,8},{10,11... | collective-permute-start | bytes 1769480 | tf_op jit(solution)/shard_map/ppermute | solution.py:45
  421.1 39.1 %collective-permute-start.60 = (bf16[192,1536]{1,0:T(8,128)(2,1)S(1)}, bf16[192,1536]{1,0:T(8,128)(2,1)S(1)}, u32[]{:S(2)}, u32[]{:S(2)}) collective-permute-start(bf16[192,1536]{1,0:T(8,128)(2,1)S(1)} %copy-done.15), channel_id=1, source_target_pairs={{0,1},{1,0},{2,3},{3,2},{4,5},{5,4},{6,7},{7,6},{8,9},{9,8},{10,11... | collective-permute-start | bytes 1769480 | tf_op jit(solution)/shard_map/ppermute | solution.py:45
  449.5 18.7 %collective-permute-start.65 = (bf16[512,384]{1,0:T(8,128)(2,1)}, bf16[512,384]{1,0:T(8,128)(2,1)S(1)}, u32[]{:S(2)}, u32[]{:S(2)}) collective-permute-start(bf16[512,384]{1,0:T(8,128)(2,1)} %get-tuple-element.82), channel_id=1, source_target_pairs={{2,0},{4,2},{6,4},{3,1},{5,3},{7,5},{10,8},{12,10},{14,12},{11,9},... | collective-permute-start | bytes 1179656 | tf_op jit(solution)/shard_map/ppermute | solution.py:646
  450.8 35.1 %collective-permute-start.66 = (bf16[512,384]{1,0:T(8,128)(2,1)}, bf16[512,384]{1,0:T(8,128)(2,1)}, u32[]{:S(2)}, u32[]{:S(2)}) collective-permute-start(bf16[512,384]{1,0:T(8,128)(2,1)} %get-tuple-element.83), channel_id=1, source_target_pairs={{4,0},{6,2},{5,1},{7,3},{12,8},{14,10},{13,9},{15,11},{20,16},{22,... | collective-permute-start | bytes 1179656 | tf_op jit(solution)/shard_map/ppermute | solution.py:646
  452.1 33.8 %collective-permute-start.67 = (bf16[512,384]{1,0:T(8,128)(2,1)}, bf16[512,384]{1,0:T(8,128)(2,1)}, u32[]{:S(2)}, u32[]{:S(2)}) collective-permute-start(bf16[512,384]{1,0:T(8,128)(2,1)} %get-tuple-element.84), channel_id=1, source_target_pairs={{6,0},{7,1},{14,8},{15,9},{22,16},{23,17},{30,24},{31,25}} | collective-permute-start | bytes 1179656 | tf_op jit(solution)/shard_map/ppermute | solution.py:646
  461.1 35.2 %collective-permute-start.71 = (bf16[384,768]{1,0:T(8,128)(2,1)}, bf16[384,768]{1,0:T(8,128)(2,1)}, u32[]{:S(2)}, u32[]{:S(2)}) collective-permute-start(bf16[384,768]{1,0:T(8,128)(2,1)} %get-tuple-element.93), channel_id=1, source_target_pairs={{0,8},{8,0},{16,24},{24,16},{1,9},{9,1},{17,25},{25,17},{2,10},{10... | collective-permute-start | bytes 1769480 | tf_op jit(solution)/shard_map/ppermute | solution.py:45
  468.2 100.6 %collective-permute-start.93 = (bf16[4,256,1536]{2,1,0:T(8,128)(2,1)}, bf16[4,256,1536]{2,1,0:T(8,128)(2,1)}, u32[]{:S(2)}, u32[]{:S(2)}) collective-permute-start(bf16[4,256,1536]{2,1,0:T(8,128)(2,1)} %get-tuple-element.110), channel_id=1, source_target_pairs={{0,8},{8,0},{16,24},{24,16},{1,9},{9,1},{17,25},{25,17},{2,10},{10... | collective-permute-start | bytes 9437192 | tf_op jit(solution)/shard_map/ppermute | solution.py:45
  495.4 15.8 %collective-permute-start.68 = (bf16[192,1536]{1,0:T(8,128)(2,1)S(1)}, bf16[192,1536]{1,0:T(8,128)(2,1)S(1)}, u32[]{:S(2)}, u32[]{:S(2)}) collective-permute-start(bf16[192,1536]{1,0:T(8,128)(2,1)S(1)} %dynamic-slice_convert_fusion), channel_id=1, source_target_pairs={{0,1},{1,0},{2,3},{3,2},{4,5},{5,4},{6,7},{7,6},{8,9},{9,8},{10,11... | collective-permute-start | bytes 1769480 | tf_op jit(solution)/shard_map/ppermute | solution.py:45
  497.8 13.8 %collective-permute-start.82 = (bf16[384,768]{1,0:T(8,128)(2,1)S(1)}, bf16[384,768]{1,0:T(8,128)(2,1)S(1)}, u32[]{:S(2)}, u32[]{:S(2)}) collective-permute-start(bf16[384,768]{1,0:T(8,128)(2,1)S(1)} %copy-done.52), channel_id=1, source_target_pairs={{0,8},{8,0},{16,24},{24,16},{1,9},{9,1},{17,25},{25,17},{2,10},{10... | collective-permute-start | bytes 1769480 | tf_op jit(solution)/shard_map/ppermute | solution.py:45
  498.4 15.5 %collective-permute-start.84 = (bf16[384,768]{1,0:T(8,128)(2,1)S(1)}, bf16[384,768]{1,0:T(8,128)(2,1)S(1)}, u32[]{:S(2)}, u32[]{:S(2)}) collective-permute-start(bf16[384,768]{1,0:T(8,128)(2,1)S(1)} %add_convert_fusion.9), channel_id=1, source_target_pairs={{0,16},{8,24},{16,0},{24,8},{1,17},{9,25},{17,1},{25,9},{2,18},{10... | collective-permute-start | bytes 1769480 | tf_op jit(solution)/shard_map/ppermute | solution.py:45
  511.6 15.8 %collective-permute-start.72 = (bf16[384,768]{1,0:T(8,128)(2,1)S(1)}, bf16[384,768]{1,0:T(8,128)(2,1)S(1)}, u32[]{:S(2)}, u32[]{:S(2)}) collective-permute-start(bf16[384,768]{1,0:T(8,128)(2,1)S(1)} %add_convert_fusion.12), channel_id=1, source_target_pairs={{0,16},{8,24},{16,0},{24,8},{1,17},{9,25},{17,1},{25,9},{2,18},{10... | collective-permute-start | bytes 1769480 | tf_op jit(solution)/shard_map/ppermute | solution.py:45
  514.3 14.0 %collective-permute-start.86 = (bf16[96,768]{1,0:T(8,128)(2,1)S(1)}, bf16[96,768]{1,0:T(8,128)(2,1)S(1)}, u32[]{:S(2)}, u32[]{:S(2)}) collective-permute-start(bf16[96,768]{1,0:T(8,128)(2,1)S(1)} %get-tuple-element.243), channel_id=1, source_target_pairs={{0,4},{2,6},{4,0},{6,2},{1,5},{3,7},{5,1},{7,3},{8,12},{10,14},{12... | collective-permute-start | bytes 442376 | tf_op jit(solution)/shard_map/ppermute | solution.py:45
  527.4 13.6 %collective-permute-start.78 = (bf16[384,640]{1,0:T(8,128)(2,1)S(1)}, bf16[384,640]{1,0:T(8,128)(2,1)S(1)}, u32[]{:S(2)}, u32[]{:S(2)}) collective-permute-start(bf16[384,640]{1,0:T(8,128)(2,1)S(1)} %add_convert_fusion.17), channel_id=1, source_target_pairs={{0,16},{8,24},{16,0},{24,8},{1,17},{9,25},{17,1},{25,9},{2,18},{10... | collective-permute-start | bytes 1474568 | tf_op jit(solution)/shard_map/ppermute | solution.py:45
  535.5 18.5 %collective-permute-start.74 = (bf16[96,768]{1,0:T(8,128)(2,1)S(1)}, bf16[96,768]{1,0:T(8,128)(2,1)S(1)}, u32[]{:S(2)}, u32[]{:S(2)}) collective-permute-start(bf16[96,768]{1,0:T(8,128)(2,1)S(1)} %get-tuple-element.246), channel_id=1, source_target_pairs={{0,4},{2,6},{4,0},{6,2},{1,5},{3,7},{5,1},{7,3},{8,12},{10,14},{12... | collective-permute-start | bytes 442376 | tf_op jit(solution)/shard_map/ppermute | solution.py:45
  554.4 55.2 %collective-permute-start.69 = (bf16[192,1536]{1,0:T(8,128)(2,1)}, bf16[192,1536]{1,0:T(8,128)(2,1)}, u32[]{:S(2)}, u32[]{:S(2)}) collective-permute-start(bf16[192,1536]{1,0:T(8,128)(2,1)} %add_convert_fusion.14), channel_id=1, source_target_pairs={{0,1},{1,0},{2,3},{3,2},{4,5},{5,4},{6,7},{7,6},{8,9},{9,8},{10,11... | collective-permute-start | bytes 1769480 | tf_op jit(solution)/shard_map/ppermute | solution.py:45
  561.3 19.7 %collective-permute-start.88 = (f32[2,96]{0,1:T(8,128)}, f32[2,96]{0,1:T(8,128)}, u32[]{:S(2)}, u32[]{:S(2)}) collective-permute-start(f32[2,96]{0,1:T(8,128)} %slice_bitcast_fusion), channel_id=1, source_target_pairs={{0,1},{1,0},{2,3},{3,2},{4,5},{5,4},{6,7},{7,6},{8,9},{9,8},{10,11... | collective-permute-start | bytes 2312 | tf_op jit(solution)/shard_map/ppermute | solution.py:45
  567.6 37.6 %collective-permute-start.91 = (bf16[2,1536,256]{2,1,0:T(8,128)(2,1)}, bf16[2,1536,256]{2,1,0:T(8,128)(2,1)}, u32[]{:S(2)}, u32[]{:S(2)}) collective-permute-start(bf16[2,1536,256]{2,1,0:T(8,128)(2,1)} %get-tuple-element.230), channel_id=1, source_target_pairs={{0,1},{1,0},{2,3},{3,2},{4,5},{5,4},{6,7},{7,6},{8,9},{9,8},{10,11... | collective-permute-start | bytes 4718600 | tf_op jit(solution)/shard_map/ppermute | solution.py:45
  572.0 18.9 %collective-permute-start.95 = (bf16[256,1536]{1,0:T(8,128)(2,1)}, bf16[256,1536]{1,0:T(8,128)(2,1)}, u32[]{:S(2)}, u32[]{:S(2)}) collective-permute-start(bf16[256,1536]{1,0:T(8,128)(2,1)} %get-tuple-element.232), channel_id=1, source_target_pairs={{0,16},{8,24},{16,0},{24,8},{1,17},{9,25},{17,1},{25,9},{2,18},{10... | collective-permute-start | bytes 2359304 | tf_op jit(solution)/shard_map/ppermute | solution.py:45
  586.8 25.3 %collective-permute-start.94 = (bf16[256,1536]{1,0:T(8,128)(2,1)}, bf16[256,1536]{1,0:T(8,128)(2,1)S(1)}, u32[]{:S(2)}, u32[]{:S(2)}) collective-permute-start(bf16[256,1536]{1,0:T(8,128)(2,1)} %get-tuple-element.231), channel_id=1, source_target_pairs={{0,16},{8,24},{16,0},{24,8},{1,17},{9,25},{17,1},{25,9},{2,18},{10... | collective-permute-start | bytes 2359304 | tf_op jit(solution)/shard_map/ppermute | solution.py:45
  592.9 29.1 %collective-permute-start.96 = (bf16[256,1536]{1,0:T(8,128)(2,1)S(1)}, bf16[256,1536]{1,0:T(8,128)(2,1)S(1)}, u32[]{:S(2)}, u32[]{:S(2)}) collective-permute-start(bf16[256,1536]{1,0:T(8,128)(2,1)S(1)} %fusion.8), channel_id=1, source_target_pairs={{0,1},{1,0},{2,3},{3,2},{4,5},{5,4},{6,7},{7,6},{8,9},{9,8},{10,11... | collective-permute-start | bytes 2359304 | tf_op jit(solution)/shard_map/ppermute | solution.py:45
  593.8 59.0 %collective-permute-start.90 = (bf16[2,1536,256]{2,1,0:T(8,128)(2,1)S(1)}, bf16[2,1536,256]{2,1,0:T(8,128)(2,1)S(1)}, u32[]{:S(2)}, u32[]{:S(2)}) collective-permute-start(bf16[2,1536,256]{2,1,0:T(8,128)(2,1)S(1)} %copy-done.20), channel_id=1, source_target_pairs={{0,1},{1,0},{2,3},{3,2},{4,5},{5,4},{6,7},{7,6},{8,9},{9,8},{10,11... | collective-permute-start | bytes 4718600 | tf_op jit(solution)/shard_map/ppermute | solution.py:45
  608.2 44.6 %collective-permute-start.92 = (bf16[2,1536,256]{2,1,0:T(8,128)(2,1)S(1)}, bf16[2,1536,256]{2,1,0:T(8,128)(2,1)S(1)}, u32[]{:S(2)}, u32[]{:S(2)}) collective-permute-start(bf16[2,1536,256]{2,1,0:T(8,128)(2,1)S(1)} %fusion), channel_id=1, source_target_pairs={{0,16},{8,24},{16,0},{24,8},{1,17},{9,25},{17,1},{25,9},{2,18},{10... | collective-permute-start | bytes 4718600 | tf_op jit(solution)/shard_map/ppermute | solution.py:45
  (110 other events, 1333.4 us)

commit v3 on v2

v3 whole, which is shorter than its diff:
```python
import functools
import math

import jax
import jax.numpy as jnp
from jax import lax
from jax.experimental import pallas as pl
from jax.experimental.pallas import tpu as pltpu
from jax.sharding import PartitionSpec as P

HD = 64
GROUP = 3


EPSILON = 1e-05
ROPE_BASE = 10000.0
MOMENTUM = 0.9
AVERAGE = 0.7
RATE_QKV = 7e-05
RATE_OUT = 0.15
RATE_GAIN = 0.0005
RATE_IN = 0.0004
RATE_DOWN = 0.001


def doc_positions(lengths_row, places):
    doc_ends = jnp.cumsum(lengths_row)
    passed = places[:, None] >= doc_ends[None, :]
    segment = jnp.sum(passed.astype(jnp.int32), axis=1)
    doc_start = jnp.sum(jnp.where(passed, lengths_row[None, :], 0), axis=1)
    return (segment, places - doc_start)


def norm_back(grad_out, normed, inverse, gain_row):
    scaled = grad_out * gain_row
    return inverse * (scaled - normed * jnp.mean(scaled * normed, axis=-1, keepdims=True))


F_MASKS = (0, 2, 1, 3)
VMEM_LIMIT = 60 * 1024 * 1024


def advance(weight, gradient, moment, average, step_rate):
    moment_new = MOMENTUM * moment + gradient
    weight_new = weight - step_rate * (gradient + MOMENTUM * moment_new)
    average_new = AVERAGE * average + (1.0 - AVERAGE) * weight_new
    return (moment_new, average_new, weight_new)


def swap(value, axis, mask):
    size = lax.axis_size(axis)
    return lax.ppermute(value, axis, [(i, i ^ mask) for i in range(size)])


def after(value, *others):
    return lax.optimization_barrier((value, *others))[0]


def nt_dot(left_mat, right_mat):
    return lax.dot_general(
        left_mat, right_mat, (((1,), (1,)), ((), ())), preferred_element_type=jnp.float32
    )


def vmem_spec():
    return pl.BlockSpec(memory_space=pltpu.VMEM)


def any_spec():
    return pl.BlockSpec(memory_space=pl.ANY)


def smem_spec():
    return pl.BlockSpec(memory_space=pltpu.SMEM)


def added(left_mat, right_mat):
    return (left_mat.astype(jnp.float32) + right_mat.astype(jnp.float32)).astype(jnp.bfloat16)


def params():
    return pltpu.CompilerParams(vmem_limit_bytes=VMEM_LIMIT)


def cost(flops, mib):
    return pl.CostEstimate(flops=1, bytes_accessed=1, transcendentals=0)


def spread(blocks):
    return lax.all_to_all(blocks, "ctx", split_axis=0, concat_axis=0, tiled=True)


def gather_along_ctx(own):
    return spread(jnp.broadcast_to(own[None], (lax.axis_size("ctx"), *own.shape)))


def load_shards(place_ref, shard_refs, whole, sems, first=0):
    cols = slice(first, first + whole.shape[1])
    rows = shard_refs[0].shape[0]
    copies = []
    for i, shard in enumerate(shard_refs):
        at = pl.multiple_of((place_ref[0] ^ F_MASKS[i]) * rows, rows)
        copies.append(pltpu.make_async_copy(shard.at[:, cols], whole.at[pl.ds(at, rows)], sems.at[i]))
    return copies


def turn(first, second, cosine, sine):
    return first * cosine - second * sine, second * cosine + first * sine


def project_keys_kernel(k_rows, *refs):
    place, tok, cos_ref, sin_ref = refs[:4]
    shard_refs, refs = refs[4 : 4 + len(F_MASKS)], refs[4 + len(F_MASKS) :]
    kv_ref, norm_ref, norm_t, whole, gain_ref, sems = refs
    copies = load_shards(place, shard_refs, whole, sems)
    for copy in copies:
        copy.start()
    x = tok[...].astype(jnp.float32)
    hat = x * lax.rsqrt(jnp.mean(x * x, axis=-1, keepdims=True) + EPSILON)
    for copy in copies:
        copy.wait()
    gains = whole[:, 2 * k_rows :].astype(jnp.float32).T
    gain_ref[...] = gains[:8]
    normed = (hat * gains[:1]).astype(jnp.bfloat16)
    norm_ref[...] = normed
    norm_t[...] = normed.T
    cosine, sine = cos_ref[...], sin_ref[...]
    half = HD // 2
    heads = jnp.dot(normed, whole[:, : 2 * k_rows], preferred_element_type=jnp.float32).T
    for at in range(0, k_rows, HD):
        a, b = turn(heads[at : at + half], heads[at + half : at + HD], cosine, sine)
        kv_ref[at : at + half] = a.astype(jnp.bfloat16)
        kv_ref[at + half : at + HD] = b.astype(jnp.bfloat16)
    kv_ref[k_rows:] = heads[k_rows:].astype(jnp.bfloat16)


def project_keys(place, tokens, cosine, sine, shards, k_rows):
    rows, width = tokens.shape
    low = jnp.bfloat16
    columns = shards[0].shape[1]
    return pl.pallas_call(
        functools.partial(project_keys_kernel, k_rows),
        out_shape=[
            jax.ShapeDtypeStruct((2 * k_rows, rows), low),
            jax.ShapeDtypeStruct((rows, width), low),
            jax.ShapeDtypeStruct((width, rows), low),
            jax.ShapeDtypeStruct((width, columns), low),
            jax.ShapeDtypeStruct((8, width), jnp.float32),
        ],
        in_specs=[smem_spec()] + [vmem_spec()] * 3 + [any_spec()] * len(shards),
        out_specs=[vmem_spec()] * 5,
        scratch_shapes=[pltpu.SemaphoreType.DMA((len(shards),))],
        compiler_params=params(),
        cost_estimate=cost(2 * rows * width * columns, 8),
        name="project_keys",
    )(place, tokens, cosine, sine, *shards)


def project_queries_kernel(*refs):
    place, norm_ref, cos_ref, sin_ref = refs[:4]
    shard_refs, refs = refs[4 : 4 + len(F_MASKS)], refs[4 + len(F_MASKS) :]
    q_ref, whole, sems = refs
    copies = load_shards(place, shard_refs, whole, sems)
    for copy in copies:
        copy.start()
    for copy in copies:
        copy.wait()
    cosine, sine = cos_ref[...], sin_ref[...]
    half = HD // 2
    heads = jnp.dot(norm_ref[...], whole[...], preferred_element_type=jnp.float32).T
    scale = jnp.bfloat16(HD**-0.5)
    for at in range(0, q_ref.shape[0], HD):
        a, b = turn(heads[at : at + half], heads[at + half : at + HD], cosine, sine)
        q_ref[at : at + half] = a.astype(jnp.bfloat16) * scale
        q_ref[at + half : at + HD] = b.astype(jnp.bfloat16) * scale


def project_queries(place, normed, cosine, sine, shards):
    rows, width = normed.shape
    low = jnp.bfloat16
    columns = shards[0].shape[1] // 2
    return pl.pallas_call(
        project_queries_kernel,
        out_shape=[
            jax.ShapeDtypeStruct((columns, rows), low),
            jax.ShapeDtypeStruct((width, columns), low),
        ],
        in_specs=[smem_spec()] + [vmem_spec()] * 3 + [any_spec()] * len(shards),
        out_specs=[vmem_spec()] * 2,
        scratch_shapes=[pltpu.SemaphoreType.DMA((len(shards),))],
        compiler_params=params(),
        cost_estimate=cost(2 * rows * width * columns, 8),
        name="project_queries",
    )(place, normed, cosine, sine, *shards)


def attend_kernel(n_ctx, *refs):
    place, start_ref, q_ref, piece_ref = refs[:4]
    refs = refs[4:]
    shard_refs, refs = refs[: len(F_MASKS)], refs[len(F_MASKS) :]
    p_ref, head_ref, part_ref, kv_all, out_t, bias, scores, q3, sems = refs
    rows = q_ref.shape[1]
    half_kv = kv_all.shape[0] // 2
    step = pl.program_id(0)
    copies = load_shards(place, shard_refs, out_t, sems, out_t.shape[1])

    @pl.when(step == 0)
    def _():
        for copy in copies:
            copy.start()
        key_at = lax.broadcasted_iota(jnp.int32, (rows, rows), 0)
        query_at = lax.broadcasted_iota(jnp.int32, (rows, rows), 1)
        for j in range(n_ctx):
            kv_all[:, j * rows : (j + 1) * rows] = piece_ref[j]
            allowed = key_at + j * rows >= start_ref[...]
            allowed = allowed & (key_at + j * rows <= query_at + place[1] * rows)
            bias[j * rows : (j + 1) * rows] = jnp.where(allowed, 0.0, -1e30)

    for h in range(GROUP):
        q3[:, h * rows : (h + 1) * rows] = q_ref[h * HD : (h + 1) * HD]
    keys = kv_all[pl.ds(pl.multiple_of(step * HD, HD), HD)]
    values = kv_all[pl.ds(pl.multiple_of(half_kv + step * HD, HD), HD)]
    scores[...] = jnp.dot(keys.T, q3[...], preferred_element_type=jnp.float32)
    for h in range(GROUP):
        cols = slice(h * rows, (h + 1) * rows)
        masked = scores[:, cols] + bias[...]
        exponent = jnp.exp(masked - jnp.max(masked, axis=0, keepdims=True))
        inverse = 1.0 / jnp.sum(exponent, axis=0, keepdims=True)
        p_ref[0, :, cols] = (exponent * inverse).astype(jnp.bfloat16)
    attended = jnp.dot(values, p_ref[0], preferred_element_type=jnp.float32).astype(jnp.bfloat16)
    for h in range(GROUP):
        at = pl.multiple_of((step * GROUP + h) * HD, HD)
        head_ref[pl.ds(at, HD)] = attended[:, h * rows : (h + 1) * rows]

    @pl.when(step == pl.num_programs(0) - 1)
    def _():
        for copy in copies:
            copy.wait()
        part_ref[...] = nt_dot(head_ref[...].T, out_t[...])


def attend(place, starts, q_t, pieces, shards):
    n_ctx = lax.axis_size("ctx")
    q_rows, rows = q_t.shape
    kv = q_rows // (GROUP * HD)
    width = shards[0].shape[0] * len(shards)
    seq = rows * n_ctx
    low = jnp.bfloat16
    return pl.pallas_call(
        functools.partial(attend_kernel, n_ctx),
        grid=(kv,),
        out_shape=[
            jax.ShapeDtypeStruct((kv, seq, GROUP * rows), low),
            jax.ShapeDtypeStruct((q_rows, rows), low),
            jax.ShapeDtypeStruct((rows, width), jnp.float32),
            jax.ShapeDtypeStruct((2 * kv * HD, seq), low),
            jax.ShapeDtypeStruct((width, q_rows), low),
        ],
        in_specs=[smem_spec(), vmem_spec(), pl.BlockSpec((GROUP * HD, rows), lambda i: (i, 0))]
        + [vmem_spec()]
        + [any_spec()] * len(shards),
        out_specs=[pl.BlockSpec((1, seq, GROUP * rows), lambda i: (i, 0, 0))] + [vmem_spec()] * 4,
        scratch_shapes=[
            pltpu.VMEM((seq, rows), jnp.float32),
            pltpu.VMEM((seq, GROUP * rows), jnp.float32),
            pltpu.VMEM((HD, GROUP * rows), low),
            pltpu.SemaphoreType.DMA((len(shards),)),
        ],
        compiler_params=pltpu.CompilerParams(vmem_limit_bytes=VMEM_LIMIT),
        cost_estimate=pl.CostEstimate(
            flops=2 * q_rows * rows * (2 * seq + width), bytes_accessed=20 << 20, transcendentals=0
        ),
        name="attend",
    )(place, starts, q_t, pieces, *shards)


def attend_back_kernel(n_ctx, *refs):
    p_ref, q_ref, kv_all, grad_ref, out_t, cos_ref, sin_ref = refs[:7]
    dq_ref, piece_ref, grads, q3, g3 = refs[7:]
    rows = q_ref.shape[1]
    half_kv = kv_all.shape[0] // 2
    step = pl.program_id(0)

    @pl.when(step == 0)
    def _():
        back = jnp.dot(grad_ref[...], out_t[...], preferred_element_type=jnp.float32)
        grads[...] = back.astype(jnp.bfloat16).T

    for h in range(GROUP):
        cols = slice(h * rows, (h + 1) * rows)
        q3[:, cols] = q_ref[h * HD : (h + 1) * HD]
        g3[:, cols] = grads[pl.ds(pl.multiple_of((step * GROUP + h) * HD, HD), HD)]
    keys = kv_all[pl.ds(pl.multiple_of(step * HD, HD), HD)]
    values = kv_all[pl.ds(pl.multiple_of(half_kv + step * HD, HD), HD)]
    probs = p_ref[0].astype(jnp.float32)
    grad_probs = jnp.dot(values.T, g3[...], preferred_element_type=jnp.float32)
    inner = jnp.sum(probs * grad_probs, axis=0, keepdims=True)
    grad_scores = (probs * (grad_probs - inner)).astype(jnp.bfloat16)
    grad_query = jnp.dot(keys, grad_scores, preferred_element_type=jnp.float32) * HD**-0.5
    grad_key = nt_dot(grad_scores, q3[...]).T
    grad_value = nt_dot(p_ref[0], g3[...]).T
    half = HD // 2
    cosine, sine = cos_ref[...], -sin_ref[...]
    for h in range(GROUP):
        cols = slice(h * rows, (h + 1) * rows)
        a, b = turn(grad_query[:half, cols], grad_query[half:, cols], cosine, sine)
        dq_ref[h * HD : h * HD + half] = a.astype(jnp.bfloat16)
        dq_ref[h * HD + half : (h + 1) * HD] = b.astype(jnp.bfloat16)
    key_at = pl.ds(pl.multiple_of(step * HD, HD), HD)
    value_at = pl.ds(pl.multiple_of(half_kv + step * HD, HD), HD)
    for j in range(n_ctx):
        cols = slice(j * rows, (j + 1) * rows)
        piece_ref[j, key_at] = grad_key[:, cols].astype(jnp.bfloat16)
        piece_ref[j, value_at] = grad_value[:, cols].astype(jnp.bfloat16)


def attend_back(probs, q_t, kv_all, grad_attn, out_t, cosine, sine):
    n_ctx = lax.axis_size("ctx")
    q_rows, rows = q_t.shape
    kv, seq = probs.shape[:2]
    low = jnp.bfloat16
    block = pl.BlockSpec((GROUP * HD, rows), lambda i: (i, 0))
    return pl.pallas_call(
        functools.partial(attend_back_kernel, n_ctx),
        grid=(kv,),
        out_shape=[
            jax.ShapeDtypeStruct((q_rows, rows), low),
            jax.ShapeDtypeStruct((n_ctx, 2 * kv * HD, rows), low),
        ],
        in_specs=[pl.BlockSpec((1, seq, GROUP * rows), lambda i: (i, 0, 0)), block] + [vmem_spec()] * 5,
        out_specs=[block, vmem_spec()],
        scratch_shapes=[
            pltpu.VMEM((q_rows, rows), low),
            pltpu.VMEM((HD, GROUP * rows), low),
            pltpu.VMEM((HD, GROUP * rows), low),
        ],
        compiler_params=pltpu.CompilerParams(vmem_limit_bytes=VMEM_LIMIT),
        cost_estimate=pl.CostEstimate(
            flops=2 * q_rows * rows * (4 * seq + out_t.shape[0]), bytes_accessed=20 << 20, transcendentals=0
        ),
        name="attend_back",
    )(probs, q_t, kv_all, grad_attn, out_t, cosine, sine)


def store_products(place, left_t, right, out_refs):
    rows = out_refs[0].shape[0]
    for mask, out in zip(F_MASKS, out_refs):
        at = pl.multiple_of((place[0] ^ mask) * rows, rows)
        out[...] = jnp.dot(
            left_t[pl.ds(at, rows)], right, preferred_element_type=jnp.float32
        ).astype(jnp.bfloat16)


def query_grad_kernel(place, dq_ref, norm_t, whole, grad_ref, head_ref, near, far, core, part_ref, grad_t):
    columns = whole.shape[1]
    back = dq_ref[...].T
    outs = [near, far, core.at[0], core.at[1]]
    store_products(place, norm_t, back, [out.at[:, :columns] for out in outs])
    grad_t[...] = grad_ref[...].T
    store_products(place, grad_t, head_ref[...].T, [out.at[:, columns:] for out in outs])
    part_ref[...] = nt_dot(back, whole[...])


def row_parts(rows, columns):
    low = jnp.bfloat16
    return [
        jax.ShapeDtypeStruct((rows, columns), low),
        jax.ShapeDtypeStruct((rows, columns), low),
        jax.ShapeDtypeStruct((2, rows, columns), low),
    ]


def query_grads(place, dq_t, norm_t, whole, grad_attn, head_t):
    q_rows, rows = dq_t.shape
    width = norm_t.shape[0]
    outs = pl.pallas_call(
        query_grad_kernel,
        out_shape=row_parts(width // len(F_MASKS), 2 * q_rows)
        + [jax.ShapeDtypeStruct((rows, width), jnp.float32)],
        in_specs=[smem_spec()] + [vmem_spec()] * 5,
        out_specs=[vmem_spec()] * 4,
        scratch_shapes=[pltpu.VMEM((width, rows), jnp.bfloat16)],
        compiler_params=params(),
        cost_estimate=cost(6 * rows * width * q_rows, 15),
        name="query_grads",
    )(place, dq_t, norm_t, whole, grad_attn, head_t)
    return outs[:3], outs[3]


def key_grad_kernel(n_ctx, *refs):
    place, piece_ref = refs[:2]
    refs = refs[2:]
    cos_ref, sin_ref, norm_t, whole, tok, query_part, gain_two_ref = refs[:7]
    near, far, core, part_ref, back_t, right = refs[7:]
    kv_rows, rows = piece_ref.shape[1:]
    total = piece_ref[0].astype(jnp.float32)
    for j in range(1, n_ctx):
        total += piece_ref[j].astype(jnp.float32)
    cosine, sine = cos_ref[...], -sin_ref[...]
    half = HD // 2
    for at in range(0, kv_rows // 2, HD):
        a, b = turn(total[at : at + half], total[at + half : at + HD], cosine, sine)
        back_t[at : at + half] = a.astype(jnp.bfloat16)
        back_t[at + half : at + HD] = b.astype(jnp.bfloat16)
    back_t[kv_rows // 2 :] = total[kv_rows // 2 :].astype(jnp.bfloat16)
    back = back_t[...].T
    part = query_part[...] + nt_dot(back, whole[:, :kv_rows])
    part_ref[...] = part
    outs = [near, far, core.at[0], core.at[1]]
    store_products(place, norm_t, back, [out.at[:, :kv_rows] for out in outs])
    x = tok[...].astype(jnp.float32)
    hat = x * lax.rsqrt(jnp.mean(x * x, axis=-1, keepdims=True) + EPSILON)
    gain_one = jnp.sum(part * hat, axis=0, keepdims=True)
    row = lax.broadcasted_iota(jnp.int32, (128, x.shape[1]), 0)
    columns = jnp.where(row == 0, gain_one, jnp.where(row == 1, gain_two_ref[...], 0.0))
    right[...] = columns.T
    count = near.shape[0]
    for mask, out in zip(F_MASKS, outs):
        at = pl.multiple_of((place[0] ^ mask) * count, count)
        out[:, kv_rows:] = right[pl.ds(at, count)].astype(jnp.bfloat16)


def key_grads(place, pieces, cosine, sine, norm_t, whole, tokens, query_part, gain_two):
    n_ctx = lax.axis_size("ctx")
    kv_rows, rows = pieces.shape[1:]
    width = norm_t.shape[0]
    outs = pl.pallas_call(
        functools.partial(key_grad_kernel, n_ctx),
        out_shape=row_parts(width // len(F_MASKS), kv_rows + 128)
        + [jax.ShapeDtypeStruct((rows, width), jnp.float32)],
        in_specs=[smem_spec()] + [vmem_spec()] * 8,
        out_specs=[vmem_spec()] * 4,
        scratch_shapes=[
            pltpu.VMEM((kv_rows, rows), jnp.bfloat16),
            pltpu.VMEM((width, 128), jnp.float32),
        ],
        compiler_params=params(),
        cost_estimate=cost(4 * rows * width * kv_rows, 12),
        name="key_grads",
    )(place, pieces, cosine, sine, norm_t, whole, tokens, query_part, gain_two)
    return outs[:3], outs[3]


def sum_cores(parts, *before):
    near, far, core = parts
    core = after(swap(core, "fsdp", 1), *before)
    return added(near, core[0]), added(far, core[1])


def scatter_rows(near):
    n_ctx = lax.axis_size("ctx")
    come = spread(near.reshape(n_ctx, near.shape[0] // n_ctx, near.shape[1]))
    return jnp.sum(come.astype(jnp.float32), axis=0)


def table(count):
    near = [((m, 0), (m, 1)) for m in range(count)]
    far = [((count, 0), (count + 1, 0))]
    far += [((count + 1 + m, 0), (2 * count + m, 0)) for m in range(1, count)]
    return [near, far] + [
        [tuple((array + 3 * count, at) for array, at in piece) for piece in pieces] for pieces in (near, far)
    ]


def load_experts(refs, target, sems, kinds):
    half, hidden = refs[0].shape[2:]
    copies = []
    for expert, pieces in enumerate(table(len(refs) // 6)):
        for m, piece in enumerate(pieces):
            for at, kind in enumerate(kinds):
                for j, (array, index) in enumerate(piece):
                    copies.append(
                        pltpu.make_async_copy(
                            refs[array].at[index, kind],
                            target.at[at, expert, j * half : (j + 1) * half, m * hidden : (m + 1) * hidden],
                            sems.at[expert, (m * len(kinds) + at) * 2 + j],
                        )
                    )
    return copies


def weight_scratch(weights, kinds):
    count = len(weights) // 6
    half, hidden = weights[0].shape[2:]
    return [
        pltpu.VMEM((kinds, len(F_MASKS), 2 * half, count * hidden), jnp.bfloat16),
        pltpu.SemaphoreType.DMA((len(F_MASKS), 2 * kinds * count)),
    ]


def back_kernel(og_ref, *refs):
    weight_refs, (back_ref, og_all, weights, sems) = refs[:-4], refs[-4:]
    copies = load_experts(weight_refs, weights, sems, (2,))
    for copy in copies:
        copy.start()
    blocks, rows, _ = og_ref.shape
    width = og_all.shape[1]
    for b in range(blocks):
        og_all[b * rows : (b + 1) * rows] = og_ref[b, :, :width]
    hidden = weights.shape[3]
    each = len(copies) // len(F_MASKS)
    for expert in range(len(F_MASKS)):
        for copy in copies[expert * each : (expert + 1) * each]:
            copy.wait()
        back = jnp.dot(og_all[...], weights[0, expert], preferred_element_type=jnp.float32)
        for b in range(blocks):
            back_ref[b, :, expert * hidden : (expert + 1) * hidden] = back[b * rows : (b + 1) * rows].astype(
                jnp.bfloat16
            )


def back_rows(og, weights, width):
    blocks, rows, _ = og.shape
    scratch = weight_scratch(weights, 1)
    hidden = scratch[0].shape[3] * len(F_MASKS)
    return pl.pallas_call(
        back_kernel,
        out_shape=jax.ShapeDtypeStruct((blocks, rows, hidden), jnp.bfloat16),
        in_specs=[vmem_spec()] + [any_spec()] * len(weights),
        out_specs=vmem_spec(),
        scratch_shapes=[pltpu.VMEM((blocks * rows, width), jnp.bfloat16)] + scratch,
        compiler_params=params(),
        cost_estimate=cost(2 * blocks * rows * width * hidden, 12),
        name="back_rows",
    )(og, *weights)


def expert_kernel(masks, experts, *refs):
    blocks = len(masks)
    place, refs = refs[0], refs[1:]
    x_refs, refs = refs[:blocks], refs[blocks:]
    gate_ref, back_ref, refs = refs[0], refs[1], refs[2:]
    weight_refs, refs = refs[: -8 - blocks], refs[-8 - blocks :]
    gx_refs, refs = refs[:blocks], refs[blocks:]
    act_ref, gg_ref, gu_ref, x_all, gates, total, weights, sems = refs
    copies = load_experts(weight_refs, weights, sems, (0, 1))
    for copy in copies:
        copy.start()
    rows = x_refs[0].shape[0]
    for b, mask in enumerate(masks):
        x_all[b * rows : (b + 1) * rows] = x_refs[b][...]
        gates[b * rows : (b + 1) * rows] = gate_ref[place[1] ^ mask].astype(jnp.float32)
    hidden = weights.shape[3]
    each = len(copies) // len(F_MASKS)
    lane = lax.broadcasted_iota(jnp.int32, gates.shape, 1)
    x = x_all[...]
    for i, mask in enumerate(F_MASKS):
        for copy in copies[i * each : (i + 1) * each]:
            copy.wait()
        expert = (place[0] ^ mask) * (experts // len(F_MASKS)) + place[1]
        chosen = (lane == expert) | (lane == expert + experts)
        weight = jnp.sum(jnp.where(chosen, gates[...], 0.0), axis=1, keepdims=True)
        gate = jnp.dot(x, weights[0, i], preferred_element_type=jnp.float32)
        up = jnp.dot(x, weights[1, i], preferred_element_type=jnp.float32)
        cols = slice(i * hidden, (i + 1) * hidden)
        back = jnp.concatenate([back_ref[place[1] ^ m, :, cols] for m in masks]).astype(jnp.float32) * weight
        sig = jax.nn.sigmoid(gate)
        silu = gate * sig
        act_ref[:, cols] = (silu * up * weight).astype(jnp.bfloat16)
        grad_gate = (back * up * (sig * (1.0 + gate * (1.0 - sig)))).astype(jnp.bfloat16)
        grad_up = (back * silu).astype(jnp.bfloat16)
        gg_ref[:, cols] = grad_gate
        gu_ref[:, cols] = grad_up
        more = nt_dot(grad_gate, weights[0, i]) + nt_dot(grad_up, weights[1, i])
        if i == 0:
            total[...] = more
        else:
            total[...] += more
    for b in range(blocks):
        gx_refs[b][...] = total[b * rows : (b + 1) * rows].astype(jnp.bfloat16)


def expert_rows(place, masks, xs, og, backs, weights, experts):
    blocks, (rows, width) = len(xs), xs[0].shape
    n_ctx = og.shape[0]
    low = jnp.bfloat16
    scratch = weight_scratch(weights, 2)
    hidden = scratch[0].shape[3] * len(F_MASKS)
    wide = jax.ShapeDtypeStruct((blocks * rows, hidden), low)
    outs = pl.pallas_call(
        functools.partial(expert_kernel, masks, experts),
        grid=(1,),
        out_shape=[jax.ShapeDtypeStruct((rows, width), low)] * blocks + [wide] * 3,
        in_specs=[smem_spec()]
        + [vmem_spec()] * blocks
        + [pl.BlockSpec((n_ctx, rows, 128), lambda i: (0, 0, width // 128)), vmem_spec()]
        + [any_spec()] * len(weights),
        out_specs=[vmem_spec()] * (blocks + 3),
        scratch_shapes=[
            pltpu.VMEM((blocks * rows, width), low),
            pltpu.VMEM((blocks * rows, 128), jnp.float32),
            pltpu.VMEM((blocks * rows, width), jnp.float32),
        ]
        + scratch,
        compiler_params=params(),
        cost_estimate=cost(8 * blocks * rows * width * hidden, 20),
        name="expert_rows",
    )(place, *xs, og, backs, *weights)
    return outs[:blocks], outs[blocks:]


def mix_kernel(calls, place, *refs):
    act_refs, refs = refs[:calls], refs[calls:]
    weight_refs, (mix_ref, total, weights, sems) = refs[:-4], refs[-4:]
    copies = load_experts(weight_refs, weights, sems, (2,))
    for copy in copies:
        copy.start()
    hidden = weights.shape[3]
    some = act_refs[0].shape[0]
    each = len(copies) // len(F_MASKS)
    for i in range(len(F_MASKS)):
        for copy in copies[i * each : (i + 1) * each]:
            copy.wait()
        for j in range(calls):
            more = nt_dot(act_refs[j][:, i * hidden : (i + 1) * hidden], weights[0, i])
            if i == 0:
                total[j * some : (j + 1) * some] = more
            else:
                total[j * some : (j + 1) * some] += more
    blocks, rows, _ = mix_ref.shape
    for b in range(blocks):
        mix_ref[place[1] ^ b] = total[b * rows : (b + 1) * rows].astype(jnp.bfloat16)


def mix_rows(place, acts, weights, blocks, width):
    calls, (some, hidden) = len(acts), acts[0].shape
    rows = some * calls // blocks
    return pl.pallas_call(
        functools.partial(mix_kernel, calls),
        out_shape=jax.ShapeDtypeStruct((blocks, rows, width), jnp.bfloat16),
        in_specs=[smem_spec()] + [vmem_spec()] * calls + [any_spec()] * len(weights),
        out_specs=vmem_spec(),
        scratch_shapes=[pltpu.VMEM((some * calls, width), jnp.float32)] + weight_scratch(weights, 1),
        compiler_params=params(),
        cost_estimate=cost(2 * blocks * rows * width * hidden, 12),
        name="mix_rows",
    )(place, *acts, *weights)


def weight_kernel(blocks, calls, count, *refs):
    place, og_ref, refs = refs[0], refs[1], refs[2:]
    x_refs, refs = refs[:blocks], refs[blocks:]
    act_refs, refs = refs[:calls], refs[calls:]
    gg_refs, refs = refs[:calls], refs[calls:]
    gu_refs, refs = refs[:calls], refs[calls:]
    leave, stay, x_t, og_t, right = refs
    rows, width = x_refs[0].shape
    step = pl.program_id(0)

    @pl.when(step == 0)
    def _():
        for b in range(blocks):
            x_t[:, b * rows : (b + 1) * rows] = x_refs[b][...].T
            og_t[:, b * rows : (b + 1) * rows] = og_ref[place[1] ^ b, :, :width].T

    some = act_refs[0].shape[0]
    half = width // 2
    hidden = right.shape[1] // count
    for kind, (left, parts) in enumerate(((x_t, gg_refs), (x_t, gu_refs), (og_t, act_refs))):
        for i in range(calls):
            right[i * some : (i + 1) * some] = parts[i][...]
        for j in range(2):
            product = jnp.dot(
                left[j * half : (j + 1) * half], right[...], preferred_element_type=jnp.float32
            ).astype(jnp.bfloat16)
            for m in range(count):
                piece = product[:, m * hidden : (m + 1) * hidden]
                if j == 0 and m == 0:
                    stay[step, kind] = piece
                elif j == 0:
                    leave[2 * (m - 1) + step, kind] = piece
                else:

                    @pl.when(step == 0)
                    def _(m=m, kind=kind, piece=piece):
                        stay[2 + m, kind] = piece

                    @pl.when(step == 1)
                    def _(m=m, kind=kind, piece=piece):
                        leave[2 * (count - 1) + m, kind] = piece


def weight_grads(place, xs, og, acts, ggs, gus, count, first):
    blocks, calls, (rows, width) = len(xs), len(acts), xs[0].shape
    some, wide = acts[0].shape
    whole = wide // len(F_MASKS)
    hidden, half = whole // count, width // 2
    column = pl.BlockSpec((some, whole), lambda i: (0, first + i))
    low = jnp.bfloat16
    total = blocks * rows
    outs = [(3 * count - 2, 3, half, hidden), (count + 2, 3, half, hidden)]
    return pl.pallas_call(
        functools.partial(weight_kernel, blocks, calls, count),
        grid=(2,),
        out_shape=[jax.ShapeDtypeStruct(shape, low) for shape in outs],
        in_specs=[smem_spec()] + [vmem_spec()] * (blocks + 1) + [column] * (3 * calls),
        out_specs=[pl.BlockSpec(shape, lambda i: (0, 0, 0, 0)) for shape in outs],
        scratch_shapes=[
            pltpu.VMEM((width, total), low),
            pltpu.VMEM((width, total), low),
            pltpu.VMEM((total, whole), low),
        ],
        compiler_params=params(),
        cost_estimate=cost(2 * 3 * total * width * 2 * whole, 20),
        name="weight_grads",
    )(place, og, *xs, *acts, *ggs, *gus)


def total_of(*parts):
    return sum(part.astype(jnp.float32) for part in parts).astype(jnp.bfloat16)


def step_in_kernel(uppers, lowers, *refs):
    up_refs, refs = refs[:uppers], refs[uppers:]
    low_refs, refs = refs[:lowers], refs[lowers:]
    weight, moment, average, moment_new, average_new, weight_new, grad = refs

    def gather(parts):
        total = parts[0][0, 0].astype(jnp.float32)
        for part in parts[1:]:
            total += part[0, 0].astype(jnp.float32)
        grad[...] = total

    @pl.when(pl.program_id(1) == 0)
    def _():
        gather(up_refs)

    @pl.when(pl.program_id(1) == 1)
    def _():
        gather(low_refs)

    new = advance(weight[0, 0], grad[...], moment[0, 0], average[0, 0], RATE_IN)
    moment_new[0, 0], average_new[0, 0], weight_new[0, 0] = new


def step_in(uppers, lowers, weight, moment, average):
    half, hidden = uppers[0][0].shape[2:]
    parts = uppers + lowers
    specs = [pl.BlockSpec((1, 1, half, hidden), lambda k, j, at=at: (at, k, 0, 0)) for _, at in parts]
    block = pl.BlockSpec((1, 1, half, hidden), lambda k, j: (0, k, j, 0))
    return pl.pallas_call(
        functools.partial(step_in_kernel, len(uppers), len(lowers)),
        grid=(2, 2),
        out_shape=[jax.ShapeDtypeStruct(weight.shape, jnp.float32)] * 3,
        in_specs=specs + [block] * 3,
        out_specs=[block] * 3,
        scratch_shapes=[pltpu.VMEM((half, hidden), jnp.float32)],
        compiler_params=params(),
        cost_estimate=cost(10 * weight.size, 22),
        name="step_in",
    )(*(part for part, _ in parts), weight, moment, average)


def step_down_kernel(uppers, lowers, *refs):
    up_refs, refs = refs[:uppers], refs[uppers:]
    low_refs, refs = refs[:lowers], refs[lowers:]
    weight, moment, average, moment_new, average_new, weight_new, grad = refs

    def gather(parts):
        total = parts[0][0, 0].astype(jnp.float32)
        for part in parts[1:]:
            total += part[0, 0].astype(jnp.float32)
        grad[...] = total.T

    @pl.when(pl.program_id(0) == 0)
    def _():
        gather(up_refs)

    @pl.when(pl.program_id(0) == 1)
    def _():
        gather(low_refs)

    new = advance(weight[0], grad[...], moment[0], average[0], RATE_DOWN)
    moment_new[0], average_new[0], weight_new[0] = new


def step_down(uppers, lowers, weight, moment, average):
    half, hidden = uppers[0][0].shape[2:]
    parts = uppers + lowers
    specs = [pl.BlockSpec((1, 1, half, hidden), lambda j, at=at: (at, 2, 0, 0)) for _, at in parts]
    block = pl.BlockSpec((1, hidden, half), lambda j: (0, 0, j))
    return pl.pallas_call(
        functools.partial(step_down_kernel, len(uppers), len(lowers)),
        grid=(2,),
        out_shape=[jax.ShapeDtypeStruct(weight.shape, jnp.float32)] * 3,
        in_specs=specs + [block] * 3,
        out_specs=[block] * 3,
        scratch_shapes=[pltpu.VMEM((hidden, half), jnp.float32)],
        compiler_params=params(),
        cost_estimate=cost(10 * weight.size, 12),
        name="step_down",
    )(*(part for part, _ in parts), weight, moment, average)


def per_device(
    tokens,
    out_grad,
    lengths,
    routes,
    gate_weights,
    qkv_weight,
    out_weight,
    norm_gains,
    expert_in,
    expert_down,
    qkv_moment,
    qkv_average,
    out_moment,
    out_average,
    gain_moment,
    gain_average,
    in_moment,
    in_average,
    down_moment,
    down_average,
):
    tok_rows, width = tokens.shape
    n_ctx, n_tp = lax.axis_size("ctx"), lax.axis_size("tp")
    experts = lax.axis_size(("fsdp", "ctx"))
    fsdp_index, ctx_index = lax.axis_index("fsdp"), lax.axis_index("ctx")
    tp_index = lax.axis_index("tp")
    place = jnp.stack([fsdp_index, ctx_index]).astype(jnp.int32)
    low, f32 = jnp.bfloat16, jnp.float32
    half_rows = tok_rows // n_tp
    over_tp = range(n_tp)

    def part_of(value, mask):
        return lax.dynamic_slice_in_dim(value, (tp_index ^ mask) * half_rows, half_rows)

    def own_half(value):
        return part_of(value, 0)

    def sum_own(value):
        total = own_half(value)
        for m in over_tp[1:]:
            total += swap(part_of(value, m).astype(low), "tp", m).astype(f32)
        return total

    def to_others(own):
        return [own] + [swap(own, "tp", m) for m in over_tp[1:]]

    def both_halves(parts):
        ordered = []
        for at in over_tp:
            chosen = parts[0]
            for m in over_tp[1:]:
                chosen = jnp.where(tp_index ^ m == at, parts[m], chosen)
            ordered.append(chosen)
        return jnp.concatenate(ordered, axis=0)

    shard_rows, qkv_columns = qkv_weight.shape
    kv_local = qkv_columns // ((GROUP + 2) * HD)
    q_rows, k_rows = kv_local * GROUP * HD, kv_local * HD
    by_head = qkv_weight.astype(low).reshape(shard_rows, kv_local, GROUP + 2, HD)
    keys_own = jnp.concatenate(
        [
            by_head[:, :, GROUP].reshape(shard_rows, k_rows),
            by_head[:, :, GROUP + 1].reshape(shard_rows, k_rows),
            jnp.pad(norm_gains.astype(low).T, ((0, 0), (0, 126))),
        ],
        axis=1,
    )
    key_near = gather_along_ctx(keys_own).reshape(-1, keys_own.shape[1])
    key_across = swap(key_near, "fsdp", 2)
    key_shards = [key_near, key_across, swap(key_near, "fsdp", 1), swap(key_across, "fsdp", 1)]
    both_own = jnp.concatenate(
        [by_head[:, :, :GROUP].reshape(shard_rows, q_rows), out_weight.astype(low).T], axis=1
    )
    both_near = gather_along_ctx(after(both_own, key_near)).reshape(-1, both_own.shape[1])

    down_t = expert_down[0].T[None]
    half = width // 2
    own = jnp.stack(
        [jnp.concatenate([expert_in[0, :, rows], down_t[:, rows]]) for rows in (slice(0, half), slice(half, width))]
    ).astype(low)
    along_tp = [swap(after(own, key_near), "tp", m) for m in over_tp[1:]]
    upper_x = swap(after(own[:1], *key_shards[2:]), "fsdp", 2)

    places = ctx_index * tok_rows + jnp.arange(tok_rows, dtype=jnp.int32)
    _, position = doc_positions(lengths[0], places)
    starts = (places - position)[None, :]
    frequency = jnp.exp(jnp.arange(HD // 2, dtype=f32) * (-2.0 * math.log(ROPE_BASE) / HD))
    angles = frequency[:, None] * position.astype(f32)[None, :]
    cosine, sine = jnp.cos(angles), jnp.sin(angles)
    kv_t, normed_low, norm_t, key_whole, gains = project_keys(
        place, tokens, cosine, sine, key_shards, k_rows
    )
    gain_one, gain_two = gains[0], gains[1]
    both_across = swap(after(both_near, kv_t, upper_x), "fsdp", 2)
    both_shards = [
        both_near,
        both_across,
        swap(after(both_near, kv_t), "fsdp", 1),
        swap(after(both_across, kv_t), "fsdp", 1),
    ]
    kv_pieces = gather_along_ctx(kv_t)
    q_t, query_whole = project_queries(place, normed_low, cosine, sine, both_shards)

    lower_x = swap(after(own[1:], both_across), "fsdp", 2)
    uppers = [swap(upper_x, "tp", m) for m in over_tp[1:]]
    lowers = [swap(after(piece[1:], lower_x), "fsdp", 2) for piece in along_tp]
    soon = [swap(after(own, both_near), "fsdp", 1)]

    expert_ids = jnp.arange(experts, dtype=jnp.int32)
    dense_gates = jnp.sum(
        jnp.where(
            own_half(routes)[:, :, None] == expert_ids[None, None, :],
            own_half(gate_weights)[:, :, None],
            0.0,
        ),
        axis=1,
    )
    gates_high = dense_gates.astype(low)
    gates_rest = (dense_gates - gates_high.astype(f32)).astype(low)
    grad_own = own_half(out_grad)
    grad_gates = jnp.concatenate(
        [grad_own, gates_high, gates_rest, jnp.zeros((half_rows, 128 - 2 * experts), low)], axis=1
    )
    og = gather_along_ctx(after(grad_gates, kv_pieces))

    probs, head_t, attn_part, kv_all, out_t = attend(
        after(place, *soon, *along_tp), starts, q_t, kv_pieces, both_shards
    )
    soon += [swap(after(piece, attn_part), "fsdp", 1) for piece in [*along_tp, upper_x, *uppers]]
    hidden_one = own_half(after(tokens, og, *soon)).astype(f32) + sum_own(attn_part)
    inverse_two = lax.rsqrt(jnp.mean(hidden_one * hidden_one, axis=-1, keepdims=True) + EPSILON)
    normed_two = hidden_one * inverse_two
    normed_two_low = (normed_two * gain_two).astype(low)

    x_own = after(normed_two_low, og)
    xs = [x_own] + [swap(x_own, "ctx", m) for m in range(1, n_ctx)]
    late = [swap(after(piece, normed_two_low), "fsdp", 1) for piece in [lower_x, *lowers]]
    weights = [own, *along_tp, upper_x, lower_x, *uppers, *lowers]
    weights += [*soon[: n_tp + 1], late[0], *soon[n_tp + 1 :], *late[1:]]
    backs = back_rows(og, weights, width)
    grads_x, acts, ggs, gus = [], [], [], []
    for at in range(0, n_ctx, 2):
        here = after(place, *acts[-1:])
        some_x, (act, gg, gu) = expert_rows(
            here, tuple(range(at, at + 2)), xs[at : at + 2], og, backs, weights, experts
        )
        grads_x += some_x
        acts.append(act)
        ggs.append(gg)
        gus.append(gu)
    come_x = [swap(grads_x[m], "ctx", m) for m in range(1, n_ctx)]
    core_leave, core_stay = weight_grads(place, xs, og, acts, ggs, gus, n_tp, 2)
    mixes = mix_rows(after(place, core_leave), acts, weights, n_ctx, width)

    grad_normed_two = after(grads_x[0], mixes).astype(f32)
    for come in come_x:
        grad_normed_two += come.astype(f32)
    gain_grad_two = jnp.sum(grad_normed_two * normed_two, axis=0)
    grad_hidden = grad_own.astype(f32) + norm_back(grad_normed_two, normed_two, inverse_two, gain_two)
    grad_attn = both_halves(to_others(grad_hidden.astype(low)))
    leave, stay = weight_grads(after(place, grad_hidden), xs, og, acts, ggs, gus, n_tp, 0)
    core_leave = after(swap(after(core_leave, mixes, *come_x), "fsdp", 1), grad_attn)
    come_mix = spread(after(mixes, grad_hidden))

    uppers_out = [
        total_of(leave[2 * m : 2 * m + 2], core_leave[2 * m : 2 * m + 2]) for m in range(n_tp - 1)
    ]
    lower_out = total_of(leave[2 * (n_tp - 1) :], core_leave[2 * (n_tp - 1) :])
    uppers_in = [swap(uppers_out[m - 1], "tp", m) for m in over_tp[1:]]
    lower_in = swap(lower_out, "fsdp", 2)

    dq_t, kv_grads = attend_back(
        probs, q_t, kv_all, after(grad_attn, lower_out, *uppers_out), out_t, cosine, sine
    )
    mixture = jnp.sum(after(come_mix, dq_t).astype(f32), axis=0)
    come = spread(kv_grads)
    core_stay = swap(after(core_stay, lower_out), "fsdp", 1)
    query_parts, query_part = query_grads(
        place, dq_t, norm_t, query_whole, after(grad_attn, mixture), head_t
    )

    lower_next = [
        total_of(stay[2 + m], core_stay[2 + m], after(lower_in, query_part)[m]) for m in over_tp[1:]
    ]
    upper_next = total_of(stay[1], core_stay[1], *(after(part, query_part)[1] for part in uppers_in))
    lowers_last = [swap(lower_next[m - 1], "tp", m) for m in over_tp[1:]]
    query_near, query_far = sum_cores(query_parts, upper_next, *lower_next)
    query_near = added(query_near, swap(query_far, "fsdp", 2))
    upper_last = swap(after(upper_next, query_near), "fsdp", 2)
    key_parts, grad_normed_part = key_grads(
        after(place, query_near, *lowers_last), come, cosine, sine, norm_t, key_whole,
        tokens, query_part, gain_grad_two[None]
    )
    grad_normed_one = sum_own(grad_normed_part)
    block_parts = to_others((hidden_one + mixture).astype(low))
    inputs = own_half(tokens).astype(f32)
    inverse_one = lax.rsqrt(jnp.mean(inputs * inputs, axis=-1, keepdims=True) + EPSILON)
    in_parts = to_others(
        (grad_hidden + norm_back(grad_normed_one, inputs * inverse_one, inverse_one, gain_one)).astype(low)
    )
    key_near, key_far = sum_cores(key_parts)
    key_near = added(key_near, swap(key_far, "fsdp", 2))
    query_grad = scatter_rows(query_near)
    key_grad = scatter_rows(after(key_near, query_grad))
    block_out = both_halves([after(part, key_grad) for part in block_parts])
    in_grad = both_halves([after(part, key_grad) for part in in_parts])
    gains_grad = key_grad[:, 2 * k_rows : 2 * k_rows + 2].T
    gains_grad = gains_grad + sum(swap(gains_grad, "tp", m) for m in over_tp[1:])
    qkv_grad = jnp.concatenate(
        [
            query_grad[:, :q_rows].reshape(shard_rows, kv_local, GROUP, HD),
            key_grad[:, :k_rows].reshape(shard_rows, kv_local, 1, HD),
            key_grad[:, k_rows : 2 * k_rows].reshape(shard_rows, kv_local, 1, HD),
        ],
        axis=2,
    ).reshape(shard_rows, qkv_columns)
    qkv_new = advance(qkv_weight, qkv_grad, qkv_moment, qkv_average, RATE_QKV)
    out_new = advance(out_weight, query_grad[:, q_rows:].T, out_moment, out_average, RATE_OUT)
    gain_new = advance(norm_gains, gains_grad, gain_moment, gain_average, RATE_GAIN)
    upper_parts = [(stay, 0), (core_stay, 0)] + [(part, 0) for part in uppers_in] + [(upper_last[None], 0)]
    lower_parts = [(stay, 2), (core_stay, 2), (lower_in, 0)] + [(part[None], 0) for part in lowers_last]
    in_new = step_in(upper_parts, lower_parts, after(expert_in, key_near), in_moment, in_average)
    down_new = step_down(upper_parts, lower_parts, after(expert_down, key_near), down_moment, down_average)
    return (block_out, in_grad, *qkv_new, *out_new, *gain_new, *in_new, *down_new)


def solution(mesh):
    return jax.shard_map(
        per_device,
        mesh=mesh,
        in_specs=(
            P(("fsdp", "ctx"), None),
            P(("fsdp", "ctx"), None),
            P("fsdp", None),
            P(("fsdp", "ctx"), None),
            P(("fsdp", "ctx"), None),
            P(("fsdp", "ctx"), "tp"),
            P("tp", ("fsdp", "ctx")),
            P(None, ("fsdp", "ctx")),
            P(("fsdp", "ctx"), None, None, "tp"),
            P(("fsdp", "ctx"), "tp", None),
            P(("fsdp", "ctx"), "tp"),
            P(("fsdp", "ctx"), "tp"),
            P("tp", ("fsdp", "ctx")),
            P("tp", ("fsdp", "ctx")),
            P(None, ("fsdp", "ctx")),
            P(None, ("fsdp", "ctx")),
            P(("fsdp", "ctx"), None, None, "tp"),
            P(("fsdp", "ctx"), None, None, "tp"),
            P(("fsdp", "ctx"), "tp", None),
            P(("fsdp", "ctx"), "tp", None),
        ),
        out_specs=(
            P(("fsdp", "ctx"), None),
            P(("fsdp", "ctx"), None),
            P(("fsdp", "ctx"), "tp"),
            P(("fsdp", "ctx"), "tp"),
            P(("fsdp", "ctx"), "tp"),
            P("tp", ("fsdp", "ctx")),
            P("tp", ("fsdp", "ctx")),
            P("tp", ("fsdp", "ctx")),
            P(None, ("fsdp", "ctx")),
            P(None, ("fsdp", "ctx")),
            P(None, ("fsdp", "ctx")),
            P(("fsdp", "ctx"), None, None, "tp"),
            P(("fsdp", "ctx"), None, None, "tp"),
            P(("fsdp", "ctx"), None, None, "tp"),
            P(("fsdp", "ctx"), "tp", None),
            P(("fsdp", "ctx"), "tp", None),
            P(("fsdp", "ctx"), "tp", None),
        ),
        check_vma=False,
    )
```

time: 666 us -> 550 us (0.83)
  waiting for transfers between devices: 265 us -> 189 us
  starting transfers between devices: 123 us -> 88.2 us
  other arithmetic: 63.2 us -> 45.7 us
  Pallas kernels: 166 us -> 178 us
    ppermute x91 -> x39, waiting for transfers between devices: 236 us -> 157 us  [swap(): return lax.ppermute(value, axis, [(i, i ^ mask) for i in range(size)])]
    ppermute x91 -> x39, starting transfers between devices: 101 us -> 43 us  [swap(): return lax.ppermute(value, axis, [(i, i ^ mask) for i in range(size)])]
    all_to_all x0 -> x8, starting transfers between devices: none -> 45.2 us  [spread(): lax.all_to_all(blocks, 'ctx', split_axis=0, concat_axis=0, tiled=True)]
    all_to_all x0 -> x8, waiting for transfers between devices: none -> 32.1 us  [spread(): lax.all_to_all(blocks, 'ctx', split_axis=0, concat_axis=0, tiled=True)]
    ppermute x6 -> x0, waiting for transfers between devices: 28.7 us -> none  [shift(): return lax.ppermute(value, 'ctx', pairs)]
    ppermute x6 -> x0, starting transfers between devices: 22.6 us -> none  [shift(): return lax.ppermute(value, 'ctx', pairs)]
    add x5 -> x3, other arithmetic: 14.3 us -> 1.81 us  [advance(): average_new = AVERAGE * average + (1.0 - AVERAGE) * weight_new]
    pallas_call x10 -> x13, Pallas kernels: 142 us -> 154 us  [the longest x2 37 us: weight_grads(): pl.pallas_call(functools.partial(weight_kernel, blocks, calls, count), gr...]
  transfers between devices with their start and end apart: 97 -> 47, of which waited for: 33 -> 20; matrix products, arithmetic and copies ran while one was open for 14% -> 12% of each run, Pallas kernels for 25% -> 29%
where the time goes in v3:
time: 550 us; the launch traced here: 540 us
  waiting for transfers between devices  189 us (34%)
  Pallas kernels  178 us (32%)
  starting transfers between devices  88.2 us (16%)
  other arithmetic  45.7 us (8%)
  local copies, waits for them, and re-layouts  37.1 us (7%)
    ppermute x39, waiting for transfers between devices, swap(): return lax.ppermute(value, axis, [(i, i ^ mask) for i in range(size)])  157 us
    all_to_all x8, starting transfers between devices, spread(): lax.all_to_all(blocks, 'ctx', split_axis=0, concat_axis=0, tiled=True)  45.2 us
    ppermute x39, starting transfers between devices, swap(): return lax.ppermute(value, axis, [(i, i ^ mask) for i in range(size)])  43 us
    pallas_call x2, Pallas kernels, weight_grads(): pl.pallas_call(functools.partial(weight_kernel, blocks, calls, count), gr...  37 us
    pallas_call x2, Pallas kernels, expert_rows(): pl.pallas_call(functools.partial(expert_kernel, masks, experts), grid=(1,...  34.6 us
    all_to_all x8, waiting for transfers between devices, spread(): lax.all_to_all(blocks, 'ctx', split_axis=0, concat_axis=0, tiled=True)  32.1 us
    pallas_call x1, Pallas kernels, attend_back(): pl.pallas_call(functools.partial(attend_back_kernel, n_ctx), grid=(kv,),...  24.4 us
    pallas_call x1, Pallas kernels, attend(): pl.pallas_call(functools.partial(attend_kernel, n_ctx), grid=(kv,), out_s...  21.3 us
  transfers between devices with their start and end apart: 47, of which 20 were waited for; matrix products, arithmetic and copies ran while one was open for 12% of the time, Pallas kernels for 29%

profile of v3, /device:TPU:0, one launch (start us, length us, event | category | flops | bytes accessed | tf_op | source)
XLA Modules:
  0.0 540.4 jit_solution(3658694657955720755)
XLA Ops:
  3.1 6.3 %all-to-all-start = ((bf16[4,96,640]{2,1,0:T(8,128)(2,1)}), bf16[4,96,640]{2,1,0:T(8,128)(2,1)S(1)}, u32[]{:S(2)}, u32[]{:S(2)}) async-start(bf16[4,96,640]{2,1,0:T(8,128)(2,1)} %broadcast_in_dim.83), calls=%async_computation | async-start | bytes 983040 | tf_op jit(solution)/shard_map/all_to_all | solution.py:90
  9.6 13.6 %all-to-all-done = bf16[4,96,640]{2,1,0:T(8,128)(2,1)S(1)} async-done(((bf16[4,96,640]{2,1,0:T(8,128)(2,1)}), bf16[4,96,640]{2,1,0:T(8,128)(2,1)S(1)}, u32[]{:S(2)}, u32[]{:S(2)}) %all-to-all-start) | async-done | bytes 491552 | tf_op jit(solution)/shard_map/all_to_all | solution.py:90
  25.1 4.4 all-to-all-start.3
  33.7 1.7 copy.143
  36.3 6.5 %collective-permute-done.refs_5_ = bf16[384,640]{1,0:T(8,128)(2,1)} collective-permute-done((bf16[384,640]{1,0:T(8,128)(2,1)}, bf16[384,640]{1,0:T(8,128)(2,1)}, u32[]{:S(2)}, u32[]{:S(2)}) %collective-permute-start) | collective-permute-done | bytes 491552 | tf_op jit(solution)/shard_map/ppermute | solution.py:52
  45.7 5.0 project_keys.1
  50.7 6.9 %all-to-all-done.3 = bf16[4,96,1536]{2,1,0:T(8,128)(2,1)} async-done(((bf16[4,96,1536]{2,1,0:T(8,128)(2,1)}), bf16[4,96,1536]{2,1,0:T(8,128)(2,1)}, u32[]{:S(2)}, u32[]{:S(2)}) %all-to-all-start.3) | async-done | bytes 1179680 | tf_op jit(solution)/shard_map/all_to_all | solution.py:90
  57.6 2.3 broadcast_in_dim.84
  59.9 3.6 all-to-all-start.1
  64.6 1.6 collective-permute-start.5
  66.2 1.8 pad_maximum_fusion.refs_0_.refs_5_.refs_2_
  68.0 1.5 collective-permute-start.4
  69.6 22.1 %collective-permute-done.5.refs_2_.refs_7_.refs_4_ = bf16[1,3,768,256]{3,2,1,0:T(8,128)(2,1)} collective-permute-done((bf16[1,3,768,256]{3,2,1,0:T(8,128)(2,1)S(1)}, bf16[1,3,768,256]{3,2,1,0:T(8,128)(2,1)}, u32[]{:S(2)}, u32[]{:S(2)}) %collective-permute-start.5) | collective-permute-done | bytes 1179680 | tf_op jit(solution)/shard_map/ppermute | solution.py:52
  95.1 4.8 all-to-all-done.1.refs_3_
  99.9 1.8 broadcast_in_dim.85
  101.8 3.6 all-to-all-start.2
  105.6 12.4 %collective-permute-done.6.refs_5_ = bf16[384,1536]{1,0:T(8,128)(2,1)} collective-permute-done((bf16[384,1536]{1,0:T(8,128)(2,1)}, bf16[384,1536]{1,0:T(8,128)(2,1)}, u32[]{:S(2)}, u32[]{:S(2)}) %collective-permute-start.6) | collective-permute-done | bytes 1179680 | tf_op jit(solution)/shard_map/ppermute | solution.py:52
  118.5 1.5 collective-permute-start.11
  121.1 5.0 project_queries.1
  126.2 21.3 %attend.1 = (bf16[4,1536,1152]{2,1,0:T(8,128)(2,1)}, bf16[768,384]{1,0:T(8,128)(2,1)}, f32[384,1536]{1,0:T(8,128)}, bf16[512,1536]{1,0:T(8,128)(2,1)}, bf16[1536,768]{1,0:T(8,128)(2,1)}) custom-call(s32[2]{0:T(128)} %pad_add_fusion.refs_0_.place, s32[1,384]{1,0:T(1,128)} %reduce_sum.94.refs_1_, bf16[768,384]{1,0:T(8,128)(2,1)} %get-tuple-element.111.refs_2_.refs_1_, ...), custom_call_target="tpu_custom_call" | custom-call | flops 2717908992 | bytes 20971520 | tf_op jit(solution)/shard_map/attend/pallas_call | solution.py:249
  151.0 1.6 collective-permute-start.13
  152.6 2.4 slice.129
  155.0 21.3 %collective-permute-done.17.refs_3_.refs_8_.refs_5_ = bf16[1,3,768,256]{3,2,1,0:T(8,128)(2,1)} collective-permute-done((bf16[1,3,768,256]{3,2,1,0:T(8,128)(2,1)}, bf16[1,3,768,256]{3,2,1,0:T(8,128)(2,1)}, u32[]{:S(2)}, u32[]{:S(2)}) %collective-permute-start.17) | collective-permute-done | bytes 1179680 | tf_op jit(solution)/shard_map/ppermute | solution.py:52
  179.3 2.8 multiply_reduce_fusion.2
  183.3 20.7 %collective-permute-done.18.refs_5_.refs_10_.refs_7_ = bf16[1,3,768,256]{3,2,1,0:T(8,128)(2,1)} collective-permute-done((bf16[1,3,768,256]{3,2,1,0:T(8,128)(2,1)}, bf16[1,3,768,256]{3,2,1,0:T(8,128)(2,1)}, u32[]{:S(2)}, u32[]{:S(2)}) %collective-permute-start.18) | collective-permute-done | bytes 1179680 | tf_op jit(solution)/shard_map/ppermute | solution.py:52
  205.9 2.4 collective-permute-start.15
  211.0 10.4 %back_rows.1.refs_4_ = bf16[4,192,2048]{2,1,0:T(8,128)(2,1)} custom-call(bf16[4,192,1664]{2,1,0:T(8,128)(2,1)} %copy-done.2, bf16[2,3,768,256]{3,2,1,0:T(8,128)(2,1)} %pad_maximum_fusion.refs_0_.refs_5_.refs_2_, bf16[2,3,768,256]{3,2,1,0:T(8,128)(2,1)} %collective-permute-done.4.refs_1_.refs_6_.refs_3_, ...), custom_call_target="tpu_custom_call" | custom-call | flops 1 | bytes 1 | tf_op jit(solution)/shard_map/back_rows/pallas_call | solution.py:516
  221.4 10.2 %collective-permute-done.14.refs_2_.refs_3_ = bf16[192,1536]{1,0:T(8,128)(2,1)S(1)} collective-permute-done((bf16[192,1536]{1,0:T(8,128)(2,1)S(1)}, bf16[192,1536]{1,0:T(8,128)(2,1)S(1)}, u32[]{:S(2)}, u32[]{:S(2)}) %collective-permute-start.14) | collective-permute-done | bytes 589856 | tf_op jit(solution)/shard_map/ppermute | solution.py:52
  232.5 17.6 %expert_rows.2 = (bf16[192,1536]{1,0:T(8,128)(2,1)}, bf16[192,1536]{1,0:T(8,128)(2,1)}, bf16[384,2048]{1,0:T(8,128)(2,1)}, bf16[384,2048]{1,0:T(8,128)(2,1)}, bf16[384,2048]{1,0:T(8,128)(2,1)}) custom-call(s32[2]{0:T(128)} %pad_add_fusion.refs_0_.place, bf16[192,1536]{1,0:T(8,128)(2,1)} %copy-done.10, bf16[192,1536]{1,0:T(8,128)(2,1)} %copy-done.14, ...), custom_call_target="tpu_custom_call" | custom-call | flops 1 | bytes 1 | tf_op jit(solution)/shard_map/expert_rows/pallas_call | solution.py:580
  250.1 17.0 %expert_rows.3 = (bf16[192,1536]{1,0:T(8,128)(2,1)}, bf16[192,1536]{1,0:T(8,128)(2,1)}, bf16[384,2048]{1,0:T(8,128)(2,1)}, bf16[384,2048]{1,0:T(8,128)(2,1)}, bf16[384,2048]{1,0:T(8,128)(2,1)}) custom-call(s32[2]{0:T(128)} %pad_add_fusion.refs_0_.place, bf16[192,1536]{1,0:T(8,128)(2,1)} %collective-permute-done.15.refs_1_.refs_4_, ...), custom_call_target="tpu_custom_call" | custom-call | flops 1 | bytes 1 | tf_op jit(solution)/shard_map/expert_rows/pallas_call | solution.py:580
  267.1 11.2 %collective-permute-start.22 = (bf16[192,1536]{1,0:T(8,128)(2,1)}, bf16[192,1536]{1,0:T(8,128)(2,1)S(1)}, u32[]{:S(2)}, u32[]{:S(2)}) collective-permute-start(bf16[192,1536]{1,0:T(8,128)(2,1)} %get-tuple-element.135), channel_id=1, source_target_pairs={{0,4},{2,6},{4,0},{6,2},{1,5},{3,7},{5,1},{7,3},{8,12},{10,14},{12... | collective-permute-start | bytes 1769480 | tf_op jit(solution)/shard_map/ppermute | solution.py:52
  279.8 18.5 %weight_grads.2 = (bf16[4,3,768,256]{3,2,1,0:T(8,128)(2,1)}, bf16[4,3,768,256]{3,2,1,0:T(8,128)(2,1)}) custom-call(s32[2]{0:T(128)} %pad_add_fusion.refs_0_.place, bf16[4,192,1664]{2,1,0:T(8,128)(2,1)} %copy-done.2, bf16[192,1536]{1,0:T(8,128)(2,1)} %copy-done.10, bf16[192,1536]{1,0:T(8,128)(2,1)} %copy-done.14, ...), custom_call_target="tpu_custom_call" | custom-call | flops 1 | bytes 1 | tf_op jit(solution)/shard_map/weight_grads/pallas_call | solution.py:692
  298.4 10.6 %mix_rows.1 = bf16[4,192,1536]{2,1,0:T(8,128)(2,1)} custom-call(s32[2]{0:T(128)} %pad_add_fusion.refs_0_.place, bf16[384,2048]{1,0:T(8,128)(2,1)} %get-tuple-element.123.refs_6_.refs_0_, bf16[384,2048]{1,0:T(8,128)(2,1)} %get-tuple-element.125.refs_7_.refs_1_, bf16[2,3,768,256]{3,2,1,0:T(8,128)(2,1)} %pad_maximum_fusion.refs_0_.refs_5_.refs_2_, ...), custom_call_target="tpu_custom_call" | custom-call | flops 1 | bytes 1 | tf_op jit(solution)/shard_map/mix_rows/pallas_call | solution.py:628
  308.9 8.7 %collective-permute-done.22 = bf16[192,1536]{1,0:T(8,128)(2,1)S(1)} collective-permute-done((bf16[192,1536]{1,0:T(8,128)(2,1)}, bf16[192,1536]{1,0:T(8,128)(2,1)S(1)}, u32[]{:S(2)}, u32[]{:S(2)}) %collective-permute-start.22) | collective-permute-done | bytes 589856 | tf_op jit(solution)/shard_map/ppermute | solution.py:52
  318.9 1.8 fusion.19
  320.8 1.5 collective-permute-start.24
  322.3 13.3 %all-to-all-start.4 = ((bf16[4,192,1536]{2,1,0:T(8,128)(2,1)}), bf16[4,192,1536]{2,1,0:T(8,128)(2,1)}, u32[]{:S(2)}, u32[]{:S(2)}) async-start(bf16[4,192,1536]{2,1,0:T(8,128)(2,1)} %mix_rows.1), calls=%async_computation.4 | async-start | bytes 4718592 | tf_op jit(solution)/shard_map/all_to_all | solution.py:90
  335.6 18.5 %weight_grads.3 = (bf16[4,3,768,256]{3,2,1,0:T(8,128)(2,1)}, bf16[4,3,768,256]{3,2,1,0:T(8,128)(2,1)}) custom-call(s32[2]{0:T(128)} %pad_add_fusion.refs_0_.place, bf16[4,192,1664]{2,1,0:T(8,128)(2,1)} %copy-done.2, bf16[192,1536]{1,0:T(8,128)(2,1)} %copy-done.10, bf16[192,1536]{1,0:T(8,128)(2,1)} %copy-done.14, ...), custom_call_target="tpu_custom_call" | custom-call | flops 1 | bytes 1 | tf_op jit(solution)/shard_map/weight_grads/pallas_call | solution.py:692
  357.0 4.4 add_convert_fusion
  363.4 24.4 %attend_back.1 = (bf16[768,384]{1,0:T(8,128)(2,1)}, bf16[4,512,384]{2,1,0:T(8,128)(2,1)}) custom-call(bf16[4,1536,1152]{2,1,0:T(8,128)(2,1)} %get-tuple-element.138.refs_0_, bf16[768,384]{1,0:T(8,128)(2,1)} %get-tuple-element.111.refs_2_.refs_1_, bf16[512,1536]{1,0:T(8,128)(2,1)} %get-tuple-element.139.refs_2_, ...), custom_call_target="tpu_custom_call" | custom-call | flops 4529848320 | bytes 20971520 | tf_op jit(solution)/shard_map/attend_back/pallas_call | solution.py:323
  387.9 2.9 all-to-all-done.4
  390.8 3.1 convert_reduce_fusion
  393.9 7.7 %query_grads.1 = (bf16[384,1536]{1,0:T(8,128)(2,1)}, bf16[384,1536]{1,0:T(8,128)(2,1)}, bf16[2,384,1536]{2,1,0:T(8,128)(2,1)}, f32[384,1536]{1,0:T(8,128)}) custom-call(s32[2]{0:T(128)} %pad_add_fusion.refs_0_.place, bf16[768,384]{1,0:T(8,128)(2,1)} %get-tuple-element.146.dq_ref, bf16[1536,384]{1,0:T(8,128)(2,1)} %get-tuple-element.148.norm_t.refs_4_, ...), custom_call_target="tpu_custom_call" | custom-call | flops 1 | bytes 1 | tf_op jit(solution)/shard_map/query_grads/pallas_call | solution.py:376
  401.6 4.3 all-to-all-start.5
  406.0 9.3 %collective-permute-done.29.refs_2_ = bf16[2,3,768,256]{3,2,1,0:T(8,128)(2,1)S(1)} collective-permute-done((bf16[2,3,768,256]{3,2,1,0:T(8,128)(2,1)}, bf16[2,3,768,256]{3,2,1,0:T(8,128)(2,1)S(1)}, u32[]{:S(2)}, u32[]{:S(2)}) %collective-permute-start.29) | collective-permute-done | bytes 2359328 | tf_op jit(solution)/shard_map/ppermute | solution.py:52
  415.6 5.1 fusion.11
  420.8 1.6 fusion
  422.5 1.6 collective-permute-start.31
  425.7 24.5 %collective-permute-done.31 = bf16[384,1536]{1,0:T(8,128)(2,1)S(1)} collective-permute-done((bf16[384,1536]{1,0:T(8,128)(2,1)S(1)}, bf16[384,1536]{1,0:T(8,128)(2,1)S(1)}, u32[]{:S(2)}, u32[]{:S(2)}) %collective-permute-start.31) | collective-permute-done | bytes 1179680 | tf_op jit(solution)/shard_map/ppermute | solution.py:52
  450.3 2.8 add_convert_fusion.2
  453.1 6.7 %key_grads.1 = (bf16[384,640]{1,0:T(8,128)(2,1)}, bf16[384,640]{1,0:T(8,128)(2,1)}, bf16[2,384,640]{2,1,0:T(8,128)(2,1)}, f32[384,1536]{1,0:T(8,128)}) custom-call(s32[2]{0:T(128)} %pad_add_fusion.refs_0_.place, bf16[4,512,384]{2,1,0:T(8,128)(2,1)} %all-to-all-done.5.refs_1_, f32[32,384]{1,0:T(8,128)} %get-tuple-element.304.refs_2_.refs_5_, ...), custom_call_target="tpu_custom_call" | custom-call | flops 1 | bytes 1 | tf_op jit(solution)/shard_map/key_grads/pallas_call | solution.py:427
  460.0 5.1 all-to-all-start.6
  465.1 2.1 copy.145
  467.3 2.1 copy.151
  472.7 1.6 collective-permute-start.34
  477.2 9.8 %collective-permute-done.35 = bf16[192,1536]{1,0:T(8,128)(2,1)S(1)} collective-permute-done((bf16[192,1536]{1,0:T(8,128)(2,1)S(1)}, bf16[192,1536]{1,0:T(8,128)(2,1)S(1)}, u32[]{:S(2)}, u32[]{:S(2)}) %collective-permute-start.35) | collective-permute-done | bytes 589856 | tf_op jit(solution)/shard_map/ppermute | solution.py:52
  488.3 2.0 add_convert_fusion.6
  490.3 4.0 all-to-all-done.6
  495.3 4.4 all-to-all-start.7
  499.8 1.7 fusion.8
  502.2 9.0 %collective-permute-done.38 = bf16[3,768,256]{2,1,0:T(8,128)(2,1)} collective-permute-done((bf16[3,768,256]{2,1,0:T(8,128)(2,1)}, bf16[3,768,256]{2,1,0:T(8,128)(2,1)}, u32[]{:S(2)}, u32[]{:S(2)}) %collective-permute-start.38) | collective-permute-done | bytes 1179680 | tf_op jit(solution)/shard_map/ppermute | solution.py:52
  511.2 5.6 %step_down.1 = (f32[1,256,1536]{2,1,0:T(8,128)}, f32[1,256,1536]{2,1,0:T(8,128)}, f32[1,256,1536]{2,1,0:T(8,128)}) custom-call(bf16[4,3,768,256]{3,2,1,0:T(8,128)(2,1)} %get-tuple-element.154.refs_0_.refs_4_, bf16[4,3,768,256]{3,2,1,0:T(8,128)(2,1)} %collective-permute-done.28.refs_1_.refs_5_, bf16[2,3,768,256]{3,2,1,0:T(8,128)(2,1)} %copy-done.8, ...), custom_call_target="tpu_custom_call" | custom-call | flops 1 | bytes 1 | tf_op jit(solution)/shard_map/step_down/pallas_call | solution.py:782
  516.8 10.1 %step_in.1 = (f32[1,2,1536,256]{3,2,1,0:T(8,128)}, f32[1,2,1536,256]{3,2,1,0:T(8,128)}, f32[1,2,1536,256]{3,2,1,0:T(8,128)}) custom-call(bf16[4,3,768,256]{3,2,1,0:T(8,128)(2,1)} %get-tuple-element.154.refs_0_.refs_4_, bf16[4,3,768,256]{3,2,1,0:T(8,128)(2,1)} %collective-permute-done.28.refs_1_.refs_5_, bf16[2,3,768,256]{3,2,1,0:T(8,128)(2,1)} %copy-done.8, ...), custom_call_target="tpu_custom_call" | custom-call | flops 1 | bytes 1 | tf_op jit(solution)/shard_map/step_in/pallas_call | solution.py:741
  535.0 1.6 pad_maximum_fusion.2
  (230 shorter events, 62.8 us)
Async XLA Ops:
  0.7 92.5 %copy-start = (f32[384,8]{0,1:T(8,128)S(1)}, f32[384,8]{0,1:T(8,128)}, u32[]{:S(2)}) copy-start(f32[384,8]{0,1:T(8,128)} %param.24) | copy-start | bytes 36868
  2.2 7.3 %copy-start.31 = (f32[768,96]{0,1:T(8,128)S(1)}, f32[768,96]{0,1:T(8,128)}, u32[]{:S(2)}) copy-start(f32[768,96]{0,1:T(8,128)} %param.26) | copy-start | bytes 884740
  3.1 20.1 %all-to-all-start = ((bf16[4,96,640]{2,1,0:T(8,128)(2,1)}), bf16[4,96,640]{2,1,0:T(8,128)(2,1)S(1)}, u32[]{:S(2)}, u32[]{:S(2)}) async-start(bf16[4,96,640]{2,1,0:T(8,128)(2,1)} %broadcast_in_dim.83), calls=%async_computation | async-start | bytes 983040 | tf_op jit(solution)/shard_map/all_to_all | solution.py:90
  24.0 8.5 %copy-start.9 = (f32[1,2,1536,256]{3,2,1,0:T(8,128)S(1)}, f32[1,2,1536,256]{3,2,1,0:T(8,128)}, u32[]{:S(2)}) copy-start(f32[1,2,1536,256]{3,2,1,0:T(8,128)} %refs_8_) | copy-start | bytes 9437188
  25.1 32.5 %all-to-all-start.3 = ((bf16[4,96,1536]{2,1,0:T(8,128)(2,1)}), bf16[4,96,1536]{2,1,0:T(8,128)(2,1)}, u32[]{:S(2)}, u32[]{:S(2)}) async-start(bf16[4,96,1536]{2,1,0:T(8,128)(2,1)} %broadcast_in_dim.87), calls=%async_computation.3 | async-start | bytes 2359296 | tf_op jit(solution)/shard_map/all_to_all | solution.py:90
  30.3 12.5 %collective-permute-start = (bf16[384,640]{1,0:T(8,128)(2,1)}, bf16[384,640]{1,0:T(8,128)(2,1)}, u32[]{:S(2)}, u32[]{:S(2)}) collective-permute-start(bf16[384,640]{1,0:T(8,128)(2,1)} %bitcast.89), channel_id=1, source_target_pairs={{0,16},{8,24},{16,0},{24,8},{1,17},{9,25},{17,1},{25,9},{2,18},{10... | collective-permute-start | bytes 1474568 | tf_op jit(solution)/shard_map/ppermute | solution.py:52
  35.5 7.4 %copy-start.47 = (f32[32]{0:T(128)S(1)}, f32[32]{0:T(128)}, u32[]{:S(2)}) copy-start(f32[32]{0:T(128)} %multiply_exponential_fusion) | copy-start | bytes 388
  35.5 8.3 %copy-start.11 = (bf16[1,2,1536,256]{3,2,1,0:T(8,128)(2,1)S(1)}, bf16[1,2,1536,256]{3,2,1,0:T(8,128)(2,1)}, u32[]{:S(2)}) copy-start(bf16[1,2,1536,256]{3,2,1,0:T(8,128)(2,1)} %convert.22) | copy-start | bytes 4718596
  36.3 7.6 %collective-permute-start.1 = (bf16[384,640]{1,0:T(8,128)(2,1)S(1)}, bf16[384,640]{1,0:T(8,128)(2,1)S(1)}, u32[]{:S(2)}, u32[]{:S(2)}) collective-permute-start(bf16[384,640]{1,0:T(8,128)(2,1)S(1)} %bitcast.91), channel_id=1, source_target_pairs={{0,8},{8,0},{16,24},{24,16},{1,9},{9,1},{17,25},{25,17},{2,10},{10... | collective-permute-start | bytes 1474568 | tf_op jit(solution)/shard_map/ppermute | solution.py:52
  42.8 2.1 collective-permute-start.2
  59.9 40.0 %all-to-all-start.1 = ((bf16[4,512,384]{2,1,0:T(8,128)(2,1)}), bf16[4,512,384]{2,1,0:T(8,128)(2,1)S(1)}, u32[]{:S(2)}, u32[]{:S(2)}) async-start(bf16[4,512,384]{2,1,0:T(8,128)(2,1)} %broadcast_in_dim.84), calls=%async_computation.1 | async-start | bytes 3145728 | tf_op jit(solution)/shard_map/all_to_all | solution.py:90
  64.6 27.1 %collective-permute-start.5 = (bf16[1,3,768,256]{3,2,1,0:T(8,128)(2,1)S(1)}, bf16[1,3,768,256]{3,2,1,0:T(8,128)(2,1)}, u32[]{:S(2)}, u32[]{:S(2)}) collective-permute-start(bf16[1,3,768,256]{3,2,1,0:T(8,128)(2,1)S(1)} %maximum_bitcast_fusion), channel_id=1, source_target_pairs={{0,16},{8,24},{16,0},{24,8},{1,17},{9,25},{17,1},{25,9},{2,18},{10... | collective-permute-start | bytes 3538952 | tf_op jit(solution)/shard_map/ppermute | solution.py:52
  66.2 27.0 %copy-start.42 = (s32[384,8]{0,1:T(8,128)S(1)}, s32[384,8]{0,1:T(8,128)}, u32[]{:S(2)}) copy-start(s32[384,8]{0,1:T(8,128)} %param.23) | copy-start | bytes 36868
  68.0 52.2 %collective-permute-start.4 = (bf16[2,3,768,256]{3,2,1,0:T(8,128)(2,1)}, bf16[2,3,768,256]{3,2,1,0:T(8,128)(2,1)}, u32[]{:S(2)}, u32[]{:S(2)}) collective-permute-start(bf16[2,3,768,256]{3,2,1,0:T(8,128)(2,1)} %pad_maximum_fusion.refs_0_.refs_5_.refs_2_), channel_id=1, source_target_pairs={{0,1},{1,0},{2,3},{3,2},{4,5},{5,4},{6,7},{7,6},{8,9},{9,8},{10,11... | collective-permute-start | bytes 7077896 | tf_op jit(solution)/shard_map/ppermute | solution.py:52
  69.6 50.7 %collective-permute-start.3 = (bf16[2,3,768,256]{3,2,1,0:T(8,128)(2,1)}, bf16[2,3,768,256]{3,2,1,0:T(8,128)(2,1)}, u32[]{:S(2)}, u32[]{:S(2)}) collective-permute-start(bf16[2,3,768,256]{3,2,1,0:T(8,128)(2,1)} %pad_maximum_fusion.refs_0_.refs_5_.refs_2_), channel_id=1, source_target_pairs={{0,8},{8,0},{16,24},{24,16},{1,9},{9,1},{17,25},{25,17},{2,10},{10... | collective-permute-start | bytes 7077896 | tf_op jit(solution)/shard_map/ppermute | solution.py:52
  91.6 26.3 %collective-permute-start.6 = (bf16[384,1536]{1,0:T(8,128)(2,1)}, bf16[384,1536]{1,0:T(8,128)(2,1)}, u32[]{:S(2)}, u32[]{:S(2)}) collective-permute-start(bf16[384,1536]{1,0:T(8,128)(2,1)} %bitcast.21.refs_4_), channel_id=1, source_target_pairs={{0,16},{8,24},{16,0},{24,8},{1,17},{9,25},{17,1},{25,9},{2,18},{10... | collective-permute-start | bytes 3538952 | tf_op jit(solution)/shard_map/ppermute | solution.py:52
  101.8 77.4 %all-to-all-start.2 = ((bf16[4,192,1664]{2,1,0:T(8,128)(2,1)}), bf16[4,192,1664]{2,1,0:T(8,128)(2,1)S(1)}, u32[]{:S(2)}, u32[]{:S(2)}) async-start(bf16[4,192,1664]{2,1,0:T(8,128)(2,1)} %broadcast_in_dim.85), calls=%async_computation.2 | async-start | bytes 5111808 | tf_op jit(solution)/shard_map/all_to_all | solution.py:90
  105.5 14.8 %collective-permute-start.7 = (bf16[384,1536]{1,0:T(8,128)(2,1)}, bf16[384,1536]{1,0:T(8,128)(2,1)}, u32[]{:S(2)}, u32[]{:S(2)}) collective-permute-start(bf16[384,1536]{1,0:T(8,128)(2,1)} %bitcast.21.refs_4_), channel_id=1, source_target_pairs={{0,8},{8,0},{16,24},{24,16},{1,9},{9,1},{17,25},{25,17},{2,10},{10... | collective-permute-start | bytes 3538952 | tf_op jit(solution)/shard_map/ppermute | solution.py:52
  118.0 3.2 collective-permute-start.8
  118.5 30.6 %collective-permute-start.11 = (bf16[1,3,768,256]{3,2,1,0:T(8,128)(2,1)}, bf16[1,3,768,256]{3,2,1,0:T(8,128)(2,1)}, u32[]{:S(2)}, u32[]{:S(2)}) collective-permute-start(bf16[1,3,768,256]{3,2,1,0:T(8,128)(2,1)} %collective-permute-done.5.refs_2_.refs_7_.refs_4_), channel_id=1, source_target_pairs={{0,1},{1,0},{2,3},{3,2},{4,5},{5,4},{6,7},{7,6},{8,9},{9,8},{10,11... | collective-permute-start | bytes 3538952 | tf_op jit(solution)/shard_map/ppermute | solution.py:52
  147.5 31.8 %collective-permute-start.9 = (bf16[2,3,768,256]{3,2,1,0:T(8,128)(2,1)}, bf16[2,3,768,256]{3,2,1,0:T(8,128)(2,1)}, u32[]{:S(2)}, u32[]{:S(2)}) collective-permute-start(bf16[2,3,768,256]{3,2,1,0:T(8,128)(2,1)} %collective-permute-done.4.refs_1_.refs_6_.refs_3_), channel_id=1, source_target_pairs={{0,8},{8,0},{16,24},{24,16},{1,9},{9,1},{17,25},{25,17},{2,10},{10... | collective-permute-start | bytes 7077896 | tf_op jit(solution)/shard_map/ppermute | solution.py:52
  147.6 28.6 %collective-permute-start.17 = (bf16[1,3,768,256]{3,2,1,0:T(8,128)(2,1)}, bf16[1,3,768,256]{3,2,1,0:T(8,128)(2,1)}, u32[]{:S(2)}, u32[]{:S(2)}) collective-permute-start(bf16[1,3,768,256]{3,2,1,0:T(8,128)(2,1)} %copy-done.17), channel_id=1, source_target_pairs={{0,16},{8,24},{16,0},{24,8},{1,17},{9,25},{17,1},{25,9},{2,18},{10... | collective-permute-start | bytes 3538952 | tf_op jit(solution)/shard_map/ppermute | solution.py:52
  149.2 30.0 %collective-permute-start.12 = (bf16[1,3,768,256]{3,2,1,0:T(8,128)(2,1)}, bf16[1,3,768,256]{3,2,1,0:T(8,128)(2,1)}, u32[]{:S(2)}, u32[]{:S(2)}) collective-permute-start(bf16[1,3,768,256]{3,2,1,0:T(8,128)(2,1)} %collective-permute-done.11.refs_4_.refs_9_.refs_6_), channel_id=1, source_target_pairs={{0,8},{8,0},{16,24},{24,16},{1,9},{9,1},{17,25},{25,17},{2,10},{10... | collective-permute-start | bytes 3538952 | tf_op jit(solution)/shard_map/ppermute | solution.py:52
  149.2 30.0 %collective-permute-start.10 = (bf16[1,3,768,256]{3,2,1,0:T(8,128)(2,1)}, bf16[1,3,768,256]{3,2,1,0:T(8,128)(2,1)}, u32[]{:S(2)}, u32[]{:S(2)}) collective-permute-start(bf16[1,3,768,256]{3,2,1,0:T(8,128)(2,1)} %collective-permute-done.5.refs_2_.refs_7_.refs_4_), channel_id=1, source_target_pairs={{0,8},{8,0},{16,24},{24,16},{1,9},{9,1},{17,25},{25,17},{2,10},{10... | collective-permute-start | bytes 3538952 | tf_op jit(solution)/shard_map/ppermute | solution.py:52
  151.0 28.2 %collective-permute-start.13 = (bf16[192,1536]{1,0:T(8,128)(2,1)S(1)}, bf16[192,1536]{1,0:T(8,128)(2,1)}, u32[]{:S(2)}, u32[]{:S(2)}) collective-permute-start(bf16[192,1536]{1,0:T(8,128)(2,1)S(1)} %dynamic-slice_convert_fusion.1), channel_id=1, source_target_pairs={{0,1},{1,0},{2,3},{3,2},{4,5},{5,4},{6,7},{7,6},{8,9},{9,8},{10,11... | collective-permute-start | bytes 1769480 | tf_op jit(solution)/shard_map/ppermute | solution.py:52
  176.2 27.8 %collective-permute-start.18 = (bf16[1,3,768,256]{3,2,1,0:T(8,128)(2,1)}, bf16[1,3,768,256]{3,2,1,0:T(8,128)(2,1)}, u32[]{:S(2)}, u32[]{:S(2)}) collective-permute-start(bf16[1,3,768,256]{3,2,1,0:T(8,128)(2,1)} %slice.129), channel_id=1, source_target_pairs={{0,16},{8,24},{16,0},{24,8},{1,17},{9,25},{17,1},{25,9},{2,18},{10... | collective-permute-start | bytes 3538952 | tf_op jit(solution)/shard_map/ppermute | solution.py:52
  183.3 38.1 %copy-start.10 = (bf16[192,1536]{1,0:T(8,128)(2,1)}, bf16[192,1536]{1,0:T(8,128)(2,1)S(1)}, u32[]{:S(2)}) copy-start(bf16[192,1536]{1,0:T(8,128)(2,1)S(1)} %multiply_convert_fusion.refs_1_.refs_2_) | copy-start | bytes 1769476
  204.0 4.9 collective-permute-start.20
  204.0 4.9 collective-permute-start.19
  204.5 27.2 %collective-permute-start.14 = (bf16[192,1536]{1,0:T(8,128)(2,1)S(1)}, bf16[192,1536]{1,0:T(8,128)(2,1)S(1)}, u32[]{:S(2)}, u32[]{:S(2)}) collective-permute-start(bf16[192,1536]{1,0:T(8,128)(2,1)S(1)} %multiply_convert_fusion.refs_1_.refs_2_), channel_id=1, source_target_pairs={{0,2},{2,0},{4,6},{6,4},{1,3},{3,1},{5,7},{7,5},{8,10},{10,8},{12,... | collective-permute-start | bytes 1769480 | tf_op jit(solution)/shard_map/ppermute | solution.py:52
  205.9 44.2 %collective-permute-start.15 = (bf16[192,1536]{1,0:T(8,128)(2,1)S(1)}, bf16[192,1536]{1,0:T(8,128)(2,1)}, u32[]{:S(2)}, u32[]{:S(2)}) collective-permute-start(bf16[192,1536]{1,0:T(8,128)(2,1)S(1)} %multiply_convert_fusion.refs_1_.refs_2_), channel_id=1, source_target_pairs={{0,4},{2,6},{4,0},{6,2},{1,5},{3,7},{5,1},{7,3},{8,12},{10,14},{12... | collective-permute-start | bytes 1769480 | tf_op jit(solution)/shard_map/ppermute | solution.py:52
  208.3 41.8 %collective-permute-start.16 = (bf16[192,1536]{1,0:T(8,128)(2,1)S(1)}, bf16[192,1536]{1,0:T(8,128)(2,1)}, u32[]{:S(2)}, u32[]{:S(2)}) collective-permute-start(bf16[192,1536]{1,0:T(8,128)(2,1)S(1)} %multiply_convert_fusion.refs_1_.refs_2_), channel_id=1, source_target_pairs={{0,6},{2,4},{4,2},{6,0},{1,7},{3,5},{5,3},{7,1},{8,14},{10,12},{12... | collective-permute-start | bytes 1769480 | tf_op jit(solution)/shard_map/ppermute | solution.py:52
  267.1 50.5 %collective-permute-start.22 = (bf16[192,1536]{1,0:T(8,128)(2,1)}, bf16[192,1536]{1,0:T(8,128)(2,1)S(1)}, u32[]{:S(2)}, u32[]{:S(2)}) collective-permute-start(bf16[192,1536]{1,0:T(8,128)(2,1)} %get-tuple-element.135), channel_id=1, source_target_pairs={{0,4},{2,6},{4,0},{6,2},{1,5},{3,7},{5,1},{7,3},{8,12},{10,14},{12... | collective-permute-start | bytes 1769480 | tf_op jit(solution)/shard_map/ppermute | solution.py:52
  278.4 39.2 %collective-permute-start.23 = (bf16[192,1536]{1,0:T(8,128)(2,1)}, bf16[192,1536]{1,0:T(8,128)(2,1)S(1)}, u32[]{:S(2)}, u32[]{:S(2)}) collective-permute-start(bf16[192,1536]{1,0:T(8,128)(2,1)} %get-tuple-element.136), channel_id=1, source_target_pairs={{0,6},{2,4},{4,2},{6,0},{1,7},{3,5},{5,3},{7,1},{8,14},{10,12},{12... | collective-permute-start | bytes 1769480 | tf_op jit(solution)/shard_map/ppermute | solution.py:52
  279.8 37.8 %collective-permute-start.21 = (bf16[192,1536]{1,0:T(8,128)(2,1)}, bf16[192,1536]{1,0:T(8,128)(2,1)S(1)}, u32[]{:S(2)}, u32[]{:S(2)}) collective-permute-start(bf16[192,1536]{1,0:T(8,128)(2,1)} %get-tuple-element.134), channel_id=1, source_target_pairs={{0,2},{2,0},{4,6},{6,4},{1,3},{3,1},{5,7},{7,5},{8,10},{10,8},{12,... | collective-permute-start | bytes 1769480 | tf_op jit(solution)/shard_map/ppermute | solution.py:52
  298.3 19.3 %copy-start.4 = (f32[192,1536]{1,0:T(8,128)S(1)}, f32[192,1536]{1,0:T(8,128)}, u32[]{:S(2)}) copy-start(f32[192,1536]{1,0:T(8,128)} %copy-done.3) | copy-start | bytes 3538948
  298.3 19.3 %copy-start.23 = (bf16[192,1536]{1,0:T(8,128)(2,1)S(1)}, bf16[192,1536]{1,0:T(8,128)(2,1)}, u32[]{:S(2)}) copy-start(bf16[192,1536]{1,0:T(8,128)(2,1)} %get-tuple-element.133) | copy-start | bytes 1769476
  317.6 38.9 %collective-permute-start.25 = (bf16[4,3,768,256]{3,2,1,0:T(8,128)(2,1)}, bf16[4,3,768,256]{3,2,1,0:T(8,128)(2,1)}, u32[]{:S(2)}, u32[]{:S(2)}) collective-permute-start(bf16[4,3,768,256]{3,2,1,0:T(8,128)(2,1)} %get-tuple-element.142), channel_id=1, source_target_pairs={{0,8},{8,0},{16,24},{24,16},{1,9},{9,1},{17,25},{25,17},{2,10},{10... | collective-permute-start | bytes 14155784 | tf_op jit(solution)/shard_map/ppermute | solution.py:52
  320.8 33.3 %collective-permute-start.24 = (bf16[192,1536]{1,0:T(8,128)(2,1)}, bf16[192,1536]{1,0:T(8,128)(2,1)S(1)}, u32[]{:S(2)}, u32[]{:S(2)}) collective-permute-start(bf16[192,1536]{1,0:T(8,128)(2,1)} %get-tuple-element.280), channel_id=1, source_target_pairs={{0,1},{1,0},{2,3},{3,2},{4,5},{5,4},{6,7},{7,6},{8,9},{9,8},{10,11... | collective-permute-start | bytes 1769480 | tf_op jit(solution)/shard_map/ppermute | solution.py:52
  322.3 68.5 %all-to-all-start.4 = ((bf16[4,192,1536]{2,1,0:T(8,128)(2,1)}), bf16[4,192,1536]{2,1,0:T(8,128)(2,1)}, u32[]{:S(2)}, u32[]{:S(2)}) async-start(bf16[4,192,1536]{2,1,0:T(8,128)(2,1)} %mix_rows.1), calls=%async_computation.4 | async-start | bytes 4718592 | tf_op jit(solution)/shard_map/all_to_all | solution.py:90
  361.4 54.2 %collective-permute-start.28 = (bf16[4,3,768,256]{3,2,1,0:T(8,128)(2,1)}, bf16[4,3,768,256]{3,2,1,0:T(8,128)(2,1)}, u32[]{:S(2)}, u32[]{:S(2)}) collective-permute-start(bf16[4,3,768,256]{3,2,1,0:T(8,128)(2,1)} %get-tuple-element.156), channel_id=1, source_target_pairs={{0,8},{8,0},{16,24},{24,16},{1,9},{9,1},{17,25},{25,17},{2,10},{10... | collective-permute-start | bytes 14155784 | tf_op jit(solution)/shard_map/ppermute | solution.py:52
  361.4 53.9 %collective-permute-start.29 = (bf16[2,3,768,256]{3,2,1,0:T(8,128)(2,1)}, bf16[2,3,768,256]{3,2,1,0:T(8,128)(2,1)S(1)}, u32[]{:S(2)}, u32[]{:S(2)}) collective-permute-start(bf16[2,3,768,256]{3,2,1,0:T(8,128)(2,1)} %get-tuple-element.286), channel_id=1, source_target_pairs={{0,1},{1,0},{2,3},{3,2},{4,5},{5,4},{6,7},{7,6},{8,9},{9,8},{10,11... | collective-permute-start | bytes 7077896 | tf_op jit(solution)/shard_map/ppermute | solution.py:52
  361.9 53.7 %collective-permute-start.30 = (bf16[2,3,768,256]{3,2,1,0:T(8,128)(2,1)}, bf16[2,3,768,256]{3,2,1,0:T(8,128)(2,1)}, u32[]{:S(2)}, u32[]{:S(2)}) collective-permute-start(bf16[2,3,768,256]{3,2,1,0:T(8,128)(2,1)} %get-tuple-element.287), channel_id=1, source_target_pairs={{0,16},{8,24},{16,0},{24,8},{1,17},{9,25},{17,1},{25,9},{2,18},{10... | collective-permute-start | bytes 7077896 | tf_op jit(solution)/shard_map/ppermute | solution.py:52
  401.6 19.2 %collective-permute-start.27 = (bf16[2,384,1536]{2,1,0:T(8,128)(2,1)}, bf16[2,384,1536]{2,1,0:T(8,128)(2,1)}, u32[]{:S(2)}, u32[]{:S(2)}) collective-permute-start(bf16[2,384,1536]{2,1,0:T(8,128)(2,1)} %get-tuple-element.153), channel_id=1, source_target_pairs={{0,8},{8,0},{16,24},{24,16},{1,9},{9,1},{17,25},{25,17},{2,10},{10... | collective-permute-start | bytes 7077896 | tf_op jit(solution)/shard_map/ppermute | solution.py:52
  401.6 51.5 %all-to-all-start.5 = ((bf16[4,512,384]{2,1,0:T(8,128)(2,1)}), bf16[4,512,384]{2,1,0:T(8,128)(2,1)}, u32[]{:S(2)}, u32[]{:S(2)}) async-start(bf16[4,512,384]{2,1,0:T(8,128)(2,1)} %get-tuple-element.163), calls=%async_computation.5 | async-start | bytes 3145728 | tf_op jit(solution)/shard_map/all_to_all | solution.py:90
  415.3 5.5 %copy-start.8 = (bf16[2,3,768,256]{3,2,1,0:T(8,128)(2,1)}, bf16[2,3,768,256]{3,2,1,0:T(8,128)(2,1)S(1)}, u32[]{:S(2)}) copy-start(bf16[2,3,768,256]{3,2,1,0:T(8,128)(2,1)S(1)} %collective-permute-done.29.refs_2_) | copy-start | bytes 7077892
  420.8 29.5 %copy-start.33 = (bf16[384,1536]{1,0:T(8,128)(2,1)S(1)}, bf16[384,1536]{1,0:T(8,128)(2,1)}, u32[]{:S(2)}) copy-start(bf16[384,1536]{1,0:T(8,128)(2,1)} %get-tuple-element.152) | copy-start | bytes 3538948
  422.5 27.8 %collective-permute-start.31 = (bf16[384,1536]{1,0:T(8,128)(2,1)S(1)}, bf16[384,1536]{1,0:T(8,128)(2,1)S(1)}, u32[]{:S(2)}, u32[]{:S(2)}) collective-permute-start(bf16[384,1536]{1,0:T(8,128)(2,1)S(1)} %fusion), channel_id=1, source_target_pairs={{0,16},{8,24},{16,0},{24,8},{1,17},{9,25},{17,1},{25,9},{2,18},{10... | collective-permute-start | bytes 3538952 | tf_op jit(solution)/shard_map/ppermute | solution.py:52
  424.0 29.1 %collective-permute-start.32 = (bf16[3,768,256]{2,1,0:T(8,128)(2,1)S(1)}, bf16[3,768,256]{2,1,0:T(8,128)(2,1)}, u32[]{:S(2)}, u32[]{:S(2)}) collective-permute-start(bf16[3,768,256]{2,1,0:T(8,128)(2,1)S(1)} %get-tuple-element.284), channel_id=1, source_target_pairs={{0,1},{1,0},{2,3},{3,2},{4,5},{5,4},{6,7},{7,6},{8,9},{9,8},{10,11... | collective-permute-start | bytes 3538952 | tf_op jit(solution)/shard_map/ppermute | solution.py:52
  453.1 6.7 %copy-start.7 = (bf16[384,1536]{1,0:T(8,128)(2,1)S(1)}, bf16[384,1536]{1,0:T(8,128)(2,1)}, u32[]{:S(2)}) copy-start(bf16[384,1536]{1,0:T(8,128)(2,1)} %refs_6_.1) | copy-start | bytes 3538948
  459.8 11.7 %collective-permute-start.33 = (bf16[2,384,640]{2,1,0:T(8,128)(2,1)}, bf16[2,384,640]{2,1,0:T(8,128)(2,1)}, u32[]{:S(2)}, u32[]{:S(2)}) collective-permute-start(bf16[2,384,640]{2,1,0:T(8,128)(2,1)} %get-tuple-element.166), channel_id=1, source_target_pairs={{0,8},{8,0},{16,24},{24,16},{1,9},{9,1},{17,25},{25,17},{2,10},{10... | collective-permute-start | bytes 2949128 | tf_op jit(solution)/shard_map/ppermute | solution.py:52
  460.0 34.3 %all-to-all-start.6 = ((bf16[4,96,1536]{2,1,0:T(8,128)(2,1)}), bf16[4,96,1536]{2,1,0:T(8,128)(2,1)S(1)}, u32[]{:S(2)}, u32[]{:S(2)}) async-start(bf16[4,96,1536]{2,1,0:T(8,128)(2,1)} %bitcast.87), calls=%async_computation.6 | async-start | bytes 2359296 | tf_op jit(solution)/shard_map/all_to_all | solution.py:90
  470.8 16.2 %collective-permute-start.35 = (bf16[192,1536]{1,0:T(8,128)(2,1)S(1)}, bf16[192,1536]{1,0:T(8,128)(2,1)S(1)}, u32[]{:S(2)}, u32[]{:S(2)}) collective-permute-start(bf16[192,1536]{1,0:T(8,128)(2,1)S(1)} %dynamic-slice_convert_fusion), channel_id=1, source_target_pairs={{0,1},{1,0},{2,3},{3,2},{4,5},{5,4},{6,7},{7,6},{8,9},{9,8},{10,11... | collective-permute-start | bytes 1769480 | tf_op jit(solution)/shard_map/ppermute | solution.py:52
  472.7 14.4 %copy-start.19 = (f32[384,1536]{1,0:T(8,128)S(1)}, f32[384,1536]{1,0:T(8,128)}, u32[]{:S(2)}) copy-start(f32[384,1536]{1,0:T(8,128)} %get-tuple-element.171) | copy-start | bytes 7077892
  472.7 14.4 %copy-start.40 = (f32[1536]{0:T(1024)S(1)}, f32[1536]{0:T(1024)}, u32[]{:S(2)}) copy-start(f32[1536]{0:T(1024)} %get-tuple-element.270) | copy-start | bytes 18436
  472.7 15.2 %collective-permute-start.34 = (bf16[384,640]{1,0:T(8,128)(2,1)S(1)}, bf16[384,640]{1,0:T(8,128)(2,1)S(1)}, u32[]{:S(2)}, u32[]{:S(2)}) collective-permute-start(bf16[384,640]{1,0:T(8,128)(2,1)S(1)} %fusion.12), channel_id=1, source_target_pairs={{0,16},{8,24},{16,0},{24,8},{1,17},{9,25},{17,1},{25,9},{2,18},{10... | collective-permute-start | bytes 1474568 | tf_op jit(solution)/shard_map/ppermute | solution.py:52
  475.3 56.7 %collective-permute-start.26 = (bf16[192,1536]{1,0:T(8,128)(2,1)}, bf16[192,1536]{1,0:T(8,128)(2,1)}, u32[]{:S(2)}, u32[]{:S(2)}) collective-permute-start(bf16[192,1536]{1,0:T(8,128)(2,1)} %add_convert_fusion.5), channel_id=1, source_target_pairs={{0,1},{1,0},{2,3},{3,2},{4,5},{5,4},{6,7},{7,6},{8,9},{9,8},{10,11... | collective-permute-start | bytes 1769480 | tf_op jit(solution)/shard_map/ppermute | solution.py:52
  476.7 34.5 %collective-permute-start.38 = (bf16[3,768,256]{2,1,0:T(8,128)(2,1)}, bf16[3,768,256]{2,1,0:T(8,128)(2,1)}, u32[]{:S(2)}, u32[]{:S(2)}) collective-permute-start(bf16[3,768,256]{2,1,0:T(8,128)(2,1)} %get-tuple-element.174), channel_id=1, source_target_pairs={{0,16},{8,24},{16,0},{24,8},{1,17},{9,25},{17,1},{25,9},{2,18},{10... | collective-permute-start | bytes 3538952 | tf_op jit(solution)/shard_map/ppermute | solution.py:52
  490.3 9.5 %copy-start.18 = (f32[192,1536]{1,0:T(8,128)S(1)}, f32[192,1536]{1,0:T(8,128)}, u32[]{:S(2)}) copy-start(f32[192,1536]{1,0:T(8,128)} %get-tuple-element.281) | copy-start | bytes 3538948
  495.3 33.8 %all-to-all-start.7 = ((bf16[4,96,640]{2,1,0:T(8,128)(2,1)}), bf16[4,96,640]{2,1,0:T(8,128)(2,1)}, u32[]{:S(2)}, u32[]{:S(2)}) async-start(bf16[4,96,640]{2,1,0:T(8,128)(2,1)} %bitcast.92), calls=%async_computation.7 | async-start | bytes 983040 | tf_op jit(solution)/shard_map/all_to_all | solution.py:90
  501.5 30.5 %collective-permute-start.36 = (bf16[192,1536]{1,0:T(8,128)(2,1)S(1)}, bf16[192,1536]{1,0:T(8,128)(2,1)S(1)}, u32[]{:S(2)}, u32[]{:S(2)}) collective-permute-start(bf16[192,1536]{1,0:T(8,128)(2,1)S(1)} %fusion.8), channel_id=1, source_target_pairs={{0,1},{1,0},{2,3},{3,2},{4,5},{5,4},{6,7},{7,6},{8,9},{9,8},{10,11... | collective-permute-start | bytes 1769480 | tf_op jit(solution)/shard_map/ppermute | solution.py:52
  516.8 10.2 %slice-start = ((f32[96,1536]{1,0:T(8,128)}), f32[96,768]{1,0:T(8,128)S(1)}, s32[]{:S(2)}) async-start(f32[96,1536]{1,0:T(8,128)} %convert_reduce_fusion.1), calls=%async_computation.8 | async-start | bytes 589824 | tf_op jit(solution)/shard_map/slice | solution.py:1006
  516.8 10.3 %copy-start.39 = (f32[768,96]{0,1:T(8,128)S(1)}, f32[768,96]{0,1:T(8,128)}, u32[]{:S(2)}) copy-start(f32[768,96]{0,1:T(8,128)} %param.32) | copy-start | bytes 884740
  530.3 9.3 %collective-permute-start.37 = (f32[2,96]{1,0:T(2,128)S(1)}, f32[2,96]{1,0:T(2,128)S(1)}, u32[]{:S(2)}, u32[]{:S(2)}) collective-permute-start(f32[2,96]{1,0:T(2,128)S(1)} %bitcast.101), channel_id=1, source_target_pairs={{0,1},{1,0},{2,3},{3,2},{4,5},{5,4},{6,7},{7,6},{8,9},{9,8},{10,11... | collective-permute-start | bytes 2312 | tf_op jit(solution)/shard_map/ppermute | solution.py:52
  (33 other events, 67.0 us)

commit v4 on v3

--- a/solution.py
+++ b/solution.py
@@ -108,10 +108,110 @@
     return first * cosine - second * sine, second * cosine + first * sine
 
 
+def key_shard_kernel(qkv, gains, out, wide, square):
+    rows, columns = qkv.shape
+    kv = columns // ((GROUP + 2) * HD)
+    for h in range(kv):
+        at = h * (GROUP + 2) * HD + GROUP * HD
+        wide[:, h * HD : (h + 1) * HD] = qkv[:, at : at + HD]
+        wide[:, (kv + h) * HD : (kv + h + 1) * HD] = qkv[:, at + HD : at + 2 * HD]
+    square[...] = jnp.zeros_like(square)
+    square[: gains.shape[0], :rows] = gains[...]
+    wide[:, 2 * kv * HD :] = square[...].T[:rows]
+    low = wide[...].astype(jnp.bfloat16)
+    for i in range(out.shape[0]):
+        out[i] = low
+
+
+def both_shard_kernel(qkv, weight, out, wide, tall):
+    rows, columns = qkv.shape
+    kv = columns // ((GROUP + 2) * HD)
+    group = GROUP * HD
+    for h in range(kv):
+        at = h * (GROUP + 2) * HD
+        wide[:, h * group : (h + 1) * group] = qkv[:, at : at + group]
+    tall[...] = jnp.zeros_like(tall)
+    tall[:, :rows] = weight[...]
+    wide[:, kv * group :] = tall[...].T[:rows]
+    low = wide[...].astype(jnp.bfloat16)
+    for i in range(out.shape[0]):
+        out[i] = low
+
+
+def shard_copies(qkv, other, keys):
+    rows, columns = qkv.shape
+    kv = columns // ((GROUP + 2) * HD)
+    wide = 2 * kv * HD + 128 if keys else 2 * GROUP * kv * HD
+    padded = pltpu.VMEM((128, 128) if keys else (other.shape[0], 128), jnp.float32)
+    return pl.pallas_call(
+        key_shard_kernel if keys else both_shard_kernel,
+        out_shape=jax.ShapeDtypeStruct((lax.axis_size("ctx"), rows, wide), jnp.bfloat16),
+        in_specs=[vmem_spec()] * 2,
+        out_specs=vmem_spec(),
+        scratch_shapes=[pltpu.VMEM((rows, wide), jnp.float32), padded],
+        compiler_params=params(),
+        cost_estimate=cost(1, 1),
+        name="key_shard" if keys else "both_shard",
+    )(qkv, other)
+
+
+def row_copies_kernel(experts, place, og, routes, gates, out):
+    copies, rows, columns = out.shape
+    width = columns - 128
+    at = pl.ds(pl.multiple_of(place[2] * rows, rows), rows)
+    lane = lax.broadcasted_iota(jnp.int32, (rows, 128), 1)
+    high = jnp.zeros((rows, 128), jnp.float32)
+    rest = jnp.zeros((rows, 128), jnp.float32)
+    chosen, weights = routes[at], gates[at]
+    for k in range(routes.shape[1]):
+        weight = weights[:, k : k + 1]
+        top = weight.astype(jnp.bfloat16).astype(jnp.float32)
+        high += jnp.where(lane == chosen[:, k : k + 1], top, 0.0)
+        rest += jnp.where(lane == chosen[:, k : k + 1] + experts, weight - top, 0.0)
+    beside = (high + rest).astype(jnp.bfloat16)
+    own = og[at]
+    for i in range(copies):
+        out[i, :, :width] = own
+        out[i, :, width:] = beside
+
+
+def row_copies(place, out_grad, routes, gate_weights, rows, experts):
+    width = out_grad.shape[1]
+    return pl.pallas_call(
+        functools.partial(row_copies_kernel, experts),
+        out_shape=jax.ShapeDtypeStruct((lax.axis_size("ctx"), rows, width + 128), jnp.bfloat16),
+        in_specs=[smem_spec()] + [vmem_spec()] * 3,
+        out_specs=vmem_spec(),
+        compiler_params=params(),
+        cost_estimate=cost(1, 1),
+        name="row_copies",
+    )(place, out_grad, routes, gate_weights)
+
+
+def join_kernel(place, *refs):
+    parts, out = refs[:-1], refs[-1]
+    rows = parts[0].shape[0]
+    for m, part in enumerate(parts):
+        out[pl.ds(pl.multiple_of((place[2] ^ m) * rows, rows), rows)] = part[...]
+
+
+def join(place, parts):
+    rows, width = parts[0].shape
+    return pl.pallas_call(
+        join_kernel,
+        out_shape=jax.ShapeDtypeStruct((len(parts) * rows, width), parts[0].dtype),
+        in_specs=[smem_spec()] + [vmem_spec()] * len(parts),
+        out_specs=vmem_spec(),
+        compiler_params=params(),
+        cost_estimate=cost(1, 1),
+        name="join",
+    )(place, *parts)
+
+
 def project_keys_kernel(k_rows, *refs):
     place, tok, cos_ref, sin_ref = refs[:4]
     shard_refs, refs = refs[4 : 4 + len(F_MASKS)], refs[4 + len(F_MASKS) :]
-    kv_ref, norm_ref, norm_t, whole, gain_ref, sems = refs
+    copies_ref, norm_ref, norm_t, whole, gain_ref, kv_ref, sems = refs
     copies = load_shards(place, shard_refs, whole, sems)
     for copy in copies:
         copy.start()
@@ -132,6 +232,8 @@
         kv_ref[at : at + half] = a.astype(jnp.bfloat16)
         kv_ref[at + half : at + HD] = b.astype(jnp.bfloat16)
     kv_ref[k_rows:] = heads[k_rows:].astype(jnp.bfloat16)
+    for i in range(copies_ref.shape[0]):
+        copies_ref[i] = kv_ref[...]
 
 
 def project_keys(place, tokens, cosine, sine, shards, k_rows):
@@ -141,7 +243,7 @@
     return pl.pallas_call(
         functools.partial(project_keys_kernel, k_rows),
         out_shape=[
-            jax.ShapeDtypeStruct((2 * k_rows, rows), low),
+            jax.ShapeDtypeStruct((lax.axis_size("ctx"), 2 * k_rows, rows), low),
             jax.ShapeDtypeStruct((rows, width), low),
             jax.ShapeDtypeStruct((width, rows), low),
             jax.ShapeDtypeStruct((width, columns), low),
@@ -149,7 +251,10 @@
         ],
         in_specs=[smem_spec()] + [vmem_spec()] * 3 + [any_spec()] * len(shards),
         out_specs=[vmem_spec()] * 5,
-        scratch_shapes=[pltpu.SemaphoreType.DMA((len(shards),))],
+        scratch_shapes=[
+            pltpu.VMEM((2 * k_rows, rows), low),
+            pltpu.SemaphoreType.DMA((len(shards),)),
+        ],
         compiler_params=params(),
         cost_estimate=cost(2 * rows * width * columns, 8),
         name="project_keys",
@@ -194,11 +299,19 @@
     )(place, normed, cosine, sine, *shards)
 
 
+def share_out(place, part, own_ref, other_refs):
+    rows = own_ref.shape[0]
+    for m, out in enumerate((own_ref, *other_refs)):
+        at = pl.multiple_of((place[2] ^ m) * rows, rows)
+        out[...] = part[pl.ds(at, rows)].astype(out.dtype)
+
+
 def attend_kernel(n_ctx, *refs):
     place, start_ref, q_ref, piece_ref = refs[:4]
     refs = refs[4:]
     shard_refs, refs = refs[: len(F_MASKS)], refs[len(F_MASKS) :]
-    p_ref, head_ref, part_ref, kv_all, out_t, bias, scores, q3, sems = refs
+    p_ref, head_ref, kv_all, out_t, own_ref = refs[:5]
+    other_refs, (bias, scores, q3, part, sems) = refs[5:-5], refs[-5:]
     rows = q_ref.shape[1]
     half_kv = kv_all.shape[0] // 2
     step = pl.program_id(0)
@@ -236,11 +349,12 @@
     def _():
         for copy in copies:
             copy.wait()
-        part_ref[...] = nt_dot(head_ref[...].T, out_t[...])
+        part[...] = nt_dot(head_ref[...].T, out_t[...])
+        share_out(place, part, own_ref, other_refs)
 
 
 def attend(place, starts, q_t, pieces, shards):
-    n_ctx = lax.axis_size("ctx")
+    n_ctx, n_tp = lax.axis_size("ctx"), lax.axis_size("tp")
     q_rows, rows = q_t.shape
     kv = q_rows // (GROUP * HD)
     width = shards[0].shape[0] * len(shards)
@@ -252,18 +366,20 @@
         out_shape=[
             jax.ShapeDtypeStruct((kv, seq, GROUP * rows), low),
             jax.ShapeDtypeStruct((q_rows, rows), low),
-            jax.ShapeDtypeStruct((rows, width), jnp.float32),
             jax.ShapeDtypeStruct((2 * kv * HD, seq), low),
             jax.ShapeDtypeStruct((width, q_rows), low),
-        ],
+            jax.ShapeDtypeStruct((rows // n_tp, width), jnp.float32),
+        ]
+        + [jax.ShapeDtypeStruct((rows // n_tp, width), low)] * (n_tp - 1),
         in_specs=[smem_spec(), vmem_spec(), pl.BlockSpec((GROUP * HD, rows), lambda i: (i, 0))]
         + [vmem_spec()]
         + [any_spec()] * len(shards),
-        out_specs=[pl.BlockSpec((1, seq, GROUP * rows), lambda i: (i, 0, 0))] + [vmem_spec()] * 4,
+        out_specs=[pl.BlockSpec((1, seq, GROUP * rows), lambda i: (i, 0, 0))] + [vmem_spec()] * (3 + n_tp),
         scratch_shapes=[
             pltpu.VMEM((seq, rows), jnp.float32),
             pltpu.VMEM((seq, GROUP * rows), jnp.float32),
             pltpu.VMEM((HD, GROUP * rows), low),
+            pltpu.VMEM((rows, width), jnp.float32),
             pltpu.SemaphoreType.DMA((len(shards),)),
         ],
         compiler_params=pltpu.CompilerParams(vmem_limit_bytes=VMEM_LIMIT),
@@ -275,15 +391,16 @@
 
 
 def attend_back_kernel(n_ctx, *refs):
-    p_ref, q_ref, kv_all, grad_ref, out_t, cos_ref, sin_ref = refs[:7]
-    dq_ref, piece_ref, grads, q3, g3 = refs[7:]
+    place, p_ref, q_ref, kv_all, out_t, cos_ref, sin_ref = refs[:7]
+    grad_refs, (dq_ref, piece_ref, grad_all, grads, q3, g3) = refs[7:-6], refs[-6:]
     rows = q_ref.shape[1]
     half_kv = kv_all.shape[0] // 2
     step = pl.program_id(0)
 
     @pl.when(step == 0)
     def _():
-        back = jnp.dot(grad_ref[...], out_t[...], preferred_element_type=jnp.float32)
+        join_kernel(place, *grad_refs, grad_all)
+        back = jnp.dot(grad_all[...], out_t[...], preferred_element_type=jnp.float32)
         grads[...] = back.astype(jnp.bfloat16).T
 
     for h in range(GROUP):
@@ -314,7 +431,7 @@
         piece_ref[j, value_at] = grad_value[:, cols].astype(jnp.bfloat16)
 
 
-def attend_back(probs, q_t, kv_all, grad_attn, out_t, cosine, sine):
+def attend_back(place, probs, q_t, kv_all, grads, out_t, cosine, sine):
     n_ctx = lax.axis_size("ctx")
     q_rows, rows = q_t.shape
     kv, seq = probs.shape[:2]
@@ -327,9 +444,11 @@
             jax.ShapeDtypeStruct((q_rows, rows), low),
             jax.ShapeDtypeStruct((n_ctx, 2 * kv * HD, rows), low),
         ],
-        in_specs=[pl.BlockSpec((1, seq, GROUP * rows), lambda i: (i, 0, 0)), block] + [vmem_spec()] * 5,
+        in_specs=[smem_spec(), pl.BlockSpec((1, seq, GROUP * rows), lambda i: (i, 0, 0)), block]
+        + [vmem_spec()] * (4 + len(grads)),
         out_specs=[block, vmem_spec()],
         scratch_shapes=[
+            pltpu.VMEM((rows, out_t.shape[0]), low),
             pltpu.VMEM((q_rows, rows), low),
             pltpu.VMEM((HD, GROUP * rows), low),
             pltpu.VMEM((HD, GROUP * rows), low),
@@ -339,7 +458,7 @@
             flops=2 * q_rows * rows * (4 * seq + out_t.shape[0]), bytes_accessed=20 << 20, transcendentals=0
         ),
         name="attend_back",
-    )(probs, q_t, kv_all, grad_attn, out_t, cosine, sine)
+    )(place, probs, q_t, kv_all, out_t, cosine, sine, *grads)
 
 
 def store_products(place, left_t, right, out_refs):
@@ -351,12 +470,14 @@
         ).astype(jnp.bfloat16)
 
 
-def query_grad_kernel(place, dq_ref, norm_t, whole, grad_ref, head_ref, near, far, core, part_ref, grad_t):
+def query_grad_kernel(place, dq_ref, norm_t, whole, head_ref, *refs):
+    grad_refs, (near, far, core, part_ref, grad_all, grad_t) = refs[:-6], refs[-6:]
     columns = whole.shape[1]
     back = dq_ref[...].T
     outs = [near, far, core.at[0], core.at[1]]
     store_products(place, norm_t, back, [out.at[:, :columns] for out in outs])
-    grad_t[...] = grad_ref[...].T
+    join_kernel(place, *grad_refs, grad_all)
+    grad_t[...] = grad_all[...].T
     store_products(place, grad_t, head_ref[...].T, [out.at[:, columns:] for out in outs])
     part_ref[...] = nt_dot(back, whole[...])
 
@@ -370,20 +491,20 @@
     ]
 
 
-def query_grads(place, dq_t, norm_t, whole, grad_attn, head_t):
+def query_grads(place, dq_t, norm_t, whole, grads, head_t):
     q_rows, rows = dq_t.shape
     width = norm_t.shape[0]
     outs = pl.pallas_call(
         query_grad_kernel,
         out_shape=row_parts(width // len(F_MASKS), 2 * q_rows)
         + [jax.ShapeDtypeStruct((rows, width), jnp.float32)],
-        in_specs=[smem_spec()] + [vmem_spec()] * 5,
+        in_specs=[smem_spec()] + [vmem_spec()] * (4 + len(grads)),
         out_specs=[vmem_spec()] * 4,
-        scratch_shapes=[pltpu.VMEM((width, rows), jnp.bfloat16)],
+        scratch_shapes=[pltpu.VMEM((rows, width), jnp.bfloat16), pltpu.VMEM((width, rows), jnp.bfloat16)],
         compiler_params=params(),
         cost_estimate=cost(6 * rows * width * q_rows, 15),
         name="query_grads",
-    )(place, dq_t, norm_t, whole, grad_attn, head_t)
+    )(place, dq_t, norm_t, whole, head_t, *grads)
     return outs[:3], outs[3]
 
 
@@ -391,7 +512,8 @@
     place, piece_ref = refs[:2]
     refs = refs[2:]
     cos_ref, sin_ref, norm_t, whole, tok, query_part, gain_two_ref = refs[:7]
-    near, far, core, part_ref, back_t, right = refs[7:]
+    near, far, core, own_ref = refs[7:11]
+    other_refs, (part_ref, back_t, right) = refs[11:-3], refs[-3:]
     kv_rows, rows = piece_ref.shape[1:]
     total = piece_ref[0].astype(jnp.float32)
     for j in range(1, n_ctx):
@@ -406,6 +528,7 @@
     back = back_t[...].T
     part = query_part[...] + nt_dot(back, whole[:, :kv_rows])
     part_ref[...] = part
+    share_out(place, part_ref, own_ref, other_refs)
     outs = [near, far, core.at[0], core.at[1]]
     store_products(place, norm_t, back, [out.at[:, :kv_rows] for out in outs])
     x = tok[...].astype(jnp.float32)
@@ -421,16 +544,18 @@
 
 
 def key_grads(place, pieces, cosine, sine, norm_t, whole, tokens, query_part, gain_two):
-    n_ctx = lax.axis_size("ctx")
+    n_ctx, n_tp = lax.axis_size("ctx"), lax.axis_size("tp")
     kv_rows, rows = pieces.shape[1:]
     width = norm_t.shape[0]
     outs = pl.pallas_call(
         functools.partial(key_grad_kernel, n_ctx),
         out_shape=row_parts(width // len(F_MASKS), kv_rows + 128)
-        + [jax.ShapeDtypeStruct((rows, width), jnp.float32)],
+        + [jax.ShapeDtypeStruct((rows // n_tp, width), jnp.float32)]
+        + [jax.ShapeDtypeStruct((rows // n_tp, width), jnp.bfloat16)] * (n_tp - 1),
         in_specs=[smem_spec()] + [vmem_spec()] * 8,
-        out_specs=[vmem_spec()] * 4,
+        out_specs=[vmem_spec()] * (3 + n_tp),
         scratch_shapes=[
+            pltpu.VMEM((rows, width), jnp.float32),
             pltpu.VMEM((kv_rows, rows), jnp.bfloat16),
             pltpu.VMEM((width, 128), jnp.float32),
         ],
@@ -438,7 +563,7 @@
         cost_estimate=cost(4 * rows * width * kv_rows, 12),
         name="key_grads",
     )(place, pieces, cosine, sine, norm_t, whole, tokens, query_part, gain_two)
-    return outs[:3], outs[3]
+    return outs[:3], outs[3:]
 
 
 def sum_cores(parts, *before):
@@ -449,23 +574,22 @@
 
 def scatter_rows(near):
     n_ctx = lax.axis_size("ctx")
-    come = spread(near.reshape(n_ctx, near.shape[0] // n_ctx, near.shape[1]))
-    return jnp.sum(come.astype(jnp.float32), axis=0)
+    return spread(near.reshape(n_ctx, near.shape[0] // n_ctx, near.shape[1]))
 
 
 def table(count):
     near = [((m, 0), (m, 1)) for m in range(count)]
-    far = [((count, 0), (count + 1, 0))]
-    far += [((count + 1 + m, 0), (2 * count + m, 0)) for m in range(1, count)]
+    far = [((count, 0), (count, 1))]
+    far += [((count + m, 0), (2 * count - 1 + m, 0)) for m in range(1, count)]
     return [near, far] + [
-        [tuple((array + 3 * count, at) for array, at in piece) for piece in pieces] for pieces in (near, far)
+        [tuple((array + 3 * count - 1, at) for array, at in piece) for piece in pieces] for pieces in (near, far)
     ]
 
 
 def load_experts(refs, target, sems, kinds):
     half, hidden = refs[0].shape[2:]
     copies = []
-    for expert, pieces in enumerate(table(len(refs) // 6)):
+    for expert, pieces in enumerate(table((len(refs) + 2) // 6)):
         for m, piece in enumerate(pieces):
             for at, kind in enumerate(kinds):
                 for j, (array, index) in enumerate(piece):
@@ -480,7 +604,7 @@
 
 
 def weight_scratch(weights, kinds):
-    count = len(weights) // 6
+    count = (len(weights) + 2) // 6
     half, hidden = weights[0].shape[2:]
     return [
         pltpu.VMEM((kinds, len(F_MASKS), 2 * half, count * hidden), jnp.bfloat16),
@@ -792,6 +916,66 @@
     )(*(part for part, _ in parts), weight, moment, average)
 
 
+def sum_first(ref, cols):
+    total = ref[0, :, cols].astype(jnp.float32)
+    for i in range(1, ref.shape[0]):
+        total += ref[i, :, cols].astype(jnp.float32)
+    return total
+
+
+def step_out_kernel(come, weight, moment, average, moment_new, average_new, weight_new, wide):
+    rows = come.shape[1]
+    wide[...] = jnp.zeros_like(wide)
+    wide[:rows] = sum_first(come, slice(come.shape[2] // 2, come.shape[2]))
+    new = advance(weight[...], wide[...].T[:, :rows], moment[...], average[...], RATE_OUT)
+    moment_new[...], average_new[...], weight_new[...] = new
+
+
+def step_out(come, weight, moment, average):
+    return pl.pallas_call(
+        step_out_kernel,
+        out_shape=[jax.ShapeDtypeStruct(weight.shape, jnp.float32)] * 3,
+        in_specs=[vmem_spec()] * 4,
+        out_specs=[vmem_spec()] * 3,
+        scratch_shapes=[pltpu.VMEM((128, weight.shape[0]), jnp.float32)],
+        compiler_params=params(),
+        cost_estimate=cost(1, 1),
+        name="step_out",
+    )(come, weight, moment, average)
+
+
+def step_qkv_kernel(
+    query_come, key_come, weight, moment, average, moment_new, average_new, weight_new, grad, wide
+):
+    kv = weight.shape[1] // ((GROUP + 2) * HD)
+    group = GROUP * HD
+    queries = sum_first(query_come, slice(0, kv * group))
+    wide[...] = sum_first(key_come, slice(None))
+    for h in range(kv):
+        at = h * (GROUP + 2) * HD
+        grad[:, at : at + group] = queries[:, h * group : (h + 1) * group]
+        grad[:, at + group : at + group + HD] = wide[:, h * HD : (h + 1) * HD]
+        grad[:, at + group + HD : at + group + 2 * HD] = wide[:, (kv + h) * HD : (kv + h + 1) * HD]
+    new = advance(weight[...], grad[...], moment[...], average[...], RATE_QKV)
+    moment_new[...], average_new[...], weight_new[...] = new
+
+
+def step_qkv(query_come, key_come, weight, moment, average):
+    return pl.pallas_call(
+        step_qkv_kernel,
+        out_shape=[jax.ShapeDtypeStruct(weight.shape, jnp.float32)] * 3,
+        in_specs=[vmem_spec()] * 5,
+        out_specs=[vmem_spec()] * 3,
+        scratch_shapes=[
+            pltpu.VMEM(weight.shape, jnp.float32),
+            pltpu.VMEM(key_come.shape[1:], jnp.float32),
+        ],
+        compiler_params=params(),
+        cost_estimate=cost(1, 1),
+        name="step_qkv",
+    )(query_come, key_come, weight, moment, average)
+
+
 def per_device(
     tokens,
     out_grad,
@@ -819,7 +1003,7 @@
     experts = lax.axis_size(("fsdp", "ctx"))
     fsdp_index, ctx_index = lax.axis_index("fsdp"), lax.axis_index("ctx")
     tp_index = lax.axis_index("tp")
-    place = jnp.stack([fsdp_index, ctx_index]).astype(jnp.int32)
+    place = jnp.stack([fsdp_index, ctx_index, tp_index]).astype(jnp.int32)
     low, f32 = jnp.bfloat16, jnp.float32
     half_rows = tok_rows // n_tp
     over_tp = range(n_tp)
@@ -830,43 +1014,21 @@
     def own_half(value):
         return part_of(value, 0)
 
-    def sum_own(value):
-        total = own_half(value)
-        for m in over_tp[1:]:
-            total += swap(part_of(value, m).astype(low), "tp", m).astype(f32)
-        return total
+    def sum_own(own, others):
+        for m, other in enumerate(others, 1):
+            own = own + swap(other, "tp", m).astype(f32)
+        return own
 
     def to_others(own):
         return [own] + [swap(own, "tp", m) for m in over_tp[1:]]
-
-    def both_halves(parts):
-        ordered = []
-        for at in over_tp:
-            chosen = parts[0]
-            for m in over_tp[1:]:
-                chosen = jnp.where(tp_index ^ m == at, parts[m], chosen)
-            ordered.append(chosen)
-        return jnp.concatenate(ordered, axis=0)
 
     shard_rows, qkv_columns = qkv_weight.shape
     kv_local = qkv_columns // ((GROUP + 2) * HD)
     q_rows, k_rows = kv_local * GROUP * HD, kv_local * HD
-    by_head = qkv_weight.astype(low).reshape(shard_rows, kv_local, GROUP + 2, HD)
-    keys_own = jnp.concatenate(
-        [
-            by_head[:, :, GROUP].reshape(shard_rows, k_rows),
-            by_head[:, :, GROUP + 1].reshape(shard_rows, k_rows),
-            jnp.pad(norm_gains.astype(low).T, ((0, 0), (0, 126))),
-        ],
-        axis=1,
-    )
-    key_near = gather_along_ctx(keys_own).reshape(-1, keys_own.shape[1])
+    key_near = spread(shard_copies(qkv_weight, norm_gains, True)).reshape(-1, 2 * k_rows + 128)
     key_across = swap(key_near, "fsdp", 2)
     key_shards = [key_near, key_across, swap(key_near, "fsdp", 1), swap(key_across, "fsdp", 1)]
-    both_own = jnp.concatenate(
-        [by_head[:, :, :GROUP].reshape(shard_rows, q_rows), out_weight.astype(low).T], axis=1
-    )
-    both_near = gather_along_ctx(after(both_own, key_near)).reshape(-1, both_own.shape[1])
+    both_near = spread(shard_copies(after(qkv_weight, key_near), out_weight, False)).reshape(-1, 2 * q_rows)
 
     down_t = expert_down[0].T[None]
     half = width // 2
@@ -874,7 +1036,7 @@
         [jnp.concatenate([expert_in[0, :, rows], down_t[:, rows]]) for rows in (slice(0, half), slice(half, width))]
     ).astype(low)
     along_tp = [swap(after(own, key_near), "tp", m) for m in over_tp[1:]]
-    upper_x = swap(after(own[:1], *key_shards[2:]), "fsdp", 2)
+    along_x = swap(after(own, *key_shards[2:]), "fsdp", 2)
 
     places = ctx_index * tok_rows + jnp.arange(tok_rows, dtype=jnp.int32)
     _, position = doc_positions(lengths[0], places)
@@ -886,52 +1048,35 @@
         place, tokens, cosine, sine, key_shards, k_rows
     )
     gain_one, gain_two = gains[0], gains[1]
-    both_across = swap(after(both_near, kv_t, upper_x), "fsdp", 2)
+    both_across = swap(after(both_near, kv_t, along_x), "fsdp", 2)
     both_shards = [
         both_near,
         both_across,
         swap(after(both_near, kv_t), "fsdp", 1),
         swap(after(both_across, kv_t), "fsdp", 1),
     ]
-    kv_pieces = gather_along_ctx(kv_t)
+    kv_pieces = spread(kv_t)
     q_t, query_whole = project_queries(place, normed_low, cosine, sine, both_shards)
 
-    lower_x = swap(after(own[1:], both_across), "fsdp", 2)
-    uppers = [swap(upper_x, "tp", m) for m in over_tp[1:]]
-    lowers = [swap(after(piece[1:], lower_x), "fsdp", 2) for piece in along_tp]
+    uppers = [swap(along_x[:1], "tp", m) for m in over_tp[1:]]
+    lowers = [swap(after(piece[1:], both_across), "fsdp", 2) for piece in along_tp]
     soon = [swap(after(own, both_near), "fsdp", 1)]
 
-    expert_ids = jnp.arange(experts, dtype=jnp.int32)
-    dense_gates = jnp.sum(
-        jnp.where(
-            own_half(routes)[:, :, None] == expert_ids[None, None, :],
-            own_half(gate_weights)[:, :, None],
-            0.0,
-        ),
-        axis=1,
-    )
-    gates_high = dense_gates.astype(low)
-    gates_rest = (dense_gates - gates_high.astype(f32)).astype(low)
-    grad_own = own_half(out_grad)
-    grad_gates = jnp.concatenate(
-        [grad_own, gates_high, gates_rest, jnp.zeros((half_rows, 128 - 2 * experts), low)], axis=1
-    )
-    og = gather_along_ctx(after(grad_gates, kv_pieces))
-
-    probs, head_t, attn_part, kv_all, out_t = attend(
+    grad_rows = row_copies(after(place, kv_t), out_grad, routes, gate_weights, half_rows, experts)
+    og = spread(after(grad_rows, kv_pieces))
+
+    probs, head_t, kv_all, out_t, attn_own, *attn_others = attend(
         after(place, *soon, *along_tp), starts, q_t, kv_pieces, both_shards
     )
-    soon += [swap(after(piece, attn_part), "fsdp", 1) for piece in [*along_tp, upper_x, *uppers]]
-    hidden_one = own_half(after(tokens, og, *soon)).astype(f32) + sum_own(attn_part)
+    soon += [swap(after(piece, attn_own), "fsdp", 1) for piece in [*along_tp, along_x, *uppers, *lowers]]
+    hidden_one = own_half(after(tokens, og, *soon)).astype(f32) + sum_own(attn_own, attn_others)
     inverse_two = lax.rsqrt(jnp.mean(hidden_one * hidden_one, axis=-1, keepdims=True) + EPSILON)
     normed_two = hidden_one * inverse_two
     normed_two_low = (normed_two * gain_two).astype(low)
 
     x_own = after(normed_two_low, og)
     xs = [x_own] + [swap(x_own, "ctx", m) for m in range(1, n_ctx)]
-    late = [swap(after(piece, normed_two_low), "fsdp", 1) for piece in [lower_x, *lowers]]
-    weights = [own, *along_tp, upper_x, lower_x, *uppers, *lowers]
-    weights += [*soon[: n_tp + 1], late[0], *soon[n_tp + 1 :], *late[1:]]
+    weights = [own, *along_tp, along_x, *uppers, *lowers, *soon]
     backs = back_rows(og, weights, width)
     grads_x, acts, ggs, gus = [], [], [], []
     for at in range(0, n_ctx, 2):
@@ -945,16 +1090,16 @@
         gus.append(gu)
     come_x = [swap(grads_x[m], "ctx", m) for m in range(1, n_ctx)]
     core_leave, core_stay = weight_grads(place, xs, og, acts, ggs, gus, n_tp, 2)
-    mixes = mix_rows(after(place, core_leave), acts, weights, n_ctx, width)
+    leave, stay = weight_grads(after(place, core_leave), xs, og, acts, ggs, gus, n_tp, 0)
+    mixes = mix_rows(after(place, leave), acts, weights, n_ctx, width)
 
     grad_normed_two = after(grads_x[0], mixes).astype(f32)
     for come in come_x:
         grad_normed_two += come.astype(f32)
     gain_grad_two = jnp.sum(grad_normed_two * normed_two, axis=0)
-    grad_hidden = grad_own.astype(f32) + norm_back(grad_normed_two, normed_two, inverse_two, gain_two)
-    grad_attn = both_halves(to_others(grad_hidden.astype(low)))
-    leave, stay = weight_grads(after(place, grad_hidden), xs, og, acts, ggs, gus, n_tp, 0)
-    core_leave = after(swap(after(core_leave, mixes, *come_x), "fsdp", 1), grad_attn)
+    grad_hidden = own_half(out_grad).astype(f32) + norm_back(grad_normed_two, normed_two, inverse_two, gain_two)
+    grad_attn = to_others(grad_hidden.astype(low))
+    core_leave = swap(after(core_leave, mixes, *come_x), "fsdp", 1)
     come_mix = spread(after(mixes, grad_hidden))
 
     uppers_out = [
@@ -965,13 +1110,13 @@
     lower_in = swap(lower_out, "fsdp", 2)
 
     dq_t, kv_grads = attend_back(
-        probs, q_t, kv_all, after(grad_attn, lower_out, *uppers_out), out_t, cosine, sine
+        after(place, lower_out, *uppers_out), probs, q_t, kv_all, grad_attn, out_t, cosine, sine
     )
     mixture = jnp.sum(after(come_mix, dq_t).astype(f32), axis=0)
     come = spread(kv_grads)
     core_stay = swap(after(core_stay, lower_out), "fsdp", 1)
     query_parts, query_part = query_grads(
-        place, dq_t, norm_t, query_whole, after(grad_attn, mixture), head_t
+        after(place, mixture), dq_t, norm_t, query_whole, grad_attn, head_t
     )
 
     lower_next = [
@@ -982,40 +1127,33 @@
     query_near, query_far = sum_cores(query_parts, upper_next, *lower_next)
     query_near = added(query_near, swap(query_far, "fsdp", 2))
     upper_last = swap(after(upper_next, query_near), "fsdp", 2)
-    key_parts, grad_normed_part = key_grads(
+    key_parts, (normed_own, *normed_others) = key_grads(
         after(place, query_near, *lowers_last), come, cosine, sine, norm_t, key_whole,
         tokens, query_part, gain_grad_two[None]
     )
-    grad_normed_one = sum_own(grad_normed_part)
+    grad_normed_one = sum_own(normed_own, normed_others)
     block_parts = to_others((hidden_one + mixture).astype(low))
     inputs = own_half(tokens).astype(f32)
     inverse_one = lax.rsqrt(jnp.mean(inputs * inputs, axis=-1, keepdims=True) + EPSILON)
     in_parts = to_others(
         (grad_hidden + norm_back(grad_normed_one, inputs * inverse_one, inverse_one, gain_one)).astype(low)
     )
-    key_near, key_far = sum_cores(key_parts)
-    key_near = added(key_near, swap(key_far, "fsdp", 2))
+    key_near, key_far = sum_cores(key_parts, upper_last)
     query_grad = scatter_rows(query_near)
-    key_grad = scatter_rows(after(key_near, query_grad))
-    block_out = both_halves([after(part, key_grad) for part in block_parts])
-    in_grad = both_halves([after(part, key_grad) for part in in_parts])
-    gains_grad = key_grad[:, 2 * k_rows : 2 * k_rows + 2].T
-    gains_grad = gains_grad + sum(swap(gains_grad, "tp", m) for m in over_tp[1:])
-    qkv_grad = jnp.concatenate(
-        [
-            query_grad[:, :q_rows].reshape(shard_rows, kv_local, GROUP, HD),
-            key_grad[:, :k_rows].reshape(shard_rows, kv_local, 1, HD),
-            key_grad[:, k_rows : 2 * k_rows].reshape(shard_rows, kv_local, 1, HD),
-        ],
-        axis=2,
-    ).reshape(shard_rows, qkv_columns)
-    qkv_new = advance(qkv_weight, qkv_grad, qkv_moment, qkv_average, RATE_QKV)
-    out_new = advance(out_weight, query_grad[:, q_rows:].T, out_moment, out_average, RATE_OUT)
-    gain_new = advance(norm_gains, gains_grad, gain_moment, gain_average, RATE_GAIN)
     upper_parts = [(stay, 0), (core_stay, 0)] + [(part, 0) for part in uppers_in] + [(upper_last[None], 0)]
     lower_parts = [(stay, 2), (core_stay, 2), (lower_in, 0)] + [(part[None], 0) for part in lowers_last]
-    in_new = step_in(upper_parts, lower_parts, after(expert_in, key_near), in_moment, in_average)
-    down_new = step_down(upper_parts, lower_parts, after(expert_down, key_near), down_moment, down_average)
+    in_new = step_in(upper_parts, lower_parts, after(expert_in, key_far), in_moment, in_average)
+    key_near = added(key_near, after(swap(key_far, "fsdp", 2), query_grad, in_new[0]))
+    key_grad = scatter_rows(key_near)
+    block_out = join(place, [after(part, key_near) for part in block_parts])
+    out_new = step_out(query_grad, after(out_weight, block_out), out_moment, out_average)
+    down_new = step_down(upper_parts, lower_parts, after(expert_down, out_new[0]), down_moment, down_average)
+    in_grad = join(place, [after(part, down_new[0]) for part in in_parts])
+    gains_grad = jnp.sum(key_grad[:, :, 2 * k_rows : 2 * k_rows + 2].astype(f32), axis=0).T
+    gains_others = [swap(gains_grad, "tp", m) for m in over_tp[1:]]
+    qkv_new = step_qkv(query_grad, after(key_grad, in_grad), qkv_weight, qkv_moment, qkv_average)
+    gains_grad = gains_grad + sum(after(other, qkv_new[0]) for other in gains_others)
+    gain_new = advance(norm_gains, gains_grad, gain_moment, gain_average, RATE_GAIN)
     return (block_out, in_grad, *qkv_new, *out_new, *gain_new, *in_new, *down_new)
 
 

time: 550 us -> 501 us (0.911)
  waiting for transfers between devices: 189 us -> 149 us
  starting transfers between devices: 88.2 us -> 64.3 us
  blocking collectives: 0 us -> 20.2 us
  Pallas kernels: 178 us -> 197 us
  local copies, waits for them, and re-layouts: 37.1 us -> 20.9 us
  other arithmetic: 45.7 us -> 38.8 us
    ppermute x39 -> x37, waiting for transfers between devices: 157 us -> 123 us  [swap(): return lax.ppermute(value, axis, [(i, i ^ mask) for i in range(size)])]
    all_to_all x0 -> x1, blocking collectives: none -> 20.2 us  [spread(): lax.all_to_all(blocks, 'ctx', split_axis=0, concat_axis=0, tiled=True)]
    pallas_call x0 -> x7, Pallas kernels: none -> 19 us  [the longest x2 4.74 us: join(): pl.pallas_call(join_kernel, out_shape=jax.ShapeDtypeStruct((len(parts) *...]
    all_to_all x8 -> x7, starting transfers between devices: 45.2 us -> 30.3 us  [spread(): lax.all_to_all(blocks, 'ctx', split_axis=0, concat_axis=0, tiled=True)]
    ppermute x39 -> x37, starting transfers between devices: 43 us -> 33.9 us  [swap(): return lax.ppermute(value, axis, [(i, i ^ mask) for i in range(size)])]
    unnamed x106 -> x97, local copies, waits for them, and re-layouts: 19.9 us -> 13 us
    broadcast_in_dim x5 -> x0, local copies, waits for them, and re-layouts: 5.96 us -> none  [the longest x4 5.95 us: gather_along_ctx(): jnp.broadcast_to(own[None], (lax.axis_size('ctx'), *own.shape))]
    all_to_all x8 -> x7, waiting for transfers between devices: 32.1 us -> 26.4 us  [spread(): lax.all_to_all(blocks, 'ctx', split_axis=0, concat_axis=0, tiled=True)]
  transfers between devices with their start and end apart: 47 -> 44, of which waited for: 20 -> 16; matrix products, arithmetic and copies ran while one was open for 12% -> 10% of each run, Pallas kernels for 29% -> 36%
where the time goes in v4:
time: 501 us; the launch traced here: 492 us
  Pallas kernels  197 us (39%)
  waiting for transfers between devices  149 us (30%)
  starting transfers between devices  64.3 us (13%)
  other arithmetic  38.8 us (8%)
  local copies, waits for them, and re-layouts  20.9 us (4%)
  blocking collectives  20.2 us (4%)
    ppermute x37, waiting for transfers between devices, swap(): return lax.ppermute(value, axis, [(i, i ^ mask) for i in range(size)])  123 us
    pallas_call x2, Pallas kernels, weight_grads(): pl.pallas_call(functools.partial(weight_kernel, blocks, calls, count), gr...  37.1 us
    pallas_call x2, Pallas kernels, expert_rows(): pl.pallas_call(functools.partial(expert_kernel, masks, experts), grid=(1,...  34.4 us
    ppermute x37, starting transfers between devices, swap(): return lax.ppermute(value, axis, [(i, i ^ mask) for i in range(size)])  33.9 us
    all_to_all x7, starting transfers between devices, spread(): lax.all_to_all(blocks, 'ctx', split_axis=0, concat_axis=0, tiled=True)  30.3 us
    all_to_all x7, waiting for transfers between devices, spread(): lax.all_to_all(blocks, 'ctx', split_axis=0, concat_axis=0, tiled=True)  26.4 us
    pallas_call x1, Pallas kernels, attend_back(): pl.pallas_call(functools.partial(attend_back_kernel, n_ctx), grid=(kv,),...  23.7 us
    pallas_call x1, Pallas kernels, attend(): pl.pallas_call(functools.partial(attend_kernel, n_ctx), grid=(kv,), out_s...  21.1 us
  transfers between devices with their start and end apart: 44, of which 16 were waited for; matrix products, arithmetic and copies ran while one was open for 10% of the time, Pallas kernels for 36%

profile of v4, /device:TPU:0, one launch (start us, length us, event | category | flops | bytes accessed | tf_op | source)
XLA Modules:
  0.0 491.6 jit_solution(10889985964642762888)
XLA Ops:
  0.7 2.0 key_shard.1
  2.6 20.2 %all_to_all.40 = bf16[4,96,640]{2,1,0:T(8,128)(2,1)} all-to-all(bf16[4,96,640]{2,1,0:T(8,128)(2,1)} %key_shard.1), channel_id=1, replica_groups=mesh['fsdp'=4,'ctx'=4,'tp'=2] {'ctx'}, dimensions={0} | all-to-all | bytes 983040 | tf_op jit(solution)/shard_map/all_to_all | solution.py:90
  22.8 1.5 collective-permute-start
  24.3 2.0 convert.22
  27.3 2.4 both_shard.1
  29.7 4.3 all-to-all-start.3
  37.8 1.6 pad_maximum_fusion.refs_0_.refs_5_.refs_2_
  41.8 5.4 %project_keys.1 = (bf16[4,512,384]{2,1,0:T(8,128)(2,1)}, bf16[384,1536]{1,0:T(8,128)(2,1)}, bf16[1536,384]{1,0:T(8,128)(2,1)}, bf16[1536,640]{1,0:T(8,128)(2,1)}, f32[8,1536]{1,0:T(8,128)}) custom-call(s32[3]{0:T(128)} %pad_add_fusion.refs_0_.place, bf16[384,1536]{1,0:T(8,128)(2,1)} %refs_6_.1, f32[32,384]{1,0:T(8,128)} %get-tuple-element.291.refs_2_.refs_5_, ...), custom_call_target="tpu_custom_call" | custom-call | flops 1 | bytes 1 | tf_op jit(solution)/shard_map/project_keys/pallas_call | solution.py:243
  47.3 14.2 %all-to-all-done.3 = bf16[4,96,1536]{2,1,0:T(8,128)(2,1)} async-done(((bf16[4,96,1536]{2,1,0:T(8,128)(2,1)}), bf16[4,96,1536]{2,1,0:T(8,128)(2,1)}, u32[]{:S(2)}, u32[]{:S(2)}) %all-to-all-start.3) | async-done | bytes 1179680 | tf_op jit(solution)/shard_map/all_to_all | solution.py:90
  61.5 4.5 all-to-all-start.1
  66.0 1.6 collective-permute-start.4
  67.6 25.0 %collective-permute-done.5.refs_2_.refs_7_.refs_4_ = bf16[2,3,768,256]{3,2,1,0:T(8,128)(2,1)S(1)} collective-permute-done((bf16[2,3,768,256]{3,2,1,0:T(8,128)(2,1)}, bf16[2,3,768,256]{3,2,1,0:T(8,128)(2,1)S(1)}, u32[]{:S(2)}, u32[]{:S(2)}) %collective-permute-start.5) | collective-permute-done | bytes 2359328 | tf_op jit(solution)/shard_map/ppermute | solution.py:52
  94.9 3.8 row_copies.1
  98.7 3.8 all-to-all-done.1.refs_3_
  102.5 3.6 all-to-all-start.2
  106.2 13.5 %collective-permute-done.6.refs_5_ = bf16[384,1536]{1,0:T(8,128)(2,1)} collective-permute-done((bf16[384,1536]{1,0:T(8,128)(2,1)}, bf16[384,1536]{1,0:T(8,128)(2,1)}, u32[]{:S(2)}, u32[]{:S(2)}) %collective-permute-start.6) | collective-permute-done | bytes 1179680 | tf_op jit(solution)/shard_map/ppermute | solution.py:52
  120.3 2.5 slice.101
  123.9 1.5 collective-permute-start.11
  126.0 5.0 %project_queries.1 = (bf16[768,384]{1,0:T(8,128)(2,1)}, bf16[1536,768]{1,0:T(8,128)(2,1)}) custom-call(s32[3]{0:T(128)} %pad_add_fusion.refs_0_.place, bf16[384,1536]{1,0:T(8,128)(2,1)} %get-tuple-element.117.refs_1_, f32[32,384]{1,0:T(8,128)} %get-tuple-element.291.refs_2_.refs_5_, f32[32,384]{1,0:T(8,128)} %get-tuple-element.290.refs_3_.refs_6_, ...), custom_call_target="tpu_custom_call" | custom-call | flops 1 | bytes 1 | tf_op jit(solution)/shard_map/project_queries/pallas_call | solution.py:287
  131.0 21.1 %attend.1 = (bf16[4,1536,1152]{2,1,0:T(8,128)(2,1)}, bf16[768,384]{1,0:T(8,128)(2,1)}, bf16[512,1536]{1,0:T(8,128)(2,1)}, bf16[1536,768]{1,0:T(8,128)(2,1)}, f32...) custom-call(s32[3]{0:T(128)} %pad_add_fusion.refs_0_.place, s32[1,384]{1,0:T(1,128)} %reduce_sum.75.refs_1_, ...), custom_call_target="tpu_custom_call" | custom-call | flops 2717908992 | bytes 20971520 | tf_op jit(solution)/shard_map/attend/pallas_call | solution.py:363
  155.8 6.4 %collective-permute-done.14.refs_9_.refs_14_.refs_11_ = bf16[1,3,768,256]{3,2,1,0:T(8,128)(2,1)} collective-permute-done((bf16[1,3,768,256]{3,2,1,0:T(8,128)(2,1)}, bf16[1,3,768,256]{3,2,1,0:T(8,128)(2,1)}, u32[]{:S(2)}, u32[]{:S(2)}) %collective-permute-start.14) | collective-permute-done | bytes 1179680 | tf_op jit(solution)/shard_map/ppermute | solution.py:52
  162.2 1.7 collective-permute-done.12.refs_8_.refs_13_.refs_10_
  163.9 5.9 %collective-permute-done.15 = bf16[192,1536]{1,0:T(8,128)(2,1)S(1)} collective-permute-done((bf16[192,1536]{1,0:T(8,128)(2,1)}, bf16[192,1536]{1,0:T(8,128)(2,1)S(1)}, u32[]{:S(2)}, u32[]{:S(2)}) %collective-permute-start.15) | collective-permute-done | bytes 589856 | tf_op jit(solution)/shard_map/ppermute | solution.py:52
  169.8 1.7 multiply_reduce_fusion.2
  172.7 2.0 collective-permute-start.16
  174.8 2.4 collective-permute-start.17
  177.2 10.4 %back_rows.1.refs_4_ = bf16[4,192,2048]{2,1,0:T(8,128)(2,1)} custom-call(bf16[4,192,1664]{2,1,0:T(8,128)(2,1)} %copy-done, bf16[2,3,768,256]{3,2,1,0:T(8,128)(2,1)} %pad_maximum_fusion.refs_0_.refs_5_.refs_2_, bf16[2,3,768,256]{3,2,1,0:T(8,128)(2,1)} %collective-permute-done.4.refs_1_.refs_6_.refs_3_, bf16[2,3,768,256]{3,2,1,0:T(8,128)(2,1)} %copy-done.1, ...), custom_call_target="tpu_custom_call" | custom-call | flops 1 | bytes 1 | tf_op jit(solution)/shard_map/back_rows/pallas_call | solution.py:640
  187.7 11.2 %collective-permute-done.16.refs_2_.refs_3_ = bf16[192,1536]{1,0:T(8,128)(2,1)S(1)} collective-permute-done((bf16[192,1536]{1,0:T(8,128)(2,1)S(1)}, bf16[192,1536]{1,0:T(8,128)(2,1)S(1)}, u32[]{:S(2)}, u32[]{:S(2)}) %collective-permute-start.16) | collective-permute-done | bytes 589856 | tf_op jit(solution)/shard_map/ppermute | solution.py:52
  199.7 17.0 %expert_rows.2 = (bf16[192,1536]{1,0:T(8,128)(2,1)}, bf16[192,1536]{1,0:T(8,128)(2,1)}, bf16[384,2048]{1,0:T(8,128)(2,1)}, bf16[384,2048]{1,0:T(8,128)(2,1)}, bf16[384,2048]{1,0:T(8,128)(2,1)}) custom-call(s32[3]{0:T(128)} %pad_add_fusion.refs_0_.place, bf16[192,1536]{1,0:T(8,128)(2,1)} %copy-done.8, bf16[192,1536]{1,0:T(8,128)(2,1)} %copy-done.10, ...), custom_call_target="tpu_custom_call" | custom-call | flops 1 | bytes 1 | tf_op jit(solution)/shard_map/expert_rows/pallas_call | solution.py:704
  218.9 17.4 %expert_rows.3 = (bf16[192,1536]{1,0:T(8,128)(2,1)}, bf16[192,1536]{1,0:T(8,128)(2,1)}, bf16[384,2048]{1,0:T(8,128)(2,1)}, bf16[384,2048]{1,0:T(8,128)(2,1)}, bf16[384,2048]{1,0:T(8,128)(2,1)}) custom-call(s32[3]{0:T(128)} %pad_add_fusion.refs_0_.place, bf16[192,1536]{1,0:T(8,128)(2,1)} %copy-done.11, bf16[192,1536]{1,0:T(8,128)(2,1)} %copy-done.12, ...), custom_call_target="tpu_custom_call" | custom-call | flops 1 | bytes 1 | tf_op jit(solution)/shard_map/expert_rows/pallas_call | solution.py:704
  236.3 11.2 %collective-permute-start.20 = (bf16[192,1536]{1,0:T(8,128)(2,1)}, bf16[192,1536]{1,0:T(8,128)(2,1)S(1)}, u32[]{:S(2)}, u32[]{:S(2)}) collective-permute-start(bf16[192,1536]{1,0:T(8,128)(2,1)} %get-tuple-element.147), channel_id=1, source_target_pairs={{0,4},{2,6},{4,0},{6,2},{1,5},{3,7},{5,1},{7,3},{8,12},{10,14},{12... | collective-permute-start | bytes 1769480 | tf_op jit(solution)/shard_map/ppermute | solution.py:52
  247.5 1.5 collective-permute-start.21
  249.0 18.5 %weight_grads.2 = (bf16[4,3,768,256]{3,2,1,0:T(8,128)(2,1)}, bf16[4,3,768,256]{3,2,1,0:T(8,128)(2,1)}) custom-call(s32[3]{0:T(128)} %pad_add_fusion.refs_0_.place, bf16[4,192,1664]{2,1,0:T(8,128)(2,1)} %copy-done, bf16[192,1536]{1,0:T(8,128)(2,1)} %copy-done.8, bf16[192,1536]{1,0:T(8,128)(2,1)} %copy-done.10, bf16[192,1536]{1,0:T(8,128)(2,1)} %copy-done.11, ...), custom_call_target="tpu_custom_call" | custom-call | flops 1 | bytes 1 | tf_op jit(solution)/shard_map/weight_grads/pallas_call | solution.py:816
  267.5 18.6 %weight_grads.3 = (bf16[4,3,768,256]{3,2,1,0:T(8,128)(2,1)}, bf16[4,3,768,256]{3,2,1,0:T(8,128)(2,1)}) custom-call(s32[3]{0:T(128)} %pad_add_fusion.refs_0_.place, bf16[4,192,1664]{2,1,0:T(8,128)(2,1)} %copy-done, bf16[192,1536]{1,0:T(8,128)(2,1)} %copy-done.8, bf16[192,1536]{1,0:T(8,128)(2,1)} %copy-done.10, bf16[192,1536]{1,0:T(8,128)(2,1)} %copy-done.11, ...), custom_call_target="tpu_custom_call" | custom-call | flops 1 | bytes 1 | tf_op jit(solution)/shard_map/weight_grads/pallas_call | solution.py:816
  286.1 10.6 %mix_rows.1 = bf16[4,192,1536]{2,1,0:T(8,128)(2,1)} custom-call(s32[3]{0:T(128)} %pad_add_fusion.refs_0_.place, bf16[384,2048]{1,0:T(8,128)(2,1)} %get-tuple-element.133.refs_6_.refs_0_, bf16[384,2048]{1,0:T(8,128)(2,1)} %get-tuple-element.135.refs_7_.refs_1_, bf16[2,3,768,256]{3,2,1,0:T(8,128)(2,1)} %pad_maximum_fusion.refs_0_.refs_5_.refs_2_, ...), custom_call_target="tpu_custom_call" | custom-call | flops 1 | bytes 1 | tf_op jit(solution)/shard_map/mix_rows/pallas_call | solution.py:752
  298.1 1.8 fusion.14
  299.9 4.5 all-to-all-start.4
  305.1 5.7 %add_convert_fusion = (bf16[2,3,768,256]{3,2,1,0:T(8,128)(2,1)}, bf16[2,3,768,256]{3,2,1,0:T(8,128)(2,1)}) fusion(bf16[4,3,768,256]{3,2,1,0:T(8,128)(2,1)} %collective-permute-done.22, bf16[4,3,768,256]{3,2,1,0:T(8,128)(2,1)} %get-tuple-element.142), kind=kLoop, calls=%fused_computation.1 | loop fusion | flops 9437184 | bytes 14155776 | tf_op jit(solution)/shard_map/convert_element_type | solution.py:834
  311.5 1.5 collective-permute-start.26
  313.5 13.9 %collective-permute-done.23.refs_8_.refs_1_ = bf16[192,1536]{1,0:T(8,128)(2,1)} collective-permute-done((bf16[192,1536]{1,0:T(8,128)(2,1)}, bf16[192,1536]{1,0:T(8,128)(2,1)}, u32[]{:S(2)}, u32[]{:S(2)}) %collective-permute-start.23) | collective-permute-done | bytes 589856 | tf_op jit(solution)/shard_map/ppermute | solution.py:52
  327.4 23.7 %attend_back.1 = (bf16[768,384]{1,0:T(8,128)(2,1)}, bf16[4,512,384]{2,1,0:T(8,128)(2,1)}) custom-call(s32[3]{0:T(128)} %pad_add_fusion.refs_0_.place, bf16[4,1536,1152]{2,1,0:T(8,128)(2,1)} %get-tuple-element.152.refs_1_, bf16[768,384]{1,0:T(8,128)(2,1)} %get-tuple-element.122.refs_2_, bf16[512,1536]{1,0:T(8,128)(2,1)} %get-tuple-element.153.refs_3_, ...), custom_call_target="tpu_custom_call" | custom-call | flops 4529848320 | bytes 20971520 | tf_op jit(solution)/shard_map/attend_back/pallas_call | solution.py:440
  351.1 8.3 %all-to-all-done.4 = bf16[4,192,1536]{2,1,0:T(8,128)(2,1)} async-done(((bf16[4,192,1536]{2,1,0:T(8,128)(2,1)}), bf16[4,192,1536]{2,1,0:T(8,128)(2,1)}, u32[]{:S(2)}, u32[]{:S(2)}) %all-to-all-start.4) | async-done | bytes 2359328 | tf_op jit(solution)/shard_map/all_to_all | solution.py:90
  359.5 3.1 convert_reduce_fusion
  362.6 7.7 %query_grads.1 = (bf16[384,1536]{1,0:T(8,128)(2,1)}, bf16[384,1536]{1,0:T(8,128)(2,1)}, bf16[2,384,1536]{2,1,0:T(8,128)(2,1)}, f32[384,1536]{1,0:T(8,128)}) custom-call(s32[3]{0:T(128)} %pad_add_fusion.refs_0_.place, bf16[768,384]{1,0:T(8,128)(2,1)} %get-tuple-element.155.dq_ref, bf16[1536,384]{1,0:T(8,128)(2,1)} %get-tuple-element.158.norm_t.refs_4_, ...), custom_call_target="tpu_custom_call" | custom-call | flops 1 | bytes 1 | tf_op jit(solution)/shard_map/query_grads/pallas_call | solution.py:497
  370.3 4.6 all-to-all-start.5
  374.9 2.4 collective-permute-done.26.refs_2_
  377.3 5.4 %fusion.11 = (bf16[3,768,256]{2,1,0:T(8,128)(2,1)S(1)}, bf16[3,768,256]{2,1,0:T(8,128)(2,1)}) fusion(bf16[4,3,768,256]{3,2,1,0:T(8,128)(2,1)} %collective-permute-done.25.refs_1_.refs_5_, bf16[2,3,768,256]{3,2,1,0:T(8,128)(2,1)} %collective-permute-done.27.refs_6_, bf16[4,3,768,256]{3,2,1,0:T(8,128)(2,1)} %get-tuple-element.163.refs_0_.refs_4_, ...), kind=kLoop, calls=%fused_computation.22 | loop fusion | flops 7077888 | bytes 9437184 | tf_op jit(solution)/shard_map/convert_element_type | solution.py:834
  382.8 1.6 fusion
  385.5 26.4 %collective-permute-done.28 = bf16[384,1536]{1,0:T(8,128)(2,1)S(1)} collective-permute-done((bf16[384,1536]{1,0:T(8,128)(2,1)S(1)}, bf16[384,1536]{1,0:T(8,128)(2,1)S(1)}, u32[]{:S(2)}, u32[]{:S(2)}) %collective-permute-start.28) | collective-permute-done | bytes 1179680 | tf_op jit(solution)/shard_map/ppermute | solution.py:52
  411.9 2.7 add_convert_fusion.2
  415.8 6.5 %key_grads.1 = (bf16[384,640]{1,0:T(8,128)(2,1)}, bf16[384,640]{1,0:T(8,128)(2,1)}, bf16[2,384,640]{2,1,0:T(8,128)(2,1)}, f32[192,1536]{1,0:T(8,128)}, bf16[192,1536]{1,0:T(8,128)(2,1)}) custom-call(s32[3]{0:T(128)} %pad_add_fusion.refs_0_.place, bf16[4,512,384]{2,1,0:T(8,128)(2,1)} %all-to-all-done.5.refs_1_, f32[32,384]{1,0:T(8,128)} %get-tuple-element.291.refs_2_.refs_5_, ...), custom_call_target="tpu_custom_call" | custom-call | flops 1 | bytes 1 | tf_op jit(solution)/shard_map/key_grads/pallas_call | solution.py:550
  422.4 4.5 all-to-all-start.6
  427.7 13.9 %collective-permute-done.31 = bf16[3,768,256]{2,1,0:T(8,128)(2,1)} collective-permute-done((bf16[3,768,256]{2,1,0:T(8,128)(2,1)}, bf16[3,768,256]{2,1,0:T(8,128)(2,1)}, u32[]{:S(2)}, u32[]{:S(2)}) %collective-permute-start.31) | collective-permute-done | bytes 1179680 | tf_op jit(solution)/shard_map/ppermute | solution.py:52
  441.6 1.3 fusion.12
  446.4 10.0 %step_in.1 = (f32[1,2,1536,256]{3,2,1,0:T(8,128)}, f32[1,2,1536,256]{3,2,1,0:T(8,128)}, f32[1,2,1536,256]{3,2,1,0:T(8,128)}) custom-call(bf16[4,3,768,256]{3,2,1,0:T(8,128)(2,1)} %get-tuple-element.163.refs_0_.refs_4_, bf16[4,3,768,256]{3,2,1,0:T(8,128)(2,1)} %collective-permute-done.25.refs_1_.refs_5_, bf16[2,3,768,256]{3,2,1,0:T(8,128)(2,1)} %copy-done.6, ...), custom_call_target="tpu_custom_call" | custom-call | flops 1 | bytes 1 | tf_op jit(solution)/shard_map/step_in/pallas_call | solution.py:865
  456.5 2.7 add_convert_fusion.6
  459.2 4.3 all-to-all-start.7
  463.5 1.9 fusion.8.refs_0_
  465.4 1.6 collective-permute-start.35
  468.9 2.4 join.2
  472.2 2.8 step_out.1
  475.0 5.5 %step_down.1 = (f32[1,256,1536]{2,1,0:T(8,128)}, f32[1,256,1536]{2,1,0:T(8,128)}, f32[1,256,1536]{2,1,0:T(8,128)}) custom-call(bf16[4,3,768,256]{3,2,1,0:T(8,128)(2,1)} %get-tuple-element.163.refs_0_.refs_4_, bf16[4,3,768,256]{3,2,1,0:T(8,128)(2,1)} %collective-permute-done.25.refs_1_.refs_5_, bf16[2,3,768,256]{3,2,1,0:T(8,128)(2,1)} %copy-done.6, ...), custom_call_target="tpu_custom_call" | custom-call | flops 1 | bytes 1 | tf_op jit(solution)/shard_map/step_down/pallas_call | solution.py:906
  482.3 2.3 join.3
  487.2 3.3 step_qkv.1
  (183 shorter events, 36.9 us)
Async XLA Ops:
  22.8 3.5 copy-start.24
  22.8 13.5 %collective-permute-start = (bf16[384,640]{1,0:T(8,128)(2,1)}, bf16[384,640]{1,0:T(8,128)(2,1)}, u32[]{:S(2)}, u32[]{:S(2)}) collective-permute-start(bf16[384,640]{1,0:T(8,128)(2,1)} %bitcast.6.refs_4_), channel_id=1, source_target_pairs={{0,16},{8,24},{16,0},{24,8},{1,17},{9,25},{17,1},{25,9},{2,18},{10... | collective-permute-start | bytes 1474568 | tf_op jit(solution)/shard_map/ppermute | solution.py:52
  29.7 31.8 %all-to-all-start.3 = ((bf16[4,96,1536]{2,1,0:T(8,128)(2,1)}), bf16[4,96,1536]{2,1,0:T(8,128)(2,1)}, u32[]{:S(2)}, u32[]{:S(2)}) async-start(bf16[4,96,1536]{2,1,0:T(8,128)(2,1)} %both_shard.1), calls=%async_computation.3 | async-start | bytes 2359296 | tf_op jit(solution)/shard_map/all_to_all | solution.py:90
  36.2 3.2 collective-permute-start.1
  36.3 3.1 collective-permute-start.2
  39.4 53.2 %collective-permute-start.5 = (bf16[2,3,768,256]{3,2,1,0:T(8,128)(2,1)}, bf16[2,3,768,256]{3,2,1,0:T(8,128)(2,1)S(1)}, u32[]{:S(2)}, u32[]{:S(2)}) collective-permute-start(bf16[2,3,768,256]{3,2,1,0:T(8,128)(2,1)} %pad_maximum_fusion.refs_0_.refs_5_.refs_2_), channel_id=1, source_target_pairs={{0,16},{8,24},{16,0},{24,8},{1,17},{9,25},{17,1},{25,9},{2,18},{10... | collective-permute-start | bytes 7077896 | tf_op jit(solution)/shard_map/ppermute | solution.py:52
  61.5 31.6 %copy-start.37 = (s32[384,8]{0,1:T(8,128)S(1)}, s32[384,8]{0,1:T(8,128)}, u32[]{:S(2)}) copy-start(s32[384,8]{0,1:T(8,128)} %param.23) | copy-start | bytes 36868
  61.5 32.5 %copy-start.38 = (f32[384,8]{0,1:T(8,128)S(1)}, f32[384,8]{0,1:T(8,128)}, u32[]{:S(2)}) copy-start(f32[384,8]{0,1:T(8,128)} %param.24) | copy-start | bytes 36868
  61.5 41.0 %all-to-all-start.1 = ((bf16[4,512,384]{2,1,0:T(8,128)(2,1)}), bf16[4,512,384]{2,1,0:T(8,128)(2,1)}, u32[]{:S(2)}, u32[]{:S(2)}) async-start(bf16[4,512,384]{2,1,0:T(8,128)(2,1)} %get-tuple-element.110), calls=%async_computation.1 | async-start | bytes 3145728 | tf_op jit(solution)/shard_map/all_to_all | solution.py:90
  66.0 54.3 %collective-permute-start.4 = (bf16[2,3,768,256]{3,2,1,0:T(8,128)(2,1)}, bf16[2,3,768,256]{3,2,1,0:T(8,128)(2,1)}, u32[]{:S(2)}, u32[]{:S(2)}) collective-permute-start(bf16[2,3,768,256]{3,2,1,0:T(8,128)(2,1)} %pad_maximum_fusion.refs_0_.refs_5_.refs_2_), channel_id=1, source_target_pairs={{0,1},{1,0},{2,3},{3,2},{4,5},{5,4},{6,7},{7,6},{8,9},{9,8},{10,11... | collective-permute-start | bytes 7077896 | tf_op jit(solution)/shard_map/ppermute | solution.py:52
  67.6 57.9 %collective-permute-start.3 = (bf16[2,3,768,256]{3,2,1,0:T(8,128)(2,1)}, bf16[2,3,768,256]{3,2,1,0:T(8,128)(2,1)}, u32[]{:S(2)}, u32[]{:S(2)}) collective-permute-start(bf16[2,3,768,256]{3,2,1,0:T(8,128)(2,1)} %pad_maximum_fusion.refs_0_.refs_5_.refs_2_), channel_id=1, source_target_pairs={{0,8},{8,0},{16,24},{24,16},{1,9},{9,1},{17,25},{25,17},{2,10},{10... | collective-permute-start | bytes 7077896 | tf_op jit(solution)/shard_map/ppermute | solution.py:52
  92.6 6.1 %copy-start.1 = (bf16[2,3,768,256]{3,2,1,0:T(8,128)(2,1)}, bf16[2,3,768,256]{3,2,1,0:T(8,128)(2,1)S(1)}, u32[]{:S(2)}) copy-start(bf16[2,3,768,256]{3,2,1,0:T(8,128)(2,1)S(1)} %collective-permute-done.5.refs_2_.refs_7_.refs_4_) | copy-start | bytes 7077892
  92.6 27.1 %collective-permute-start.6 = (bf16[384,1536]{1,0:T(8,128)(2,1)}, bf16[384,1536]{1,0:T(8,128)(2,1)}, u32[]{:S(2)}, u32[]{:S(2)}) collective-permute-start(bf16[384,1536]{1,0:T(8,128)(2,1)} %bitcast.16.refs_4_), channel_id=1, source_target_pairs={{0,16},{8,24},{16,0},{24,8},{1,17},{9,25},{17,1},{25,9},{2,18},{10... | collective-permute-start | bytes 3538952 | tf_op jit(solution)/shard_map/ppermute | solution.py:52
  102.5 61.4 %all-to-all-start.2 = ((bf16[4,192,1664]{2,1,0:T(8,128)(2,1)}), bf16[4,192,1664]{2,1,0:T(8,128)(2,1)S(1)}, u32[]{:S(2)}, u32[]{:S(2)}) async-start(bf16[4,192,1664]{2,1,0:T(8,128)(2,1)} %row_copies.1), calls=%async_computation.2 | async-start | bytes 5111808 | tf_op jit(solution)/shard_map/all_to_all | solution.py:90
  106.2 19.8 %collective-permute-start.7 = (bf16[384,1536]{1,0:T(8,128)(2,1)}, bf16[384,1536]{1,0:T(8,128)(2,1)}, u32[]{:S(2)}, u32[]{:S(2)}) collective-permute-start(bf16[384,1536]{1,0:T(8,128)(2,1)} %bitcast.16.refs_4_), channel_id=1, source_target_pairs={{0,8},{8,0},{16,24},{24,16},{1,9},{9,1},{17,25},{25,17},{2,10},{10... | collective-permute-start | bytes 3538952 | tf_op jit(solution)/shard_map/ppermute | solution.py:52
  119.7 6.2 %collective-permute-start.8 = (bf16[384,1536]{1,0:T(8,128)(2,1)}, bf16[384,1536]{1,0:T(8,128)(2,1)}, u32[]{:S(2)}, u32[]{:S(2)}) collective-permute-start(bf16[384,1536]{1,0:T(8,128)(2,1)} %collective-permute-done.6.refs_5_), channel_id=1, source_target_pairs={{0,8},{8,0},{16,24},{24,16},{1,9},{9,1},{17,25},{25,17},{2,10},{10... | collective-permute-start | bytes 3538952 | tf_op jit(solution)/shard_map/ppermute | solution.py:52
  123.9 29.9 %collective-permute-start.11 = (bf16[1,3,768,256]{3,2,1,0:T(8,128)(2,1)}, bf16[1,3,768,256]{3,2,1,0:T(8,128)(2,1)}, u32[]{:S(2)}, u32[]{:S(2)}) collective-permute-start(bf16[1,3,768,256]{3,2,1,0:T(8,128)(2,1)} %slice.100), channel_id=1, source_target_pairs={{0,1},{1,0},{2,3},{3,2},{4,5},{5,4},{6,7},{7,6},{8,9},{9,8},{10,11... | collective-permute-start | bytes 3538952 | tf_op jit(solution)/shard_map/ppermute | solution.py:52
  125.4 28.4 %collective-permute-start.13 = (bf16[1,3,768,256]{3,2,1,0:T(8,128)(2,1)}, bf16[1,3,768,256]{3,2,1,0:T(8,128)(2,1)}, u32[]{:S(2)}, u32[]{:S(2)}) collective-permute-start(bf16[1,3,768,256]{3,2,1,0:T(8,128)(2,1)} %slice.101), channel_id=1, source_target_pairs={{0,16},{8,24},{16,0},{24,8},{1,17},{9,25},{17,1},{25,9},{2,18},{10... | collective-permute-start | bytes 3538952 | tf_op jit(solution)/shard_map/ppermute | solution.py:52
  152.2 11.7 %collective-permute-start.10 = (bf16[2,3,768,256]{3,2,1,0:T(8,128)(2,1)}, bf16[2,3,768,256]{3,2,1,0:T(8,128)(2,1)}, u32[]{:S(2)}, u32[]{:S(2)}) collective-permute-start(bf16[2,3,768,256]{3,2,1,0:T(8,128)(2,1)} %copy-done.1), channel_id=1, source_target_pairs={{0,8},{8,0},{16,24},{24,16},{1,9},{9,1},{17,25},{25,17},{2,10},{10... | collective-permute-start | bytes 7077896 | tf_op jit(solution)/shard_map/ppermute | solution.py:52
  152.2 11.6 %collective-permute-start.9 = (bf16[2,3,768,256]{3,2,1,0:T(8,128)(2,1)}, bf16[2,3,768,256]{3,2,1,0:T(8,128)(2,1)}, u32[]{:S(2)}, u32[]{:S(2)}) collective-permute-start(bf16[2,3,768,256]{3,2,1,0:T(8,128)(2,1)} %collective-permute-done.4.refs_1_.refs_6_.refs_3_), channel_id=1, source_target_pairs={{0,8},{8,0},{16,24},{24,16},{1,9},{9,1},{17,25},{25,17},{2,10},{10... | collective-permute-start | bytes 7077896 | tf_op jit(solution)/shard_map/ppermute | solution.py:52
  153.8 8.3 %collective-permute-start.14 = (bf16[1,3,768,256]{3,2,1,0:T(8,128)(2,1)}, bf16[1,3,768,256]{3,2,1,0:T(8,128)(2,1)}, u32[]{:S(2)}, u32[]{:S(2)}) collective-permute-start(bf16[1,3,768,256]{3,2,1,0:T(8,128)(2,1)} %collective-permute-done.13.refs_4_.refs_9_.refs_6_), channel_id=1, source_target_pairs={{0,8},{8,0},{16,24},{24,16},{1,9},{9,1},{17,25},{25,17},{2,10},{10... | collective-permute-start | bytes 3538952 | tf_op jit(solution)/shard_map/ppermute | solution.py:52
  153.8 10.0 %collective-permute-start.12 = (bf16[1,3,768,256]{3,2,1,0:T(8,128)(2,1)}, bf16[1,3,768,256]{3,2,1,0:T(8,128)(2,1)}, u32[]{:S(2)}, u32[]{:S(2)}) collective-permute-start(bf16[1,3,768,256]{3,2,1,0:T(8,128)(2,1)} %collective-permute-done.11.refs_3_.refs_8_.refs_5_), channel_id=1, source_target_pairs={{0,8},{8,0},{16,24},{24,16},{1,9},{9,1},{17,25},{25,17},{2,10},{10... | collective-permute-start | bytes 3538952 | tf_op jit(solution)/shard_map/ppermute | solution.py:52
  154.4 15.4 %collective-permute-start.15 = (bf16[192,1536]{1,0:T(8,128)(2,1)}, bf16[192,1536]{1,0:T(8,128)(2,1)S(1)}, u32[]{:S(2)}, u32[]{:S(2)}) collective-permute-start(bf16[192,1536]{1,0:T(8,128)(2,1)} %get-tuple-element.130), channel_id=1, source_target_pairs={{0,1},{1,0},{2,3},{3,2},{4,5},{5,4},{6,7},{7,6},{8,9},{9,8},{10,11... | collective-permute-start | bytes 1769480 | tf_op jit(solution)/shard_map/ppermute | solution.py:52
  163.9 7.7 %copy-start = (bf16[4,192,1664]{2,1,0:T(8,128)(2,1)}, bf16[4,192,1664]{2,1,0:T(8,128)(2,1)S(1)}, u32[]{:S(2)}) copy-start(bf16[4,192,1664]{2,1,0:T(8,128)(2,1)S(1)} %all-to-all-done.2.og_ref.refs_3_.refs_1_) | copy-start | bytes 7667716
  172.7 14.9 %copy-start.8 = (bf16[192,1536]{1,0:T(8,128)(2,1)}, bf16[192,1536]{1,0:T(8,128)(2,1)S(1)}, u32[]{:S(2)}) copy-start(bf16[192,1536]{1,0:T(8,128)(2,1)S(1)} %multiply_convert_fusion.refs_1_.refs_2_) | copy-start | bytes 1769476
  172.7 26.1 %collective-permute-start.16 = (bf16[192,1536]{1,0:T(8,128)(2,1)S(1)}, bf16[192,1536]{1,0:T(8,128)(2,1)S(1)}, u32[]{:S(2)}, u32[]{:S(2)}) collective-permute-start(bf16[192,1536]{1,0:T(8,128)(2,1)S(1)} %multiply_convert_fusion.refs_1_.refs_2_), channel_id=1, source_target_pairs={{0,2},{2,0},{4,6},{6,4},{1,3},{3,1},{5,7},{7,5},{8,10},{10,8},{12,... | collective-permute-start | bytes 1769480 | tf_op jit(solution)/shard_map/ppermute | solution.py:52
  174.8 42.4 %collective-permute-start.17 = (bf16[192,1536]{1,0:T(8,128)(2,1)S(1)}, bf16[192,1536]{1,0:T(8,128)(2,1)S(1)}, u32[]{:S(2)}, u32[]{:S(2)}) collective-permute-start(bf16[192,1536]{1,0:T(8,128)(2,1)S(1)} %multiply_convert_fusion.refs_1_.refs_2_), channel_id=1, source_target_pairs={{0,4},{2,6},{4,0},{6,2},{1,5},{3,7},{5,1},{7,3},{8,12},{10,14},{12... | collective-permute-start | bytes 1769480 | tf_op jit(solution)/shard_map/ppermute | solution.py:52
  177.1 40.1 %collective-permute-start.18 = (bf16[192,1536]{1,0:T(8,128)(2,1)S(1)}, bf16[192,1536]{1,0:T(8,128)(2,1)S(1)}, u32[]{:S(2)}, u32[]{:S(2)}) collective-permute-start(bf16[192,1536]{1,0:T(8,128)(2,1)S(1)} %multiply_convert_fusion.refs_1_.refs_2_), channel_id=1, source_target_pairs={{0,6},{2,4},{4,2},{6,0},{1,7},{3,5},{5,3},{7,1},{8,14},{10,12},{12... | collective-permute-start | bytes 1769480 | tf_op jit(solution)/shard_map/ppermute | solution.py:52
  236.3 60.4 %collective-permute-start.20 = (bf16[192,1536]{1,0:T(8,128)(2,1)}, bf16[192,1536]{1,0:T(8,128)(2,1)S(1)}, u32[]{:S(2)}, u32[]{:S(2)}) collective-permute-start(bf16[192,1536]{1,0:T(8,128)(2,1)} %get-tuple-element.147), channel_id=1, source_target_pairs={{0,4},{2,6},{4,0},{6,2},{1,5},{3,7},{5,1},{7,3},{8,12},{10,14},{12... | collective-permute-start | bytes 1769480 | tf_op jit(solution)/shard_map/ppermute | solution.py:52
  247.5 49.2 %collective-permute-start.21 = (bf16[192,1536]{1,0:T(8,128)(2,1)}, bf16[192,1536]{1,0:T(8,128)(2,1)S(1)}, u32[]{:S(2)}, u32[]{:S(2)}) collective-permute-start(bf16[192,1536]{1,0:T(8,128)(2,1)} %get-tuple-element.148), channel_id=1, source_target_pairs={{0,6},{2,4},{4,2},{6,0},{1,7},{3,5},{5,3},{7,1},{8,14},{10,12},{12... | collective-permute-start | bytes 1769480 | tf_op jit(solution)/shard_map/ppermute | solution.py:52
  249.0 47.7 %collective-permute-start.19 = (bf16[192,1536]{1,0:T(8,128)(2,1)}, bf16[192,1536]{1,0:T(8,128)(2,1)S(1)}, u32[]{:S(2)}, u32[]{:S(2)}) collective-permute-start(bf16[192,1536]{1,0:T(8,128)(2,1)} %get-tuple-element.146), channel_id=1, source_target_pairs={{0,2},{2,0},{4,6},{6,4},{1,3},{3,1},{5,7},{7,5},{8,10},{10,8},{12,... | collective-permute-start | bytes 1769480 | tf_op jit(solution)/shard_map/ppermute | solution.py:52
  286.1 10.8 %copy-start.4 = (f32[192,1536]{1,0:T(8,128)S(1)}, f32[192,1536]{1,0:T(8,128)}, u32[]{:S(2)}) copy-start(f32[192,1536]{1,0:T(8,128)} %copy-done.3) | copy-start | bytes 3538948
  286.1 10.7 %copy-start.20 = (bf16[192,1536]{1,0:T(8,128)(2,1)S(1)}, bf16[192,1536]{1,0:T(8,128)(2,1)}, u32[]{:S(2)}) copy-start(bf16[192,1536]{1,0:T(8,128)(2,1)} %get-tuple-element.145) | copy-start | bytes 1769476
  286.1 10.7 %copy-start.36 = (f32[192]{0:T(256)S(1)}, f32[192]{0:T(256)}, u32[]{:S(2)}) copy-start(f32[192]{0:T(256)} %copy-done.35) | copy-start | bytes 2308
  296.7 8.3 %collective-permute-start.22 = (bf16[4,3,768,256]{3,2,1,0:T(8,128)(2,1)}, bf16[4,3,768,256]{3,2,1,0:T(8,128)(2,1)}, u32[]{:S(2)}, u32[]{:S(2)}) collective-permute-start(bf16[4,3,768,256]{3,2,1,0:T(8,128)(2,1)} %get-tuple-element.150), channel_id=1, source_target_pairs={{0,8},{8,0},{16,24},{24,16},{1,9},{9,1},{17,25},{25,17},{2,10},{10... | collective-permute-start | bytes 14155784 | tf_op jit(solution)/shard_map/ppermute | solution.py:52
  299.9 59.6 %all-to-all-start.4 = ((bf16[4,192,1536]{2,1,0:T(8,128)(2,1)}), bf16[4,192,1536]{2,1,0:T(8,128)(2,1)}, u32[]{:S(2)}, u32[]{:S(2)}) async-start(bf16[4,192,1536]{2,1,0:T(8,128)(2,1)} %mix_rows.1), calls=%async_computation.4 | async-start | bytes 4718592 | tf_op jit(solution)/shard_map/all_to_all | solution.py:90
  310.8 66.5 %collective-permute-start.25 = (bf16[4,3,768,256]{3,2,1,0:T(8,128)(2,1)}, bf16[4,3,768,256]{3,2,1,0:T(8,128)(2,1)}, u32[]{:S(2)}, u32[]{:S(2)}) collective-permute-start(bf16[4,3,768,256]{3,2,1,0:T(8,128)(2,1)} %get-tuple-element.165), channel_id=1, source_target_pairs={{0,8},{8,0},{16,24},{24,16},{1,9},{9,1},{17,25},{25,17},{2,10},{10... | collective-permute-start | bytes 14155784 | tf_op jit(solution)/shard_map/ppermute | solution.py:52
  310.9 16.5 %collective-permute-start.23 = (bf16[192,1536]{1,0:T(8,128)(2,1)}, bf16[192,1536]{1,0:T(8,128)(2,1)}, u32[]{:S(2)}, u32[]{:S(2)}) collective-permute-start(bf16[192,1536]{1,0:T(8,128)(2,1)} %get-tuple-element.278.refs_7_.refs_0_), channel_id=1, source_target_pairs={{0,1},{1,0},{2,3},{3,2},{4,5},{5,4},{6,7},{7,6},{8,9},{9,8},{10,11... | collective-permute-start | bytes 1769480 | tf_op jit(solution)/shard_map/ppermute | solution.py:52
  311.5 65.9 %collective-permute-start.26 = (bf16[2,3,768,256]{3,2,1,0:T(8,128)(2,1)}, bf16[2,3,768,256]{3,2,1,0:T(8,128)(2,1)S(1)}, u32[]{:S(2)}, u32[]{:S(2)}) collective-permute-start(bf16[2,3,768,256]{3,2,1,0:T(8,128)(2,1)} %get-tuple-element.284), channel_id=1, source_target_pairs={{0,1},{1,0},{2,3},{3,2},{4,5},{5,4},{6,7},{7,6},{8,9},{9,8},{10,11... | collective-permute-start | bytes 7077896 | tf_op jit(solution)/shard_map/ppermute | solution.py:52
  313.0 64.3 %collective-permute-start.27 = (bf16[2,3,768,256]{3,2,1,0:T(8,128)(2,1)}, bf16[2,3,768,256]{3,2,1,0:T(8,128)(2,1)}, u32[]{:S(2)}, u32[]{:S(2)}) collective-permute-start(bf16[2,3,768,256]{3,2,1,0:T(8,128)(2,1)} %get-tuple-element.285), channel_id=1, source_target_pairs={{0,16},{8,24},{16,0},{24,8},{1,17},{9,25},{17,1},{25,9},{2,18},{10... | collective-permute-start | bytes 7077896 | tf_op jit(solution)/shard_map/ppermute | solution.py:52
  370.3 12.4 %collective-permute-start.24 = (bf16[2,384,1536]{2,1,0:T(8,128)(2,1)}, bf16[2,384,1536]{2,1,0:T(8,128)(2,1)}, u32[]{:S(2)}, u32[]{:S(2)}) collective-permute-start(bf16[2,384,1536]{2,1,0:T(8,128)(2,1)} %get-tuple-element.162), channel_id=1, source_target_pairs={{0,8},{8,0},{16,24},{24,16},{1,9},{9,1},{17,25},{25,17},{2,10},{10... | collective-permute-start | bytes 7077896 | tf_op jit(solution)/shard_map/ppermute | solution.py:52
  370.3 45.4 %all-to-all-start.5 = ((bf16[4,512,384]{2,1,0:T(8,128)(2,1)}), bf16[4,512,384]{2,1,0:T(8,128)(2,1)}, u32[]{:S(2)}, u32[]{:S(2)}) async-start(bf16[4,512,384]{2,1,0:T(8,128)(2,1)} %get-tuple-element.172), calls=%async_computation.5 | async-start | bytes 3145728 | tf_op jit(solution)/shard_map/all_to_all | solution.py:90
  377.3 5.5 %copy-start.6 = (bf16[2,3,768,256]{3,2,1,0:T(8,128)(2,1)}, bf16[2,3,768,256]{3,2,1,0:T(8,128)(2,1)S(1)}, u32[]{:S(2)}) copy-start(bf16[2,3,768,256]{3,2,1,0:T(8,128)(2,1)S(1)} %collective-permute-done.26.refs_2_) | copy-start | bytes 7077892
  377.3 5.5 %copy-start.22 = (bf16[384,1536]{1,0:T(8,128)(2,1)S(1)}, bf16[384,1536]{1,0:T(8,128)(2,1)}, u32[]{:S(2)}) copy-start(bf16[384,1536]{1,0:T(8,128)(2,1)} %get-tuple-element.170) | copy-start | bytes 3538948
  382.8 29.2 %copy-start.23 = (bf16[384,1536]{1,0:T(8,128)(2,1)S(1)}, bf16[384,1536]{1,0:T(8,128)(2,1)}, u32[]{:S(2)}) copy-start(bf16[384,1536]{1,0:T(8,128)(2,1)} %get-tuple-element.161) | copy-start | bytes 3538948
  384.4 27.5 %collective-permute-start.28 = (bf16[384,1536]{1,0:T(8,128)(2,1)S(1)}, bf16[384,1536]{1,0:T(8,128)(2,1)S(1)}, u32[]{:S(2)}, u32[]{:S(2)}) collective-permute-start(bf16[384,1536]{1,0:T(8,128)(2,1)S(1)} %fusion), channel_id=1, source_target_pairs={{0,16},{8,24},{16,0},{24,8},{1,17},{9,25},{17,1},{25,9},{2,18},{10... | collective-permute-start | bytes 3538952 | tf_op jit(solution)/shard_map/ppermute | solution.py:52
  385.0 30.8 %collective-permute-start.29 = (bf16[3,768,256]{2,1,0:T(8,128)(2,1)S(1)}, bf16[3,768,256]{2,1,0:T(8,128)(2,1)}, u32[]{:S(2)}, u32[]{:S(2)}) collective-permute-start(bf16[3,768,256]{2,1,0:T(8,128)(2,1)S(1)} %get-tuple-element.282), channel_id=1, source_target_pairs={{0,1},{1,0},{2,3},{3,2},{4,5},{5,4},{6,7},{7,6},{8,9},{9,8},{10,11... | collective-permute-start | bytes 3538952 | tf_op jit(solution)/shard_map/ppermute | solution.py:52
  414.6 26.9 %collective-permute-start.31 = (bf16[3,768,256]{2,1,0:T(8,128)(2,1)}, bf16[3,768,256]{2,1,0:T(8,128)(2,1)}, u32[]{:S(2)}, u32[]{:S(2)}) collective-permute-start(bf16[3,768,256]{2,1,0:T(8,128)(2,1)} %get-tuple-element.176), channel_id=1, source_target_pairs={{0,16},{8,24},{16,0},{24,8},{1,17},{9,25},{17,1},{25,9},{2,18},{10... | collective-permute-start | bytes 3538952 | tf_op jit(solution)/shard_map/ppermute | solution.py:52
  422.3 5.3 %collective-permute-start.30 = (bf16[2,384,640]{2,1,0:T(8,128)(2,1)}, bf16[2,384,640]{2,1,0:T(8,128)(2,1)}, u32[]{:S(2)}, u32[]{:S(2)}) collective-permute-start(bf16[2,384,640]{2,1,0:T(8,128)(2,1)} %get-tuple-element.175), channel_id=1, source_target_pairs={{0,8},{8,0},{16,24},{24,16},{1,9},{9,1},{17,25},{25,17},{2,10},{10... | collective-permute-start | bytes 2949128 | tf_op jit(solution)/shard_map/ppermute | solution.py:52
  422.3 4.5 copy-start.5
  422.4 34.1 %all-to-all-start.6 = ((bf16[4,96,1536]{2,1,0:T(8,128)(2,1)}), bf16[4,96,1536]{2,1,0:T(8,128)(2,1)S(1)}, u32[]{:S(2)}, u32[]{:S(2)}) async-start(bf16[4,96,1536]{2,1,0:T(8,128)(2,1)} %bitcast.51), calls=%async_computation.6 | async-start | bytes 2359296 | tf_op jit(solution)/shard_map/all_to_all | solution.py:90
  426.9 16.6 %copy-start.13 = (f32[192,1536]{1,0:T(8,128)S(1)}, f32[192,1536]{1,0:T(8,128)}, u32[]{:S(2)}) copy-start(f32[192,1536]{1,0:T(8,128)} %convert_reduce_fusion) | copy-start | bytes 3538948
  427.1 17.9 %collective-permute-start.34 = (bf16[192,1536]{1,0:T(8,128)(2,1)}, bf16[192,1536]{1,0:T(8,128)(2,1)S(1)}, u32[]{:S(2)}, u32[]{:S(2)}) collective-permute-start(bf16[192,1536]{1,0:T(8,128)(2,1)} %get-tuple-element.185), channel_id=1, source_target_pairs={{0,1},{1,0},{2,3},{3,2},{4,5},{5,4},{6,7},{7,6},{8,9},{9,8},{10,11... | collective-permute-start | bytes 1769480 | tf_op jit(solution)/shard_map/ppermute | solution.py:52
  442.9 13.5 %collective-permute-start.32 = (bf16[384,640]{1,0:T(8,128)(2,1)S(1)}, bf16[384,640]{1,0:T(8,128)(2,1)}, u32[]{:S(2)}, u32[]{:S(2)}) collective-permute-start(bf16[384,640]{1,0:T(8,128)(2,1)S(1)} %fusion.12), channel_id=1, source_target_pairs={{0,16},{8,24},{16,0},{24,8},{1,17},{9,25},{17,1},{25,9},{2,18},{10... | collective-permute-start | bytes 1474568 | tf_op jit(solution)/shard_map/ppermute | solution.py:52
  444.5 24.4 %collective-permute-start.33 = (bf16[192,1536]{1,0:T(8,128)(2,1)}, bf16[192,1536]{1,0:T(8,128)(2,1)}, u32[]{:S(2)}, u32[]{:S(2)}) collective-permute-start(bf16[192,1536]{1,0:T(8,128)(2,1)} %add_convert_fusion.5.refs_0_), channel_id=1, source_target_pairs={{0,1},{1,0},{2,3},{3,2},{4,5},{5,4},{6,7},{7,6},{8,9},{9,8},{10,11... | collective-permute-start | bytes 1769480 | tf_op jit(solution)/shard_map/ppermute | solution.py:52
  456.4 7.1 %copy-start.15 = (f32[192,1536]{1,0:T(8,128)S(1)}, f32[192,1536]{1,0:T(8,128)}, u32[]{:S(2)}) copy-start(f32[192,1536]{1,0:T(8,128)} %get-tuple-element.184) | copy-start | bytes 3538948
  456.4 7.1 %copy-start.40 = (f32[192]{0:T(256)S(1)}, f32[192]{0:T(256)}, u32[]{:S(2)}) copy-start(f32[192]{0:T(256)} %broadcast_multiply_fusion) | copy-start | bytes 2308
  459.2 21.4 %all-to-all-start.7 = ((bf16[4,96,640]{2,1,0:T(8,128)(2,1)}), bf16[4,96,640]{2,1,0:T(8,128)(2,1)}, u32[]{:S(2)}, u32[]{:S(2)}) async-start(bf16[4,96,640]{2,1,0:T(8,128)(2,1)} %bitcast.53), calls=%async_computation.7 | async-start | bytes 983040 | tf_op jit(solution)/shard_map/all_to_all | solution.py:90
  463.5 3.5 copy-start.32
  463.5 4.4 copy-start.33
  465.4 5.8 %copy-start.19 = (bf16[192,1536]{1,0:T(8,128)(2,1)}, bf16[192,1536]{1,0:T(8,128)(2,1)S(1)}, u32[]{:S(2)}) copy-start(bf16[192,1536]{1,0:T(8,128)(2,1)S(1)} %fusion.8.refs_0_) | copy-start | bytes 1769476
  465.4 15.1 %collective-permute-start.35 = (bf16[192,1536]{1,0:T(8,128)(2,1)S(1)}, bf16[192,1536]{1,0:T(8,128)(2,1)S(1)}, u32[]{:S(2)}, u32[]{:S(2)}) collective-permute-start(bf16[192,1536]{1,0:T(8,128)(2,1)S(1)} %fusion.8.refs_0_), channel_id=1, source_target_pairs={{0,1},{1,0},{2,3},{3,2},{4,5},{5,4},{6,7},{7,6},{8,9},{9,8},{10,11... | collective-permute-start | bytes 1769480 | tf_op jit(solution)/shard_map/ppermute | solution.py:52
  481.7 3.8 copy-start.30
  481.7 8.8 %collective-permute-start.36 = (f32[2,96]{1,0:T(2,128)S(1)}, f32[2,96]{1,0:T(2,128)S(1)}, u32[]{:S(2)}, u32[]{:S(2)}) collective-permute-start(f32[2,96]{1,0:T(2,128)S(1)} %bitcast.54), channel_id=1, source_target_pairs={{0,1},{1,0},{2,3},{3,2},{4,5},{5,4},{6,7},{7,6},{8,9},{9,8},{10,11... | collective-permute-start | bytes 2312 | tf_op jit(solution)/shard_map/ppermute | solution.py:52
  (24 other events, 49.6 us)

commit v5 on v4

--- a/solution.py
+++ b/solution.py
@@ -294,7 +294,7 @@
         out_specs=[vmem_spec()] * 2,
         scratch_shapes=[pltpu.SemaphoreType.DMA((len(shards),))],
         compiler_params=params(),
-        cost_estimate=cost(2 * rows * width * columns, 8),
+        cost_estimate=cost(1, 1),
         name="project_queries",
     )(place, normed, cosine, sine, *shards)
 
@@ -454,9 +454,7 @@
             pltpu.VMEM((HD, GROUP * rows), low),
         ],
         compiler_params=pltpu.CompilerParams(vmem_limit_bytes=VMEM_LIMIT),
-        cost_estimate=pl.CostEstimate(
-            flops=2 * q_rows * rows * (4 * seq + out_t.shape[0]), bytes_accessed=20 << 20, transcendentals=0
-        ),
+        cost_estimate=pl.CostEstimate(flops=1, bytes_accessed=90 << 20, transcendentals=0),
         name="attend_back",
     )(place, probs, q_t, kv_all, out_t, cosine, sine, *grads)
 
@@ -834,6 +832,25 @@
     return sum(part.astype(jnp.float32) for part in parts).astype(jnp.bfloat16)
 
 
+def pair_kernel(own, core, out):
+    out[...] = (own[...].astype(jnp.float32) + core[...].astype(jnp.float32)).astype(jnp.bfloat16)
+
+
+def pair_sum(own, core, first, count):
+    block = (1, *own.shape[1:])
+    part = pl.BlockSpec(block, lambda i: (first + i, 0, 0, 0))
+    return pl.pallas_call(
+        pair_kernel,
+        grid=(count,),
+        out_shape=jax.ShapeDtypeStruct((count, *own.shape[1:]), own.dtype),
+        in_specs=[part] * 2,
+        out_specs=pl.BlockSpec(block, lambda i: (i, 0, 0, 0)),
+        compiler_params=params(),
+        cost_estimate=cost(1, 1),
+        name="pair_sum",
+    )(own, core)
+
+
 def step_in_kernel(uppers, lowers, *refs):
     up_refs, refs = refs[:uppers], refs[uppers:]
     low_refs, refs = refs[:lowers], refs[lowers:]
@@ -1028,7 +1045,8 @@
     key_near = spread(shard_copies(qkv_weight, norm_gains, True)).reshape(-1, 2 * k_rows + 128)
     key_across = swap(key_near, "fsdp", 2)
     key_shards = [key_near, key_across, swap(key_near, "fsdp", 1), swap(key_across, "fsdp", 1)]
-    both_near = spread(shard_copies(after(qkv_weight, key_near), out_weight, False)).reshape(-1, 2 * q_rows)
+    both_copies = shard_copies(qkv_weight, out_weight, False)
+    both_near = spread(after(both_copies, key_near)).reshape(-1, 2 * q_rows)
 
     down_t = expert_down[0].T[None]
     half = width // 2
@@ -1102,21 +1120,20 @@
     core_leave = swap(after(core_leave, mixes, *come_x), "fsdp", 1)
     come_mix = spread(after(mixes, grad_hidden))
 
-    uppers_out = [
-        total_of(leave[2 * m : 2 * m + 2], core_leave[2 * m : 2 * m + 2]) for m in range(n_tp - 1)
-    ]
-    lower_out = total_of(leave[2 * (n_tp - 1) :], core_leave[2 * (n_tp - 1) :])
+    core_leave = after(core_leave, grad_hidden)
+    uppers_out = [pair_sum(leave, core_leave, 2 * m, 2) for m in range(n_tp - 1)]
+    lower_out = pair_sum(leave, core_leave, 2 * (n_tp - 1), n_tp)
     uppers_in = [swap(uppers_out[m - 1], "tp", m) for m in over_tp[1:]]
     lower_in = swap(lower_out, "fsdp", 2)
 
     dq_t, kv_grads = attend_back(
         after(place, lower_out, *uppers_out), probs, q_t, kv_all, grad_attn, out_t, cosine, sine
     )
-    mixture = jnp.sum(after(come_mix, dq_t).astype(f32), axis=0)
+    come_mix = after(come_mix, dq_t)
     come = spread(kv_grads)
     core_stay = swap(after(core_stay, lower_out), "fsdp", 1)
     query_parts, query_part = query_grads(
-        after(place, mixture), dq_t, norm_t, query_whole, grad_attn, head_t
+        after(place, come_mix), dq_t, norm_t, query_whole, grad_attn, head_t
     )
 
     lower_next = [
@@ -1125,6 +1142,7 @@
     upper_next = total_of(stay[1], core_stay[1], *(after(part, query_part)[1] for part in uppers_in))
     lowers_last = [swap(lower_next[m - 1], "tp", m) for m in over_tp[1:]]
     query_near, query_far = sum_cores(query_parts, upper_next, *lower_next)
+    mixture = jnp.sum(after(come_mix, query_far).astype(f32), axis=0)
     query_near = added(query_near, swap(query_far, "fsdp", 2))
     upper_last = swap(after(upper_next, query_near), "fsdp", 2)
     key_parts, (normed_own, *normed_others) = key_grads(
@@ -1149,9 +1167,10 @@
     out_new = step_out(query_grad, after(out_weight, block_out), out_moment, out_average)
     down_new = step_down(upper_parts, lower_parts, after(expert_down, out_new[0]), down_moment, down_average)
     in_grad = join(place, [after(part, down_new[0]) for part in in_parts])
+    key_grad = after(key_grad, in_grad)
     gains_grad = jnp.sum(key_grad[:, :, 2 * k_rows : 2 * k_rows + 2].astype(f32), axis=0).T
     gains_others = [swap(gains_grad, "tp", m) for m in over_tp[1:]]
-    qkv_new = step_qkv(query_grad, after(key_grad, in_grad), qkv_weight, qkv_moment, qkv_average)
+    qkv_new = step_qkv(query_grad, key_grad, qkv_weight, qkv_moment, qkv_average)
     gains_grad = gains_grad + sum(after(other, qkv_new[0]) for other in gains_others)
     gain_new = advance(norm_gains, gains_grad, gain_moment, gain_average, RATE_GAIN)
     return (block_out, in_grad, *qkv_new, *out_new, *gain_new, *in_new, *down_new)

time: 501 us -> 500 us (level)
  other arithmetic: 38.8 us -> 31.2 us
  Pallas kernels: 197 us -> 204 us
    pallas_call x0 -> x2, Pallas kernels: none -> 7.25 us  [pair_sum(): pl.pallas_call(pair_kernel, grid=(count,), out_shape=jax.ShapeDtypeStruct...]
    convert_element_type x2 -> x1, other arithmetic: 11.2 us -> 5.43 us  [total_of(): sum((part.astype(jnp.float32) for part in parts)).astype(jnp.bfloat16)]
    unnamed x97 -> x103, local copies, waits for them, and re-layouts: 13 us -> 13.8 us
  transfers between devices with their start and end apart: 44 -> 44, of which waited for: 16 -> 17; matrix products, arithmetic and copies ran while one was open for 10% -> 9% of each run, Pallas kernels for 36% -> 38%
where the time goes in v5:
time: 500 us; the launch traced here: 491 us
  Pallas kernels  204 us (41%)
  waiting for transfers between devices  146 us (29%)
  starting transfers between devices  65.5 us (13%)
  other arithmetic  31.2 us (6%)
  local copies, waits for them, and re-layouts  21.8 us (4%)
  blocking collectives  20.5 us (4%)
    ppermute x37, waiting for transfers between devices, swap(): return lax.ppermute(value, axis, [(i, i ^ mask) for i in range(size)])  118 us
    pallas_call x2, Pallas kernels, weight_grads(): pl.pallas_call(functools.partial(weight_kernel, blocks, calls, count), gr...  37.1 us
    pallas_call x2, Pallas kernels, expert_rows(): pl.pallas_call(functools.partial(expert_kernel, masks, experts), grid=(1,...  34.4 us
    ppermute x37, starting transfers between devices, swap(): return lax.ppermute(value, axis, [(i, i ^ mask) for i in range(size)])  33.9 us
    all_to_all x7, starting transfers between devices, spread(): lax.all_to_all(blocks, 'ctx', split_axis=0, concat_axis=0, tiled=True)  31.5 us
    all_to_all x7, waiting for transfers between devices, spread(): lax.all_to_all(blocks, 'ctx', split_axis=0, concat_axis=0, tiled=True)  28.5 us
    pallas_call x1, Pallas kernels, attend_back(): pl.pallas_call(functools.partial(attend_back_kernel, n_ctx), grid=(kv,),...  23.7 us
    pallas_call x1, Pallas kernels, attend(): pl.pallas_call(functools.partial(attend_kernel, n_ctx), grid=(kv,), out_s...  21.1 us
  transfers between devices with their start and end apart: 44, of which 17 were waited for; matrix products, arithmetic and copies ran while one was open for 9% of the time, Pallas kernels for 38%

profile of v5, /device:TPU:0, one launch (start us, length us, event | category | flops | bytes accessed | tf_op | source)
XLA Modules:
  0.0 490.8 jit_solution(2864524867763691815)
XLA Ops:
  0.7 2.0 key_shard.1
  2.7 20.5 %all_to_all.40 = bf16[4,96,640]{2,1,0:T(8,128)(2,1)} all-to-all(bf16[4,96,640]{2,1,0:T(8,128)(2,1)} %key_shard.1), channel_id=1, replica_groups=mesh['fsdp'=4,'ctx'=4,'tp'=2] {'ctx'}, dimensions={0} | all-to-all | bytes 983040 | tf_op jit(solution)/shard_map/all_to_all | solution.py:90
  23.2 1.5 collective-permute-start
  25.6 2.4 both_shard.1
  28.0 1.3 convert.22
  29.3 4.4 all-to-all-start.3
  37.5 1.6 pad_maximum_fusion.refs_0_.refs_5_.refs_2_
  41.6 5.4 %project_keys.1 = (bf16[4,512,384]{2,1,0:T(8,128)(2,1)}, bf16[384,1536]{1,0:T(8,128)(2,1)}, bf16[1536,384]{1,0:T(8,128)(2,1)}, bf16[1536,640]{1,0:T(8,128)(2,1)}, f32[8,1536]{1,0:T(8,128)}) custom-call(s32[3]{0:T(128)} %pad_add_fusion.refs_0_.place, bf16[384,1536]{1,0:T(8,128)(2,1)} %refs_6_.1, f32[32,384]{1,0:T(8,128)} %get-tuple-element.293.refs_2_.refs_5_, ...), custom_call_target="tpu_custom_call" | custom-call | flops 1 | bytes 1 | tf_op jit(solution)/shard_map/project_keys/pallas_call | solution.py:243
  47.0 14.2 %all-to-all-done.3 = bf16[4,96,1536]{2,1,0:T(8,128)(2,1)} async-done(((bf16[4,96,1536]{2,1,0:T(8,128)(2,1)}), bf16[4,96,1536]{2,1,0:T(8,128)(2,1)}, u32[]{:S(2)}, u32[]{:S(2)}) %all-to-all-start.3) | async-done | bytes 1179680 | tf_op jit(solution)/shard_map/all_to_all | solution.py:90
  61.2 4.5 all-to-all-start.1
  65.7 1.6 collective-permute-start.4
  67.3 25.0 %collective-permute-done.5.refs_2_.refs_7_.refs_4_ = bf16[2,3,768,256]{3,2,1,0:T(8,128)(2,1)S(1)} collective-permute-done((bf16[2,3,768,256]{3,2,1,0:T(8,128)(2,1)}, bf16[2,3,768,256]{3,2,1,0:T(8,128)(2,1)S(1)}, u32[]{:S(2)}, u32[]{:S(2)}) %collective-permute-start.5) | collective-permute-done | bytes 2359328 | tf_op jit(solution)/shard_map/ppermute | solution.py:52
  94.6 3.8 row_copies.1
  98.4 3.8 all-to-all-done.1.refs_3_
  102.2 3.6 all-to-all-start.2
  105.9 13.5 %collective-permute-done.6.refs_5_ = bf16[384,1536]{1,0:T(8,128)(2,1)} collective-permute-done((bf16[384,1536]{1,0:T(8,128)(2,1)}, bf16[384,1536]{1,0:T(8,128)(2,1)}, u32[]{:S(2)}, u32[]{:S(2)}) %collective-permute-start.6) | collective-permute-done | bytes 1179680 | tf_op jit(solution)/shard_map/ppermute | solution.py:52
  120.0 2.5 slice.85
  123.6 1.5 collective-permute-start.11
  125.7 5.0 %project_queries.1 = (bf16[768,384]{1,0:T(8,128)(2,1)}, bf16[1536,768]{1,0:T(8,128)(2,1)}) custom-call(s32[3]{0:T(128)} %pad_add_fusion.refs_0_.place, bf16[384,1536]{1,0:T(8,128)(2,1)} %get-tuple-element.119.refs_1_, f32[32,384]{1,0:T(8,128)} %get-tuple-element.293.refs_2_.refs_5_, f32[32,384]{1,0:T(8,128)} %get-tuple-element.292.refs_3_.refs_6_, ...), custom_call_target="tpu_custom_call" | custom-call | flops 1 | bytes 1 | tf_op jit(solution)/shard_map/project_queries/pallas_call | solution.py:287
  130.7 21.1 %attend.1 = (bf16[4,1536,1152]{2,1,0:T(8,128)(2,1)}, bf16[768,384]{1,0:T(8,128)(2,1)}, bf16[512,1536]{1,0:T(8,128)(2,1)}, bf16[1536,768]{1,0:T(8,128)(2,1)}, f32...) custom-call(s32[3]{0:T(128)} %pad_add_fusion.refs_0_.place, s32[1,384]{1,0:T(1,128)} %reduce_sum.75.refs_1_, ...), custom_call_target="tpu_custom_call" | custom-call | flops 2717908992 | bytes 20971520 | tf_op jit(solution)/shard_map/attend/pallas_call | solution.py:363
  155.5 6.4 %collective-permute-done.14.refs_9_.refs_14_.refs_11_ = bf16[1,3,768,256]{3,2,1,0:T(8,128)(2,1)} collective-permute-done((bf16[1,3,768,256]{3,2,1,0:T(8,128)(2,1)}, bf16[1,3,768,256]{3,2,1,0:T(8,128)(2,1)}, u32[]{:S(2)}, u32[]{:S(2)}) %collective-permute-start.14) | collective-permute-done | bytes 1179680 | tf_op jit(solution)/shard_map/ppermute | solution.py:52
  161.9 1.7 collective-permute-done.12.refs_8_.refs_13_.refs_10_
  163.6 5.9 %collective-permute-done.15 = bf16[192,1536]{1,0:T(8,128)(2,1)S(1)} collective-permute-done((bf16[192,1536]{1,0:T(8,128)(2,1)}, bf16[192,1536]{1,0:T(8,128)(2,1)S(1)}, u32[]{:S(2)}, u32[]{:S(2)}) %collective-permute-start.15) | collective-permute-done | bytes 589856 | tf_op jit(solution)/shard_map/ppermute | solution.py:52
  169.5 1.7 multiply_reduce_fusion.2
  172.4 2.0 collective-permute-start.16
  174.5 2.4 collective-permute-start.17
  176.9 10.4 %back_rows.1.refs_4_ = bf16[4,192,2048]{2,1,0:T(8,128)(2,1)} custom-call(bf16[4,192,1664]{2,1,0:T(8,128)(2,1)} %copy-done, bf16[2,3,768,256]{3,2,1,0:T(8,128)(2,1)} %pad_maximum_fusion.refs_0_.refs_5_.refs_2_, bf16[2,3,768,256]{3,2,1,0:T(8,128)(2,1)} %collective-permute-done.4.refs_1_.refs_6_.refs_3_, bf16[2,3,768,256]{3,2,1,0:T(8,128)(2,1)} %copy-done.1, ...), custom_call_target="tpu_custom_call" | custom-call | flops 1 | bytes 1 | tf_op jit(solution)/shard_map/back_rows/pallas_call | solution.py:638
  187.4 11.2 %collective-permute-done.16.refs_2_.refs_3_ = bf16[192,1536]{1,0:T(8,128)(2,1)S(1)} collective-permute-done((bf16[192,1536]{1,0:T(8,128)(2,1)S(1)}, bf16[192,1536]{1,0:T(8,128)(2,1)S(1)}, u32[]{:S(2)}, u32[]{:S(2)}) %collective-permute-start.16) | collective-permute-done | bytes 589856 | tf_op jit(solution)/shard_map/ppermute | solution.py:52
  199.4 17.0 %expert_rows.2 = (bf16[192,1536]{1,0:T(8,128)(2,1)}, bf16[192,1536]{1,0:T(8,128)(2,1)}, bf16[384,2048]{1,0:T(8,128)(2,1)}, bf16[384,2048]{1,0:T(8,128)(2,1)}, bf16[384,2048]{1,0:T(8,128)(2,1)}) custom-call(s32[3]{0:T(128)} %pad_add_fusion.refs_0_.place, bf16[192,1536]{1,0:T(8,128)(2,1)} %copy-done.9, bf16[192,1536]{1,0:T(8,128)(2,1)} %copy-done.12, ...), custom_call_target="tpu_custom_call" | custom-call | flops 1 | bytes 1 | tf_op jit(solution)/shard_map/expert_rows/pallas_call | solution.py:702
  218.6 17.4 %expert_rows.3 = (bf16[192,1536]{1,0:T(8,128)(2,1)}, bf16[192,1536]{1,0:T(8,128)(2,1)}, bf16[384,2048]{1,0:T(8,128)(2,1)}, bf16[384,2048]{1,0:T(8,128)(2,1)}, bf16[384,2048]{1,0:T(8,128)(2,1)}) custom-call(s32[3]{0:T(128)} %pad_add_fusion.refs_0_.place, bf16[192,1536]{1,0:T(8,128)(2,1)} %copy-done.13, bf16[192,1536]{1,0:T(8,128)(2,1)} %copy-done.14, ...), custom_call_target="tpu_custom_call" | custom-call | flops 1 | bytes 1 | tf_op jit(solution)/shard_map/expert_rows/pallas_call | solution.py:702
  236.0 11.2 %collective-permute-start.20 = (bf16[192,1536]{1,0:T(8,128)(2,1)}, bf16[192,1536]{1,0:T(8,128)(2,1)S(1)}, u32[]{:S(2)}, u32[]{:S(2)}) collective-permute-start(bf16[192,1536]{1,0:T(8,128)(2,1)} %get-tuple-element.149), channel_id=1, source_target_pairs={{0,4},{2,6},{4,0},{6,2},{1,5},{3,7},{5,1},{7,3},{8,12},{10,14},{12... | collective-permute-start | bytes 1769480 | tf_op jit(solution)/shard_map/ppermute | solution.py:52
  247.2 1.5 collective-permute-start.21
  248.7 18.5 %weight_grads.2 = (bf16[4,3,768,256]{3,2,1,0:T(8,128)(2,1)}, bf16[4,3,768,256]{3,2,1,0:T(8,128)(2,1)}) custom-call(s32[3]{0:T(128)} %pad_add_fusion.refs_0_.place, bf16[4,192,1664]{2,1,0:T(8,128)(2,1)} %copy-done, bf16[192,1536]{1,0:T(8,128)(2,1)} %copy-done.9, bf16[192,1536]{1,0:T(8,128)(2,1)} %copy-done.12, bf16[192,1536]{1,0:T(8,128)(2,1)} %copy-done.13, ...), custom_call_target="tpu_custom_call" | custom-call | flops 1 | bytes 1 | tf_op jit(solution)/shard_map/weight_grads/pallas_call | solution.py:814
  267.2 18.5 %weight_grads.3 = (bf16[4,3,768,256]{3,2,1,0:T(8,128)(2,1)}, bf16[4,3,768,256]{3,2,1,0:T(8,128)(2,1)}) custom-call(s32[3]{0:T(128)} %pad_add_fusion.refs_0_.place, bf16[4,192,1664]{2,1,0:T(8,128)(2,1)} %copy-done, bf16[192,1536]{1,0:T(8,128)(2,1)} %copy-done.9, bf16[192,1536]{1,0:T(8,128)(2,1)} %copy-done.12, bf16[192,1536]{1,0:T(8,128)(2,1)} %copy-done.13, ...), custom_call_target="tpu_custom_call" | custom-call | flops 1 | bytes 1 | tf_op jit(solution)/shard_map/weight_grads/pallas_call | solution.py:814
  285.8 10.6 %mix_rows.1 = bf16[4,192,1536]{2,1,0:T(8,128)(2,1)} custom-call(s32[3]{0:T(128)} %pad_add_fusion.refs_0_.place, bf16[384,2048]{1,0:T(8,128)(2,1)} %get-tuple-element.135.refs_6_.refs_0_, bf16[384,2048]{1,0:T(8,128)(2,1)} %get-tuple-element.137.refs_7_.refs_1_, bf16[2,3,768,256]{3,2,1,0:T(8,128)(2,1)} %pad_maximum_fusion.refs_0_.refs_5_.refs_2_, ...), custom_call_target="tpu_custom_call" | custom-call | flops 1 | bytes 1 | tf_op jit(solution)/shard_map/mix_rows/pallas_call | solution.py:750
  297.8 1.8 fusion.14
  299.6 4.5 all-to-all-start.4
  304.8 3.6 pair_sum.2
  309.0 3.6 pair_sum.3
  312.7 1.5 collective-permute-start.26
  314.7 10.3 %collective-permute-done.23.refs_8_.refs_1_ = bf16[192,1536]{1,0:T(8,128)(2,1)} collective-permute-done((bf16[192,1536]{1,0:T(8,128)(2,1)}, bf16[192,1536]{1,0:T(8,128)(2,1)}, u32[]{:S(2)}, u32[]{:S(2)}) %collective-permute-start.23) | collective-permute-done | bytes 589856 | tf_op jit(solution)/shard_map/ppermute | solution.py:52
  325.0 23.7 %attend_back.1 = (bf16[768,384]{1,0:T(8,128)(2,1)}, bf16[4,512,384]{2,1,0:T(8,128)(2,1)}) custom-call(s32[3]{0:T(128)} %pad_add_fusion.refs_0_.place, bf16[4,1536,1152]{2,1,0:T(8,128)(2,1)} %get-tuple-element.155.refs_1_, bf16[768,384]{1,0:T(8,128)(2,1)} %get-tuple-element.124.refs_2_, bf16[512,1536]{1,0:T(8,128)(2,1)} %get-tuple-element.156.refs_3_, ...), custom_call_target="tpu_custom_call" | custom-call | flops 1 | bytes 94371840 | tf_op jit(solution)/shard_map/attend_back/pallas_call | solution.py:440
  348.7 10.5 %all-to-all-done.4 = bf16[4,192,1536]{2,1,0:T(8,128)(2,1)} async-done(((bf16[4,192,1536]{2,1,0:T(8,128)(2,1)}), bf16[4,192,1536]{2,1,0:T(8,128)(2,1)}, u32[]{:S(2)}, u32[]{:S(2)}) %all-to-all-start.4) | async-done | bytes 2359328 | tf_op jit(solution)/shard_map/all_to_all | solution.py:90
  359.2 7.7 %query_grads.1 = (bf16[384,1536]{1,0:T(8,128)(2,1)}, bf16[384,1536]{1,0:T(8,128)(2,1)}, bf16[2,384,1536]{2,1,0:T(8,128)(2,1)}, f32[384,1536]{1,0:T(8,128)}) custom-call(s32[3]{0:T(128)} %pad_add_fusion.refs_0_.place, bf16[768,384]{1,0:T(8,128)(2,1)} %get-tuple-element.158.dq_ref, bf16[1536,384]{1,0:T(8,128)(2,1)} %get-tuple-element.161.norm_t.refs_4_, ...), custom_call_target="tpu_custom_call" | custom-call | flops 1 | bytes 1 | tf_op jit(solution)/shard_map/query_grads/pallas_call | solution.py:495
  367.0 4.6 all-to-all-start.5
  371.6 3.3 collective-permute-done.26.refs_2_
  374.9 5.4 %fusion.11 = (bf16[3,768,256]{2,1,0:T(8,128)(2,1)S(1)}, bf16[3,768,256]{2,1,0:T(8,128)(2,1)}) fusion(bf16[4,3,768,256]{3,2,1,0:T(8,128)(2,1)} %collective-permute-done.25.refs_1_.refs_5_, bf16[2,3,768,256]{3,2,1,0:T(8,128)(2,1)} %collective-permute-done.27.refs_6_, bf16[4,3,768,256]{3,2,1,0:T(8,128)(2,1)} %get-tuple-element.166.refs_0_.refs_4_, ...), kind=kLoop, calls=%fused_computation.20 | loop fusion | flops 7077888 | bytes 9437184 | tf_op jit(solution)/shard_map/convert_element_type | solution.py:832
  380.4 1.6 fusion.1
  383.1 26.4 %collective-permute-done.28 = bf16[384,1536]{1,0:T(8,128)(2,1)S(1)} collective-permute-done((bf16[384,1536]{1,0:T(8,128)(2,1)S(1)}, bf16[384,1536]{1,0:T(8,128)(2,1)S(1)}, u32[]{:S(2)}, u32[]{:S(2)}) %collective-permute-start.28) | collective-permute-done | bytes 1179680 | tf_op jit(solution)/shard_map/ppermute | solution.py:52
  409.5 2.7 add_convert_fusion
  413.4 6.5 %key_grads.1 = (bf16[384,640]{1,0:T(8,128)(2,1)}, bf16[384,640]{1,0:T(8,128)(2,1)}, bf16[2,384,640]{2,1,0:T(8,128)(2,1)}, f32[192,1536]{1,0:T(8,128)}, bf16[192,1536]{1,0:T(8,128)(2,1)}) custom-call(s32[3]{0:T(128)} %pad_add_fusion.refs_0_.place, bf16[4,512,384]{2,1,0:T(8,128)(2,1)} %all-to-all-done.5.refs_1_, f32[32,384]{1,0:T(8,128)} %get-tuple-element.293.refs_2_.refs_5_, ...), custom_call_target="tpu_custom_call" | custom-call | flops 1 | bytes 1 | tf_op jit(solution)/shard_map/key_grads/pallas_call | solution.py:548
  420.0 4.6 all-to-all-start.6
  424.7 2.2 convert_reduce_fusion
  427.6 11.6 %collective-permute-done.31 = bf16[3,768,256]{2,1,0:T(8,128)(2,1)} collective-permute-done((bf16[3,768,256]{2,1,0:T(8,128)(2,1)}, bf16[3,768,256]{2,1,0:T(8,128)(2,1)}, u32[]{:S(2)}, u32[]{:S(2)}) %collective-permute-start.31) | collective-permute-done | bytes 1179680 | tf_op jit(solution)/shard_map/ppermute | solution.py:52
  444.0 10.0 %step_in.1 = (f32[1,2,1536,256]{3,2,1,0:T(8,128)}, f32[1,2,1536,256]{3,2,1,0:T(8,128)}, f32[1,2,1536,256]{3,2,1,0:T(8,128)}) custom-call(bf16[4,3,768,256]{3,2,1,0:T(8,128)(2,1)} %get-tuple-element.166.refs_0_.refs_4_, bf16[4,3,768,256]{3,2,1,0:T(8,128)(2,1)} %collective-permute-done.25.refs_1_.refs_5_, bf16[2,3,768,256]{3,2,1,0:T(8,128)(2,1)} %copy-done.6, ...), custom_call_target="tpu_custom_call" | custom-call | flops 1 | bytes 1 | tf_op jit(solution)/shard_map/step_in/pallas_call | solution.py:882
  454.0 2.7 add_convert_fusion.4
  456.7 5.3 %all-to-all-start.7 = ((bf16[4,96,640]{2,1,0:T(8,128)(2,1)}), bf16[4,96,640]{2,1,0:T(8,128)(2,1)}, u32[]{:S(2)}, u32[]{:S(2)}) async-start(bf16[4,96,640]{2,1,0:T(8,128)(2,1)} %bitcast.53), calls=%async_computation.7 | async-start | bytes 983040 | tf_op jit(solution)/shard_map/all_to_all | solution.py:90
  462.1 1.9 fusion.8.refs_0_
  466.4 2.4 join.2
  469.7 2.8 step_out.1
  472.5 5.5 %step_down.1 = (f32[1,256,1536]{2,1,0:T(8,128)}, f32[1,256,1536]{2,1,0:T(8,128)}, f32[1,256,1536]{2,1,0:T(8,128)}) custom-call(bf16[4,3,768,256]{3,2,1,0:T(8,128)(2,1)} %get-tuple-element.166.refs_0_.refs_4_, bf16[4,3,768,256]{3,2,1,0:T(8,128)(2,1)} %collective-permute-done.25.refs_1_.refs_5_, bf16[2,3,768,256]{3,2,1,0:T(8,128)(2,1)} %copy-done.6, ...), custom_call_target="tpu_custom_call" | custom-call | flops 1 | bytes 1 | tf_op jit(solution)/shard_map/step_down/pallas_call | solution.py:923
  478.9 2.3 join.3
  482.3 1.5 collective-permute-start.36
  486.5 3.3 step_qkv.1
  (190 shorter events, 39.0 us)
Async XLA Ops:
  0.7 24.0 %copy-start.25 = (f32[768,96]{0,1:T(8,128)S(1)}, f32[768,96]{0,1:T(8,128)}, u32[]{:S(2)}) copy-start(f32[768,96]{0,1:T(8,128)} %param.26) | copy-start | bytes 884740
  2.7 25.3 %copy-start.7 = (f32[1,2,1536,256]{3,2,1,0:T(8,128)S(1)}, f32[1,2,1536,256]{3,2,1,0:T(8,128)}, u32[]{:S(2)}) copy-start(f32[1,2,1536,256]{3,2,1,0:T(8,128)} %refs_8_) | copy-start | bytes 9437188
  23.2 12.9 %collective-permute-start = (bf16[384,640]{1,0:T(8,128)(2,1)}, bf16[384,640]{1,0:T(8,128)(2,1)}, u32[]{:S(2)}, u32[]{:S(2)}) collective-permute-start(bf16[384,640]{1,0:T(8,128)(2,1)} %bitcast.6.refs_4_), channel_id=1, source_target_pairs={{0,16},{8,24},{16,0},{24,8},{1,17},{9,25},{17,1},{25,9},{2,18},{10... | collective-permute-start | bytes 1474568 | tf_op jit(solution)/shard_map/ppermute | solution.py:52
  29.3 31.9 %all-to-all-start.3 = ((bf16[4,96,1536]{2,1,0:T(8,128)(2,1)}), bf16[4,96,1536]{2,1,0:T(8,128)(2,1)}, u32[]{:S(2)}, u32[]{:S(2)}) async-start(bf16[4,96,1536]{2,1,0:T(8,128)(2,1)} %both_shard.1), calls=%async_computation.3 | async-start | bytes 2359296 | tf_op jit(solution)/shard_map/all_to_all | solution.py:90
  36.0 3.2 collective-permute-start.1
  36.0 3.1 collective-permute-start.2
  39.2 53.1 %collective-permute-start.5 = (bf16[2,3,768,256]{3,2,1,0:T(8,128)(2,1)}, bf16[2,3,768,256]{3,2,1,0:T(8,128)(2,1)S(1)}, u32[]{:S(2)}, u32[]{:S(2)}) collective-permute-start(bf16[2,3,768,256]{3,2,1,0:T(8,128)(2,1)} %pad_maximum_fusion.refs_0_.refs_5_.refs_2_), channel_id=1, source_target_pairs={{0,16},{8,24},{16,0},{24,8},{1,17},{9,25},{17,1},{25,9},{2,18},{10... | collective-permute-start | bytes 7077896 | tf_op jit(solution)/shard_map/ppermute | solution.py:52
  61.2 31.6 %copy-start.39 = (s32[384,8]{0,1:T(8,128)S(1)}, s32[384,8]{0,1:T(8,128)}, u32[]{:S(2)}) copy-start(s32[384,8]{0,1:T(8,128)} %param.23) | copy-start | bytes 36868
  61.2 32.6 %copy-start.40 = (f32[384,8]{0,1:T(8,128)S(1)}, f32[384,8]{0,1:T(8,128)}, u32[]{:S(2)}) copy-start(f32[384,8]{0,1:T(8,128)} %param.24) | copy-start | bytes 36868
  61.2 41.0 %all-to-all-start.1 = ((bf16[4,512,384]{2,1,0:T(8,128)(2,1)}), bf16[4,512,384]{2,1,0:T(8,128)(2,1)}, u32[]{:S(2)}, u32[]{:S(2)}) async-start(bf16[4,512,384]{2,1,0:T(8,128)(2,1)} %get-tuple-element.112), calls=%async_computation.1 | async-start | bytes 3145728 | tf_op jit(solution)/shard_map/all_to_all | solution.py:90
  65.7 54.3 %collective-permute-start.4 = (bf16[2,3,768,256]{3,2,1,0:T(8,128)(2,1)}, bf16[2,3,768,256]{3,2,1,0:T(8,128)(2,1)}, u32[]{:S(2)}, u32[]{:S(2)}) collective-permute-start(bf16[2,3,768,256]{3,2,1,0:T(8,128)(2,1)} %pad_maximum_fusion.refs_0_.refs_5_.refs_2_), channel_id=1, source_target_pairs={{0,1},{1,0},{2,3},{3,2},{4,5},{5,4},{6,7},{7,6},{8,9},{9,8},{10,11... | collective-permute-start | bytes 7077896 | tf_op jit(solution)/shard_map/ppermute | solution.py:52
  67.3 57.8 %collective-permute-start.3 = (bf16[2,3,768,256]{3,2,1,0:T(8,128)(2,1)}, bf16[2,3,768,256]{3,2,1,0:T(8,128)(2,1)}, u32[]{:S(2)}, u32[]{:S(2)}) collective-permute-start(bf16[2,3,768,256]{3,2,1,0:T(8,128)(2,1)} %pad_maximum_fusion.refs_0_.refs_5_.refs_2_), channel_id=1, source_target_pairs={{0,8},{8,0},{16,24},{24,16},{1,9},{9,1},{17,25},{25,17},{2,10},{10... | collective-permute-start | bytes 7077896 | tf_op jit(solution)/shard_map/ppermute | solution.py:52
  92.3 6.1 %copy-start.1 = (bf16[2,3,768,256]{3,2,1,0:T(8,128)(2,1)}, bf16[2,3,768,256]{3,2,1,0:T(8,128)(2,1)S(1)}, u32[]{:S(2)}) copy-start(bf16[2,3,768,256]{3,2,1,0:T(8,128)(2,1)S(1)} %collective-permute-done.5.refs_2_.refs_7_.refs_4_) | copy-start | bytes 7077892
  92.3 27.1 %collective-permute-start.6 = (bf16[384,1536]{1,0:T(8,128)(2,1)}, bf16[384,1536]{1,0:T(8,128)(2,1)}, u32[]{:S(2)}, u32[]{:S(2)}) collective-permute-start(bf16[384,1536]{1,0:T(8,128)(2,1)} %bitcast.16.refs_4_), channel_id=1, source_target_pairs={{0,16},{8,24},{16,0},{24,8},{1,17},{9,25},{17,1},{25,9},{2,18},{10... | collective-permute-start | bytes 3538952 | tf_op jit(solution)/shard_map/ppermute | solution.py:52
  102.2 61.4 %all-to-all-start.2 = ((bf16[4,192,1664]{2,1,0:T(8,128)(2,1)}), bf16[4,192,1664]{2,1,0:T(8,128)(2,1)S(1)}, u32[]{:S(2)}, u32[]{:S(2)}) async-start(bf16[4,192,1664]{2,1,0:T(8,128)(2,1)} %row_copies.1), calls=%async_computation.2 | async-start | bytes 5111808 | tf_op jit(solution)/shard_map/all_to_all | solution.py:90
  105.9 19.8 %collective-permute-start.7 = (bf16[384,1536]{1,0:T(8,128)(2,1)}, bf16[384,1536]{1,0:T(8,128)(2,1)}, u32[]{:S(2)}, u32[]{:S(2)}) collective-permute-start(bf16[384,1536]{1,0:T(8,128)(2,1)} %bitcast.16.refs_4_), channel_id=1, source_target_pairs={{0,8},{8,0},{16,24},{24,16},{1,9},{9,1},{17,25},{25,17},{2,10},{10... | collective-permute-start | bytes 3538952 | tf_op jit(solution)/shard_map/ppermute | solution.py:52
  119.4 6.2 %collective-permute-start.8 = (bf16[384,1536]{1,0:T(8,128)(2,1)}, bf16[384,1536]{1,0:T(8,128)(2,1)}, u32[]{:S(2)}, u32[]{:S(2)}) collective-permute-start(bf16[384,1536]{1,0:T(8,128)(2,1)} %collective-permute-done.6.refs_5_), channel_id=1, source_target_pairs={{0,8},{8,0},{16,24},{24,16},{1,9},{9,1},{17,25},{25,17},{2,10},{10... | collective-permute-start | bytes 3538952 | tf_op jit(solution)/shard_map/ppermute | solution.py:52
  123.6 29.9 %collective-permute-start.11 = (bf16[1,3,768,256]{3,2,1,0:T(8,128)(2,1)}, bf16[1,3,768,256]{3,2,1,0:T(8,128)(2,1)}, u32[]{:S(2)}, u32[]{:S(2)}) collective-permute-start(bf16[1,3,768,256]{3,2,1,0:T(8,128)(2,1)} %slice.84), channel_id=1, source_target_pairs={{0,1},{1,0},{2,3},{3,2},{4,5},{5,4},{6,7},{7,6},{8,9},{9,8},{10,11... | collective-permute-start | bytes 3538952 | tf_op jit(solution)/shard_map/ppermute | solution.py:52
  125.1 28.4 %collective-permute-start.13 = (bf16[1,3,768,256]{3,2,1,0:T(8,128)(2,1)}, bf16[1,3,768,256]{3,2,1,0:T(8,128)(2,1)}, u32[]{:S(2)}, u32[]{:S(2)}) collective-permute-start(bf16[1,3,768,256]{3,2,1,0:T(8,128)(2,1)} %slice.85), channel_id=1, source_target_pairs={{0,16},{8,24},{16,0},{24,8},{1,17},{9,25},{17,1},{25,9},{2,18},{10... | collective-permute-start | bytes 3538952 | tf_op jit(solution)/shard_map/ppermute | solution.py:52
  151.9 11.7 %collective-permute-start.10 = (bf16[2,3,768,256]{3,2,1,0:T(8,128)(2,1)}, bf16[2,3,768,256]{3,2,1,0:T(8,128)(2,1)}, u32[]{:S(2)}, u32[]{:S(2)}) collective-permute-start(bf16[2,3,768,256]{3,2,1,0:T(8,128)(2,1)} %copy-done.1), channel_id=1, source_target_pairs={{0,8},{8,0},{16,24},{24,16},{1,9},{9,1},{17,25},{25,17},{2,10},{10... | collective-permute-start | bytes 7077896 | tf_op jit(solution)/shard_map/ppermute | solution.py:52
  152.0 11.6 %collective-permute-start.9 = (bf16[2,3,768,256]{3,2,1,0:T(8,128)(2,1)}, bf16[2,3,768,256]{3,2,1,0:T(8,128)(2,1)}, u32[]{:S(2)}, u32[]{:S(2)}) collective-permute-start(bf16[2,3,768,256]{3,2,1,0:T(8,128)(2,1)} %collective-permute-done.4.refs_1_.refs_6_.refs_3_), channel_id=1, source_target_pairs={{0,8},{8,0},{16,24},{24,16},{1,9},{9,1},{17,25},{25,17},{2,10},{10... | collective-permute-start | bytes 7077896 | tf_op jit(solution)/shard_map/ppermute | solution.py:52
  153.5 8.3 %collective-permute-start.14 = (bf16[1,3,768,256]{3,2,1,0:T(8,128)(2,1)}, bf16[1,3,768,256]{3,2,1,0:T(8,128)(2,1)}, u32[]{:S(2)}, u32[]{:S(2)}) collective-permute-start(bf16[1,3,768,256]{3,2,1,0:T(8,128)(2,1)} %collective-permute-done.13.refs_4_.refs_9_.refs_6_), channel_id=1, source_target_pairs={{0,8},{8,0},{16,24},{24,16},{1,9},{9,1},{17,25},{25,17},{2,10},{10... | collective-permute-start | bytes 3538952 | tf_op jit(solution)/shard_map/ppermute | solution.py:52
  153.6 10.0 %collective-permute-start.12 = (bf16[1,3,768,256]{3,2,1,0:T(8,128)(2,1)}, bf16[1,3,768,256]{3,2,1,0:T(8,128)(2,1)}, u32[]{:S(2)}, u32[]{:S(2)}) collective-permute-start(bf16[1,3,768,256]{3,2,1,0:T(8,128)(2,1)} %collective-permute-done.11.refs_3_.refs_8_.refs_5_), channel_id=1, source_target_pairs={{0,8},{8,0},{16,24},{24,16},{1,9},{9,1},{17,25},{25,17},{2,10},{10... | collective-permute-start | bytes 3538952 | tf_op jit(solution)/shard_map/ppermute | solution.py:52
  154.1 15.4 %collective-permute-start.15 = (bf16[192,1536]{1,0:T(8,128)(2,1)}, bf16[192,1536]{1,0:T(8,128)(2,1)S(1)}, u32[]{:S(2)}, u32[]{:S(2)}) collective-permute-start(bf16[192,1536]{1,0:T(8,128)(2,1)} %get-tuple-element.132), channel_id=1, source_target_pairs={{0,1},{1,0},{2,3},{3,2},{4,5},{5,4},{6,7},{7,6},{8,9},{9,8},{10,11... | collective-permute-start | bytes 1769480 | tf_op jit(solution)/shard_map/ppermute | solution.py:52
  163.6 7.7 %copy-start = (bf16[4,192,1664]{2,1,0:T(8,128)(2,1)}, bf16[4,192,1664]{2,1,0:T(8,128)(2,1)S(1)}, u32[]{:S(2)}) copy-start(bf16[4,192,1664]{2,1,0:T(8,128)(2,1)S(1)} %all-to-all-done.2.og_ref.refs_3_.refs_1_) | copy-start | bytes 7667716
  172.4 14.9 %copy-start.9 = (bf16[192,1536]{1,0:T(8,128)(2,1)}, bf16[192,1536]{1,0:T(8,128)(2,1)S(1)}, u32[]{:S(2)}) copy-start(bf16[192,1536]{1,0:T(8,128)(2,1)S(1)} %multiply_convert_fusion.refs_1_.refs_2_) | copy-start | bytes 1769476
  172.4 26.1 %collective-permute-start.16 = (bf16[192,1536]{1,0:T(8,128)(2,1)S(1)}, bf16[192,1536]{1,0:T(8,128)(2,1)S(1)}, u32[]{:S(2)}, u32[]{:S(2)}) collective-permute-start(bf16[192,1536]{1,0:T(8,128)(2,1)S(1)} %multiply_convert_fusion.refs_1_.refs_2_), channel_id=1, source_target_pairs={{0,2},{2,0},{4,6},{6,4},{1,3},{3,1},{5,7},{7,5},{8,10},{10,8},{12,... | collective-permute-start | bytes 1769480 | tf_op jit(solution)/shard_map/ppermute | solution.py:52
  174.5 42.4 %collective-permute-start.17 = (bf16[192,1536]{1,0:T(8,128)(2,1)S(1)}, bf16[192,1536]{1,0:T(8,128)(2,1)S(1)}, u32[]{:S(2)}, u32[]{:S(2)}) collective-permute-start(bf16[192,1536]{1,0:T(8,128)(2,1)S(1)} %multiply_convert_fusion.refs_1_.refs_2_), channel_id=1, source_target_pairs={{0,4},{2,6},{4,0},{6,2},{1,5},{3,7},{5,1},{7,3},{8,12},{10,14},{12... | collective-permute-start | bytes 1769480 | tf_op jit(solution)/shard_map/ppermute | solution.py:52
  176.8 40.1 %collective-permute-start.18 = (bf16[192,1536]{1,0:T(8,128)(2,1)S(1)}, bf16[192,1536]{1,0:T(8,128)(2,1)S(1)}, u32[]{:S(2)}, u32[]{:S(2)}) collective-permute-start(bf16[192,1536]{1,0:T(8,128)(2,1)S(1)} %multiply_convert_fusion.refs_1_.refs_2_), channel_id=1, source_target_pairs={{0,6},{2,4},{4,2},{6,0},{1,7},{3,5},{5,3},{7,1},{8,14},{10,12},{12... | collective-permute-start | bytes 1769480 | tf_op jit(solution)/shard_map/ppermute | solution.py:52
  236.0 60.4 %collective-permute-start.20 = (bf16[192,1536]{1,0:T(8,128)(2,1)}, bf16[192,1536]{1,0:T(8,128)(2,1)S(1)}, u32[]{:S(2)}, u32[]{:S(2)}) collective-permute-start(bf16[192,1536]{1,0:T(8,128)(2,1)} %get-tuple-element.149), channel_id=1, source_target_pairs={{0,4},{2,6},{4,0},{6,2},{1,5},{3,7},{5,1},{7,3},{8,12},{10,14},{12... | collective-permute-start | bytes 1769480 | tf_op jit(solution)/shard_map/ppermute | solution.py:52
  247.2 49.2 %collective-permute-start.21 = (bf16[192,1536]{1,0:T(8,128)(2,1)}, bf16[192,1536]{1,0:T(8,128)(2,1)S(1)}, u32[]{:S(2)}, u32[]{:S(2)}) collective-permute-start(bf16[192,1536]{1,0:T(8,128)(2,1)} %get-tuple-element.150), channel_id=1, source_target_pairs={{0,6},{2,4},{4,2},{6,0},{1,7},{3,5},{5,3},{7,1},{8,14},{10,12},{12... | collective-permute-start | bytes 1769480 | tf_op jit(solution)/shard_map/ppermute | solution.py:52
  248.7 47.7 %collective-permute-start.19 = (bf16[192,1536]{1,0:T(8,128)(2,1)}, bf16[192,1536]{1,0:T(8,128)(2,1)S(1)}, u32[]{:S(2)}, u32[]{:S(2)}) collective-permute-start(bf16[192,1536]{1,0:T(8,128)(2,1)} %get-tuple-element.148), channel_id=1, source_target_pairs={{0,2},{2,0},{4,6},{6,4},{1,3},{3,1},{5,7},{7,5},{8,10},{10,8},{12,... | collective-permute-start | bytes 1769480 | tf_op jit(solution)/shard_map/ppermute | solution.py:52
  285.8 10.7 %copy-start.4 = (f32[192,1536]{1,0:T(8,128)S(1)}, f32[192,1536]{1,0:T(8,128)}, u32[]{:S(2)}) copy-start(f32[192,1536]{1,0:T(8,128)} %copy-done.3) | copy-start | bytes 3538948
  285.8 10.7 %copy-start.21 = (bf16[192,1536]{1,0:T(8,128)(2,1)S(1)}, bf16[192,1536]{1,0:T(8,128)(2,1)}, u32[]{:S(2)}) copy-start(bf16[192,1536]{1,0:T(8,128)(2,1)} %get-tuple-element.147) | copy-start | bytes 1769476
  285.8 10.7 %copy-start.38 = (f32[192]{0:T(256)S(1)}, f32[192]{0:T(256)}, u32[]{:S(2)}) copy-start(f32[192]{0:T(256)} %copy-done.37) | copy-start | bytes 2308
  296.4 8.3 %collective-permute-start.22 = (bf16[4,3,768,256]{3,2,1,0:T(8,128)(2,1)}, bf16[4,3,768,256]{3,2,1,0:T(8,128)(2,1)}, u32[]{:S(2)}, u32[]{:S(2)}) collective-permute-start(bf16[4,3,768,256]{3,2,1,0:T(8,128)(2,1)} %get-tuple-element.152), channel_id=1, source_target_pairs={{0,8},{8,0},{16,24},{24,16},{1,9},{9,1},{17,25},{25,17},{2,10},{10... | collective-permute-start | bytes 14155784 | tf_op jit(solution)/shard_map/ppermute | solution.py:52
  299.6 59.6 %all-to-all-start.4 = ((bf16[4,192,1536]{2,1,0:T(8,128)(2,1)}), bf16[4,192,1536]{2,1,0:T(8,128)(2,1)}, u32[]{:S(2)}, u32[]{:S(2)}) async-start(bf16[4,192,1536]{2,1,0:T(8,128)(2,1)} %mix_rows.1), calls=%async_computation.4 | async-start | bytes 4718592 | tf_op jit(solution)/shard_map/all_to_all | solution.py:90
  308.4 66.5 %collective-permute-start.25 = (bf16[4,3,768,256]{3,2,1,0:T(8,128)(2,1)}, bf16[4,3,768,256]{3,2,1,0:T(8,128)(2,1)}, u32[]{:S(2)}, u32[]{:S(2)}) collective-permute-start(bf16[4,3,768,256]{3,2,1,0:T(8,128)(2,1)} %get-tuple-element.168), channel_id=1, source_target_pairs={{0,8},{8,0},{16,24},{24,16},{1,9},{9,1},{17,25},{25,17},{2,10},{10... | collective-permute-start | bytes 14155784 | tf_op jit(solution)/shard_map/ppermute | solution.py:52
  308.5 16.5 %collective-permute-start.23 = (bf16[192,1536]{1,0:T(8,128)(2,1)}, bf16[192,1536]{1,0:T(8,128)(2,1)}, u32[]{:S(2)}, u32[]{:S(2)}) collective-permute-start(bf16[192,1536]{1,0:T(8,128)(2,1)} %get-tuple-element.282.refs_7_.refs_0_), channel_id=1, source_target_pairs={{0,1},{1,0},{2,3},{3,2},{4,5},{5,4},{6,7},{7,6},{8,9},{9,8},{10,11... | collective-permute-start | bytes 1769480 | tf_op jit(solution)/shard_map/ppermute | solution.py:52
  312.7 62.2 %collective-permute-start.26 = (bf16[2,3,768,256]{3,2,1,0:T(8,128)(2,1)}, bf16[2,3,768,256]{3,2,1,0:T(8,128)(2,1)S(1)}, u32[]{:S(2)}, u32[]{:S(2)}) collective-permute-start(bf16[2,3,768,256]{3,2,1,0:T(8,128)(2,1)} %pair_sum.3), channel_id=1, source_target_pairs={{0,1},{1,0},{2,3},{3,2},{4,5},{5,4},{6,7},{7,6},{8,9},{9,8},{10,11... | collective-permute-start | bytes 7077896 | tf_op jit(solution)/shard_map/ppermute | solution.py:52
  314.2 60.7 %collective-permute-start.27 = (bf16[2,3,768,256]{3,2,1,0:T(8,128)(2,1)}, bf16[2,3,768,256]{3,2,1,0:T(8,128)(2,1)}, u32[]{:S(2)}, u32[]{:S(2)}) collective-permute-start(bf16[2,3,768,256]{3,2,1,0:T(8,128)(2,1)} %pair_sum.2), channel_id=1, source_target_pairs={{0,16},{8,24},{16,0},{24,8},{1,17},{9,25},{17,1},{25,9},{2,18},{10... | collective-permute-start | bytes 7077896 | tf_op jit(solution)/shard_map/ppermute | solution.py:52
  367.0 13.4 %collective-permute-start.24 = (bf16[2,384,1536]{2,1,0:T(8,128)(2,1)}, bf16[2,384,1536]{2,1,0:T(8,128)(2,1)}, u32[]{:S(2)}, u32[]{:S(2)}) collective-permute-start(bf16[2,384,1536]{2,1,0:T(8,128)(2,1)} %get-tuple-element.165), channel_id=1, source_target_pairs={{0,8},{8,0},{16,24},{24,16},{1,9},{9,1},{17,25},{25,17},{2,10},{10... | collective-permute-start | bytes 7077896 | tf_op jit(solution)/shard_map/ppermute | solution.py:52
  367.0 46.4 %all-to-all-start.5 = ((bf16[4,512,384]{2,1,0:T(8,128)(2,1)}), bf16[4,512,384]{2,1,0:T(8,128)(2,1)}, u32[]{:S(2)}, u32[]{:S(2)}) async-start(bf16[4,512,384]{2,1,0:T(8,128)(2,1)} %get-tuple-element.176), calls=%async_computation.5 | async-start | bytes 3145728 | tf_op jit(solution)/shard_map/all_to_all | solution.py:90
  374.9 5.5 %copy-start.6 = (bf16[2,3,768,256]{3,2,1,0:T(8,128)(2,1)}, bf16[2,3,768,256]{3,2,1,0:T(8,128)(2,1)S(1)}, u32[]{:S(2)}) copy-start(bf16[2,3,768,256]{3,2,1,0:T(8,128)(2,1)S(1)} %collective-permute-done.26.refs_2_) | copy-start | bytes 7077892
  374.9 5.5 %copy-start.23 = (bf16[384,1536]{1,0:T(8,128)(2,1)S(1)}, bf16[384,1536]{1,0:T(8,128)(2,1)}, u32[]{:S(2)}) copy-start(bf16[384,1536]{1,0:T(8,128)(2,1)} %get-tuple-element.164) | copy-start | bytes 3538948
  380.4 29.2 %copy-start.24 = (bf16[384,1536]{1,0:T(8,128)(2,1)S(1)}, bf16[384,1536]{1,0:T(8,128)(2,1)}, u32[]{:S(2)}) copy-start(bf16[384,1536]{1,0:T(8,128)(2,1)} %get-tuple-element.174) | copy-start | bytes 3538948
  382.0 27.5 %collective-permute-start.28 = (bf16[384,1536]{1,0:T(8,128)(2,1)S(1)}, bf16[384,1536]{1,0:T(8,128)(2,1)S(1)}, u32[]{:S(2)}, u32[]{:S(2)}) collective-permute-start(bf16[384,1536]{1,0:T(8,128)(2,1)S(1)} %fusion.1), channel_id=1, source_target_pairs={{0,16},{8,24},{16,0},{24,8},{1,17},{9,25},{17,1},{25,9},{2,18},{10... | collective-permute-start | bytes 3538952 | tf_op jit(solution)/shard_map/ppermute | solution.py:52
  382.6 30.8 %collective-permute-start.29 = (bf16[3,768,256]{2,1,0:T(8,128)(2,1)S(1)}, bf16[3,768,256]{2,1,0:T(8,128)(2,1)}, u32[]{:S(2)}, u32[]{:S(2)}) collective-permute-start(bf16[3,768,256]{2,1,0:T(8,128)(2,1)S(1)} %get-tuple-element.286), channel_id=1, source_target_pairs={{0,1},{1,0},{2,3},{3,2},{4,5},{5,4},{6,7},{7,6},{8,9},{9,8},{10,11... | collective-permute-start | bytes 3538952 | tf_op jit(solution)/shard_map/ppermute | solution.py:52
  412.2 26.9 %collective-permute-start.31 = (bf16[3,768,256]{2,1,0:T(8,128)(2,1)}, bf16[3,768,256]{2,1,0:T(8,128)(2,1)}, u32[]{:S(2)}, u32[]{:S(2)}) collective-permute-start(bf16[3,768,256]{2,1,0:T(8,128)(2,1)} %get-tuple-element.180), channel_id=1, source_target_pairs={{0,16},{8,24},{16,0},{24,8},{1,17},{9,25},{17,1},{25,9},{2,18},{10... | collective-permute-start | bytes 3538952 | tf_op jit(solution)/shard_map/ppermute | solution.py:52
  419.9 7.6 %collective-permute-start.30 = (bf16[2,384,640]{2,1,0:T(8,128)(2,1)}, bf16[2,384,640]{2,1,0:T(8,128)(2,1)}, u32[]{:S(2)}, u32[]{:S(2)}) collective-permute-start(bf16[2,384,640]{2,1,0:T(8,128)(2,1)} %get-tuple-element.179), channel_id=1, source_target_pairs={{0,8},{8,0},{16,24},{24,16},{1,9},{9,1},{17,25},{25,17},{2,10},{10... | collective-permute-start | bytes 2949128 | tf_op jit(solution)/shard_map/ppermute | solution.py:52
  419.9 4.6 copy-start.5
  420.0 34.0 %all-to-all-start.6 = ((bf16[4,96,1536]{2,1,0:T(8,128)(2,1)}), bf16[4,96,1536]{2,1,0:T(8,128)(2,1)S(1)}, u32[]{:S(2)}, u32[]{:S(2)}) async-start(bf16[4,96,1536]{2,1,0:T(8,128)(2,1)} %bitcast.51), calls=%async_computation.6 | async-start | bytes 2359296 | tf_op jit(solution)/shard_map/all_to_all | solution.py:90
  424.7 14.5 %copy-start.30 = (bf16[384,640]{1,0:T(8,128)(2,1)S(1)}, bf16[384,640]{1,0:T(8,128)(2,1)}, u32[]{:S(2)}) copy-start(bf16[384,640]{1,0:T(8,128)(2,1)} %get-tuple-element.182) | copy-start | bytes 1474564
  427.0 15.6 %collective-permute-start.34 = (bf16[192,1536]{1,0:T(8,128)(2,1)S(1)}, bf16[192,1536]{1,0:T(8,128)(2,1)S(1)}, u32[]{:S(2)}, u32[]{:S(2)}) collective-permute-start(bf16[192,1536]{1,0:T(8,128)(2,1)S(1)} %copy-done.46), channel_id=1, source_target_pairs={{0,1},{1,0},{2,3},{3,2},{4,5},{5,4},{6,7},{7,6},{8,9},{9,8},{10,11... | collective-permute-start | bytes 1769480 | tf_op jit(solution)/shard_map/ppermute | solution.py:52
  440.4 13.6 %collective-permute-start.32 = (bf16[384,640]{1,0:T(8,128)(2,1)S(1)}, bf16[384,640]{1,0:T(8,128)(2,1)}, u32[]{:S(2)}, u32[]{:S(2)}) collective-permute-start(bf16[384,640]{1,0:T(8,128)(2,1)S(1)} %fusion.12), channel_id=1, source_target_pairs={{0,16},{8,24},{16,0},{24,8},{1,17},{9,25},{17,1},{25,9},{2,18},{10... | collective-permute-start | bytes 1474568 | tf_op jit(solution)/shard_map/ppermute | solution.py:52
  441.9 24.5 %collective-permute-start.33 = (bf16[192,1536]{1,0:T(8,128)(2,1)}, bf16[192,1536]{1,0:T(8,128)(2,1)}, u32[]{:S(2)}, u32[]{:S(2)}) collective-permute-start(bf16[192,1536]{1,0:T(8,128)(2,1)} %add_convert_fusion.3.refs_0_), channel_id=1, source_target_pairs={{0,1},{1,0},{2,3},{3,2},{4,5},{5,4},{6,7},{7,6},{8,9},{9,8},{10,11... | collective-permute-start | bytes 1769480 | tf_op jit(solution)/shard_map/ppermute | solution.py:52
  454.0 8.1 %copy-start.16 = (f32[192,1536]{1,0:T(8,128)S(1)}, f32[192,1536]{1,0:T(8,128)}, u32[]{:S(2)}) copy-start(f32[192,1536]{1,0:T(8,128)} %get-tuple-element.188) | copy-start | bytes 3538948
  454.0 8.1 %copy-start.42 = (f32[192]{0:T(256)S(1)}, f32[192]{0:T(256)}, u32[]{:S(2)}) copy-start(f32[192]{0:T(256)} %broadcast_multiply_fusion) | copy-start | bytes 2308
  456.7 24.5 %all-to-all-start.7 = ((bf16[4,96,640]{2,1,0:T(8,128)(2,1)}), bf16[4,96,640]{2,1,0:T(8,128)(2,1)}, u32[]{:S(2)}, u32[]{:S(2)}) async-start(bf16[4,96,640]{2,1,0:T(8,128)(2,1)} %bitcast.53), calls=%async_computation.7 | async-start | bytes 983040 | tf_op jit(solution)/shard_map/all_to_all | solution.py:90
  464.0 4.8 copy-start.20
  464.0 14.1 %collective-permute-start.35 = (bf16[192,1536]{1,0:T(8,128)(2,1)S(1)}, bf16[192,1536]{1,0:T(8,128)(2,1)S(1)}, u32[]{:S(2)}, u32[]{:S(2)}) collective-permute-start(bf16[192,1536]{1,0:T(8,128)(2,1)S(1)} %fusion.8.refs_0_), channel_id=1, source_target_pairs={{0,1},{1,0},{2,3},{3,2},{4,5},{5,4},{6,7},{7,6},{8,9},{9,8},{10,11... | collective-permute-start | bytes 1769480 | tf_op jit(solution)/shard_map/ppermute | solution.py:52
  478.1 5.8 %copy-start.33 = (f32[768,96]{1,0:T(8,128)S(1)}, f32[768,96]{1,0:T(8,128)}, u32[]{:S(2)}) copy-start(f32[768,96]{1,0:T(8,128)} %get-tuple-element.263) | copy-start | bytes 884740
  478.1 6.6 %copy-start.32 = (f32[768,96]{1,0:T(8,128)S(1)}, f32[768,96]{1,0:T(8,128)}, u32[]{:S(2)}) copy-start(f32[768,96]{1,0:T(8,128)} %get-tuple-element.264) | copy-start | bytes 884740
  482.3 7.4 %collective-permute-start.36 = (f32[2,96]{1,0:T(2,128)S(1)}, f32[2,96]{1,0:T(2,128)S(1)}, u32[]{:S(2)}, u32[]{:S(2)}) collective-permute-start(f32[2,96]{1,0:T(2,128)S(1)} %bitcast.54), channel_id=1, source_target_pairs={{0,1},{1,0},{2,3},{3,2},{4,5},{5,4},{6,7},{7,6},{8,9},{9,8},{10,11... | collective-permute-start | bytes 2312 | tf_op jit(solution)/shard_map/ppermute | solution.py:52
  (27 other events, 61.2 us)

commit v6 on v5

--- a/solution.py
+++ b/solution.py
@@ -851,86 +851,39 @@
     )(own, core)
 
 
-def step_in_kernel(uppers, lowers, *refs):
-    up_refs, refs = refs[:uppers], refs[uppers:]
-    low_refs, refs = refs[:lowers], refs[lowers:]
-    weight, moment, average, moment_new, average_new, weight_new, grad = refs
-
-    def gather(parts):
-        total = parts[0][0, 0].astype(jnp.float32)
-        for part in parts[1:]:
-            total += part[0, 0].astype(jnp.float32)
-        grad[...] = total
-
-    @pl.when(pl.program_id(1) == 0)
-    def _():
-        gather(up_refs)
-
-    @pl.when(pl.program_id(1) == 1)
-    def _():
-        gather(low_refs)
-
-    new = advance(weight[0, 0], grad[...], moment[0, 0], average[0, 0], RATE_IN)
-    moment_new[0, 0], average_new[0, 0], weight_new[0, 0] = new
-
-
-def step_in(uppers, lowers, weight, moment, average):
-    half, hidden = uppers[0][0].shape[2:]
-    parts = uppers + lowers
-    specs = [pl.BlockSpec((1, 1, half, hidden), lambda k, j, at=at: (at, k, 0, 0)) for _, at in parts]
-    block = pl.BlockSpec((1, 1, half, hidden), lambda k, j: (0, k, j, 0))
-    return pl.pallas_call(
-        functools.partial(step_in_kernel, len(uppers), len(lowers)),
-        grid=(2, 2),
+def step_experts_kernel(parts, rate, down, *refs):
+    part_refs, refs = refs[:parts], refs[parts:]
+    weight, moment, average = refs[:3]
+    moment_new, average_new, weight_new = refs[-3:]
+    total = part_refs[0][0, 0].astype(jnp.float32)
+    for part in part_refs[1:]:
+        total += part[0, 0].astype(jnp.float32)
+    at = (0,) if down else (0, 0)
+    new = advance(weight[at], total.T if down else total, moment[at], average[at], rate)
+    moment_new[at], average_new[at], weight_new[at] = new
+
+
+def step_experts(parts, lower, weight, moment, average, before):
+    down = weight.ndim == 3
+    half, hidden = parts[0][0].shape[2:]
+    if down:
+        grid, block = (1,), pl.BlockSpec((1, hidden, half), lambda k: (0, 0, lower))
+        specs = [pl.BlockSpec((1, 1, half, hidden), lambda k, at=at: (at, 2, 0, 0)) for _, at in parts]
+    else:
+        grid, block = (2,), pl.BlockSpec((1, 1, half, hidden), lambda k: (0, k, lower, 0))
+        specs = [pl.BlockSpec((1, 1, half, hidden), lambda k, at=at: (at, k, 0, 0)) for _, at in parts]
+    first = len(parts) + 3
+    return pl.pallas_call(
+        functools.partial(step_experts_kernel, len(parts), RATE_DOWN if down else RATE_IN, down),
+        grid=grid,
         out_shape=[jax.ShapeDtypeStruct(weight.shape, jnp.float32)] * 3,
-        in_specs=specs + [block] * 3,
+        in_specs=specs + [block] * 3 + [any_spec()] * len(before),
         out_specs=[block] * 3,
-        scratch_shapes=[pltpu.VMEM((half, hidden), jnp.float32)],
-        compiler_params=params(),
-        cost_estimate=cost(10 * weight.size, 22),
-        name="step_in",
-    )(*(part for part, _ in parts), weight, moment, average)
-
-
-def step_down_kernel(uppers, lowers, *refs):
-    up_refs, refs = refs[:uppers], refs[uppers:]
-    low_refs, refs = refs[:lowers], refs[lowers:]
-    weight, moment, average, moment_new, average_new, weight_new, grad = refs
-
-    def gather(parts):
-        total = parts[0][0, 0].astype(jnp.float32)
-        for part in parts[1:]:
-            total += part[0, 0].astype(jnp.float32)
-        grad[...] = total.T
-
-    @pl.when(pl.program_id(0) == 0)
-    def _():
-        gather(up_refs)
-
-    @pl.when(pl.program_id(0) == 1)
-    def _():
-        gather(low_refs)
-
-    new = advance(weight[0], grad[...], moment[0], average[0], RATE_DOWN)
-    moment_new[0], average_new[0], weight_new[0] = new
-
-
-def step_down(uppers, lowers, weight, moment, average):
-    half, hidden = uppers[0][0].shape[2:]
-    parts = uppers + lowers
-    specs = [pl.BlockSpec((1, 1, half, hidden), lambda j, at=at: (at, 2, 0, 0)) for _, at in parts]
-    block = pl.BlockSpec((1, hidden, half), lambda j: (0, 0, j))
-    return pl.pallas_call(
-        functools.partial(step_down_kernel, len(uppers), len(lowers)),
-        grid=(2,),
-        out_shape=[jax.ShapeDtypeStruct(weight.shape, jnp.float32)] * 3,
-        in_specs=specs + [block] * 3,
-        out_specs=[block] * 3,
-        scratch_shapes=[pltpu.VMEM((hidden, half), jnp.float32)],
-        compiler_params=params(),
-        cost_estimate=cost(10 * weight.size, 12),
-        name="step_down",
-    )(*(part for part, _ in parts), weight, moment, average)
+        input_output_aliases={first + i: i for i in range(len(before))},
+        compiler_params=params(),
+        cost_estimate=cost(1, 1),
+        name="step_down" if down else "step_in",
+    )(*(part for part, _ in parts), weight, moment, average, *before)
 
 
 def sum_first(ref, cols):
@@ -1144,7 +1097,6 @@
     query_near, query_far = sum_cores(query_parts, upper_next, *lower_next)
     mixture = jnp.sum(after(come_mix, query_far).astype(f32), axis=0)
     query_near = added(query_near, swap(query_far, "fsdp", 2))
-    upper_last = swap(after(upper_next, query_near), "fsdp", 2)
     key_parts, (normed_own, *normed_others) = key_grads(
         after(place, query_near, *lowers_last), come, cosine, sine, norm_t, key_whole,
         tokens, query_part, gain_grad_two[None]
@@ -1153,19 +1105,24 @@
     block_parts = to_others((hidden_one + mixture).astype(low))
     inputs = own_half(tokens).astype(f32)
     inverse_one = lax.rsqrt(jnp.mean(inputs * inputs, axis=-1, keepdims=True) + EPSILON)
-    in_parts = to_others(
+    in_own = (
         (grad_hidden + norm_back(grad_normed_one, inputs * inverse_one, inverse_one, gain_one)).astype(low)
     )
-    key_near, key_far = sum_cores(key_parts, upper_last)
+    in_parts = to_others(in_own)
+    key_near, key_far = sum_cores(key_parts)
+    key_come = swap(key_far, "fsdp", 2)
+    upper_last = swap(after(upper_next, key_come), "fsdp", 2)
+    lower_parts = [(stay, 2), (core_stay, 2), (lower_in, 0)] + [(part[None], 0) for part in lowers_last]
+    in_new = step_experts(lower_parts, 1, after(expert_in, key_far, in_own), in_moment, in_average, ())
     query_grad = scatter_rows(query_near)
     upper_parts = [(stay, 0), (core_stay, 0)] + [(part, 0) for part in uppers_in] + [(upper_last[None], 0)]
-    lower_parts = [(stay, 2), (core_stay, 2), (lower_in, 0)] + [(part[None], 0) for part in lowers_last]
-    in_new = step_in(upper_parts, lower_parts, after(expert_in, key_far), in_moment, in_average)
-    key_near = added(key_near, after(swap(key_far, "fsdp", 2), query_grad, in_new[0]))
+    key_near = added(key_near, after(key_come, query_grad, in_new[0]))
     key_grad = scatter_rows(key_near)
     block_out = join(place, [after(part, key_near) for part in block_parts])
     out_new = step_out(query_grad, after(out_weight, block_out), out_moment, out_average)
-    down_new = step_down(upper_parts, lower_parts, after(expert_down, out_new[0]), down_moment, down_average)
+    down_new = step_experts(lower_parts, 1, after(expert_down, out_new[0]), down_moment, down_average, ())
+    in_new = step_experts(upper_parts, 0, after(expert_in, down_new[0]), in_moment, in_average, in_new)
+    down_new = step_experts(upper_parts, 0, after(expert_down, in_new[0]), down_moment, down_average, down_new)
     in_grad = join(place, [after(part, down_new[0]) for part in in_parts])
     key_grad = after(key_grad, in_grad)
     gains_grad = jnp.sum(key_grad[:, :, 2 * k_rows : 2 * k_rows + 2].astype(f32), axis=0).T

time: 500 us -> 521 us (1.042)
  waiting for transfers between devices: 146 us -> 159 us
    ppermute x37, waiting for transfers between devices: 118 us -> 125 us  [swap(): return lax.ppermute(value, axis, [(i, i ^ mask) for i in range(size)])]
    all_to_all x7, waiting for transfers between devices: 28.5 us -> 34 us  [spread(): lax.all_to_all(blocks, 'ctx', split_axis=0, concat_axis=0, tiled=True)]
    pallas_call x2 -> x4, Pallas kernels: 15.5 us -> 18.1 us  [step_experts(): pl.pallas_call(functools.partial(step_experts_kernel, len(parts), RATE_DO...]
    unnamed x103 -> x97, local copies, waits for them, and re-layouts: 13.8 us -> 16.3 us
  transfers between devices with their start and end apart: 44 -> 44, of which waited for: 17 -> 19; matrix products, arithmetic and copies ran while one was open for 9% -> 9% of each run, Pallas kernels for 38% -> 35%
where the time goes in v6:
time: 521 us; the launch traced here: 511 us
  Pallas kernels  207 us (40%)
  waiting for transfers between devices  159 us (31%)
  starting transfers between devices  65.2 us (13%)
  other arithmetic  33.8 us (6%)
  local copies, waits for them, and re-layouts  24.3 us (5%)
  blocking collectives  20.5 us (4%)
    ppermute x37, waiting for transfers between devices, swap(): return lax.ppermute(value, axis, [(i, i ^ mask) for i in range(size)])  125 us
    pallas_call x2, Pallas kernels, weight_grads(): pl.pallas_call(functools.partial(weight_kernel, blocks, calls, count), gr...  37.1 us
    ppermute x37, starting transfers between devices, swap(): return lax.ppermute(value, axis, [(i, i ^ mask) for i in range(size)])  34.8 us
    pallas_call x2, Pallas kernels, expert_rows(): pl.pallas_call(functools.partial(expert_kernel, masks, experts), grid=(1,...  34.5 us
    all_to_all x7, waiting for transfers between devices, spread(): lax.all_to_all(blocks, 'ctx', split_axis=0, concat_axis=0, tiled=True)  34 us
    all_to_all x7, starting transfers between devices, spread(): lax.all_to_all(blocks, 'ctx', split_axis=0, concat_axis=0, tiled=True)  30.4 us
    pallas_call x1, Pallas kernels, attend_back(): pl.pallas_call(functools.partial(attend_back_kernel, n_ctx), grid=(kv,),...  23.7 us
    pallas_call x1, Pallas kernels, attend(): pl.pallas_call(functools.partial(attend_kernel, n_ctx), grid=(kv,), out_s...  21.1 us
  transfers between devices with their start and end apart: 44, of which 19 were waited for; matrix products, arithmetic and copies ran while one was open for 9% of the time, Pallas kernels for 35%

profile of v6, /device:TPU:0, one launch (start us, length us, event | category | flops | bytes accessed | tf_op | source)
XLA Modules:
  0.0 510.8 jit_solution(4177091153303025448)
XLA Ops:
  0.7 2.0 key_shard.1
  2.7 20.5 %all_to_all.40 = bf16[4,96,640]{2,1,0:T(8,128)(2,1)} all-to-all(bf16[4,96,640]{2,1,0:T(8,128)(2,1)} %key_shard.1), channel_id=1, replica_groups=mesh['fsdp'=4,'ctx'=4,'tp'=2] {'ctx'}, dimensions={0} | all-to-all | bytes 983040 | tf_op jit(solution)/shard_map/all_to_all | solution.py:90
  25.6 2.4 both_shard.1
  29.3 4.4 all-to-all-start.3
  37.5 1.6 pad_maximum_fusion.refs_0_.refs_5_.refs_2_
  41.6 5.4 %project_keys.1 = (bf16[4,512,384]{2,1,0:T(8,128)(2,1)}, bf16[384,1536]{1,0:T(8,128)(2,1)}, bf16[1536,384]{1,0:T(8,128)(2,1)}, bf16[1536,640]{1,0:T(8,128)(2,1)}, f32[8,1536]{1,0:T(8,128)}) custom-call(s32[3]{0:T(128)} %pad_add_fusion.refs_0_.place, bf16[384,1536]{1,0:T(8,128)(2,1)} %refs_6_.5, f32[32,384]{1,0:T(8,128)} %get-tuple-element.307.refs_2_.refs_5_, ...), custom_call_target="tpu_custom_call" | custom-call | flops 1 | bytes 1 | tf_op jit(solution)/shard_map/project_keys/pallas_call | solution.py:243
  47.0 14.2 %all-to-all-done.3 = bf16[4,96,1536]{2,1,0:T(8,128)(2,1)} async-done(((bf16[4,96,1536]{2,1,0:T(8,128)(2,1)}), bf16[4,96,1536]{2,1,0:T(8,128)(2,1)}, u32[]{:S(2)}, u32[]{:S(2)}) %all-to-all-start.3) | async-done | bytes 1179680 | tf_op jit(solution)/shard_map/all_to_all | solution.py:90
  61.2 4.5 all-to-all-start.1
  67.3 25.0 %collective-permute-done.5.refs_2_.refs_7_.refs_4_ = bf16[2,3,768,256]{3,2,1,0:T(8,128)(2,1)S(1)} collective-permute-done((bf16[2,3,768,256]{3,2,1,0:T(8,128)(2,1)}, bf16[2,3,768,256]{3,2,1,0:T(8,128)(2,1)S(1)}, u32[]{:S(2)}, u32[]{:S(2)}) %collective-permute-start.5) | collective-permute-done | bytes 2359328 | tf_op jit(solution)/shard_map/ppermute | solution.py:52
  94.6 3.8 row_copies.1
  98.4 3.8 all-to-all-done.1.refs_3_
  102.2 3.6 all-to-all-start.2
  106.0 13.5 %collective-permute-done.6.refs_5_ = bf16[384,1536]{1,0:T(8,128)(2,1)} collective-permute-done((bf16[384,1536]{1,0:T(8,128)(2,1)}, bf16[384,1536]{1,0:T(8,128)(2,1)}, u32[]{:S(2)}, u32[]{:S(2)}) %collective-permute-start.6) | collective-permute-done | bytes 1179680 | tf_op jit(solution)/shard_map/ppermute | solution.py:52
  120.0 2.5 slice.85
  125.7 5.1 project_queries.1
  130.7 21.1 %attend.1 = (bf16[4,1536,1152]{2,1,0:T(8,128)(2,1)}, bf16[768,384]{1,0:T(8,128)(2,1)}, bf16[512,1536]{1,0:T(8,128)(2,1)}, bf16[1536,768]{1,0:T(8,128)(2,1)}, f32...) custom-call(s32[3]{0:T(128)} %pad_add_fusion.refs_0_.place, s32[1,384]{1,0:T(1,128)} %reduce_sum.75.refs_1_, ...), custom_call_target="tpu_custom_call" | custom-call | flops 2717908992 | bytes 20971520 | tf_op jit(solution)/shard_map/attend/pallas_call | solution.py:363
  155.5 6.4 %collective-permute-done.14.refs_9_.refs_14_.refs_11_ = bf16[1,3,768,256]{3,2,1,0:T(8,128)(2,1)} collective-permute-done((bf16[1,3,768,256]{3,2,1,0:T(8,128)(2,1)}, bf16[1,3,768,256]{3,2,1,0:T(8,128)(2,1)}, u32[]{:S(2)}, u32[]{:S(2)}) %collective-permute-start.14) | collective-permute-done | bytes 1179680 | tf_op jit(solution)/shard_map/ppermute | solution.py:52
  161.9 1.7 collective-permute-done.12.refs_8_.refs_13_.refs_10_
  163.6 5.9 %collective-permute-done.15 = bf16[192,1536]{1,0:T(8,128)(2,1)S(1)} collective-permute-done((bf16[192,1536]{1,0:T(8,128)(2,1)}, bf16[192,1536]{1,0:T(8,128)(2,1)S(1)}, u32[]{:S(2)}, u32[]{:S(2)}) %collective-permute-start.15) | collective-permute-done | bytes 589856 | tf_op jit(solution)/shard_map/ppermute | solution.py:52
  169.5 1.7 multiply_reduce_fusion.2
  172.4 2.0 collective-permute-start.16
  174.5 2.4 collective-permute-start.17
  176.9 10.4 %back_rows.1.refs_4_ = bf16[4,192,2048]{2,1,0:T(8,128)(2,1)} custom-call(bf16[4,192,1664]{2,1,0:T(8,128)(2,1)} %copy-done, bf16[2,3,768,256]{3,2,1,0:T(8,128)(2,1)} %pad_maximum_fusion.refs_0_.refs_5_.refs_2_, bf16[2,3,768,256]{3,2,1,0:T(8,128)(2,1)} %collective-permute-done.4.refs_1_.refs_6_.refs_3_, bf16[2,3,768,256]{3,2,1,0:T(8,128)(2,1)} %copy-done.1, ...), custom_call_target="tpu_custom_call" | custom-call | flops 1 | bytes 1 | tf_op jit(solution)/shard_map/back_rows/pallas_call | solution.py:638
  187.4 11.2 %collective-permute-done.16.refs_2_.refs_3_ = bf16[192,1536]{1,0:T(8,128)(2,1)S(1)} collective-permute-done((bf16[192,1536]{1,0:T(8,128)(2,1)S(1)}, bf16[192,1536]{1,0:T(8,128)(2,1)S(1)}, u32[]{:S(2)}, u32[]{:S(2)}) %collective-permute-start.16) | collective-permute-done | bytes 589856 | tf_op jit(solution)/shard_map/ppermute | solution.py:52
  199.4 17.0 %expert_rows.2 = (bf16[192,1536]{1,0:T(8,128)(2,1)}, bf16[192,1536]{1,0:T(8,128)(2,1)}, bf16[384,2048]{1,0:T(8,128)(2,1)}, bf16[384,2048]{1,0:T(8,128)(2,1)}, bf16[384,2048]{1,0:T(8,128)(2,1)}) custom-call(s32[3]{0:T(128)} %pad_add_fusion.refs_0_.place, bf16[192,1536]{1,0:T(8,128)(2,1)} %copy-done.10, bf16[192,1536]{1,0:T(8,128)(2,1)} %copy-done.12, ...), custom_call_target="tpu_custom_call" | custom-call | flops 1 | bytes 1 | tf_op jit(solution)/shard_map/expert_rows/pallas_call | solution.py:702
  218.6 17.4 %expert_rows.3 = (bf16[192,1536]{1,0:T(8,128)(2,1)}, bf16[192,1536]{1,0:T(8,128)(2,1)}, bf16[384,2048]{1,0:T(8,128)(2,1)}, bf16[384,2048]{1,0:T(8,128)(2,1)}, bf16[384,2048]{1,0:T(8,128)(2,1)}) custom-call(s32[3]{0:T(128)} %pad_add_fusion.refs_0_.place, bf16[192,1536]{1,0:T(8,128)(2,1)} %copy-done.13, bf16[192,1536]{1,0:T(8,128)(2,1)} %copy-done.14, ...), custom_call_target="tpu_custom_call" | custom-call | flops 1 | bytes 1 | tf_op jit(solution)/shard_map/expert_rows/pallas_call | solution.py:702
  236.0 11.2 %collective-permute-start.20 = (bf16[192,1536]{1,0:T(8,128)(2,1)}, bf16[192,1536]{1,0:T(8,128)(2,1)S(1)}, u32[]{:S(2)}, u32[]{:S(2)}) collective-permute-start(bf16[192,1536]{1,0:T(8,128)(2,1)} %get-tuple-element.156), channel_id=1, source_target_pairs={{0,4},{2,6},{4,0},{6,2},{1,5},{3,7},{5,1},{7,3},{8,12},{10,14},{12... | collective-permute-start | bytes 1769480 | tf_op jit(solution)/shard_map/ppermute | solution.py:52
  248.7 18.6 %weight_grads.2 = (bf16[4,3,768,256]{3,2,1,0:T(8,128)(2,1)}, bf16[4,3,768,256]{3,2,1,0:T(8,128)(2,1)}) custom-call(s32[3]{0:T(128)} %pad_add_fusion.refs_0_.place, bf16[4,192,1664]{2,1,0:T(8,128)(2,1)} %copy-done, bf16[192,1536]{1,0:T(8,128)(2,1)} %copy-done.10, bf16[192,1536]{1,0:T(8,128)(2,1)} %copy-done.12, bf16[192,1536]{1,0:T(8,128)(2,1)} %copy-done.13, ...), custom_call_target="tpu_custom_call" | custom-call | flops 1 | bytes 1 | tf_op jit(solution)/shard_map/weight_grads/pallas_call | solution.py:814
  267.3 18.5 %weight_grads.3 = (bf16[4,3,768,256]{3,2,1,0:T(8,128)(2,1)}, bf16[4,3,768,256]{3,2,1,0:T(8,128)(2,1)}) custom-call(s32[3]{0:T(128)} %pad_add_fusion.refs_0_.place, bf16[4,192,1664]{2,1,0:T(8,128)(2,1)} %copy-done, bf16[192,1536]{1,0:T(8,128)(2,1)} %copy-done.10, bf16[192,1536]{1,0:T(8,128)(2,1)} %copy-done.12, bf16[192,1536]{1,0:T(8,128)(2,1)} %copy-done.13, ...), custom_call_target="tpu_custom_call" | custom-call | flops 1 | bytes 1 | tf_op jit(solution)/shard_map/weight_grads/pallas_call | solution.py:814
  285.9 10.6 %mix_rows.1 = bf16[4,192,1536]{2,1,0:T(8,128)(2,1)} custom-call(s32[3]{0:T(128)} %pad_add_fusion.refs_0_.place, bf16[384,2048]{1,0:T(8,128)(2,1)} %get-tuple-element.142.refs_6_.refs_0_, bf16[384,2048]{1,0:T(8,128)(2,1)} %get-tuple-element.144.refs_7_.refs_1_, bf16[2,3,768,256]{3,2,1,0:T(8,128)(2,1)} %pad_maximum_fusion.refs_0_.refs_5_.refs_2_, ...), custom_call_target="tpu_custom_call" | custom-call | flops 1 | bytes 1 | tf_op jit(solution)/shard_map/mix_rows/pallas_call | solution.py:750
  297.9 1.8 fusion.14
  299.7 4.5 all-to-all-start.4
  304.8 3.6 pair_sum.2
  309.1 3.6 pair_sum.3
  314.8 10.3 %collective-permute-done.23.refs_8_.refs_1_ = bf16[192,1536]{1,0:T(8,128)(2,1)} collective-permute-done((bf16[192,1536]{1,0:T(8,128)(2,1)}, bf16[192,1536]{1,0:T(8,128)(2,1)}, u32[]{:S(2)}, u32[]{:S(2)}) %collective-permute-start.23) | collective-permute-done | bytes 589856 | tf_op jit(solution)/shard_map/ppermute | solution.py:52
  325.0 23.7 %attend_back.1 = (bf16[768,384]{1,0:T(8,128)(2,1)}, bf16[4,512,384]{2,1,0:T(8,128)(2,1)}) custom-call(s32[3]{0:T(128)} %pad_add_fusion.refs_0_.place, bf16[4,1536,1152]{2,1,0:T(8,128)(2,1)} %get-tuple-element.162.refs_1_, bf16[768,384]{1,0:T(8,128)(2,1)} %get-tuple-element.131.refs_2_, bf16[512,1536]{1,0:T(8,128)(2,1)} %get-tuple-element.163.refs_3_, ...), custom_call_target="tpu_custom_call" | custom-call | flops 1 | bytes 94371840 | tf_op jit(solution)/shard_map/attend_back/pallas_call | solution.py:440
  348.8 10.5 %all-to-all-done.4 = bf16[4,192,1536]{2,1,0:T(8,128)(2,1)} async-done(((bf16[4,192,1536]{2,1,0:T(8,128)(2,1)}), bf16[4,192,1536]{2,1,0:T(8,128)(2,1)}, u32[]{:S(2)}, u32[]{:S(2)}) %all-to-all-start.4) | async-done | bytes 2359328 | tf_op jit(solution)/shard_map/all_to_all | solution.py:90
  359.3 7.7 %query_grads.1 = (bf16[384,1536]{1,0:T(8,128)(2,1)}, bf16[384,1536]{1,0:T(8,128)(2,1)}, bf16[2,384,1536]{2,1,0:T(8,128)(2,1)}, f32[384,1536]{1,0:T(8,128)}) custom-call(s32[3]{0:T(128)} %pad_add_fusion.refs_0_.place, bf16[768,384]{1,0:T(8,128)(2,1)} %get-tuple-element.165.dq_ref, bf16[1536,384]{1,0:T(8,128)(2,1)} %get-tuple-element.168.norm_t.refs_4_, ...), custom_call_target="tpu_custom_call" | custom-call | flops 1 | bytes 1 | tf_op jit(solution)/shard_map/query_grads/pallas_call | solution.py:495
  367.0 4.6 all-to-all-start.5
  371.6 3.4 collective-permute-done.26.refs_2_
  375.1 5.4 %fusion.11 = (bf16[3,768,256]{2,1,0:T(8,128)(2,1)S(1)}, bf16[3,768,256]{2,1,0:T(8,128)(2,1)}) fusion(bf16[4,3,768,256]{3,2,1,0:T(8,128)(2,1)} %collective-permute-done.25.refs_1_, bf16[2,3,768,256]{3,2,1,0:T(8,128)(2,1)S(1)} %collective-permute-done.27.refs_2_, bf16[4,3,768,256]{3,2,1,0:T(8,128)(2,1)} %get-tuple-element.173.refs_0_, ...), kind=kLoop, calls=%fused_computation.20 | loop fusion | flops 7077888 | bytes 9437184 | tf_op jit(solution)/shard_map/convert_element_type | solution.py:832
  380.5 1.6 fusion.1
  383.9 25.8 %collective-permute-done.28 = bf16[384,1536]{1,0:T(8,128)(2,1)S(1)} collective-permute-done((bf16[384,1536]{1,0:T(8,128)(2,1)S(1)}, bf16[384,1536]{1,0:T(8,128)(2,1)S(1)}, u32[]{:S(2)}, u32[]{:S(2)}) %collective-permute-start.28) | collective-permute-done | bytes 1179680 | tf_op jit(solution)/shard_map/ppermute | solution.py:52
  409.7 2.8 add_convert_fusion
  412.4 6.5 %key_grads.1 = (bf16[384,640]{1,0:T(8,128)(2,1)}, bf16[384,640]{1,0:T(8,128)(2,1)}, bf16[2,384,640]{2,1,0:T(8,128)(2,1)}, f32[192,1536]{1,0:T(8,128)}, bf16[192,1536]{1,0:T(8,128)(2,1)}) custom-call(s32[3]{0:T(128)} %pad_add_fusion.refs_0_.place, bf16[4,512,384]{2,1,0:T(8,128)(2,1)} %all-to-all-done.5.refs_1_, f32[32,384]{1,0:T(8,128)} %get-tuple-element.307.refs_2_.refs_5_, ...), custom_call_target="tpu_custom_call" | custom-call | flops 1 | bytes 1 | tf_op jit(solution)/shard_map/key_grads/pallas_call | solution.py:548
  419.5 4.6 all-to-all-start.6
  424.3 3.2 convert_reduce_fusion
  427.5 5.8 %collective-permute-done.32 = bf16[192,1536]{1,0:T(8,128)(2,1)} collective-permute-done((bf16[192,1536]{1,0:T(8,128)(2,1)}, bf16[192,1536]{1,0:T(8,128)(2,1)}, u32[]{:S(2)}, u32[]{:S(2)}) %collective-permute-start.32) | collective-permute-done | bytes 589856 | tf_op jit(solution)/shard_map/ppermute | solution.py:52
  436.7 2.3 fusion.8.refs_0_
  439.0 5.2 %step_in.2 = (f32[1,2,1536,256]{3,2,1,0:T(8,128)}, f32[1,2,1536,256]{3,2,1,0:T(8,128)}, f32[1,2,1536,256]{3,2,1,0:T(8,128)}) custom-call(bf16[4,3,768,256]{3,2,1,0:T(8,128)(2,1)} %get-tuple-element.173.refs_0_, bf16[4,3,768,256]{3,2,1,0:T(8,128)(2,1)} %collective-permute-done.25.refs_1_, bf16[2,3,768,256]{3,2,1,0:T(8,128)(2,1)} %copy-done.7, ...), custom_call_target="tpu_custom_call" | custom-call | flops 1 | bytes 1 | tf_op jit(solution)/shard_map/step_in/pallas_call | solution.py:876
  444.2 3.2 collective-permute-done.31
  447.9 5.4 %all-to-all-done.6.come.query_come = bf16[4,96,1536]{2,1,0:T(8,128)(2,1)S(1)} async-done(((bf16[4,96,1536]{2,1,0:T(8,128)(2,1)}), bf16[4,96,1536]{2,1,0:T(8,128)(2,1)S(1)}, u32[]{:S(2)}, u32[]{:S(2)}) %all-to-all-start.6) | async-done | bytes 1179680 | tf_op jit(solution)/shard_map/all_to_all | solution.py:90
  453.3 2.7 add_convert_fusion.4
  456.0 4.1 all-to-all-start.7
  463.7 1.9 copy.94.moment
  465.6 1.9 copy.95.average
  467.4 10.6 %collective-permute-done.33.refs_1_ = bf16[192,1536]{1,0:T(8,128)(2,1)} collective-permute-done((bf16[192,1536]{1,0:T(8,128)(2,1)S(1)}, bf16[192,1536]{1,0:T(8,128)(2,1)}, u32[]{:S(2)}, u32[]{:S(2)}) %collective-permute-start.33) | collective-permute-done | bytes 589856 | tf_op jit(solution)/shard_map/ppermute | solution.py:52
  478.0 2.3 join.2
  481.3 2.8 step_out.1
  484.1 3.9 step_down.2
  489.0 5.2 %step_in.3 = (f32[1,2,1536,256]{3,2,1,0:T(8,128)}, f32[1,2,1536,256]{3,2,1,0:T(8,128)}, f32[1,2,1536,256]{3,2,1,0:T(8,128)}) custom-call(bf16[4,3,768,256]{3,2,1,0:T(8,128)(2,1)} %get-tuple-element.173.refs_0_, bf16[4,3,768,256]{3,2,1,0:T(8,128)(2,1)} %collective-permute-done.25.refs_1_, ...), custom_call_target="tpu_custom_call", output_to_operand_aliasing={{0}: (7, {}), {1}: (8, {}), {2}: (9, {})} | custom-call | flops 1 | bytes 1 | tf_op jit(solution)/shard_map/step_in/pallas_call | solution.py:876
  494.2 3.9 step_down.3
  498.9 2.3 join.3
  506.5 3.3 step_qkv.1
  (186 shorter events, 49.9 us)
Async XLA Ops:
  0.7 24.0 %copy-start.26 = (f32[768,96]{0,1:T(8,128)S(1)}, f32[768,96]{0,1:T(8,128)}, u32[]{:S(2)}) copy-start(f32[768,96]{0,1:T(8,128)} %param.26) | copy-start | bytes 884740
  2.7 25.3 %copy-start.5 = (f32[1,2,1536,256]{3,2,1,0:T(8,128)S(1)}, f32[1,2,1536,256]{3,2,1,0:T(8,128)}, u32[]{:S(2)}) copy-start(f32[1,2,1536,256]{3,2,1,0:T(8,128)} %refs_4_.2) | copy-start | bytes 9437188
  23.2 12.9 %collective-permute-start = (bf16[384,640]{1,0:T(8,128)(2,1)}, bf16[384,640]{1,0:T(8,128)(2,1)}, u32[]{:S(2)}, u32[]{:S(2)}) collective-permute-start(bf16[384,640]{1,0:T(8,128)(2,1)} %bitcast.6.refs_4_), channel_id=1, source_target_pairs={{0,16},{8,24},{16,0},{24,8},{1,17},{9,25},{17,1},{25,9},{2,18},{10... | collective-permute-start | bytes 1474568 | tf_op jit(solution)/shard_map/ppermute | solution.py:52
  29.3 4.4 copy-start.11
  29.3 32.0 %all-to-all-start.3 = ((bf16[4,96,1536]{2,1,0:T(8,128)(2,1)}), bf16[4,96,1536]{2,1,0:T(8,128)(2,1)}, u32[]{:S(2)}, u32[]{:S(2)}) async-start(bf16[4,96,1536]{2,1,0:T(8,128)(2,1)} %both_shard.1), calls=%async_computation.3 | async-start | bytes 2359296 | tf_op jit(solution)/shard_map/all_to_all | solution.py:90
  36.0 3.2 collective-permute-start.1
  36.1 3.1 collective-permute-start.2
  39.2 53.1 %collective-permute-start.5 = (bf16[2,3,768,256]{3,2,1,0:T(8,128)(2,1)}, bf16[2,3,768,256]{3,2,1,0:T(8,128)(2,1)S(1)}, u32[]{:S(2)}, u32[]{:S(2)}) collective-permute-start(bf16[2,3,768,256]{3,2,1,0:T(8,128)(2,1)} %pad_maximum_fusion.refs_0_.refs_5_.refs_2_), channel_id=1, source_target_pairs={{0,16},{8,24},{16,0},{24,8},{1,17},{9,25},{17,1},{25,9},{2,18},{10... | collective-permute-start | bytes 7077896 | tf_op jit(solution)/shard_map/ppermute | solution.py:52
  61.2 31.6 %copy-start.38 = (s32[384,8]{0,1:T(8,128)S(1)}, s32[384,8]{0,1:T(8,128)}, u32[]{:S(2)}) copy-start(s32[384,8]{0,1:T(8,128)} %param.23) | copy-start | bytes 36868
  61.2 32.6 %copy-start.39 = (f32[384,8]{0,1:T(8,128)S(1)}, f32[384,8]{0,1:T(8,128)}, u32[]{:S(2)}) copy-start(f32[384,8]{0,1:T(8,128)} %param.24) | copy-start | bytes 36868
  61.2 41.0 %all-to-all-start.1 = ((bf16[4,512,384]{2,1,0:T(8,128)(2,1)}), bf16[4,512,384]{2,1,0:T(8,128)(2,1)}, u32[]{:S(2)}, u32[]{:S(2)}) async-start(bf16[4,512,384]{2,1,0:T(8,128)(2,1)} %get-tuple-element.119), calls=%async_computation.1 | async-start | bytes 3145728 | tf_op jit(solution)/shard_map/all_to_all | solution.py:90
  65.7 54.3 %collective-permute-start.4 = (bf16[2,3,768,256]{3,2,1,0:T(8,128)(2,1)}, bf16[2,3,768,256]{3,2,1,0:T(8,128)(2,1)}, u32[]{:S(2)}, u32[]{:S(2)}) collective-permute-start(bf16[2,3,768,256]{3,2,1,0:T(8,128)(2,1)} %pad_maximum_fusion.refs_0_.refs_5_.refs_2_), channel_id=1, source_target_pairs={{0,1},{1,0},{2,3},{3,2},{4,5},{5,4},{6,7},{7,6},{8,9},{9,8},{10,11... | collective-permute-start | bytes 7077896 | tf_op jit(solution)/shard_map/ppermute | solution.py:52
  67.3 57.8 %collective-permute-start.3 = (bf16[2,3,768,256]{3,2,1,0:T(8,128)(2,1)}, bf16[2,3,768,256]{3,2,1,0:T(8,128)(2,1)}, u32[]{:S(2)}, u32[]{:S(2)}) collective-permute-start(bf16[2,3,768,256]{3,2,1,0:T(8,128)(2,1)} %pad_maximum_fusion.refs_0_.refs_5_.refs_2_), channel_id=1, source_target_pairs={{0,8},{8,0},{16,24},{24,16},{1,9},{9,1},{17,25},{25,17},{2,10},{10... | collective-permute-start | bytes 7077896 | tf_op jit(solution)/shard_map/ppermute | solution.py:52
  92.3 6.1 %copy-start.1 = (bf16[2,3,768,256]{3,2,1,0:T(8,128)(2,1)}, bf16[2,3,768,256]{3,2,1,0:T(8,128)(2,1)S(1)}, u32[]{:S(2)}) copy-start(bf16[2,3,768,256]{3,2,1,0:T(8,128)(2,1)S(1)} %collective-permute-done.5.refs_2_.refs_7_.refs_4_) | copy-start | bytes 7077892
  92.3 27.1 %collective-permute-start.6 = (bf16[384,1536]{1,0:T(8,128)(2,1)}, bf16[384,1536]{1,0:T(8,128)(2,1)}, u32[]{:S(2)}, u32[]{:S(2)}) collective-permute-start(bf16[384,1536]{1,0:T(8,128)(2,1)} %bitcast.16.refs_4_), channel_id=1, source_target_pairs={{0,16},{8,24},{16,0},{24,8},{1,17},{9,25},{17,1},{25,9},{2,18},{10... | collective-permute-start | bytes 3538952 | tf_op jit(solution)/shard_map/ppermute | solution.py:52
  102.2 61.4 %all-to-all-start.2 = ((bf16[4,192,1664]{2,1,0:T(8,128)(2,1)}), bf16[4,192,1664]{2,1,0:T(8,128)(2,1)S(1)}, u32[]{:S(2)}, u32[]{:S(2)}) async-start(bf16[4,192,1664]{2,1,0:T(8,128)(2,1)} %row_copies.1), calls=%async_computation.2 | async-start | bytes 5111808 | tf_op jit(solution)/shard_map/all_to_all | solution.py:90
  105.9 19.8 %collective-permute-start.7 = (bf16[384,1536]{1,0:T(8,128)(2,1)}, bf16[384,1536]{1,0:T(8,128)(2,1)}, u32[]{:S(2)}, u32[]{:S(2)}) collective-permute-start(bf16[384,1536]{1,0:T(8,128)(2,1)} %bitcast.16.refs_4_), channel_id=1, source_target_pairs={{0,8},{8,0},{16,24},{24,16},{1,9},{9,1},{17,25},{25,17},{2,10},{10... | collective-permute-start | bytes 3538952 | tf_op jit(solution)/shard_map/ppermute | solution.py:52
  119.4 6.2 %collective-permute-start.8 = (bf16[384,1536]{1,0:T(8,128)(2,1)}, bf16[384,1536]{1,0:T(8,128)(2,1)}, u32[]{:S(2)}, u32[]{:S(2)}) collective-permute-start(bf16[384,1536]{1,0:T(8,128)(2,1)} %collective-permute-done.6.refs_5_), channel_id=1, source_target_pairs={{0,8},{8,0},{16,24},{24,16},{1,9},{9,1},{17,25},{25,17},{2,10},{10... | collective-permute-start | bytes 3538952 | tf_op jit(solution)/shard_map/ppermute | solution.py:52
  123.6 29.9 %collective-permute-start.11 = (bf16[1,3,768,256]{3,2,1,0:T(8,128)(2,1)}, bf16[1,3,768,256]{3,2,1,0:T(8,128)(2,1)}, u32[]{:S(2)}, u32[]{:S(2)}) collective-permute-start(bf16[1,3,768,256]{3,2,1,0:T(8,128)(2,1)} %slice.84), channel_id=1, source_target_pairs={{0,1},{1,0},{2,3},{3,2},{4,5},{5,4},{6,7},{7,6},{8,9},{9,8},{10,11... | collective-permute-start | bytes 3538952 | tf_op jit(solution)/shard_map/ppermute | solution.py:52
  125.1 28.4 %collective-permute-start.13 = (bf16[1,3,768,256]{3,2,1,0:T(8,128)(2,1)}, bf16[1,3,768,256]{3,2,1,0:T(8,128)(2,1)}, u32[]{:S(2)}, u32[]{:S(2)}) collective-permute-start(bf16[1,3,768,256]{3,2,1,0:T(8,128)(2,1)} %slice.85), channel_id=1, source_target_pairs={{0,16},{8,24},{16,0},{24,8},{1,17},{9,25},{17,1},{25,9},{2,18},{10... | collective-permute-start | bytes 3538952 | tf_op jit(solution)/shard_map/ppermute | solution.py:52
  151.9 11.7 %collective-permute-start.10 = (bf16[2,3,768,256]{3,2,1,0:T(8,128)(2,1)}, bf16[2,3,768,256]{3,2,1,0:T(8,128)(2,1)}, u32[]{:S(2)}, u32[]{:S(2)}) collective-permute-start(bf16[2,3,768,256]{3,2,1,0:T(8,128)(2,1)} %copy-done.1), channel_id=1, source_target_pairs={{0,8},{8,0},{16,24},{24,16},{1,9},{9,1},{17,25},{25,17},{2,10},{10... | collective-permute-start | bytes 7077896 | tf_op jit(solution)/shard_map/ppermute | solution.py:52
  152.0 11.6 %collective-permute-start.9 = (bf16[2,3,768,256]{3,2,1,0:T(8,128)(2,1)}, bf16[2,3,768,256]{3,2,1,0:T(8,128)(2,1)}, u32[]{:S(2)}, u32[]{:S(2)}) collective-permute-start(bf16[2,3,768,256]{3,2,1,0:T(8,128)(2,1)} %collective-permute-done.4.refs_1_.refs_6_.refs_3_), channel_id=1, source_target_pairs={{0,8},{8,0},{16,24},{24,16},{1,9},{9,1},{17,25},{25,17},{2,10},{10... | collective-permute-start | bytes 7077896 | tf_op jit(solution)/shard_map/ppermute | solution.py:52
  153.6 8.3 %collective-permute-start.14 = (bf16[1,3,768,256]{3,2,1,0:T(8,128)(2,1)}, bf16[1,3,768,256]{3,2,1,0:T(8,128)(2,1)}, u32[]{:S(2)}, u32[]{:S(2)}) collective-permute-start(bf16[1,3,768,256]{3,2,1,0:T(8,128)(2,1)} %collective-permute-done.13.refs_4_.refs_9_.refs_6_), channel_id=1, source_target_pairs={{0,8},{8,0},{16,24},{24,16},{1,9},{9,1},{17,25},{25,17},{2,10},{10... | collective-permute-start | bytes 3538952 | tf_op jit(solution)/shard_map/ppermute | solution.py:52
  153.6 10.0 %collective-permute-start.12 = (bf16[1,3,768,256]{3,2,1,0:T(8,128)(2,1)}, bf16[1,3,768,256]{3,2,1,0:T(8,128)(2,1)}, u32[]{:S(2)}, u32[]{:S(2)}) collective-permute-start(bf16[1,3,768,256]{3,2,1,0:T(8,128)(2,1)} %collective-permute-done.11.refs_3_.refs_8_.refs_5_), channel_id=1, source_target_pairs={{0,8},{8,0},{16,24},{24,16},{1,9},{9,1},{17,25},{25,17},{2,10},{10... | collective-permute-start | bytes 3538952 | tf_op jit(solution)/shard_map/ppermute | solution.py:52
  154.1 15.4 %collective-permute-start.15 = (bf16[192,1536]{1,0:T(8,128)(2,1)}, bf16[192,1536]{1,0:T(8,128)(2,1)S(1)}, u32[]{:S(2)}, u32[]{:S(2)}) collective-permute-start(bf16[192,1536]{1,0:T(8,128)(2,1)} %get-tuple-element.139), channel_id=1, source_target_pairs={{0,1},{1,0},{2,3},{3,2},{4,5},{5,4},{6,7},{7,6},{8,9},{9,8},{10,11... | collective-permute-start | bytes 1769480 | tf_op jit(solution)/shard_map/ppermute | solution.py:52
  163.6 7.7 %copy-start = (bf16[4,192,1664]{2,1,0:T(8,128)(2,1)}, bf16[4,192,1664]{2,1,0:T(8,128)(2,1)S(1)}, u32[]{:S(2)}) copy-start(bf16[4,192,1664]{2,1,0:T(8,128)(2,1)S(1)} %all-to-all-done.2.og_ref.refs_3_.refs_1_) | copy-start | bytes 7667716
  172.4 14.9 %copy-start.10 = (bf16[192,1536]{1,0:T(8,128)(2,1)}, bf16[192,1536]{1,0:T(8,128)(2,1)S(1)}, u32[]{:S(2)}) copy-start(bf16[192,1536]{1,0:T(8,128)(2,1)S(1)} %multiply_convert_fusion.refs_1_.refs_2_) | copy-start | bytes 1769476
  172.4 26.1 %collective-permute-start.16 = (bf16[192,1536]{1,0:T(8,128)(2,1)S(1)}, bf16[192,1536]{1,0:T(8,128)(2,1)S(1)}, u32[]{:S(2)}, u32[]{:S(2)}) collective-permute-start(bf16[192,1536]{1,0:T(8,128)(2,1)S(1)} %multiply_convert_fusion.refs_1_.refs_2_), channel_id=1, source_target_pairs={{0,2},{2,0},{4,6},{6,4},{1,3},{3,1},{5,7},{7,5},{8,10},{10,8},{12,... | collective-permute-start | bytes 1769480 | tf_op jit(solution)/shard_map/ppermute | solution.py:52
  174.5 42.4 %collective-permute-start.17 = (bf16[192,1536]{1,0:T(8,128)(2,1)S(1)}, bf16[192,1536]{1,0:T(8,128)(2,1)S(1)}, u32[]{:S(2)}, u32[]{:S(2)}) collective-permute-start(bf16[192,1536]{1,0:T(8,128)(2,1)S(1)} %multiply_convert_fusion.refs_1_.refs_2_), channel_id=1, source_target_pairs={{0,4},{2,6},{4,0},{6,2},{1,5},{3,7},{5,1},{7,3},{8,12},{10,14},{12... | collective-permute-start | bytes 1769480 | tf_op jit(solution)/shard_map/ppermute | solution.py:52
  176.8 40.1 %collective-permute-start.18 = (bf16[192,1536]{1,0:T(8,128)(2,1)S(1)}, bf16[192,1536]{1,0:T(8,128)(2,1)S(1)}, u32[]{:S(2)}, u32[]{:S(2)}) collective-permute-start(bf16[192,1536]{1,0:T(8,128)(2,1)S(1)} %multiply_convert_fusion.refs_1_.refs_2_), channel_id=1, source_target_pairs={{0,6},{2,4},{4,2},{6,0},{1,7},{3,5},{5,3},{7,1},{8,14},{10,12},{12... | collective-permute-start | bytes 1769480 | tf_op jit(solution)/shard_map/ppermute | solution.py:52
  236.0 60.4 %collective-permute-start.20 = (bf16[192,1536]{1,0:T(8,128)(2,1)}, bf16[192,1536]{1,0:T(8,128)(2,1)S(1)}, u32[]{:S(2)}, u32[]{:S(2)}) collective-permute-start(bf16[192,1536]{1,0:T(8,128)(2,1)} %get-tuple-element.156), channel_id=1, source_target_pairs={{0,4},{2,6},{4,0},{6,2},{1,5},{3,7},{5,1},{7,3},{8,12},{10,14},{12... | collective-permute-start | bytes 1769480 | tf_op jit(solution)/shard_map/ppermute | solution.py:52
  247.3 49.2 %collective-permute-start.21 = (bf16[192,1536]{1,0:T(8,128)(2,1)}, bf16[192,1536]{1,0:T(8,128)(2,1)S(1)}, u32[]{:S(2)}, u32[]{:S(2)}) collective-permute-start(bf16[192,1536]{1,0:T(8,128)(2,1)} %get-tuple-element.157), channel_id=1, source_target_pairs={{0,6},{2,4},{4,2},{6,0},{1,7},{3,5},{5,3},{7,1},{8,14},{10,12},{12... | collective-permute-start | bytes 1769480 | tf_op jit(solution)/shard_map/ppermute | solution.py:52
  248.7 47.8 %collective-permute-start.19 = (bf16[192,1536]{1,0:T(8,128)(2,1)}, bf16[192,1536]{1,0:T(8,128)(2,1)S(1)}, u32[]{:S(2)}, u32[]{:S(2)}) collective-permute-start(bf16[192,1536]{1,0:T(8,128)(2,1)} %get-tuple-element.155), channel_id=1, source_target_pairs={{0,2},{2,0},{4,6},{6,4},{1,3},{3,1},{5,7},{7,5},{8,10},{10,8},{12,... | collective-permute-start | bytes 1769480 | tf_op jit(solution)/shard_map/ppermute | solution.py:52
  285.8 10.7 %copy-start.4 = (f32[192,1536]{1,0:T(8,128)S(1)}, f32[192,1536]{1,0:T(8,128)}, u32[]{:S(2)}) copy-start(f32[192,1536]{1,0:T(8,128)} %copy-done.3) | copy-start | bytes 3538948
  285.8 10.7 %copy-start.23 = (bf16[192,1536]{1,0:T(8,128)(2,1)S(1)}, bf16[192,1536]{1,0:T(8,128)(2,1)}, u32[]{:S(2)}) copy-start(bf16[192,1536]{1,0:T(8,128)(2,1)} %get-tuple-element.154) | copy-start | bytes 1769476
  285.9 10.7 %copy-start.37 = (f32[192]{0:T(256)S(1)}, f32[192]{0:T(256)}, u32[]{:S(2)}) copy-start(f32[192]{0:T(256)} %copy-done.36) | copy-start | bytes 2308
  296.5 8.3 %collective-permute-start.22 = (bf16[4,3,768,256]{3,2,1,0:T(8,128)(2,1)}, bf16[4,3,768,256]{3,2,1,0:T(8,128)(2,1)}, u32[]{:S(2)}, u32[]{:S(2)}) collective-permute-start(bf16[4,3,768,256]{3,2,1,0:T(8,128)(2,1)} %get-tuple-element.159), channel_id=1, source_target_pairs={{0,8},{8,0},{16,24},{24,16},{1,9},{9,1},{17,25},{25,17},{2,10},{10... | collective-permute-start | bytes 14155784 | tf_op jit(solution)/shard_map/ppermute | solution.py:52
  299.7 59.6 %all-to-all-start.4 = ((bf16[4,192,1536]{2,1,0:T(8,128)(2,1)}), bf16[4,192,1536]{2,1,0:T(8,128)(2,1)}, u32[]{:S(2)}, u32[]{:S(2)}) async-start(bf16[4,192,1536]{2,1,0:T(8,128)(2,1)} %mix_rows.1), calls=%async_computation.4 | async-start | bytes 4718592 | tf_op jit(solution)/shard_map/all_to_all | solution.py:90
  308.4 66.6 %collective-permute-start.25 = (bf16[4,3,768,256]{3,2,1,0:T(8,128)(2,1)}, bf16[4,3,768,256]{3,2,1,0:T(8,128)(2,1)}, u32[]{:S(2)}, u32[]{:S(2)}) collective-permute-start(bf16[4,3,768,256]{3,2,1,0:T(8,128)(2,1)} %get-tuple-element.175), channel_id=1, source_target_pairs={{0,8},{8,0},{16,24},{24,16},{1,9},{9,1},{17,25},{25,17},{2,10},{10... | collective-permute-start | bytes 14155784 | tf_op jit(solution)/shard_map/ppermute | solution.py:52
  308.6 16.5 %collective-permute-start.23 = (bf16[192,1536]{1,0:T(8,128)(2,1)}, bf16[192,1536]{1,0:T(8,128)(2,1)}, u32[]{:S(2)}, u32[]{:S(2)}) collective-permute-start(bf16[192,1536]{1,0:T(8,128)(2,1)} %get-tuple-element.296.refs_7_.refs_0_), channel_id=1, source_target_pairs={{0,1},{1,0},{2,3},{3,2},{4,5},{5,4},{6,7},{7,6},{8,9},{9,8},{10,11... | collective-permute-start | bytes 1769480 | tf_op jit(solution)/shard_map/ppermute | solution.py:52
  312.7 62.4 %collective-permute-start.26 = (bf16[2,3,768,256]{3,2,1,0:T(8,128)(2,1)}, bf16[2,3,768,256]{3,2,1,0:T(8,128)(2,1)}, u32[]{:S(2)}, u32[]{:S(2)}) collective-permute-start(bf16[2,3,768,256]{3,2,1,0:T(8,128)(2,1)} %pair_sum.3), channel_id=1, source_target_pairs={{0,1},{1,0},{2,3},{3,2},{4,5},{5,4},{6,7},{7,6},{8,9},{9,8},{10,11... | collective-permute-start | bytes 7077896 | tf_op jit(solution)/shard_map/ppermute | solution.py:52
  314.2 60.8 %collective-permute-start.27 = (bf16[2,3,768,256]{3,2,1,0:T(8,128)(2,1)}, bf16[2,3,768,256]{3,2,1,0:T(8,128)(2,1)S(1)}, u32[]{:S(2)}, u32[]{:S(2)}) collective-permute-start(bf16[2,3,768,256]{3,2,1,0:T(8,128)(2,1)} %pair_sum.2), channel_id=1, source_target_pairs={{0,16},{8,24},{16,0},{24,8},{1,17},{9,25},{17,1},{25,9},{2,18},{10... | collective-permute-start | bytes 7077896 | tf_op jit(solution)/shard_map/ppermute | solution.py:52
  367.0 13.5 %collective-permute-start.24 = (bf16[2,384,1536]{2,1,0:T(8,128)(2,1)}, bf16[2,384,1536]{2,1,0:T(8,128)(2,1)}, u32[]{:S(2)}, u32[]{:S(2)}) collective-permute-start(bf16[2,384,1536]{2,1,0:T(8,128)(2,1)} %get-tuple-element.172), channel_id=1, source_target_pairs={{0,8},{8,0},{16,24},{24,16},{1,9},{9,1},{17,25},{25,17},{2,10},{10... | collective-permute-start | bytes 7077896 | tf_op jit(solution)/shard_map/ppermute | solution.py:52
  367.0 45.4 %all-to-all-start.5 = ((bf16[4,512,384]{2,1,0:T(8,128)(2,1)}), bf16[4,512,384]{2,1,0:T(8,128)(2,1)}, u32[]{:S(2)}, u32[]{:S(2)}) async-start(bf16[4,512,384]{2,1,0:T(8,128)(2,1)} %get-tuple-element.183), calls=%async_computation.5 | async-start | bytes 3145728 | tf_op jit(solution)/shard_map/all_to_all | solution.py:90
  375.0 5.5 %copy-start.7 = (bf16[2,3,768,256]{3,2,1,0:T(8,128)(2,1)}, bf16[2,3,768,256]{3,2,1,0:T(8,128)(2,1)S(1)}, u32[]{:S(2)}) copy-start(bf16[2,3,768,256]{3,2,1,0:T(8,128)(2,1)S(1)} %collective-permute-done.27.refs_2_) | copy-start | bytes 7077892
  375.1 5.5 %copy-start.24 = (bf16[384,1536]{1,0:T(8,128)(2,1)S(1)}, bf16[384,1536]{1,0:T(8,128)(2,1)}, u32[]{:S(2)}) copy-start(bf16[384,1536]{1,0:T(8,128)(2,1)} %get-tuple-element.171) | copy-start | bytes 3538948
  380.5 29.2 %copy-start.25 = (bf16[384,1536]{1,0:T(8,128)(2,1)S(1)}, bf16[384,1536]{1,0:T(8,128)(2,1)}, u32[]{:S(2)}) copy-start(bf16[384,1536]{1,0:T(8,128)(2,1)} %get-tuple-element.181) | copy-start | bytes 3538948
  382.2 27.5 %collective-permute-start.28 = (bf16[384,1536]{1,0:T(8,128)(2,1)S(1)}, bf16[384,1536]{1,0:T(8,128)(2,1)S(1)}, u32[]{:S(2)}, u32[]{:S(2)}) collective-permute-start(bf16[384,1536]{1,0:T(8,128)(2,1)S(1)} %fusion.1), channel_id=1, source_target_pairs={{0,16},{8,24},{16,0},{24,8},{1,17},{9,25},{17,1},{25,9},{2,18},{10... | collective-permute-start | bytes 3538952 | tf_op jit(solution)/shard_map/ppermute | solution.py:52
  382.8 29.7 %collective-permute-start.29 = (bf16[3,768,256]{2,1,0:T(8,128)(2,1)S(1)}, bf16[3,768,256]{2,1,0:T(8,128)(2,1)}, u32[]{:S(2)}, u32[]{:S(2)}) collective-permute-start(bf16[3,768,256]{2,1,0:T(8,128)(2,1)S(1)} %get-tuple-element.300), channel_id=1, source_target_pairs={{0,1},{1,0},{2,3},{3,2},{4,5},{5,4},{6,7},{7,6},{8,9},{9,8},{10,11... | collective-permute-start | bytes 3538952 | tf_op jit(solution)/shard_map/ppermute | solution.py:52
  419.0 14.3 %collective-permute-start.32 = (bf16[192,1536]{1,0:T(8,128)(2,1)}, bf16[192,1536]{1,0:T(8,128)(2,1)}, u32[]{:S(2)}, u32[]{:S(2)}) collective-permute-start(bf16[192,1536]{1,0:T(8,128)(2,1)} %get-tuple-element.189), channel_id=1, source_target_pairs={{0,1},{1,0},{2,3},{3,2},{4,5},{5,4},{6,7},{7,6},{8,9},{9,8},{10,11... | collective-permute-start | bytes 1769480 | tf_op jit(solution)/shard_map/ppermute | solution.py:52
  419.5 15.3 %collective-permute-start.30 = (bf16[2,384,640]{2,1,0:T(8,128)(2,1)}, bf16[2,384,640]{2,1,0:T(8,128)(2,1)}, u32[]{:S(2)}, u32[]{:S(2)}) collective-permute-start(bf16[2,384,640]{2,1,0:T(8,128)(2,1)} %get-tuple-element.186), channel_id=1, source_target_pairs={{0,8},{8,0},{16,24},{24,16},{1,9},{9,1},{17,25},{25,17},{2,10},{10... | collective-permute-start | bytes 2949128 | tf_op jit(solution)/shard_map/ppermute | solution.py:52
  419.5 4.6 copy-start.6
  419.5 33.8 %all-to-all-start.6 = ((bf16[4,96,1536]{2,1,0:T(8,128)(2,1)}), bf16[4,96,1536]{2,1,0:T(8,128)(2,1)S(1)}, u32[]{:S(2)}, u32[]{:S(2)}) async-start(bf16[4,96,1536]{2,1,0:T(8,128)(2,1)} %bitcast.57), calls=%async_computation.6 | async-start | bytes 2359296 | tf_op jit(solution)/shard_map/all_to_all | solution.py:90
  424.3 9.0 %copy-start.16 = (f32[192,1536]{1,0:T(8,128)S(1)}, f32[192,1536]{1,0:T(8,128)}, u32[]{:S(2)}) copy-start(f32[192,1536]{1,0:T(8,128)} %get-tuple-element.188) | copy-start | bytes 3538948
  436.1 11.2 %collective-permute-start.31 = (bf16[384,640]{1,0:T(8,128)(2,1)S(1)}, bf16[384,640]{1,0:T(8,128)(2,1)}, u32[]{:S(2)}, u32[]{:S(2)}) collective-permute-start(bf16[384,640]{1,0:T(8,128)(2,1)S(1)} %fusion.12), channel_id=1, source_target_pairs={{0,16},{8,24},{16,0},{24,8},{1,17},{9,25},{17,1},{25,9},{2,18},{10... | collective-permute-start | bytes 1474568 | tf_op jit(solution)/shard_map/ppermute | solution.py:52
  447.3 40.7 %collective-permute-start.34 = (bf16[3,768,256]{2,1,0:T(8,128)(2,1)}, bf16[3,768,256]{2,1,0:T(8,128)(2,1)S(1)}, u32[]{:S(2)}, u32[]{:S(2)}) collective-permute-start(bf16[3,768,256]{2,1,0:T(8,128)(2,1)} %get-tuple-element.195), channel_id=1, source_target_pairs={{0,16},{8,24},{16,0},{24,8},{1,17},{9,25},{17,1},{25,9},{2,18},{10... | collective-permute-start | bytes 3538952 | tf_op jit(solution)/shard_map/ppermute | solution.py:52
  456.0 45.3 %all-to-all-start.7 = ((bf16[4,96,640]{2,1,0:T(8,128)(2,1)}), bf16[4,96,640]{2,1,0:T(8,128)(2,1)}, u32[]{:S(2)}, u32[]{:S(2)}) async-start(bf16[4,96,640]{2,1,0:T(8,128)(2,1)} %bitcast.59), calls=%async_computation.7 | async-start | bytes 983040 | tf_op jit(solution)/shard_map/all_to_all | solution.py:90
  461.6 16.4 %copy-start.22 = (bf16[192,1536]{1,0:T(8,128)(2,1)}, bf16[192,1536]{1,0:T(8,128)(2,1)S(1)}, u32[]{:S(2)}) copy-start(bf16[192,1536]{1,0:T(8,128)(2,1)S(1)} %add_convert_fusion.3.refs_0_) | copy-start | bytes 1769476
  461.6 16.4 %collective-permute-start.33 = (bf16[192,1536]{1,0:T(8,128)(2,1)S(1)}, bf16[192,1536]{1,0:T(8,128)(2,1)}, u32[]{:S(2)}, u32[]{:S(2)}) collective-permute-start(bf16[192,1536]{1,0:T(8,128)(2,1)S(1)} %add_convert_fusion.3.refs_0_), channel_id=1, source_target_pairs={{0,1},{1,0},{2,3},{3,2},{4,5},{5,4},{6,7},{7,6},{8,9},{9,8},{10,11... | collective-permute-start | bytes 1769480 | tf_op jit(solution)/shard_map/ppermute | solution.py:52
  463.2 34.9 %collective-permute-start.35 = (bf16[192,1536]{1,0:T(8,128)(2,1)S(1)}, bf16[192,1536]{1,0:T(8,128)(2,1)S(1)}, u32[]{:S(2)}, u32[]{:S(2)}) collective-permute-start(bf16[192,1536]{1,0:T(8,128)(2,1)S(1)} %copy-done.21), channel_id=1, source_target_pairs={{0,1},{1,0},{2,3},{3,2},{4,5},{5,4},{6,7},{7,6},{8,9},{9,8},{10,11... | collective-permute-start | bytes 1769480 | tf_op jit(solution)/shard_map/ppermute | solution.py:52
  467.4 12.9 %copy-start.27 = (f32[768,96]{0,1:T(8,128)S(1)}, f32[768,96]{0,1:T(8,128)}, u32[]{:S(2)}) copy-start(f32[768,96]{0,1:T(8,128)} %param.26) | copy-start | bytes 884740
  498.1 5.8 %copy-start.34 = (f32[768,96]{1,0:T(8,128)S(1)}, f32[768,96]{1,0:T(8,128)}, u32[]{:S(2)}) copy-start(f32[768,96]{1,0:T(8,128)} %get-tuple-element.277) | copy-start | bytes 884740
  498.1 6.6 %copy-start.33 = (f32[768,96]{1,0:T(8,128)S(1)}, f32[768,96]{1,0:T(8,128)}, u32[]{:S(2)}) copy-start(f32[768,96]{1,0:T(8,128)} %get-tuple-element.278) | copy-start | bytes 884740
  502.3 7.5 %collective-permute-start.36 = (f32[2,96]{1,0:T(2,128)S(1)}, f32[2,96]{1,0:T(2,128)S(1)}, u32[]{:S(2)}, u32[]{:S(2)}) collective-permute-start(f32[2,96]{1,0:T(2,128)S(1)} %bitcast.60), channel_id=1, source_target_pairs={{0,1},{1,0},{2,3},{3,2},{4,5},{5,4},{6,7},{7,6},{8,9},{9,8},{10,11... | collective-permute-start | bytes 2312 | tf_op jit(solution)/shard_map/ppermute | solution.py:52
  (24 other events, 50.1 us)
